TPU v7x, 32 devices: a whole 2x2x4 slice. The times are simulated.
32 devices in a mesh: dp: 8 (over y, x, core), ctx: 4 (over z).
Axes of the slice: x: 2, y: 2, z: 4, core: 2. Of those that a mesh axis runs over, the one named last changes fastest.
Arguments:
- frames_in: bfloat16 [8, 256, 768], P('dp', 'ctx'), may hold values from -6 to 6
- segment_ids: int32 [8, 256], P('dp'), may hold values from 0 to 4, as said below
- span_ids: int32 [8, 256], P('dp'), may hold values from 0 to 3, as said below
- ffn_gain: float32 [768], replicated, may hold values from 0.1 to 1.9
- w_up: bfloat16 [768, 3072], P('dp', 'ctx'), may hold values from -0.21875 to 0.21875
- w_down: bfloat16 [768, 3072], P('dp', 'ctx'), may hold values from -0.109375 to 0.109375
- attn_gain: float32 [768], replicated, may hold values from 0.1 to 1.9
- w_query: bfloat16 [768, 2048], P('dp', 'ctx'), may hold values from -0.21875 to 0.21875
- w_key: bfloat16 [768, 2048], P('dp', 'ctx'), may hold values from -0.21875 to 0.21875
- w_value: bfloat16 [768, 2048], P('dp', 'ctx'), may hold values from -0.21875 to 0.21875
- w_out: bfloat16 [768, 2048], P('dp', 'ctx'), may hold values from -0.125 to 0.125
- offset_bias: float32 [16, 9], P('ctx'), may hold values from -2 to 257
- cotangent: bfloat16 [8, 256, 768], P('dp', 'ctx'), may hold values from -6 to 6
Outputs:
- block_out: bfloat16 [8, 256, 768], P('dp', 'ctx')
- grad_up: float32 [768, 3072], P('dp', 'ctx')
- grad_down: float32 [768, 3072], P('dp', 'ctx')
- grad_query: float32 [768, 2048], P('dp', 'ctx')
- grad_key: float32 [768, 2048], P('dp', 'ctx')
- grad_value: float32 [768, 2048], P('dp', 'ctx')
- grad_out: float32 [768, 2048], P('dp', 'ctx')
Inputs may be any that keep to these rules, and one draw needn't show every extreme that they name: `segment_ids`: in each stream the utterance number starts at 0 and never falls; every utterance but the stream's last has 56 to 224 frames. `span_ids`: A frame's span number is its position within its utterance divided by 64, rounded down.
All inputs are finite; a program needn't handle non-finite values.
Results may differ from a plain program's by a relative error of at most 0.024.
Values may be sent and summed in bfloat16 or wider, within the bound.
No kernel may reach another device: no remote copies, remote signals or barrier semaphores. Data moves between devices by JAX's collectives and lax.ppermute only.
A program may use at most 128 MiB of HBM per device.

v0:
```python
import math

import jax
import jax.numpy as jnp
from jax import lax
from jax.sharding import PartitionSpec as P

SPAN = 64


def layer_norm(values, gain):
    center = values - jnp.mean(values, axis=-1, keepdims=True)
    variance = jnp.mean(center * center, axis=-1, keepdims=True)
    return center * lax.rsqrt(variance + 1e-05) * gain


def norm_slope(values, upstream, gain):
    center = values - jnp.mean(values, axis=-1, keepdims=True)
    variance = jnp.mean(center * center, axis=-1, keepdims=True)
    inverse = lax.rsqrt(variance + 1e-05)
    normed = center * inverse
    scaled = upstream * gain
    first_mean = jnp.mean(scaled, axis=-1, keepdims=True)
    second_mean = jnp.mean(scaled * normed, axis=-1, keepdims=True)
    return inverse * (scaled - first_mean - normed * second_mean)


def silu_slope(pre):
    sigma = jax.nn.sigmoid(pre)
    return sigma * (1.0 + pre * (1.0 - sigma))


def pad_rows(values, before_rows, after_rows, fill):
    widths = [(before_rows, after_rows)] + [(0, 0)] * (values.ndim - 1)
    return jnp.pad(values, widths, constant_values=fill)


def span_windows(padded, first_row, per_group, span_rows, window_rows):
    slab = lax.dynamic_slice_in_dim(padded, first_row, (per_group - 1) * span_rows + window_rows, 0)
    return jnp.stack(
        [slab[index * span_rows : index * span_rows + window_rows] for index in range(per_group)]
    )


def fold_windows(windows, span_rows):
    per_group, window_rows = (windows.shape[0], windows.shape[1])
    slab_rows = (per_group - 1) * span_rows + window_rows
    total = jnp.zeros((slab_rows,) + windows.shape[2:], jnp.float32)
    for index in range(per_group):
        total = total + pad_rows(
            windows[index], index * span_rows, slab_rows - index * span_rows - window_rows, 0.0
        )
    return total


def per_device(
    frames_in,
    segment_ids,
    span_ids,
    ffn_gain,
    w_up,
    w_down,
    attn_gain,
    w_query,
    w_key,
    w_value,
    w_out,
    offset_bias,
    cotangent,
):
    own_rows = frames_in.shape[1]
    inputs_all, cot_all = (
        lax.all_gather(frames_in, "ctx", axis=1, tiled=True),
        lax.all_gather(cotangent, "ctx", axis=1, tiled=True),
    )
    inputs_all = inputs_all[0]
    cot_all = cot_all[0]
    frames = inputs_all.shape[0]
    query_full, key_full, value_full, out_full, up_full, down_full = (
        lax.all_gather(w_query, "dp", axis=0, tiled=True),
        lax.all_gather(w_key, "dp", axis=0, tiled=True),
        lax.all_gather(w_value, "dp", axis=0, tiled=True),
        lax.all_gather(w_out, "dp", axis=0, tiled=True),
        lax.all_gather(w_up, "dp", axis=0, tiled=True),
        lax.all_gather(w_down, "dp", axis=0, tiled=True),
    )
    head_count = offset_bias.shape[0]
    head_width = query_full.shape[1] // head_count
    score_scale = head_width ** (-0.5)
    start_row = lax.axis_index("ctx") * own_rows
    window = offset_bias.shape[1] - 1
    before_spans = window + 1
    span_rows = SPAN
    window_rows = (before_spans + 2) * span_rows
    span_count = frames // span_rows
    per_group = math.gcd(span_count, max(1, 512 // span_rows))
    group_count = span_count // per_group
    group_rows = per_group * span_rows
    segments = segment_ids[0]
    spans = span_ids[0]
    segment_pad = pad_rows(segments, before_spans * span_rows, span_rows, -1)
    spans_pad = pad_rows(spans, before_spans * span_rows, span_rows, 0)
    ffn_normed = layer_norm(inputs_all.astype(jnp.float32), ffn_gain).astype(jnp.bfloat16)
    ffn_pre = jnp.dot(ffn_normed, up_full, preferred_element_type=jnp.float32)
    ffn_hidden = jax.nn.silu(ffn_pre).astype(jnp.bfloat16)
    ffn_part = jnp.einsum("fj,dj->fd", ffn_hidden, down_full, preferred_element_type=jnp.float32)
    ffn_sum = lax.psum(ffn_part.astype(jnp.bfloat16), "ctx").astype(jnp.float32)
    mid_all = inputs_all.astype(jnp.float32) + 0.5 * ffn_sum
    attn_normed = layer_norm(mid_all, attn_gain).astype(jnp.bfloat16)
    mid_own = lax.dynamic_slice_in_dim(mid_all, start_row, own_rows, 0)

    def project(weight):
        made = jnp.dot(attn_normed, weight, preferred_element_type=jnp.float32)
        return made.astype(jnp.bfloat16).reshape(frames, head_count, head_width)

    query_rows = project(query_full)
    key_rows = project(key_full)
    value_rows = project(value_full)
    key_pad = pad_rows(key_rows, before_spans * span_rows, span_rows, 0.0)
    value_pad = pad_rows(value_rows, before_spans * span_rows, span_rows, 0.0)

    def group_weights(group):
        first_row = group * group_rows
        query_group = lax.dynamic_slice_in_dim(query_rows, first_row, group_rows, 0)
        query_group = query_group.reshape(per_group, span_rows, head_count, head_width)
        key_window = span_windows(key_pad, first_row, per_group, span_rows, window_rows)
        value_window = span_windows(value_pad, first_row, per_group, span_rows, window_rows)
        seg_query = lax.dynamic_slice_in_dim(segments, first_row, group_rows, 0).reshape(
            per_group, span_rows
        )
        span_query = lax.dynamic_slice_in_dim(spans, first_row, group_rows, 0).reshape(
            per_group, span_rows
        )
        seg_key = span_windows(segment_pad, first_row, per_group, span_rows, window_rows)
        span_key = span_windows(spans_pad, first_row, per_group, span_rows, window_rows)
        distance = span_query[:, :, None] - span_key[:, None, :]
        allowed = (
            (seg_query[:, :, None] == seg_key[:, None, :]) & (distance >= 0) & (distance <= window)
        )
        bias = jnp.zeros((per_group, head_count, span_rows, window_rows), jnp.float32)
        for offset_step in range(window + 1):
            bias = bias + jnp.where(
                distance[:, None] == offset_step,
                offset_bias[:, offset_step][None, :, None, None],
                0.0,
            )
        scores = (
            jnp.einsum(
                "bqhd,bkhd->bhqk", query_group, key_window, preferred_element_type=jnp.float32
            )
            * score_scale
            + bias
        )
        scores = jnp.where(allowed[:, None], scores, -1e30)
        top_score = jnp.max(scores, axis=-1, keepdims=True)
        expo = jnp.exp(scores - top_score)
        soft_weights = expo / jnp.sum(expo, axis=-1, keepdims=True)
        return (query_group, key_window, value_window, soft_weights)

    def group_context(group):
        unused_q, unused_k, value_window, soft_weights = group_weights(group)
        soft_low = soft_weights.astype(jnp.bfloat16)
        made = jnp.einsum(
            "bhqk,bkhd->bqhd", soft_low, value_window, preferred_element_type=jnp.float32
        )
        return made.astype(jnp.bfloat16).reshape(group_rows, head_count * head_width)

    context = lax.map(group_context, jnp.arange(group_count, dtype=jnp.int32)).reshape(
        frames, head_count * head_width
    )
    attn_own = lax.psum_scatter(
        jnp.einsum("fi,di->fd", context, out_full, preferred_element_type=jnp.float32).astype(
            jnp.bfloat16
        ),
        "ctx",
        scatter_dimension=0,
        tiled=True,
    ).astype(jnp.float32)
    block_out = (mid_own + attn_own).astype(jnp.bfloat16)[None]
    cot_scale = 1.0 / math.sqrt(lax.axis_size("dp") * frames)
    scaled_cot = (cot_all.astype(jnp.float32) * cot_scale).astype(jnp.bfloat16)
    grad_out = jnp.einsum("fd,fi->di", scaled_cot, context, preferred_element_type=jnp.float32)
    grad_context = jnp.dot(scaled_cot, out_full, preferred_element_type=jnp.float32)
    grad_context = grad_context.astype(jnp.bfloat16).reshape(frames, head_count, head_width)
    padded_rows = frames + (before_spans + 1) * span_rows
    empty = jnp.zeros((padded_rows, head_count, head_width), jnp.float32)

    def group_slopes(carry, group):
        key_total, value_total = carry
        first_row = group * group_rows
        query_group, key_window, value_window, soft_weights = group_weights(group)
        soft_low = soft_weights.astype(jnp.bfloat16)
        slope_group = lax.dynamic_slice_in_dim(grad_context, first_row, group_rows, 0)
        slope_group = slope_group.reshape(per_group, span_rows, head_count, head_width)
        grad_probs = jnp.einsum(
            "bqhd,bkhd->bhqk", slope_group, value_window, preferred_element_type=jnp.float32
        )
        row_total = jnp.sum(soft_weights * grad_probs, axis=-1, keepdims=True)
        grad_scores = (soft_weights * (grad_probs - row_total)).astype(jnp.bfloat16)
        query_slope = (
            jnp.einsum(
                "bhqk,bkhd->bqhd", grad_scores, key_window, preferred_element_type=jnp.float32
            )
            * score_scale
        )
        query_slope = query_slope.astype(jnp.bfloat16).reshape(group_rows, head_count * head_width)
        key_slope = (
            jnp.einsum(
                "bhqk,bqhd->bkhd", grad_scores, query_group, preferred_element_type=jnp.float32
            )
            * score_scale
        )
        value_slope = jnp.einsum(
            "bhqk,bqhd->bkhd", soft_low, slope_group, preferred_element_type=jnp.float32
        )
        key_slab = fold_windows(key_slope, span_rows)
        value_slab = fold_windows(value_slope, span_rows)
        slab_rows = key_slab.shape[0]
        key_total = lax.dynamic_update_slice_in_dim(
            key_total,
            lax.dynamic_slice_in_dim(key_total, first_row, slab_rows, 0) + key_slab,
            first_row,
            0,
        )
        value_total = lax.dynamic_update_slice_in_dim(
            value_total,
            lax.dynamic_slice_in_dim(value_total, first_row, slab_rows, 0) + value_slab,
            first_row,
            0,
        )
        return ((key_total, value_total), query_slope)

    totals, query_slopes = lax.scan(
        group_slopes, (empty, empty), jnp.arange(group_count, dtype=jnp.int32)
    )
    grad_q_rows = query_slopes.reshape(frames, head_count * head_width)
    first_key = before_spans * span_rows
    grad_k_rows = totals[0][first_key : first_key + frames].astype(jnp.bfloat16).reshape(frames, -1)
    grad_v_rows = totals[1][first_key : first_key + frames].astype(jnp.bfloat16).reshape(frames, -1)
    grad_query = jnp.einsum(
        "fd,fi->di", attn_normed, grad_q_rows, preferred_element_type=jnp.float32
    )
    grad_key = jnp.einsum("fd,fi->di", attn_normed, grad_k_rows, preferred_element_type=jnp.float32)
    grad_value = jnp.einsum(
        "fd,fi->di", attn_normed, grad_v_rows, preferred_element_type=jnp.float32
    )
    normed_part = jnp.einsum(
        "fi,di->fd", grad_q_rows, query_full, preferred_element_type=jnp.float32
    )
    normed_part = normed_part + jnp.einsum(
        "fi,di->fd", grad_k_rows, key_full, preferred_element_type=jnp.float32
    )
    normed_part = normed_part + jnp.einsum(
        "fi,di->fd", grad_v_rows, value_full, preferred_element_type=jnp.float32
    )
    grad_normed = lax.psum(normed_part.astype(jnp.bfloat16), "ctx").astype(jnp.float32)
    grad_mid = (
        scaled_cot.astype(jnp.float32) + norm_slope(mid_all, grad_normed, attn_gain)
    ).astype(jnp.bfloat16)
    grad_down = 0.5 * jnp.einsum(
        "fd,fj->dj", grad_mid, ffn_hidden, preferred_element_type=jnp.float32
    )
    grad_hidden = (
        0.5 * jnp.dot(grad_mid, down_full, preferred_element_type=jnp.float32) * silu_slope(ffn_pre)
    )
    grad_hidden = grad_hidden.astype(jnp.bfloat16)
    grad_up = jnp.einsum("fd,fj->dj", ffn_normed, grad_hidden, preferred_element_type=jnp.float32)
    summed = (
        lax.psum_scatter(
            grad_up.astype(jnp.bfloat16), "dp", scatter_dimension=0, tiled=True
        ).astype(jnp.float32),
        lax.psum_scatter(
            grad_down.astype(jnp.bfloat16), "dp", scatter_dimension=0, tiled=True
        ).astype(jnp.float32),
        lax.psum_scatter(
            grad_query.astype(jnp.bfloat16), "dp", scatter_dimension=0, tiled=True
        ).astype(jnp.float32),
        lax.psum_scatter(
            grad_key.astype(jnp.bfloat16), "dp", scatter_dimension=0, tiled=True
        ).astype(jnp.float32),
        lax.psum_scatter(
            grad_value.astype(jnp.bfloat16), "dp", scatter_dimension=0, tiled=True
        ).astype(jnp.float32),
        lax.psum_scatter(
            grad_out.astype(jnp.bfloat16), "dp", scatter_dimension=0, tiled=True
        ).astype(jnp.float32),
    )
    return (block_out, summed[0], summed[1], summed[2], summed[3], summed[4], summed[5])


def solution(mesh):
    placed = (
        P("dp", "ctx", None),
        P("dp", None),
        P("dp", None),
        P(),
        P("dp", "ctx"),
        P("dp", "ctx"),
        P(),
        P("dp", "ctx"),
        P("dp", "ctx"),
        P("dp", "ctx"),
        P("dp", "ctx"),
        P("ctx", None),
        P("dp", "ctx", None),
    )
    return jax.shard_map(
        per_device,
        mesh=mesh,
        in_specs=placed,
        out_specs=(
            P("dp", "ctx", None),
            P("dp", "ctx"),
            P("dp", "ctx"),
            P("dp", "ctx"),
            P("dp", "ctx"),
            P("dp", "ctx"),
            P("dp", "ctx"),
        ),
        check_vma=False,
    )
```

profile of v0, /device:TPU:0, one launch (start us, length us, event | category | flops | bytes accessed | tf_op | source)
XLA Modules:
  0.0 484.0 jit_solution(13432698486519639771)
XLA Ops:
  8.7 12.2 %all_gather.30 = bf16[768,512]{1,0:T(8,128)(2,1)S(1)} all-gather(bf16[96,512]{1,0:T(8,128)(2,1)} %param.23), channel_id=1, replica_groups=mesh['dp'=8,'ctx'=4] {'dp'}, dimensions={0}, use_global_device_ids=true | all-gather | bytes 884736 | tf_op jit(solution)/shard_map/all_gather | solution.py:83
  22.4 1.3 reduce.26
  23.8 1.3 reduce.25
  26.2 15.1 %all_gather.31 = bf16[1,256,768]{2,1,0:T(8,128)(2,1)S(1)} all-gather(bf16[1,64,768]{2,1,0:T(8,128)(2,1)} %param.25), channel_id=1, replica_groups=mesh['dp'=8,'ctx'=4] {'ctx'}, dimensions={1}, use_global_device_ids=true | all-gather | bytes 491520 | tf_op jit(solution)/shard_map/all_gather | solution.py:74
  43.6 15.1 %all_gather.24 = bf16[1,256,768]{2,1,0:T(8,128)(2,1)S(1)} all-gather(bf16[1,64,768]{2,1,0:T(8,128)(2,1)S(1)} %copy-done.26), channel_id=1, replica_groups=mesh['dp'=8,'ctx'=4] {'ctx'}, dimensions={1}, use_global_device_ids=true | all-gather | bytes 491520 | tf_op jit(solution)/shard_map/all_gather | solution.py:73
  59.1 10.3 %all_gather.27 = bf16[768,512]{1,0:T(8,128)(2,1)S(1)} all-gather(bf16[96,512]{1,0:T(8,128)(2,1)S(1)} %copy-done.23), channel_id=1, replica_groups=mesh['dp'=8,'ctx'=4] {'dp'}, dimensions={0}, use_global_device_ids=true | all-gather | bytes 884736 | tf_op jit(solution)/shard_map/all_gather | solution.py:82
  69.5 9.5 %all_gather.29 = bf16[768,512]{1,0:T(8,128)(2,1)S(1)} all-gather(bf16[96,512]{1,0:T(8,128)(2,1)S(1)} %copy-done.24), channel_id=1, replica_groups=mesh['dp'=8,'ctx'=4] {'dp'}, dimensions={0}, use_global_device_ids=true | all-gather | bytes 884736 | tf_op jit(solution)/shard_map/all_gather | solution.py:81
  79.0 10.3 %all_gather.28 = bf16[768,512]{1,0:T(8,128)(2,1)S(1)} all-gather(bf16[96,512]{1,0:T(8,128)(2,1)S(1)} %copy-done.25), channel_id=1, replica_groups=mesh['dp'=8,'ctx'=4] {'dp'}, dimensions={0}, use_global_device_ids=true | all-gather | bytes 884736 | tf_op jit(solution)/shard_map/all_gather | solution.py:80
  89.3 2.7 fusion.64
  92.0 2.8 convolution_convert_fusion.6
  95.1 2.3 fusion.24
  97.4 34.5 %all-reduce.15.cloned.1.call-done = bf16[256,768]{1,0:T(8,128)(2,1)} async-done(((bf16[256,768]{1,0:T(8,128)(2,1)}), bf16[256,768]{1,0:T(8,128)(2,1)}) %all-reduce.15.cloned.1.call-update) | async-done | bytes 393232 | tf_op jit(solution)/shard_map/psum | solution.py:107
  136.0 1.9 fusion.25
  138.4 2.0 fusion.29
  141.5 6.6 %add_select_fusion = f32[4,4,64,704]{3,2,1,0:T(8,128)S(1)} fusion(f32[4]{0:T(128)S(1)} %get-tuple-element.72, f32[4]{0:T(128)S(1)} %get-tuple-element.73, f32[4]{0:T(128)S(1)} %get-tuple-element.66, f32[4]{0:T(128)S(1)} %get-tuple-element.67, f32[4]{0:T(128)S(1)} %get-tuple-element.68, f32[4]{0:T(128)S(1)} %get-tuple-element.69, ...), kind=kOutput, calls=%fused_computation.16 | convolution fusion | flops 203292672 | bytes 7831696 | tf_op jit(solution)/shard_map/while/body/eval_jaxpr/bqhd,bkhd->bhqk/dot_general | solution.py:148
  148.1 3.5 fusion.67
  151.7 2.0 multiply_reduce_fusion
  155.5 1.4 fusion.5
  156.9 3.5 multiply_bitcast_fusion
  160.4 8.3 %convolution_bitcast_fusion = f32[4,704,4,128]{3,1,2,0:T(8,128)} fusion(bf16[4,64,4,128]{3,2,1,0:T(4,128)(2,1)S(1)} %copy-done.21, f32[4,4,64]{2,1,0:T(4,128)S(1)} %get-tuple-element.122, f32[4,4,64,704]{3,2,1,0:T(8,128)} %copy-done.1), kind=kOutput, calls=%fused_computation.19 | convolution fusion | flops 186713792 | bytes 8916992 | tf_op jit(solution)/shard_map/while/body/eval_jaxpr/bhqk,bqhd->bkhd/dot_general | solution.py:213
  171.1 3.1 slice_bitcast_fusion.7
  175.2 3.1 slice_bitcast_fusion.3
  179.1 1.8 copy.35
  180.9 1.4 convolution_add_fusion.1
  182.3 2.1 fusion.2
  184.4 5.8 %fusion.6 = bf16[4,64,4,128]{3,1,2,0:T(8,128)(2,1)S(1)} fusion(bf16[1,704,4,128]{3,1,2,0:T(8,128)(2,1)} %get-tuple-element.103, bf16[1,704,4,128]{3,1,2,0:T(8,128)(2,1)} %get-tuple-element.102, bf16[1,704,4,128]{3,1,2,0:T(8,128)(2,1)} %get-tuple-element.101, bf16[1,704,4,128]{3,1,2,0:T(8,128)(2,1)} %get-tuple-element.100, ...), kind=kOutput, calls=%fused_computation.59 | convolution fusion | flops 198379200 | bytes 6033408 | tf_op jit(solution)/shard_map/while/body/eval_jaxpr/bhqk,bkhd->bqhd/dot_general | solution.py:163
  191.7 1.3 convolution_convert_fusion.4
  193.1 1.3 convolution_convert_fusion.3
  194.5 1.3 convolution_convert_fusion.2
  195.9 1.3 convolution_convert_fusion.1
  197.5 23.7 %all-reduce.17.cloned.1.call-done = bf16[256,768]{1,0:T(8,128)(2,1)} async-done(((bf16[256,768]{1,0:T(8,128)(2,1)}), bf16[256,768]{1,0:T(8,128)(2,1)}) %all-reduce.17.cloned.1.call-update) | async-done | bytes 393232 | tf_op jit(solution)/shard_map/psum | solution.py:256
  221.2 1.4 fusion.20
  222.6 3.7 convolution_convert_fusion
  226.5 2.0 multiply_convert_fusion.1
  228.5 15.0 %reduce-scatter.8.cloned.1.call-done = bf16[64,768]{1,0:T(8,128)(2,1)} async-done(((bf16[256,768]{1,0:T(8,128)(2,1)}), bf16[64,768]{1,0:T(8,128)(2,1)}) %reduce-scatter.8.cloned.1.call-update) | async-done | bytes 98320 | tf_op jit(solution)/shard_map/reduce_scatter | solution.py:171
  243.5 1.6 fusion.54
  245.1 35.1 %reduce-scatter.14.cloned.1.call-done = bf16[96,512]{1,0:T(8,128)(2,1)} async-done(((bf16[768,512]{1,0:T(8,128)(2,1)}), bf16[96,512]{1,0:T(8,128)(2,1)}) %reduce-scatter.14.cloned.1.call-update) | async-done | bytes 98320 | tf_op jit(solution)/shard_map/reduce_scatter | solution.py:275
  280.2 1.6 convert_element_type.168
  281.8 36.9 %reduce-scatter.16.cloned.1.call-done = bf16[96,512]{1,0:T(8,128)(2,1)} async-done(((bf16[768,512]{1,0:T(8,128)(2,1)}), bf16[96,512]{1,0:T(8,128)(2,1)}) %reduce-scatter.16.cloned.1.call-update) | async-done | bytes 98320 | tf_op jit(solution)/shard_map/reduce_scatter | solution.py:278
  318.6 1.6 convert_element_type.170
  320.2 36.9 %reduce-scatter.18.cloned.1.call-done = bf16[96,512]{1,0:T(8,128)(2,1)} async-done(((bf16[768,512]{1,0:T(8,128)(2,1)}), bf16[96,512]{1,0:T(8,128)(2,1)}) %reduce-scatter.18.cloned.1.call-update) | async-done | bytes 98320 | tf_op jit(solution)/shard_map/reduce_scatter | solution.py:281
  357.1 1.6 convert_element_type.172
  358.7 36.9 %reduce-scatter.20.cloned.1.call-done = bf16[96,512]{1,0:T(8,128)(2,1)} async-done(((bf16[768,512]{1,0:T(8,128)(2,1)}), bf16[96,512]{1,0:T(8,128)(2,1)}) %reduce-scatter.20.cloned.1.call-update) | async-done | bytes 98320 | tf_op jit(solution)/shard_map/reduce_scatter | solution.py:284
  395.6 1.6 convert_element_type.174
  397.1 38.6 %reduce-scatter.10.cloned.1.call-done = bf16[96,768]{1,0:T(8,128)(2,1)} async-done(((bf16[768,768]{1,0:T(8,128)(2,1)}), bf16[96,768]{1,0:T(8,128)(2,1)}) %reduce-scatter.10.cloned.1.call-update) | async-done | bytes 147472 | tf_op jit(solution)/shard_map/reduce_scatter | solution.py:269
  435.8 1.6 convert_element_type.164
  437.4 38.4 %reduce-scatter.12.cloned.1.call-done = bf16[96,768]{1,0:T(8,128)(2,1)} async-done(((bf16[768,768]{1,0:T(8,128)(2,1)}), bf16[96,768]{1,0:T(8,128)(2,1)}) %reduce-scatter.12.cloned.1.call-update) | async-done | bytes 147472 | tf_op jit(solution)/shard_map/reduce_scatter | solution.py:272
  475.8 1.6 convert_element_type.166
  (126 shorter events, 20.6 us)
Async XLA Ops:
  7.2 36.1 %copy-start.22 = (f32[4,9]{1,0:T(4,128)S(1)}, f32[4,9]{1,0:T(4,128)}, u32[]{:S(2)}) copy-start(f32[4,9]{1,0:T(4,128)} %param.24) | copy-start | bytes 436
  7.2 36.4 %copy-start.26 = (bf16[1,64,768]{2,1,0:T(8,128)(2,1)S(1)}, bf16[1,64,768]{2,1,0:T(8,128)(2,1)}, u32[]{:S(2)}) copy-start(bf16[1,64,768]{2,1,0:T(8,128)(2,1)} %param.13) | copy-start | bytes 294916
  7.2 51.9 %copy-start.23 = (bf16[96,512]{1,0:T(8,128)(2,1)S(1)}, bf16[96,512]{1,0:T(8,128)(2,1)}, u32[]{:S(2)}) copy-start(bf16[96,512]{1,0:T(8,128)(2,1)} %param.22) | copy-start | bytes 294916
  7.2 62.3 %copy-start.24 = (bf16[96,512]{1,0:T(8,128)(2,1)S(1)}, bf16[96,512]{1,0:T(8,128)(2,1)}, u32[]{:S(2)}) copy-start(bf16[96,512]{1,0:T(8,128)(2,1)} %param.21) | copy-start | bytes 294916
  7.2 82.1 %all-gather.3.cloned.1.call-start = ((), (), s32[]{:S(2)}) async-start(), calls=%async_computation.7 | async-start | bytes 1327104 | tf_op jit(solution)/shard_map/all_gather | solution.py:84
  7.9 84.0 %all-gather.5.cloned.1.call-start = ((), (), s32[]{:S(2)}) async-start(), calls=%async_computation.8 | async-start | bytes 1327104 | tf_op jit(solution)/shard_map/all_gather | solution.py:85
  8.7 70.3 %copy-start.25 = (bf16[96,512]{1,0:T(8,128)(2,1)S(1)}, bf16[96,512]{1,0:T(8,128)(2,1)}, u32[]{:S(2)}) copy-start(bf16[96,512]{1,0:T(8,128)(2,1)} %param.20) | copy-start | bytes 294916
  8.7 123.2 %all-reduce.15.cloned.1.call-start = ((), (), s32[]{:S(2)}) async-start(), calls=%async_computation.9 | async-start | bytes 786432 | tf_op jit(solution)/shard_map/psum | solution.py:107
  21.0 22.6 %copy-start.3 = (bf16[768,512]{1,0:T(8,128)(2,1)}, bf16[768,512]{1,0:T(8,128)(2,1)S(1)}, u32[]{:S(2)}) copy-start(bf16[768,512]{1,0:T(8,128)(2,1)S(1)} %all_gather.30) | copy-start | bytes 2359300
  41.3 0.7 copy-start.17
  42.1 47.2 %copy-start.28 = (f32[768]{0:T(1024)S(1)}, f32[768]{0:T(1024)}, u32[]{:S(2)}) copy-start(f32[768]{0:T(1024)} %param.16) | copy-start | bytes 9220
  89.3 5.5 %copy-start.29 = (f32[256]{0:T(256)}, f32[256]{0:T(256)S(1)}, u32[]{:S(2)}) copy-start(f32[256]{0:T(256)S(1)} %add_rsqrt_fusion.1) | copy-start | bytes 3076
  94.8 39.6 %copy-start.27 = (f32[768]{0:T(1024)S(1)}, f32[768]{0:T(1024)}, u32[]{:S(2)}) copy-start(f32[768]{0:T(1024)} %param.19) | copy-start | bytes 9220
  94.8 126.4 %all-reduce.17.cloned.1.call-start = ((), (), s32[]{:S(2)}) async-start(), calls=%async_computation.11 | async-start | bytes 786432 | tf_op jit(solution)/shard_map/psum | solution.py:256
  148.0 3.6 copy-start.1
  148.1 3.6 copy-start.9
  148.1 3.6 copy-start.10
  148.1 3.6 copy-start.11
  148.1 3.6 copy-start.12
  148.1 3.6 copy-start.21
  153.7 1.1 copy-start.13
  153.7 1.3 copy-start.14
  153.7 1.5 copy-start.15
  153.7 1.7 copy-start.16
  155.5 1.4 copy-start.7
  178.3 2.6 copy-start.2
  184.4 6.0 %copy-start.4 = (bf16[768,512]{1,0:T(8,128)(2,1)S(1)}, bf16[768,512]{1,0:T(8,128)(2,1)}, u32[]{:S(2)}) copy-start(bf16[768,512]{1,0:T(8,128)(2,1)} %copy-done.3) | copy-start | bytes 2359300
  184.4 59.1 %reduce-scatter.8.cloned.1.call-start = ((), (), s32[]{:S(2)}) async-start(), calls=%async_computation.10 | async-start | bytes 491520 | tf_op jit(solution)/shard_map/reduce_scatter | solution.py:171
  190.2 2.9 copy-start.5
  190.4 4.0 copy-start.6
  191.6 4.2 copy-start.18
  191.7 88.5 %reduce-scatter.14.cloned.1.call-start = ((), (), s32[]{:S(2)}) async-start(), calls=%async_computation.14 | async-start | bytes 884736 | tf_op jit(solution)/shard_map/reduce_scatter | solution.py:275
  193.0 28.2 %copy-start = (bf16[256,768]{1,0:T(8,128)(2,1)S(1)}, bf16[256,768]{1,0:T(8,128)(2,1)}, u32[]{:S(2)}) copy-start(bf16[256,768]{1,0:T(8,128)(2,1)} %all-reduce.15.cloned.1.call-done) | copy-start | bytes 1179652
  193.0 125.6 %reduce-scatter.16.cloned.1.call-start = ((), (), s32[]{:S(2)}) async-start(), calls=%async_computation.15 | async-start | bytes 884736 | tf_op jit(solution)/shard_map/reduce_scatter | solution.py:278
  194.4 28.2 %copy-start.8 = (f32[256,768]{1,0:T(8,128)S(1)}, f32[256,768]{1,0:T(8,128)}, u32[]{:S(2)}) copy-start(f32[256,768]{1,0:T(8,128)} %fusion.64) | copy-start | bytes 2359300
  194.4 28.2 %copy-start.19 = (bf16[1,256,768]{2,1,0:T(8,128)(2,1)S(1)}, bf16[1,256,768]{2,1,0:T(8,128)(2,1)}, u32[]{:S(2)}) copy-start(bf16[1,256,768]{2,1,0:T(8,128)(2,1)} %copy-done.17) | copy-start | bytes 1179652
  194.4 162.6 %reduce-scatter.18.cloned.1.call-start = ((), (), s32[]{:S(2)}) async-start(), calls=%async_computation.16 | async-start | bytes 884736 | tf_op jit(solution)/shard_map/reduce_scatter | solution.py:281
  195.8 199.7 %reduce-scatter.20.cloned.1.call-start = ((), (), s32[]{:S(2)}) async-start(), calls=%async_computation.17 | async-start | bytes 884736 | tf_op jit(solution)/shard_map/reduce_scatter | solution.py:284
  197.2 238.6 %reduce-scatter.10.cloned.1.call-start = ((), (), s32[]{:S(2)}) async-start(), calls=%async_computation.12 | async-start | bytes 1327104 | tf_op jit(solution)/shard_map/reduce_scatter | solution.py:269
  222.6 3.8 copy-start.20
  226.4 249.4 %reduce-scatter.12.cloned.1.call-start = ((), (), s32[]{:S(2)}) async-start(), calls=%async_computation.13 | async-start | bytes 1327104 | tf_op jit(solution)/shard_map/reduce_scatter | solution.py:272
Sparse Core Ops, SparseCore 0:
  9.9 26.7 all-gather.2
  38.6 24.0 all-gather.4
  94.9 36.8 all-reduce.14
  184.5 36.6 all-reduce.16
  223.3 20.1 reduce-scatter.7
  246.9 33.2 reduce-scatter.13
  283.6 34.9 reduce-scatter.15
  322.1 34.9 reduce-scatter.17
  360.6 34.9 reduce-scatter.19
  399.0 36.7 reduce-scatter.9
  439.0 36.7 reduce-scatter.11
where the time goes:
time: 485 us; the launch traced here: 484 us
  waiting for transfers between devices  297 us (61%)
  blocking collectives  72.6 us (15%)
  matrix products  51.5 us (11%)
  other arithmetic  26.6 us (5%)
  local copies, waits for them, and re-layouts  20.5 us (4%)
  between operations  14.4 us (3%)
    reduce_scatter x1, waiting for transfers between devices, per_device(): lax.psum_scatter(grad_up.astype(jnp.bfloat16), 'dp', scatter_dimension=0,...  38.6 us
    reduce_scatter x1, waiting for transfers between devices, per_device(): lax.psum_scatter(grad_down.astype(jnp.bfloat16), 'dp', scatter_dimension=...  38.4 us
    reduce_scatter x1, waiting for transfers between devices, per_device(): lax.psum_scatter(grad_out.astype(jnp.bfloat16), 'dp', scatter_dimension=0...  36.9 us
    reduce_scatter x1, waiting for transfers between devices, per_device(): lax.psum_scatter(grad_value.astype(jnp.bfloat16), 'dp', scatter_dimension...  36.9 us
    reduce_scatter x1, waiting for transfers between devices, per_device(): lax.psum_scatter(grad_key.astype(jnp.bfloat16), 'dp', scatter_dimension=0...  36.9 us
    reduce_scatter x1, waiting for transfers between devices, per_device(): lax.psum_scatter(grad_query.astype(jnp.bfloat16), 'dp', scatter_dimension...  35.1 us
    psum x1, waiting for transfers between devices, per_device(): ffn_sum = lax.psum(ffn_part.astype(jnp.bfloat16), 'ctx').astype(jnp.float32)  34.5 us
    psum x1, waiting for transfers between devices, per_device(): lax.psum(normed_part.astype(jnp.bfloat16), 'ctx').astype(jnp.float32)  23.7 us
  transfers between devices with their start and end apart: 11, of which 9 were waited for; matrix products, arithmetic and copies ran while one was open for 8% of the time, Pallas kernels for 0%

commit v1 on v0

v1 whole, which is shorter than its diff:
```python
import functools
import math

import jax
import jax.numpy as jnp
from jax import lax
from jax.experimental import pallas as pl
from jax.experimental.pallas import tpu as pltpu
from jax.sharding import PartitionSpec as P

SPAN = 64
BF = jnp.bfloat16
F32 = jnp.float32
VMEM_BYTES = 56 * 1024 * 1024


def exchange(values, axis, mask):
    size = lax.axis_size(axis)
    return lax.ppermute(values, axis, [(one, one ^ mask) for one in range(size)])


def call(body, outs, args, scratch=(), flops=0, smem=0):
    specs = [pl.BlockSpec(memory_space=pltpu.SMEM)] * smem
    specs += [pl.BlockSpec(memory_space=pltpu.VMEM)] * (len(args) - smem)
    moved = sum(math.prod(one.shape) * one.dtype.itemsize for one in list(args) + list(outs))
    return pl.pallas_call(
        body,
        out_shape=tuple(outs),
        in_specs=specs,
        out_specs=tuple(pl.BlockSpec(memory_space=pltpu.VMEM) for _ in outs),
        scratch_shapes=list(scratch),
        compiler_params=pltpu.CompilerParams(vmem_limit_bytes=VMEM_BYTES),
        cost_estimate=pl.CostEstimate(flops=flops, bytes_accessed=moved, transcendentals=0),
    )(*args)


def shape(dims, dtype):
    return jax.ShapeDtypeStruct(dims, dtype)


def dot(left, right, left_dim, right_dim):
    return lax.dot_general(
        left, right, (((left_dim,), (right_dim,)), ((), ())), preferred_element_type=F32
    )


def normalise(values):
    center = values - jnp.mean(values, axis=-1, keepdims=True)
    variance = jnp.mean(center * center, axis=-1, keepdims=True)
    inverse = lax.rsqrt(variance + 1e-05)
    return center * inverse, inverse


def collect(me_ref, pieces, ids, target, columns=None):
    rows = pieces[0].shape[0]
    for piece, mask in zip(pieces, ids):
        if len(ids) == 1:
            first = 0
        else:
            first = pl.multiple_of((me_ref[0] ^ mask) * rows, 16)
        target[pl.ds(first, rows), :] = piece[...]


def hand_out(me_ref, total, ids, outs, first_column):
    width = total.shape[1]
    rows = outs[0].shape[0]
    for out, mask in zip(outs, ids):
        if len(ids) == 1:
            first = 0
        else:
            first = pl.multiple_of((me_ref[0] ^ mask) * rows, 8)
        out[:, first_column : first_column + width] = total[pl.ds(first, rows), :].astype(BF)


def ffn_kernel(parts, ids, *refs):
    count = len(ids)
    me_ref, gain = refs[0], refs[1]
    frames = refs[2 : 2 + parts]
    ups = refs[2 + parts : 2 + parts + count]
    downs = refs[2 + parts + count : 2 + parts + 2 * count]
    rest = refs[2 + parts + 2 * count :]
    normed_out, pre_out, hidden_out = rest[:3]
    partials = rest[3 : 3 + parts]
    up, down = rest[3 + parts :]
    collect(me_ref, ups, ids, up)
    collect(me_ref, downs, ids, down)
    own = frames[0].shape[0]
    for index, piece in enumerate(frames):
        normed = normalise(piece[...].astype(F32))[0] * gain[...]
        normed_out[index * own : (index + 1) * own, :] = normed.astype(BF)
    pre = dot(normed_out[...], up[...], 1, 0)
    pre_out[...] = pre
    hidden_out[...] = (pre * jax.nn.sigmoid(pre)).astype(BF)
    made = dot(hidden_out[...], down[...], 1, 1)
    for index, out in enumerate(partials):
        out[...] = made[index * own : (index + 1) * own].astype(BF)


def mid_kernel(parts, *refs):
    gain, frames = refs[0], refs[1]
    pieces = refs[2 : 2 + parts]
    mid_out, normed_out = refs[2 + parts :]
    total = pieces[0][...].astype(F32)
    for piece in pieces[1:]:
        total = total + piece[...].astype(F32)
    mid = frames[...].astype(F32) + 0.5 * total
    mid_out[...] = mid
    normed_out[...] = (normalise(mid)[0] * gain[...]).astype(BF)


def attention_kernel(parts, ids, heads, window, cot_scale, *refs):
    count = len(ids)
    me_ref, bias = refs[0], refs[1]
    seg_q, span_q, seg_k, span_k = refs[2:6]
    at = 6
    normed_parts = refs[at : at + parts]
    at += parts
    cot_parts = refs[at : at + parts]
    at += parts
    pieces = refs[at : at + count]
    at += count
    normed, scaled, context, slopes = refs[at : at + 4]
    at += 4
    attn_outs = refs[at : at + parts]
    at += parts
    normed_outs = refs[at : at + parts]
    at += parts
    weights, qkv, grad_context, key_total, value_total = refs[at:]
    frames = normed.shape[0]
    own = normed_parts[0].shape[0]
    inner = weights.shape[1] // 4
    width = inner // heads
    scale = width ** (-0.5)
    for index in range(parts):
        rows = slice(index * own, (index + 1) * own)
        normed[rows, :] = normed_parts[index][...]
        scaled[rows, :] = (cot_parts[index][...].astype(F32) * cot_scale).astype(BF)
    collect(me_ref, pieces, ids, weights)
    qkv[...] = dot(normed[...], weights[:, : 3 * inner], 1, 0).astype(BF)
    grad_context[...] = dot(scaled[...], weights[:, 3 * inner :], 1, 0).astype(BF)
    block = min(frames, 256)
    reach = min(window, (frames - 1) // SPAN)
    for head in range(heads):
        cols = slice(head * width, (head + 1) * width)
        key_cols = slice(inner + head * width, inner + (head + 1) * width)
        value_cols = slice(2 * inner + head * width, 2 * inner + (head + 1) * width)
        key = qkv[:, key_cols]
        value = qkv[:, value_cols]
        if frames > block:
            key_total[...] = jnp.zeros_like(key_total)
            value_total[...] = jnp.zeros_like(value_total)

        def step(turn, carry):
            rows = pl.ds(pl.multiple_of(turn * block, block), block)
            query = qkv[rows, cols]
            distance = span_q[rows, :] - span_k[...]
            allowed = (seg_q[rows, :] == seg_k[...]) & (distance >= 0) & (distance <= window)
            added = jnp.full((block, frames), bias[head, 0], F32)
            for far in range(1, reach + 1):
                added = jnp.where(distance == far, bias[head, far], added)
            scores = dot(query, key, 1, 1) * scale + added
            scores = jnp.where(allowed, scores, -1e30)
            expo = jnp.exp(scores - jnp.max(scores, axis=-1, keepdims=True))
            soft = expo / jnp.sum(expo, axis=-1, keepdims=True)
            low = soft.astype(BF)
            context[rows, cols] = dot(low, value, 1, 0).astype(BF)
            slope = grad_context[rows, cols]
            probs = dot(slope, value, 1, 1)
            probs = probs - jnp.sum(soft * probs, axis=-1, keepdims=True)
            grad = (soft * probs).astype(BF)
            slopes[rows, cols] = (dot(grad, key, 1, 0) * scale).astype(BF)
            key_slope = dot(grad, query, 0, 0)
            value_slope = dot(low, slope, 0, 0)
            if frames > block:
                key_total[...] += key_slope
                value_total[...] += value_slope
            else:
                slopes[:, key_cols] = (key_slope * scale).astype(BF)
                slopes[:, value_cols] = value_slope.astype(BF)
            return carry

        if frames > block:
            lax.fori_loop(0, frames // block, step, 0)
            slopes[:, key_cols] = (key_total[...] * scale).astype(BF)
            slopes[:, value_cols] = value_total[...].astype(BF)
        else:
            step(0, 0)
    made = dot(slopes[...], weights[:, : 3 * inner], 1, 1)
    for index, out in enumerate(normed_outs):
        out[...] = made[index * own : (index + 1) * own].astype(BF)
    made = dot(context[...], weights[:, 3 * inner :], 1, 1)
    for index, out in enumerate(attn_outs):
        out[...] = made[index * own : (index + 1) * own].astype(BF)


def attention_grads_kernel(ids, *refs):
    count = len(ids)
    me_ref, normed, scaled, context, slopes = refs[:5]
    outs = refs[5 : 5 + count]
    total = refs[5 + count]
    inner = context.shape[1]
    for index in range(3):
        total[...] = dot(normed[...], slopes[:, index * inner : (index + 1) * inner], 0, 0)
        hand_out(me_ref, total, ids, outs, index * inner)
    total[...] = dot(scaled[...], context[...], 0, 0)
    hand_out(me_ref, total, ids, outs, 3 * inner)


def grad_mid_kernel(parts, cot_scale, *refs):
    gain, mid, cot = refs[:3]
    pieces = refs[3 : 3 + parts]
    out = refs[3 + parts]
    upstream = pieces[0][...].astype(F32)
    for piece in pieces[1:]:
        upstream = upstream + piece[...].astype(F32)
    normed, inverse = normalise(mid[...])
    scaled = upstream * gain[...]
    first = jnp.mean(scaled, axis=-1, keepdims=True)
    second = jnp.mean(scaled * normed, axis=-1, keepdims=True)
    slope = inverse * (scaled - first - normed * second)
    low_cot = (cot[...].astype(F32) * cot_scale).astype(BF).astype(F32)
    out[...] = (low_cot + slope).astype(BF)


def ffn_grads_kernel(parts, ids, *refs):
    count = len(ids)
    me_ref, normed, pre, hidden = refs[:4]
    mids = refs[4 : 4 + parts]
    downs = refs[4 + parts : 4 + parts + count]
    outs = refs[4 + parts + count : 4 + parts + 2 * count]
    down, grad_mid, total = refs[4 + parts + 2 * count :]
    own = mids[0].shape[0]
    collect(me_ref, downs, ids, down)
    for index, piece in enumerate(mids):
        grad_mid[index * own : (index + 1) * own, :] = piece[...]
    total[...] = 0.5 * dot(grad_mid[...], hidden[...], 0, 0)
    hand_out(me_ref, total, ids, outs, down.shape[1])
    sigma = jax.nn.sigmoid(pre[...])
    slope = sigma * (1.0 + pre[...] * (1.0 - sigma))
    grad_hidden = (0.5 * dot(grad_mid[...], down[...], 1, 0) * slope).astype(BF)
    total[...] = dot(normed[...], grad_hidden, 0, 0)
    hand_out(me_ref, total, ids, outs, 0)


def pair_sum_kernel(*refs):
    count = len(refs) // 3
    for index in range(count):
        total = refs[index][...].astype(F32) + refs[count + index][...].astype(F32)
        refs[2 * count + index][...] = total.astype(BF)


def per_device(
    frames_in,
    segment_ids,
    span_ids,
    ffn_gain,
    w_up,
    w_down,
    attn_gain,
    w_query,
    w_key,
    w_value,
    w_out,
    offset_bias,
    cotangent,
):
    dp, ctx = lax.axis_size("dp"), lax.axis_size("ctx")
    own, model = frames_in.shape[1:]
    frames = own * ctx
    heads = offset_bias.shape[0]
    window = offset_bias.shape[1] - 1
    hidden, inner = w_up.shape[1], w_query.shape[1]
    rows = w_up.shape[0]
    direct_rows = dp == 8 and rows % 16 == 0
    direct_frames = ctx == 4 and own % 16 == 0
    ids = (0, 2, 4, 6, 1, 3, 5, 7) if direct_rows else (0,)
    parts = ctx if direct_frames else 1
    part_rows = frames // parts
    me = lax.axis_index("dp").astype(jnp.int32).reshape(1)
    place = lax.axis_index("ctx")
    cot_scale = 1.0 / math.sqrt(dp * frames)

    def gather_rows(weight):
        if not direct_rows:
            return [lax.all_gather(weight, "dp", axis=0, tiled=True)]
        near = [weight] + [exchange(weight, "dp", mask) for mask in ids[1:4]]
        return near + [exchange(one, "dp", 1) for one in near]

    def gather_frames(values):
        if not direct_frames:
            return [lax.all_gather(values, "ctx", axis=0, tiled=True)]
        return [values] + [exchange(values, "ctx", mask) for mask in range(1, ctx)]

    def scatter_frames(pieces):
        if not direct_frames:
            return [lax.psum_scatter(pieces[0], "ctx", scatter_dimension=0, tiled=True)]
        return [pieces[0]] + [exchange(pieces[mask], "ctx", mask) for mask in range(1, ctx)]

    def scatter_rows(pieces):
        if not direct_rows:
            made = lax.psum_scatter(pieces[0], "dp", scatter_dimension=0, tiled=True)
            return made.astype(F32)
        came = [exchange(one, "dp", 1) for one in pieces[4:]]
        outs = [shape(one.shape, BF) for one in came]
        sums = call(pair_sum_kernel, outs, list(pieces[:4]) + came)
        total = sums[0].astype(F32)
        for one, mask in zip(sums[1:], ids[1:4]):
            total = total + exchange(one, "dp", mask).astype(F32)
        return total

    frames_own, cot_own = frames_in[0], cotangent[0]
    frame_parts = gather_frames(frames_own)
    ups, downs = gather_rows(w_up), gather_rows(w_down)
    attn_weights = jnp.concatenate([w_query, w_key, w_value, w_out], axis=1)
    attn_pieces = gather_rows(attn_weights)
    cot_parts = gather_frames(cot_own)

    segments, spans = segment_ids[0], span_ids[0]
    if direct_frames:
        order = place ^ jnp.arange(ctx, dtype=jnp.int32)
        segments = segments.reshape(ctx, own)[order].reshape(frames)
        spans = spans.reshape(ctx, own)[order].reshape(frames)
    marks = [
        segments.reshape(frames, 1),
        spans.reshape(frames, 1),
        segments.reshape(1, frames),
        spans.reshape(1, frames),
    ]
    ffn_gain = ffn_gain.reshape(1, model)
    attn_gain = attn_gain.reshape(1, model)

    made = call(
        functools.partial(ffn_kernel, parts, ids),
        [shape((frames, model), BF), shape((frames, hidden), F32), shape((frames, hidden), BF)]
        + [shape((part_rows, model), BF)] * parts,
        [me, ffn_gain] + frame_parts + ups + downs,
        [pltpu.VMEM((model, hidden), BF)] * 2,
        flops=4 * frames * model * hidden,
        smem=1,
    )
    ffn_normed, ffn_pre, ffn_hidden = made[:3]
    summed = scatter_frames(list(made[3:]))
    mid_own, normed_own = call(
        functools.partial(mid_kernel, len(summed)),
        [shape((own, model), F32), shape((own, model), BF)],
        [attn_gain, frames_own] + summed,
    )
    normed_parts = gather_frames(normed_own)
    made = call(
        functools.partial(attention_kernel, parts, ids, heads, window, cot_scale),
        [
            shape((frames, model), BF),
            shape((frames, model), BF),
            shape((frames, inner), BF),
            shape((frames, 3 * inner), BF),
        ]
        + [shape((part_rows, model), BF)] * (2 * parts),
        [me, offset_bias] + marks + normed_parts + cot_parts + attn_pieces,
        [
            pltpu.VMEM((model, 4 * inner), BF),
            pltpu.VMEM((frames, 3 * inner), BF),
            pltpu.VMEM((frames, inner), BF),
            pltpu.VMEM((frames, inner // heads), F32),
            pltpu.VMEM((frames, inner // heads), F32),
        ],
        flops=16 * frames * model * inner + 12 * frames * frames * inner,
        smem=2,
    )
    attn_normed, scaled_cot, context, slopes = made[:4]
    attn_partials = list(made[4 : 4 + parts])
    normed_partials = list(made[4 + parts :])
    upstream = scatter_frames(normed_partials)
    attn_grads = call(
        functools.partial(attention_grads_kernel, ids),
        [shape((model // len(ids), 4 * inner), BF)] * len(ids),
        [me, attn_normed, scaled_cot, context, slopes],
        [pltpu.VMEM((model, inner), F32)],
        flops=8 * frames * model * inner,
        smem=1,
    )
    attn_total = scatter_rows(attn_grads)
    (grad_mid_own,) = call(
        functools.partial(grad_mid_kernel, len(upstream), cot_scale),
        [shape((own, model), BF)],
        [attn_gain, mid_own, cot_own] + upstream,
    )
    grad_mid_parts = gather_frames(grad_mid_own)
    ffn_grads = call(
        functools.partial(ffn_grads_kernel, parts, ids),
        [shape((model // len(ids), 2 * hidden), BF)] * len(ids),
        [me, ffn_normed, ffn_pre, ffn_hidden] + grad_mid_parts + downs,
        [
            pltpu.VMEM((model, hidden), BF),
            pltpu.VMEM((frames, model), BF),
            pltpu.VMEM((model, hidden), F32),
        ],
        flops=6 * frames * model * hidden,
        smem=1,
    )
    attn_sum = sum(one.astype(F32) for one in scatter_frames(attn_partials))
    block_out = (mid_own + attn_sum).astype(BF)[None]
    ffn_total = scatter_rows(ffn_grads)
    return (
        block_out,
        ffn_total[:, :hidden],
        ffn_total[:, hidden:],
        attn_total[:, :inner],
        attn_total[:, inner : 2 * inner],
        attn_total[:, 2 * inner : 3 * inner],
        attn_total[:, 3 * inner :],
    )


def solution(mesh):
    placed = (
        P("dp", "ctx", None),
        P("dp", None),
        P("dp", None),
        P(),
        P("dp", "ctx"),
        P("dp", "ctx"),
        P(),
        P("dp", "ctx"),
        P("dp", "ctx"),
        P("dp", "ctx"),
        P("dp", "ctx"),
        P("ctx", None),
        P("dp", "ctx", None),
    )
    return jax.shard_map(
        per_device,
        mesh=mesh,
        in_specs=placed,
        out_specs=(P("dp", "ctx", None),) + (P("dp", "ctx"),) * 6,
        check_vma=False,
    )
```

time: 485 us -> 164 us (0.34)
  waiting for transfers between devices: 297 us -> 60.8 us
  blocking collectives: 72.6 us -> 0 us
  starting transfers between devices: 0.89 us -> 54.8 us
  matrix products: 51.5 us -> 0 us
  Pallas kernels: 0 us -> 30.6 us
  other arithmetic: 26.6 us -> 2.38 us
  between operations: 14.4 us -> 1.27 us
  local copies, waits for them, and re-layouts: 20.5 us -> 13.7 us
    reduce_scatter x7 -> x0, waiting for transfers between devices: 238 us -> none  [the longest x1 38.6 us: per_device(): lax.psum_scatter(grad_up.astype(jnp.bfloat16), 'dp', scatter_dimension=0,...]
    all_gather x6 -> x0, blocking collectives: 72.6 us -> none  [the longest x1 15.1 us: per_device(): lax.all_gather(frames_in, 'ctx', axis=1, tiled=True)]
    ppermute x0 -> x56, waiting for transfers between devices: none -> 60.8 us  [exchange(): lax.ppermute(values, axis, [(one, one ^ mask) for one in range(size)])]
    psum x2 -> x0, waiting for transfers between devices: 58.2 us -> none  [the longest x1 34.5 us: per_device(): ffn_sum = lax.psum(ffn_part.astype(jnp.bfloat16), 'ctx').astype(jnp.float32)]
    ppermute x0 -> x56, starting transfers between devices: none -> 54.8 us  [exchange(): lax.ppermute(values, axis, [(one, one ^ mask) for one in range(size)])]
    dot_general x22 -> x0, matrix products: 51.5 us -> none  [the longest x1 8.3 us: group_slopes(): jnp.einsum('bhqk,bqhd->bkhd', soft_low, slope_group, preferred_element_ty...]
    pallas_call x0 -> x8, Pallas kernels: none -> 30.6 us  [call(): pl.pallas_call(body, out_shape=tuple(outs), in_specs=specs, out_specs=tup...]
    convert_element_type x8 -> x0, other arithmetic: 11.4 us -> none  [the longest x6 9.63 us: per_device(): summed = (lax.psum_scatter(grad_up.astype(jnp.bfloat16), 'dp', scatter_di...]
  transfers between devices with their start and end apart: 11 -> 56, of which waited for: 9 -> 23; matrix products, arithmetic and copies ran while one was open for 8% -> 7% of each run, Pallas kernels for 0% -> 14%
where the time goes in v1:
time: 164 us
  waiting for transfers between devices  60.8 us (37%)
  starting transfers between devices  54.8 us (33%)
  Pallas kernels  30.6 us (19%)
  local copies, waits for them, and re-layouts  13.7 us (8%)
  other arithmetic  2.38 us (1%)
    ppermute x56, waiting for transfers between devices, exchange(): lax.ppermute(values, axis, [(one, one ^ mask) for one in range(size)])  60.8 us
    ppermute x56, starting transfers between devices, exchange(): lax.ppermute(values, axis, [(one, one ^ mask) for one in range(size)])  54.8 us
    pallas_call x8, Pallas kernels, call(): pl.pallas_call(body, out_shape=tuple(outs), in_specs=specs, out_specs=tup...  30.6 us
    unnamed x138, local copies, waits for them, and re-layouts  6.69 us
  transfers between devices with their start and end apart: 56, of which 23 were waited for; matrix products, arithmetic and copies ran while one was open for 7% of the time, Pallas kernels for 14%

profile of v1, /device:TPU:0, one launch (start us, length us, event | category | flops | bytes accessed | tf_op | source)
XLA Modules:
  0.0 163.6 jit_solution(11261196846675192809)
XLA Ops:
  0.6 5.1 %collective-permute-start.2 = (bf16[64,768]{1,0:T(8,128)(2,1)}, bf16[64,768]{1,0:T(8,128)(2,1)S(1)}, u32[]{:S(2)}, u32[]{:S(2)}) collective-permute-start(bf16[64,768]{1,0:T(8,128)(2,1)} %bitcast.7), channel_id=1, source_target_pairs={{0,3},{1,2},{2,1},{3,0},{4,7},{5,6},{6,5},{7,4},{8,11},{9,10},{10,... | collective-permute-start | bytes 294920 | tf_op jit(solution)/shard_map/ppermute | solution.py:19
  5.8 2.4 %collective-permute-start.5 = (bf16[96,768]{1,0:T(8,128)(2,1)}, bf16[96,768]{1,0:T(8,128)(2,1)S(1)}, u32[]{:S(2)}, u32[]{:S(2)}) collective-permute-start(bf16[96,768]{1,0:T(8,128)(2,1)} %refs_6_.1), channel_id=1, source_target_pairs={{0,24},{4,28},{8,16},{12,20},{16,8},{20,12},{24,0},{28,4},{1,25},{... | collective-permute-start | bytes 442376 | tf_op jit(solution)/shard_map/ppermute | solution.py:19
  9.5 3.6 %collective-permute-start.25 = (bf16[64,768]{1,0:T(8,128)(2,1)}, bf16[64,768]{1,0:T(8,128)(2,1)S(1)}, u32[]{:S(2)}, u32[]{:S(2)}) collective-permute-start(bf16[64,768]{1,0:T(8,128)(2,1)} %bitcast.12), channel_id=1, source_target_pairs={{0,3},{1,2},{2,1},{3,0},{4,7},{5,6},{6,5},{7,4},{8,11},{9,10},{10,... | collective-permute-start | bytes 294920 | tf_op jit(solution)/shard_map/ppermute | solution.py:19
  14.0 3.5 %collective-permute-done.1.refs_4_ = bf16[64,768]{1,0:T(8,128)(2,1)S(1)} collective-permute-done((bf16[64,768]{1,0:T(8,128)(2,1)}, bf16[64,768]{1,0:T(8,128)(2,1)S(1)}, u32[]{:S(2)}, u32[]{:S(2)}) %collective-permute-start.1) | collective-permute-done | bytes 98336 | tf_op jit(solution)/shard_map/ppermute | solution.py:19
  17.5 1.1 collective-permute-start.3
  19.1 1.6 collective-permute-start.12
  22.6 1.2 collective-permute-start.10
  24.4 2.5 %collective-permute-done.12.refs_17_.refs_11_ = bf16[96,768]{1,0:T(8,128)(2,1)S(1)} collective-permute-done((bf16[96,768]{1,0:T(8,128)(2,1)}, bf16[96,768]{1,0:T(8,128)(2,1)S(1)}, u32[]{:S(2)}, u32[]{:S(2)}) %collective-permute-start.12) | collective-permute-done | bytes 147488 | tf_op jit(solution)/shard_map/ppermute | solution.py:19
  27.1 2.5 %collective-permute-done.11.refs_16_.refs_10_ = bf16[96,768]{1,0:T(8,128)(2,1)S(1)} collective-permute-done((bf16[96,768]{1,0:T(8,128)(2,1)S(1)}, bf16[96,768]{1,0:T(8,128)(2,1)S(1)}, u32[]{:S(2)}, u32[]{:S(2)}) %collective-permute-start.11) | collective-permute-done | bytes 147488 | tf_op jit(solution)/shard_map/ppermute | solution.py:19
  29.6 1.4 collective-permute-start.28
  31.0 1.6 %collective-permute-start.27 = (bf16[96,2048]{1,0:T(8,128)(2,1)S(1)}, bf16[96,2048]{1,0:T(8,128)(2,1)S(1)}, u32[]{:S(2)}, u32[]{:S(2)}) collective-permute-start(bf16[96,2048]{1,0:T(8,128)(2,1)S(1)} %constant_dynamic-update-slice_fusion.refs_14_), channel_id=1, source_target_pairs={{0,16},{4,20},{8,24},{12,28},{16,0},{20,4},{24,8},{28,12},{1,17},{... | collective-permute-start | bytes 1179656 | tf_op jit(solution)/shard_map/ppermute | solution.py:19
  34.6 1.1 collective-permute-start.24
  36.9 3.9 %shard_map.180 = (bf16[256,768]{1,0:T(8,128)(2,1)}, f32[256,768]{1,0:T(8,128)}, bf16[256,768]{1,0:T(8,128)(2,1)}, bf16[64,768]{1,0:T(8,128)(2,1)}, bf16[64,768]{...) custom-call(s32[1]{0:T(128)} %bitcast.1.refs_0_, f32[1,768]{1,0:T(1,128)} %reshape.41.refs_1_, ...), custom_call_target="tpu_custom_call" | custom-call | flops 603979776 | bytes 4721668 | tf_op jit(solution)/shard_map/pallas_call | solution.py:26
  40.8 1.2 collective-permute-done.24.refs_12_
  42.5 1.6 collective-permute-start.18
  44.1 5.8 %collective-permute-done.27.refs_16_ = bf16[96,2048]{1,0:T(8,128)(2,1)S(1)} collective-permute-done((bf16[96,2048]{1,0:T(8,128)(2,1)S(1)}, bf16[96,2048]{1,0:T(8,128)(2,1)S(1)}, u32[]{:S(2)}, u32[]{:S(2)}) %collective-permute-start.27) | collective-permute-done | bytes 393248 | tf_op jit(solution)/shard_map/ppermute | solution.py:19
  49.9 1.1 collective-permute-start.19
  51.6 5.1 %collective-permute-done.19.refs_5_ = bf16[64,768]{1,0:T(8,128)(2,1)S(1)} collective-permute-done((bf16[64,768]{1,0:T(8,128)(2,1)}, bf16[64,768]{1,0:T(8,128)(2,1)S(1)}, u32[]{:S(2)}, u32[]{:S(2)}) %collective-permute-start.19) | collective-permute-done | bytes 98336 | tf_op jit(solution)/shard_map/ppermute | solution.py:19
  58.6 2.0 %shard_map.181 = (f32[64,768]{1,0:T(8,128)}, bf16[64,768]{1,0:T(8,128)(2,1)}) custom-call(f32[1,768]{1,0:T(1,128)} %reshape.39.refs_0_, bf16[64,768]{1,0:T(8,128)(2,1)} %bitcast.11, bf16[64,768]{1,0:T(8,128)(2,1)} %get-tuple-element.52.refs_2_, bf16[64,768]{1,0:T(8,128)(2,1)} %copy-done.37, bf16[64,768]{1,0:T(8,128)(2,1)} %copy-done.38, ...), custom_call_target="tpu_custom_call" | custom-call | bytes 789504 | tf_op jit(solution)/shard_map/pallas_call | solution.py:26
  61.3 2.1 %collective-permute-start.22 = (bf16[64,768]{1,0:T(8,128)(2,1)}, bf16[64,768]{1,0:T(8,128)(2,1)S(1)}, u32[]{:S(2)}, u32[]{:S(2)}) collective-permute-start(bf16[64,768]{1,0:T(8,128)(2,1)} %get-tuple-element.57.refs_6_), channel_id=1, source_target_pairs={{0,3},{1,2},{2,1},{3,0},{4,7},{5,6},{6,5},{7,4},{8,11},{9,10},{10,... | collective-permute-start | bytes 294920 | tf_op jit(solution)/shard_map/ppermute | solution.py:19
  64.2 3.9 %collective-permute-done.22.refs_9_ = bf16[64,768]{1,0:T(8,128)(2,1)S(1)} collective-permute-done((bf16[64,768]{1,0:T(8,128)(2,1)}, bf16[64,768]{1,0:T(8,128)(2,1)S(1)}, u32[]{:S(2)}, u32[]{:S(2)}) %collective-permute-start.22) | collective-permute-done | bytes 98336 | tf_op jit(solution)/shard_map/ppermute | solution.py:19
  68.0 3.5 %collective-permute-start.20 = (bf16[64,768]{1,0:T(8,128)(2,1)}, bf16[64,768]{1,0:T(8,128)(2,1)S(1)}, u32[]{:S(2)}, u32[]{:S(2)}) collective-permute-start(bf16[64,768]{1,0:T(8,128)(2,1)} %get-tuple-element.57.refs_6_), channel_id=1, source_target_pairs={{0,1},{1,0},{2,3},{3,2},{4,5},{5,4},{6,7},{7,6},{8,9},{9,8},{10,11... | collective-permute-start | bytes 294920 | tf_op jit(solution)/shard_map/ppermute | solution.py:19
  77.9 7.5 %shard_map.182 = (bf16[256,768]{1,0:T(8,128)(2,1)}, bf16[256,768]{1,0:T(8,128)(2,1)}, bf16[256,512]{1,0:T(8,128)(2,1)}, bf16[256,1536]{1,0:T(8,128)(2,1)}, bf16[...) custom-call(s32[1]{0:T(128)} %bitcast.1.refs_0_, ...), custom_call_target="tpu_custom_call" | custom-call | flops 2013265920 | bytes 6557844 | tf_op jit(solution)/shard_map/pallas_call | solution.py:26
  85.5 3.0 %collective-permute-start.37 = (bf16[64,768]{1,0:T(8,128)(2,1)}, bf16[64,768]{1,0:T(8,128)(2,1)S(1)}, u32[]{:S(2)}, u32[]{:S(2)}) collective-permute-start(bf16[64,768]{1,0:T(8,128)(2,1)} %get-tuple-element.67), channel_id=1, source_target_pairs={{0,2},{1,3},{2,0},{3,1},{4,6},{5,7},{6,4},{7,5},{8,10},{9,11},{10,... | collective-permute-start | bytes 294920 | tf_op jit(solution)/shard_map/ppermute | solution.py:19
  88.5 1.4 collective-permute-start.38
  89.9 4.4 %shard_map.186 = (bf16[96,2048]{1,0:T(8,128)(2,1)}, bf16[96,2048]{1,0:T(8,128)(2,1)}, bf16[96,2048]{1,0:T(8,128)(2,1)}, bf16[96,2048]{1,0:T(8,128)(2,1)}, bf16[9...) custom-call(s32[1]{0:T(128)} %bitcast.1.refs_0_, ...), custom_call_target="tpu_custom_call" | custom-call | flops 805306368 | bytes 4980740 | tf_op jit(solution)/shard_map/pallas_call | solution.py:26
  95.9 2.2 %shard_map.183.refs_4_ = bf16[64,768]{1,0:T(8,128)(2,1)} custom-call(f32[1,768]{1,0:T(1,128)} %reshape.39.refs_0_, f32[64,768]{1,0:T(8,128)} %get-tuple-element.56.refs_1_, bf16[64,768]{1,0:T(8,128)(2,1)} %bitcast.14, bf16[64,768]{1,0:T(8,128)(2,1)} %get-tuple-element.65.refs_3_, bf16[64,768]{1,0:T(8,128)(2,1)} %copy-done.31, bf16[64,768]{1,0:T(8,128)(2,1)} %copy-done.32, ...), custom_call_target="tpu_custom_call" | custom-call | bytes 789504 | tf_op jit(solution)/shard_map/pallas_call | solution.py:26
  98.0 1.6 collective-permute-start.41
  100.4 4.3 %collective-permute-done.41.refs_7_ = bf16[64,768]{1,0:T(8,128)(2,1)S(1)} collective-permute-done((bf16[64,768]{1,0:T(8,128)(2,1)}, bf16[64,768]{1,0:T(8,128)(2,1)S(1)}, u32[]{:S(2)}, u32[]{:S(2)}) %collective-permute-start.41) | collective-permute-done | bytes 98336 | tf_op jit(solution)/shard_map/ppermute | solution.py:19
  104.7 1.6 collective-permute-start.40
  106.4 5.2 %collective-permute-done.40.refs_6_ = bf16[64,768]{1,0:T(8,128)(2,1)S(1)} collective-permute-done((bf16[64,768]{1,0:T(8,128)(2,1)}, bf16[64,768]{1,0:T(8,128)(2,1)S(1)}, u32[]{:S(2)}, u32[]{:S(2)}) %collective-permute-start.40) | collective-permute-done | bytes 98336 | tf_op jit(solution)/shard_map/ppermute | solution.py:19
  111.9 4.5 %collective-permute-done.39.refs_5_ = bf16[64,768]{1,0:T(8,128)(2,1)S(1)} collective-permute-done((bf16[64,768]{1,0:T(8,128)(2,1)}, bf16[64,768]{1,0:T(8,128)(2,1)S(1)}, u32[]{:S(2)}, u32[]{:S(2)}) %collective-permute-start.39) | collective-permute-done | bytes 98336 | tf_op jit(solution)/shard_map/ppermute | solution.py:19
  117.0 4.8 %shard_map.184 = (bf16[96,1536]{1,0:T(8,128)(2,1)}, bf16[96,1536]{1,0:T(8,128)(2,1)}, bf16[96,1536]{1,0:T(8,128)(2,1)}, bf16[96,1536]{1,0:T(8,128)(2,1)}, bf16[9...) custom-call(s32[1]{0:T(128)} %bitcast.1.refs_0_, ...), custom_call_target="tpu_custom_call" | custom-call | flops 905969664 | bytes 5505028 | tf_op jit(solution)/shard_map/pallas_call | solution.py:26
  122.7 2.5 %collective-permute-start.34 = (bf16[64,768]{1,0:T(8,128)(2,1)S(1)}, bf16[64,768]{1,0:T(8,128)(2,1)S(1)}, u32[]{:S(2)}, u32[]{:S(2)}) collective-permute-start(bf16[64,768]{1,0:T(8,128)(2,1)S(1)} %copy-done.57), channel_id=1, source_target_pairs={{0,2},{1,3},{2,0},{3,1},{4,6},{5,7},{6,4},{7,5},{8,10},{9,11},{10,... | collective-permute-start | bytes 294920 | tf_op jit(solution)/shard_map/ppermute | solution.py:19
  125.3 1.6 collective-permute-start.35
  127.0 3.1 %shard_map.187 = (bf16[96,2048]{1,0:T(8,128)(2,1)}, bf16[96,2048]{1,0:T(8,128)(2,1)}, bf16[96,2048]{1,0:T(8,128)(2,1)}, bf16[96,2048]{1,0:T(8,128)(2,1)}) custom-call(bf16[96,2048]{1,0:T(8,128)(2,1)} %get-tuple-element.85.refs_0_, bf16[96,2048]{1,0:T(8,128)(2,1)} %get-tuple-element.86.refs_1_, bf16[96,2048]{1,0:T(8,128)(2,1)} %get-tuple-element.87.refs_2_, ...), custom_call_target="tpu_custom_call" | custom-call | bytes 4718592 | tf_op jit(solution)/shard_map/pallas_call | solution.py:26
  130.1 1.1 collective-permute-start.53
  131.2 2.3 %collective-permute-done.34 = bf16[64,768]{1,0:T(8,128)(2,1)S(1)} collective-permute-done((bf16[64,768]{1,0:T(8,128)(2,1)S(1)}, bf16[64,768]{1,0:T(8,128)(2,1)S(1)}, u32[]{:S(2)}, u32[]{:S(2)}) %collective-permute-start.34) | collective-permute-done | bytes 98336 | tf_op jit(solution)/shard_map/ppermute | solution.py:19
  133.5 1.4 collective-permute-start.54
  134.9 1.3 collective-permute-start.55
  139.1 2.7 %shard_map.185 = (bf16[96,1536]{1,0:T(8,128)(2,1)}, bf16[96,1536]{1,0:T(8,128)(2,1)}, bf16[96,1536]{1,0:T(8,128)(2,1)}, bf16[96,1536]{1,0:T(8,128)(2,1)}) custom-call(bf16[96,1536]{1,0:T(8,128)(2,1)} %get-tuple-element.69.refs_0_, bf16[96,1536]{1,0:T(8,128)(2,1)} %get-tuple-element.70.refs_1_, bf16[96,1536]{1,0:T(8,128)(2,1)} %get-tuple-element.71.refs_2_, ...), custom_call_target="tpu_custom_call" | custom-call | bytes 3538944 | tf_op jit(solution)/shard_map/pallas_call | solution.py:26
  142.6 1.4 collective-permute-start.47
  144.0 1.3 collective-permute-start.48
  145.3 3.6 %collective-permute-done.54 = bf16[96,2048]{1,0:T(8,128)(2,1)S(1)} collective-permute-done((bf16[96,2048]{1,0:T(8,128)(2,1)}, bf16[96,2048]{1,0:T(8,128)(2,1)S(1)}, u32[]{:S(2)}, u32[]{:S(2)}) %collective-permute-start.54) | collective-permute-done | bytes 393248 | tf_op jit(solution)/shard_map/ppermute | solution.py:19
  148.9 2.8 %collective-permute-done.55 = bf16[96,2048]{1,0:T(8,128)(2,1)S(1)} collective-permute-done((bf16[96,2048]{1,0:T(8,128)(2,1)}, bf16[96,2048]{1,0:T(8,128)(2,1)S(1)}, u32[]{:S(2)}, u32[]{:S(2)}) %collective-permute-start.55) | collective-permute-done | bytes 393248 | tf_op jit(solution)/shard_map/ppermute | solution.py:19
  152.9 4.3 %collective-permute-done.46 = bf16[96,1536]{1,0:T(8,128)(2,1)S(1)} collective-permute-done((bf16[96,1536]{1,0:T(8,128)(2,1)}, bf16[96,1536]{1,0:T(8,128)(2,1)S(1)}, u32[]{:S(2)}, u32[]{:S(2)}) %collective-permute-start.46) | collective-permute-done | bytes 294944 | tf_op jit(solution)/shard_map/ppermute | solution.py:19
  157.2 4.5 %collective-permute-done.47 = bf16[96,1536]{1,0:T(8,128)(2,1)S(1)} collective-permute-done((bf16[96,1536]{1,0:T(8,128)(2,1)}, bf16[96,1536]{1,0:T(8,128)(2,1)S(1)}, u32[]{:S(2)}, u32[]{:S(2)}) %collective-permute-start.47) | collective-permute-done | bytes 294944 | tf_op jit(solution)/shard_map/ppermute | solution.py:19
  161.6 1.0 collective-permute-done.48
  (230 shorter events, 29.0 us)
Async XLA Ops:
  0.6 8.9 %collective-permute-start.2 = (bf16[64,768]{1,0:T(8,128)(2,1)}, bf16[64,768]{1,0:T(8,128)(2,1)S(1)}, u32[]{:S(2)}, u32[]{:S(2)}) collective-permute-start(bf16[64,768]{1,0:T(8,128)(2,1)} %bitcast.7), channel_id=1, source_target_pairs={{0,3},{1,2},{2,1},{3,0},{4,7},{5,6},{6,5},{7,4},{8,11},{9,10},{10,... | collective-permute-start | bytes 294920 | tf_op jit(solution)/shard_map/ppermute | solution.py:19
  5.8 13.4 %collective-permute-start.5 = (bf16[96,768]{1,0:T(8,128)(2,1)}, bf16[96,768]{1,0:T(8,128)(2,1)S(1)}, u32[]{:S(2)}, u32[]{:S(2)}) collective-permute-start(bf16[96,768]{1,0:T(8,128)(2,1)} %refs_6_.1), channel_id=1, source_target_pairs={{0,24},{4,28},{8,16},{12,20},{16,8},{20,12},{24,0},{28,4},{1,25},{... | collective-permute-start | bytes 442376 | tf_op jit(solution)/shard_map/ppermute | solution.py:19
  8.2 9.3 %collective-permute-start.1 = (bf16[64,768]{1,0:T(8,128)(2,1)}, bf16[64,768]{1,0:T(8,128)(2,1)S(1)}, u32[]{:S(2)}, u32[]{:S(2)}) collective-permute-start(bf16[64,768]{1,0:T(8,128)(2,1)} %bitcast.8), channel_id=1, source_target_pairs={{0,2},{1,3},{2,0},{3,1},{4,6},{5,7},{6,4},{7,5},{8,10},{9,11},{10,... | collective-permute-start | bytes 294920 | tf_op jit(solution)/shard_map/ppermute | solution.py:19
  8.2 10.4 %collective-permute-start = (bf16[64,768]{1,0:T(8,128)(2,1)}, bf16[64,768]{1,0:T(8,128)(2,1)S(1)}, u32[]{:S(2)}, u32[]{:S(2)}) collective-permute-start(bf16[64,768]{1,0:T(8,128)(2,1)} %bitcast.9), channel_id=1, source_target_pairs={{0,1},{1,0},{2,3},{3,2},{4,5},{5,4},{6,7},{7,6},{8,9},{9,8},{10,11... | collective-permute-start | bytes 294920 | tf_op jit(solution)/shard_map/ppermute | solution.py:19
  9.0 12.6 %collective-permute-start.4 = (bf16[96,768]{1,0:T(8,128)(2,1)}, bf16[96,768]{1,0:T(8,128)(2,1)S(1)}, u32[]{:S(2)}, u32[]{:S(2)}) collective-permute-start(bf16[96,768]{1,0:T(8,128)(2,1)} %refs_6_.1), channel_id=1, source_target_pairs={{0,16},{4,20},{8,24},{12,28},{16,0},{20,4},{24,8},{28,12},{1,17},{... | collective-permute-start | bytes 442376 | tf_op jit(solution)/shard_map/ppermute | solution.py:19
  9.5 9.1 %collective-permute-start.25 = (bf16[64,768]{1,0:T(8,128)(2,1)}, bf16[64,768]{1,0:T(8,128)(2,1)S(1)}, u32[]{:S(2)}, u32[]{:S(2)}) collective-permute-start(bf16[64,768]{1,0:T(8,128)(2,1)} %bitcast.12), channel_id=1, source_target_pairs={{0,3},{1,2},{2,1},{3,0},{4,7},{5,6},{6,5},{7,4},{8,11},{9,10},{10,... | collective-permute-start | bytes 294920 | tf_op jit(solution)/shard_map/ppermute | solution.py:19
  18.6 5.3 %collective-permute-start.6 = (bf16[96,768]{1,0:T(8,128)(2,1)S(1)}, bf16[96,768]{1,0:T(8,128)(2,1)S(1)}, u32[]{:S(2)}, u32[]{:S(2)}) collective-permute-start(bf16[96,768]{1,0:T(8,128)(2,1)S(1)} %copy-done.11), channel_id=1, source_target_pairs={{0,4},{4,0},{8,12},{12,8},{16,20},{20,16},{24,28},{28,24},{1,5},{5... | collective-permute-start | bytes 442376 | tf_op jit(solution)/shard_map/ppermute | solution.py:19
  18.6 5.3 %collective-permute-start.13 = (bf16[96,768]{1,0:T(8,128)(2,1)}, bf16[96,768]{1,0:T(8,128)(2,1)S(1)}, u32[]{:S(2)}, u32[]{:S(2)}) collective-permute-start(bf16[96,768]{1,0:T(8,128)(2,1)} %refs_8_.1), channel_id=1, source_target_pairs={{0,4},{4,0},{8,12},{12,8},{16,20},{20,16},{24,28},{28,24},{1,5},{5... | collective-permute-start | bytes 442376 | tf_op jit(solution)/shard_map/ppermute | solution.py:19
  19.1 7.9 %collective-permute-start.12 = (bf16[96,768]{1,0:T(8,128)(2,1)}, bf16[96,768]{1,0:T(8,128)(2,1)S(1)}, u32[]{:S(2)}, u32[]{:S(2)}) collective-permute-start(bf16[96,768]{1,0:T(8,128)(2,1)} %refs_8_.1), channel_id=1, source_target_pairs={{0,24},{4,28},{8,16},{12,20},{16,8},{20,12},{24,0},{28,4},{1,25},{... | collective-permute-start | bytes 442376 | tf_op jit(solution)/shard_map/ppermute | solution.py:19
  21.6 8.0 %collective-permute-start.11 = (bf16[96,768]{1,0:T(8,128)(2,1)S(1)}, bf16[96,768]{1,0:T(8,128)(2,1)S(1)}, u32[]{:S(2)}, u32[]{:S(2)}) collective-permute-start(bf16[96,768]{1,0:T(8,128)(2,1)S(1)} %copy-done.12), channel_id=1, source_target_pairs={{0,16},{4,20},{8,24},{12,28},{16,0},{20,4},{24,8},{28,12},{1,17},{... | collective-permute-start | bytes 442376 | tf_op jit(solution)/shard_map/ppermute | solution.py:19
  22.6 8.3 %collective-permute-start.10 = (bf16[96,768]{1,0:T(8,128)(2,1)S(1)}, bf16[96,768]{1,0:T(8,128)(2,1)S(1)}, u32[]{:S(2)}, u32[]{:S(2)}) collective-permute-start(bf16[96,768]{1,0:T(8,128)(2,1)S(1)} %copy-done.12), channel_id=1, source_target_pairs={{0,8},{4,12},{8,0},{12,4},{16,24},{20,28},{24,16},{28,20},{1,9},{5... | collective-permute-start | bytes 442376 | tf_op jit(solution)/shard_map/ppermute | solution.py:19
  23.9 7.1 %collective-permute-start.9 = (bf16[96,768]{1,0:T(8,128)(2,1)S(1)}, bf16[96,768]{1,0:T(8,128)(2,1)S(1)}, u32[]{:S(2)}, u32[]{:S(2)}) collective-permute-start(bf16[96,768]{1,0:T(8,128)(2,1)S(1)} %collective-permute-done.5.refs_9_), channel_id=1, source_target_pairs={{0,4},{4,0},{8,12},{12,8},{16,20},{20,16},{24,28},{28,24},{1,5},{5... | collective-permute-start | bytes 442376 | tf_op jit(solution)/shard_map/ppermute | solution.py:19
  24.0 8.7 %collective-permute-start.8 = (bf16[96,768]{1,0:T(8,128)(2,1)S(1)}, bf16[96,768]{1,0:T(8,128)(2,1)S(1)}, u32[]{:S(2)}, u32[]{:S(2)}) collective-permute-start(bf16[96,768]{1,0:T(8,128)(2,1)S(1)} %collective-permute-done.4.refs_8_), channel_id=1, source_target_pairs={{0,4},{4,0},{8,12},{12,8},{16,20},{20,16},{24,28},{28,24},{1,5},{5... | collective-permute-start | bytes 442376 | tf_op jit(solution)/shard_map/ppermute | solution.py:19
  27.0 6.2 %collective-permute-start.7 = (bf16[96,768]{1,0:T(8,128)(2,1)S(1)}, bf16[96,768]{1,0:T(8,128)(2,1)S(1)}, u32[]{:S(2)}, u32[]{:S(2)}) collective-permute-start(bf16[96,768]{1,0:T(8,128)(2,1)S(1)} %collective-permute-done.3.refs_7_), channel_id=1, source_target_pairs={{0,4},{4,0},{8,12},{12,8},{16,20},{20,16},{24,28},{28,24},{1,5},{5... | collective-permute-start | bytes 442376 | tf_op jit(solution)/shard_map/ppermute | solution.py:19
  29.6 12.9 %collective-permute-start.28 = (bf16[96,2048]{1,0:T(8,128)(2,1)S(1)}, bf16[96,2048]{1,0:T(8,128)(2,1)S(1)}, u32[]{:S(2)}, u32[]{:S(2)}) collective-permute-start(bf16[96,2048]{1,0:T(8,128)(2,1)S(1)} %constant_dynamic-update-slice_fusion.refs_14_), channel_id=1, source_target_pairs={{0,24},{4,28},{8,16},{12,20},{16,8},{20,12},{24,0},{28,4},{1,25},{... | collective-permute-start | bytes 1179656 | tf_op jit(solution)/shard_map/ppermute | solution.py:19
  31.0 19.0 %collective-permute-start.27 = (bf16[96,2048]{1,0:T(8,128)(2,1)S(1)}, bf16[96,2048]{1,0:T(8,128)(2,1)S(1)}, u32[]{:S(2)}, u32[]{:S(2)}) collective-permute-start(bf16[96,2048]{1,0:T(8,128)(2,1)S(1)} %constant_dynamic-update-slice_fusion.refs_14_), channel_id=1, source_target_pairs={{0,16},{4,20},{8,24},{12,28},{16,0},{20,4},{24,8},{28,12},{1,17},{... | collective-permute-start | bytes 1179656 | tf_op jit(solution)/shard_map/ppermute | solution.py:19
  32.6 18.4 %collective-permute-start.26 = (bf16[96,2048]{1,0:T(8,128)(2,1)S(1)}, bf16[96,2048]{1,0:T(8,128)(2,1)S(1)}, u32[]{:S(2)}, u32[]{:S(2)}) collective-permute-start(bf16[96,2048]{1,0:T(8,128)(2,1)S(1)} %constant_dynamic-update-slice_fusion.refs_14_), channel_id=1, source_target_pairs={{0,8},{4,12},{8,0},{12,4},{16,24},{20,28},{24,16},{28,20},{1,9},{5... | collective-permute-start | bytes 1179656 | tf_op jit(solution)/shard_map/ppermute | solution.py:19
  34.6 7.4 %collective-permute-start.24 = (bf16[64,768]{1,0:T(8,128)(2,1)S(1)}, bf16[64,768]{1,0:T(8,128)(2,1)S(1)}, u32[]{:S(2)}, u32[]{:S(2)}) collective-permute-start(bf16[64,768]{1,0:T(8,128)(2,1)S(1)} %bitcast.15), channel_id=1, source_target_pairs={{0,2},{1,3},{2,0},{3,1},{4,6},{5,7},{6,4},{7,5},{8,10},{9,11},{10,... | collective-permute-start | bytes 294920 | tf_op jit(solution)/shard_map/ppermute | solution.py:19
  36.2 27.3 %collective-permute-start.29 = (bf16[96,2048]{1,0:T(8,128)(2,1)S(1)}, bf16[96,2048]{1,0:T(8,128)(2,1)}, u32[]{:S(2)}, u32[]{:S(2)}) collective-permute-start(bf16[96,2048]{1,0:T(8,128)(2,1)S(1)} %constant_dynamic-update-slice_fusion.refs_14_), channel_id=1, source_target_pairs={{0,4},{4,0},{8,12},{12,8},{16,20},{20,16},{24,28},{28,24},{1,5},{5... | collective-permute-start | bytes 1179656 | tf_op jit(solution)/shard_map/ppermute | solution.py:19
  42.0 9.0 %collective-permute-start.17 = (bf16[64,768]{1,0:T(8,128)(2,1)}, bf16[64,768]{1,0:T(8,128)(2,1)S(1)}, u32[]{:S(2)}, u32[]{:S(2)}) collective-permute-start(bf16[64,768]{1,0:T(8,128)(2,1)} %get-tuple-element.53), channel_id=1, source_target_pairs={{0,1},{1,0},{2,3},{3,2},{4,5},{5,4},{6,7},{7,6},{8,9},{9,8},{10,11... | collective-permute-start | bytes 294920 | tf_op jit(solution)/shard_map/ppermute | solution.py:19
  42.5 9.0 %collective-permute-start.18 = (bf16[64,768]{1,0:T(8,128)(2,1)}, bf16[64,768]{1,0:T(8,128)(2,1)S(1)}, u32[]{:S(2)}, u32[]{:S(2)}) collective-permute-start(bf16[64,768]{1,0:T(8,128)(2,1)} %get-tuple-element.54), channel_id=1, source_target_pairs={{0,2},{1,3},{2,0},{3,1},{4,6},{5,7},{6,4},{7,5},{8,10},{9,11},{10,... | collective-permute-start | bytes 294920 | tf_op jit(solution)/shard_map/ppermute | solution.py:19
  49.9 6.8 %collective-permute-start.19 = (bf16[64,768]{1,0:T(8,128)(2,1)}, bf16[64,768]{1,0:T(8,128)(2,1)S(1)}, u32[]{:S(2)}, u32[]{:S(2)}) collective-permute-start(bf16[64,768]{1,0:T(8,128)(2,1)} %get-tuple-element.55), channel_id=1, source_target_pairs={{0,3},{1,2},{2,1},{3,0},{4,7},{5,6},{6,5},{7,4},{8,11},{9,10},{10,... | collective-permute-start | bytes 294920 | tf_op jit(solution)/shard_map/ppermute | solution.py:19
  51.0 25.3 %collective-permute-start.32 = (bf16[96,2048]{1,0:T(8,128)(2,1)S(1)}, bf16[96,2048]{1,0:T(8,128)(2,1)S(1)}, u32[]{:S(2)}, u32[]{:S(2)}) collective-permute-start(bf16[96,2048]{1,0:T(8,128)(2,1)S(1)} %collective-permute-done.28.refs_17_), channel_id=1, source_target_pairs={{0,4},{4,0},{8,12},{12,8},{16,20},{20,16},{24,28},{28,24},{1,5},{5... | collective-permute-start | bytes 1179656 | tf_op jit(solution)/shard_map/ppermute | solution.py:19
  51.1 25.3 %collective-permute-start.31 = (bf16[96,2048]{1,0:T(8,128)(2,1)S(1)}, bf16[96,2048]{1,0:T(8,128)(2,1)S(1)}, u32[]{:S(2)}, u32[]{:S(2)}) collective-permute-start(bf16[96,2048]{1,0:T(8,128)(2,1)S(1)} %collective-permute-done.27.refs_16_), channel_id=1, source_target_pairs={{0,4},{4,0},{8,12},{12,8},{16,20},{20,16},{24,28},{28,24},{1,5},{5... | collective-permute-start | bytes 1179656 | tf_op jit(solution)/shard_map/ppermute | solution.py:19
  51.5 24.8 %collective-permute-start.30 = (bf16[96,2048]{1,0:T(8,128)(2,1)S(1)}, bf16[96,2048]{1,0:T(8,128)(2,1)S(1)}, u32[]{:S(2)}, u32[]{:S(2)}) collective-permute-start(bf16[96,2048]{1,0:T(8,128)(2,1)S(1)} %collective-permute-done.26.refs_15_), channel_id=1, source_target_pairs={{0,4},{4,0},{8,12},{12,8},{16,20},{20,16},{24,28},{28,24},{1,5},{5... | collective-permute-start | bytes 1179656 | tf_op jit(solution)/shard_map/ppermute | solution.py:19
  61.3 6.7 %collective-permute-start.22 = (bf16[64,768]{1,0:T(8,128)(2,1)}, bf16[64,768]{1,0:T(8,128)(2,1)S(1)}, u32[]{:S(2)}, u32[]{:S(2)}) collective-permute-start(bf16[64,768]{1,0:T(8,128)(2,1)} %get-tuple-element.57.refs_6_), channel_id=1, source_target_pairs={{0,3},{1,2},{2,1},{3,0},{4,7},{5,6},{6,5},{7,4},{8,11},{9,10},{10,... | collective-permute-start | bytes 294920 | tf_op jit(solution)/shard_map/ppermute | solution.py:19
  63.5 12.8 %collective-permute-start.21 = (bf16[64,768]{1,0:T(8,128)(2,1)}, bf16[64,768]{1,0:T(8,128)(2,1)S(1)}, u32[]{:S(2)}, u32[]{:S(2)}) collective-permute-start(bf16[64,768]{1,0:T(8,128)(2,1)} %get-tuple-element.57.refs_6_), channel_id=1, source_target_pairs={{0,2},{1,3},{2,0},{3,1},{4,6},{5,7},{6,4},{7,5},{8,10},{9,11},{10,... | collective-permute-start | bytes 294920 | tf_op jit(solution)/shard_map/ppermute | solution.py:19
  68.0 8.2 %collective-permute-start.20 = (bf16[64,768]{1,0:T(8,128)(2,1)}, bf16[64,768]{1,0:T(8,128)(2,1)S(1)}, u32[]{:S(2)}, u32[]{:S(2)}) collective-permute-start(bf16[64,768]{1,0:T(8,128)(2,1)} %get-tuple-element.57.refs_6_), channel_id=1, source_target_pairs={{0,1},{1,0},{2,3},{3,2},{4,5},{5,4},{6,7},{7,6},{8,9},{9,8},{10,11... | collective-permute-start | bytes 294920 | tf_op jit(solution)/shard_map/ppermute | solution.py:19
  85.4 8.9 %collective-permute-start.36 = (bf16[64,768]{1,0:T(8,128)(2,1)}, bf16[64,768]{1,0:T(8,128)(2,1)S(1)}, u32[]{:S(2)}, u32[]{:S(2)}) collective-permute-start(bf16[64,768]{1,0:T(8,128)(2,1)} %get-tuple-element.66), channel_id=1, source_target_pairs={{0,1},{1,0},{2,3},{3,2},{4,5},{5,4},{6,7},{7,6},{8,9},{9,8},{10,11... | collective-permute-start | bytes 294920 | tf_op jit(solution)/shard_map/ppermute | solution.py:19
  85.5 8.8 %collective-permute-start.37 = (bf16[64,768]{1,0:T(8,128)(2,1)}, bf16[64,768]{1,0:T(8,128)(2,1)S(1)}, u32[]{:S(2)}, u32[]{:S(2)}) collective-permute-start(bf16[64,768]{1,0:T(8,128)(2,1)} %get-tuple-element.67), channel_id=1, source_target_pairs={{0,2},{1,3},{2,0},{3,1},{4,6},{5,7},{6,4},{7,5},{8,10},{9,11},{10,... | collective-permute-start | bytes 294920 | tf_op jit(solution)/shard_map/ppermute | solution.py:19
  88.5 6.7 %collective-permute-start.38 = (bf16[64,768]{1,0:T(8,128)(2,1)}, bf16[64,768]{1,0:T(8,128)(2,1)S(1)}, u32[]{:S(2)}, u32[]{:S(2)}) collective-permute-start(bf16[64,768]{1,0:T(8,128)(2,1)} %get-tuple-element.68), channel_id=1, source_target_pairs={{0,3},{1,2},{2,1},{3,0},{4,7},{5,6},{6,5},{7,4},{8,11},{9,10},{10,... | collective-permute-start | bytes 294920 | tf_op jit(solution)/shard_map/ppermute | solution.py:19
  94.3 27.5 %collective-permute-start.49 = (bf16[96,2048]{1,0:T(8,128)(2,1)}, bf16[96,2048]{1,0:T(8,128)(2,1)S(1)}, u32[]{:S(2)}, u32[]{:S(2)}) collective-permute-start(bf16[96,2048]{1,0:T(8,128)(2,1)} %get-tuple-element.89), channel_id=1, source_target_pairs={{0,4},{4,0},{8,12},{12,8},{16,20},{20,16},{24,28},{28,24},{1,5},{5... | collective-permute-start | bytes 1179656 | tf_op jit(solution)/shard_map/ppermute | solution.py:19
  98.0 6.7 %collective-permute-start.41 = (bf16[64,768]{1,0:T(8,128)(2,1)}, bf16[64,768]{1,0:T(8,128)(2,1)S(1)}, u32[]{:S(2)}, u32[]{:S(2)}) collective-permute-start(bf16[64,768]{1,0:T(8,128)(2,1)} %shard_map.183.refs_4_), channel_id=1, source_target_pairs={{0,3},{1,2},{2,1},{3,0},{4,7},{5,6},{6,5},{7,4},{8,11},{9,10},{10,... | collective-permute-start | bytes 294920 | tf_op jit(solution)/shard_map/ppermute | solution.py:19
  99.7 22.6 %collective-permute-start.50 = (bf16[96,2048]{1,0:T(8,128)(2,1)}, bf16[96,2048]{1,0:T(8,128)(2,1)S(1)}, u32[]{:S(2)}, u32[]{:S(2)}) collective-permute-start(bf16[96,2048]{1,0:T(8,128)(2,1)} %get-tuple-element.90), channel_id=1, source_target_pairs={{0,4},{4,0},{8,12},{12,8},{16,20},{20,16},{24,28},{28,24},{1,5},{5... | collective-permute-start | bytes 1179656 | tf_op jit(solution)/shard_map/ppermute | solution.py:19
  99.9 22.8 %collective-permute-start.51 = (bf16[96,2048]{1,0:T(8,128)(2,1)S(1)}, bf16[96,2048]{1,0:T(8,128)(2,1)S(1)}, u32[]{:S(2)}, u32[]{:S(2)}) collective-permute-start(bf16[96,2048]{1,0:T(8,128)(2,1)S(1)} %copy-done.50), channel_id=1, source_target_pairs={{0,4},{4,0},{8,12},{12,8},{16,20},{20,16},{24,28},{28,24},{1,5},{5... | collective-permute-start | bytes 1179656 | tf_op jit(solution)/shard_map/ppermute | solution.py:19
  100.2 25.1 %collective-permute-start.52 = (bf16[96,2048]{1,0:T(8,128)(2,1)S(1)}, bf16[96,2048]{1,0:T(8,128)(2,1)S(1)}, u32[]{:S(2)}, u32[]{:S(2)}) collective-permute-start(bf16[96,2048]{1,0:T(8,128)(2,1)S(1)} %copy-done.48), channel_id=1, source_target_pairs={{0,4},{4,0},{8,12},{12,8},{16,20},{20,16},{24,28},{28,24},{1,5},{5... | collective-permute-start | bytes 1179656 | tf_op jit(solution)/shard_map/ppermute | solution.py:19
  104.7 6.8 %collective-permute-start.40 = (bf16[64,768]{1,0:T(8,128)(2,1)}, bf16[64,768]{1,0:T(8,128)(2,1)S(1)}, u32[]{:S(2)}, u32[]{:S(2)}) collective-permute-start(bf16[64,768]{1,0:T(8,128)(2,1)} %shard_map.183.refs_4_), channel_id=1, source_target_pairs={{0,2},{1,3},{2,0},{3,1},{4,6},{5,7},{6,4},{7,5},{8,10},{9,11},{10,... | collective-permute-start | bytes 294920 | tf_op jit(solution)/shard_map/ppermute | solution.py:19
  121.8 14.5 %collective-permute-start.42 = (bf16[96,1536]{1,0:T(8,128)(2,1)}, bf16[96,1536]{1,0:T(8,128)(2,1)S(1)}, u32[]{:S(2)}, u32[]{:S(2)}) collective-permute-start(bf16[96,1536]{1,0:T(8,128)(2,1)} %get-tuple-element.73), channel_id=1, source_target_pairs={{0,4},{4,0},{8,12},{12,8},{16,20},{20,16},{24,28},{28,24},{1,5},{5... | collective-permute-start | bytes 884744 | tf_op jit(solution)/shard_map/ppermute | solution.py:19
  121.8 14.5 %collective-permute-start.43 = (bf16[96,1536]{1,0:T(8,128)(2,1)}, bf16[96,1536]{1,0:T(8,128)(2,1)S(1)}, u32[]{:S(2)}, u32[]{:S(2)}) collective-permute-start(bf16[96,1536]{1,0:T(8,128)(2,1)} %get-tuple-element.74), channel_id=1, source_target_pairs={{0,4},{4,0},{8,12},{12,8},{16,20},{20,16},{24,28},{28,24},{1,5},{5... | collective-permute-start | bytes 884744 | tf_op jit(solution)/shard_map/ppermute | solution.py:19
  122.3 7.8 %collective-permute-start.33 = (bf16[64,768]{1,0:T(8,128)(2,1)S(1)}, bf16[64,768]{1,0:T(8,128)(2,1)S(1)}, u32[]{:S(2)}, u32[]{:S(2)}) collective-permute-start(bf16[64,768]{1,0:T(8,128)(2,1)S(1)} %copy-done.58), channel_id=1, source_target_pairs={{0,1},{1,0},{2,3},{3,2},{4,5},{5,4},{6,7},{7,6},{8,9},{9,8},{10,11... | collective-permute-start | bytes 294920 | tf_op jit(solution)/shard_map/ppermute | solution.py:19
  122.7 10.8 %collective-permute-start.34 = (bf16[64,768]{1,0:T(8,128)(2,1)S(1)}, bf16[64,768]{1,0:T(8,128)(2,1)S(1)}, u32[]{:S(2)}, u32[]{:S(2)}) collective-permute-start(bf16[64,768]{1,0:T(8,128)(2,1)S(1)} %copy-done.57), channel_id=1, source_target_pairs={{0,2},{1,3},{2,0},{3,1},{4,6},{5,7},{6,4},{7,5},{8,10},{9,11},{10,... | collective-permute-start | bytes 294920 | tf_op jit(solution)/shard_map/ppermute | solution.py:19
  125.3 9.7 %collective-permute-start.35 = (bf16[64,768]{1,0:T(8,128)(2,1)S(1)}, bf16[64,768]{1,0:T(8,128)(2,1)S(1)}, u32[]{:S(2)}, u32[]{:S(2)}) collective-permute-start(bf16[64,768]{1,0:T(8,128)(2,1)S(1)} %copy-done.56), channel_id=1, source_target_pairs={{0,3},{1,2},{2,1},{3,0},{4,7},{5,6},{6,5},{7,4},{8,11},{9,10},{10,... | collective-permute-start | bytes 294920 | tf_op jit(solution)/shard_map/ppermute | solution.py:19
  130.1 13.9 %collective-permute-start.53 = (bf16[96,2048]{1,0:T(8,128)(2,1)}, bf16[96,2048]{1,0:T(8,128)(2,1)S(1)}, u32[]{:S(2)}, u32[]{:S(2)}) collective-permute-start(bf16[96,2048]{1,0:T(8,128)(2,1)} %get-tuple-element.94), channel_id=1, source_target_pairs={{0,8},{4,12},{8,0},{12,4},{16,24},{20,28},{24,16},{28,20},{1,9},{5... | collective-permute-start | bytes 1179656 | tf_op jit(solution)/shard_map/ppermute | solution.py:19
  133.5 15.4 %collective-permute-start.54 = (bf16[96,2048]{1,0:T(8,128)(2,1)}, bf16[96,2048]{1,0:T(8,128)(2,1)S(1)}, u32[]{:S(2)}, u32[]{:S(2)}) collective-permute-start(bf16[96,2048]{1,0:T(8,128)(2,1)} %get-tuple-element.95), channel_id=1, source_target_pairs={{0,16},{4,20},{8,24},{12,28},{16,0},{20,4},{24,8},{28,12},{1,17},{... | collective-permute-start | bytes 1179656 | tf_op jit(solution)/shard_map/ppermute | solution.py:19
  134.9 16.8 %collective-permute-start.55 = (bf16[96,2048]{1,0:T(8,128)(2,1)}, bf16[96,2048]{1,0:T(8,128)(2,1)S(1)}, u32[]{:S(2)}, u32[]{:S(2)}) collective-permute-start(bf16[96,2048]{1,0:T(8,128)(2,1)} %get-tuple-element.96), channel_id=1, source_target_pairs={{0,24},{4,28},{8,16},{12,20},{16,8},{20,12},{24,0},{28,4},{1,25},{... | collective-permute-start | bytes 1179656 | tf_op jit(solution)/shard_map/ppermute | solution.py:19
  141.8 15.3 %collective-permute-start.46 = (bf16[96,1536]{1,0:T(8,128)(2,1)}, bf16[96,1536]{1,0:T(8,128)(2,1)S(1)}, u32[]{:S(2)}, u32[]{:S(2)}) collective-permute-start(bf16[96,1536]{1,0:T(8,128)(2,1)} %get-tuple-element.78), channel_id=1, source_target_pairs={{0,8},{4,12},{8,0},{12,4},{16,24},{20,28},{24,16},{28,20},{1,9},{5... | collective-permute-start | bytes 884744 | tf_op jit(solution)/shard_map/ppermute | solution.py:19
  142.6 19.1 %collective-permute-start.47 = (bf16[96,1536]{1,0:T(8,128)(2,1)}, bf16[96,1536]{1,0:T(8,128)(2,1)S(1)}, u32[]{:S(2)}, u32[]{:S(2)}) collective-permute-start(bf16[96,1536]{1,0:T(8,128)(2,1)} %get-tuple-element.79), channel_id=1, source_target_pairs={{0,16},{4,20},{8,24},{12,28},{16,0},{20,4},{24,8},{28,12},{1,17},{... | collective-permute-start | bytes 884744 | tf_op jit(solution)/shard_map/ppermute | solution.py:19
  144.0 18.6 %collective-permute-start.48 = (bf16[96,1536]{1,0:T(8,128)(2,1)}, bf16[96,1536]{1,0:T(8,128)(2,1)S(1)}, u32[]{:S(2)}, u32[]{:S(2)}) collective-permute-start(bf16[96,1536]{1,0:T(8,128)(2,1)} %get-tuple-element.80), channel_id=1, source_target_pairs={{0,24},{4,28},{8,16},{12,20},{16,8},{20,12},{24,0},{28,4},{1,25},{... | collective-permute-start | bytes 884744 | tf_op jit(solution)/shard_map/ppermute | solution.py:19
  (75 other events, 526.7 us)

commit v2 on v1

v2 whole, which is shorter than its diff:
```python
import functools
import math

import jax
import jax.numpy as jnp
from jax import lax
from jax.experimental import pallas as pl
from jax.experimental.pallas import tpu as pltpu
from jax.sharding import PartitionSpec as P

SPAN = 64
BF = jnp.bfloat16
F32 = jnp.float32
VMEM_BYTES = 56 * 1024 * 1024


def exchange(values, axis, mask):
    size = lax.axis_size(axis)
    return lax.ppermute(values, axis, [(one, one ^ mask) for one in range(size)])


def call(body, outs, args, scratch=(), flops=0, smem=0, after=()):
    count = len(args)
    specs = [pl.BlockSpec(memory_space=pltpu.SMEM)] * smem
    specs += [pl.BlockSpec(memory_space=pltpu.VMEM)] * (count - smem)
    specs += [pl.BlockSpec(memory_space=pl.ANY)] * len(after)
    moved = sum(math.prod(one.shape) * one.dtype.itemsize for one in list(args) + list(outs))
    return pl.pallas_call(
        lambda *refs: body(*refs[:count], *refs[count + len(after) :]),
        out_shape=tuple(outs),
        in_specs=specs,
        out_specs=tuple(pl.BlockSpec(memory_space=pltpu.VMEM) for _ in outs),
        scratch_shapes=list(scratch),
        compiler_params=pltpu.CompilerParams(vmem_limit_bytes=VMEM_BYTES),
        cost_estimate=pl.CostEstimate(flops=flops, bytes_accessed=moved, transcendentals=0),
    )(*args, *after)


def shape(dims, dtype):
    return jax.ShapeDtypeStruct(dims, dtype)


def dot(left, right, left_dim, right_dim):
    return lax.dot_general(
        left, right, (((left_dim,), (right_dim,)), ((), ())), preferred_element_type=F32
    )


def normalise(values):
    center = values - jnp.mean(values, axis=-1, keepdims=True)
    variance = jnp.mean(center * center, axis=-1, keepdims=True)
    inverse = lax.rsqrt(variance + 1e-05)
    return center * inverse, inverse


def collect(me_ref, pieces, ids, first_column, target):
    rows, width = target.shape
    rows = rows // len(ids)
    columns = slice(first_column, first_column + width)
    if len(ids) == 1:
        target[...] = pieces[0][:, columns]
        return
    blocks = [(piece, at) for piece in pieces for at in range(0, piece.shape[0], rows)]
    for (piece, at), mask in zip(blocks, ids):
        first = pl.multiple_of((me_ref[0] ^ mask) * rows, 16)
        target[pl.ds(first, rows), :] = piece[at : at + rows, columns]


def hand_out(me_ref, total, firsts, rows, outs, first_column):
    width = total.shape[1]
    columns = slice(first_column, first_column + width)
    if len(outs) == 1:
        outs[0][:, columns] = total[...].astype(BF)
        return
    blocks = [(out, at) for out in outs for at in range(0, out.shape[0], rows)]
    for (out, at), first in zip(blocks, firsts):
        block = total[pl.ds(pl.multiple_of(first * rows, 8), rows), :]
        out[at : at + rows, columns] = block.astype(BF)


def ffn_kernel(parts, ids, *refs):
    me_ref, gain = refs[:2]
    frames = refs[2 : 2 + parts]
    at = 2 + parts + (1 if len(ids) == 1 else 2)
    weights, rest = refs[2 + parts : at], refs[at:]
    normed_out, pre_out, hidden_out, down = rest[:4]
    partials = rest[4 : 4 + parts]
    up = rest[4 + parts]
    model, width = up.shape
    collect(me_ref, weights, ids, 0, up)
    collect(me_ref, weights, ids, width, down)
    own = frames[0].shape[0]
    for index, piece in enumerate(frames):
        normed = normalise(piece[:, :model].astype(F32))[0] * gain[...].reshape(1, -1)
        normed_out[index * own : (index + 1) * own, :] = normed.astype(BF)
    pre = dot(normed_out[...], up[...], 1, 0)
    pre_out[...] = pre
    hidden_out[...] = (pre * jax.nn.sigmoid(pre)).astype(BF)
    made = dot(hidden_out[...], down[...], 1, 1)
    for index, out in enumerate(partials):
        out[...] = made[index * own : (index + 1) * own].astype(BF)


def mid_kernel(parts, *refs):
    gain, frames = refs[0], refs[1]
    pieces = refs[2 : 2 + parts]
    stacked = (len(refs) - parts - 4) // 4 * 4
    weights = refs[2 + parts : 2 + parts + stacked]
    mid_out, normed_out = refs[2 + parts + stacked : 4 + parts + stacked]
    if stacked:
        stack_kernel(*weights, refs[-1])
    total = pieces[0][...].astype(F32)
    for piece in pieces[1:]:
        total = total + piece[...].astype(F32)
    mid = frames[...].astype(F32) + 0.5 * total
    mid_out[...] = mid
    normed_out[...] = (normalise(mid)[0] * gain[...].reshape(1, -1)).astype(BF)


def attention_kernel(parts, ids, window, cot_scale, *refs):
    place_ref, me_ref, bias = refs[:3]
    segments, spans = refs[3:5]
    normed_parts = refs[5 : 5 + parts]
    cot_parts = refs[5 + parts : 5 + 2 * parts]
    at = 5 + 2 * parts + (1 if len(ids) == 1 else 2)
    weights_in, rest = refs[5 + 2 * parts : at], refs[at:]
    normed, scaled, context, slopes = rest[:4]
    attn_out, outs = rest[4], rest[5 : 5 + parts]
    weights, qkv, grad_context, key_total, value_total, total = rest[5 + parts :]
    heads = bias.shape[0]
    frames = normed.shape[0]
    own = normed_parts[0].shape[0]
    inner = context.shape[1]
    width = inner // heads
    scale = width ** (-0.5)
    firsts = [0]
    if parts > 1:
        firsts = [pl.multiple_of((place_ref[0] ^ mask) * own, 16) for mask in range(parts)]
    for first, piece, both in zip(firsts, normed_parts, cot_parts):
        normed[pl.ds(first, own), :] = piece[...]
        cot = both[:, normed.shape[1] :].astype(F32)
        scaled[pl.ds(first, own), :] = (cot * cot_scale).astype(BF)
    collect(me_ref, weights_in, ids, 0, weights)
    qkv[...] = dot(normed[...], weights[:, : 3 * inner], 1, 0).astype(BF)
    grad_context[...] = dot(scaled[...], weights[:, 3 * inner :], 1, 0).astype(BF)
    seg_k, span_k = segments[...], spans[...]
    seg_q = jnp.transpose(jnp.broadcast_to(seg_k, (8, frames)))[:, :1]
    span_q = jnp.transpose(jnp.broadcast_to(span_k, (8, frames)))[:, :1]
    block = min(frames, 256)
    reach = min(window, (frames - 1) // SPAN)
    for head in range(heads):
        cols = slice(head * width, (head + 1) * width)
        key_cols = slice(inner + head * width, inner + (head + 1) * width)
        value_cols = slice(2 * inner + head * width, 2 * inner + (head + 1) * width)
        key = qkv[:, key_cols]
        value = qkv[:, value_cols]
        for first in range(0, frames, block):
            mine = slice(first, first + block)
            query = qkv[mine, cols]
            distance = span_q[mine, :] - span_k
            allowed = (seg_q[mine, :] == seg_k) & (distance >= 0) & (distance <= window)
            added = jnp.full((block, frames), bias[head, 0], F32)
            for far in range(1, reach + 1):
                added = jnp.where(distance == far, bias[head, far], added)
            scores = dot(query, key, 1, 1) * scale + added
            scores = jnp.where(allowed, scores, -1e30)
            expo = jnp.exp(scores - jnp.max(scores, axis=-1, keepdims=True))
            soft = expo / jnp.sum(expo, axis=-1, keepdims=True)
            low = soft.astype(BF)
            context[mine, cols] = dot(low, value, 1, 0).astype(BF)
            slope = grad_context[mine, cols]
            probs = dot(slope, value, 1, 1)
            probs = probs - jnp.sum(soft * probs, axis=-1, keepdims=True)
            grad = (soft * probs).astype(BF)
            slopes[mine, cols] = (dot(grad, key, 1, 0) * scale).astype(BF)
            key_slope = dot(grad, query, 0, 0)
            value_slope = dot(low, slope, 0, 0)
            if first > 0:
                key_slope = key_total[...] + key_slope
                value_slope = value_total[...] + value_slope
            if first + block < frames:
                key_total[...] = key_slope
                value_total[...] = value_slope
        slopes[:, key_cols] = (key_slope * scale).astype(BF)
        slopes[:, value_cols] = value_slope.astype(BF)
    total[...] = dot(slopes[...], weights[:, : 3 * inner], 1, 1)
    for first, out in zip(firsts, outs):
        out[...] = total[pl.ds(first, own), :].astype(BF)
    total[...] = dot(context[...], weights[:, 3 * inner :], 1, 1)
    attn_out[...] = total[...].astype(BF)


def attention_grads_kernel(*refs):
    me_ref, normed, scaled, context, slopes = refs[:5]
    outs, total = refs[5:-1], refs[-1]
    inner = context.shape[1]
    rows = total.shape[0] // 8
    firsts = [me_ref[0] ^ mask for mask in (0, 2, 4, 6, 1, 3, 5, 7)]
    for index in range(3):
        total[...] = dot(normed[...], slopes[:, index * inner : (index + 1) * inner], 0, 0)
        hand_out(me_ref, total, firsts, rows, outs, index * inner)
    total[...] = dot(scaled[...], context[...], 0, 0)
    hand_out(me_ref, total, firsts, rows, outs, 3 * inner)


def grad_mid_kernel(parts, cot_scale, *refs):
    gain, mid, cot = refs[:3]
    pieces = refs[3 : 3 + parts]
    out = refs[3 + parts]
    upstream = pieces[0][...].astype(F32)
    for piece in pieces[1:]:
        upstream = upstream + piece[...].astype(F32)
    normed, inverse = normalise(mid[...])
    scaled = upstream * gain[...].reshape(1, -1)
    first = jnp.mean(scaled, axis=-1, keepdims=True)
    second = jnp.mean(scaled * normed, axis=-1, keepdims=True)
    slope = inverse * (scaled - first - normed * second)
    low_cot = (cot[...].astype(F32) * cot_scale).astype(BF).astype(F32)
    out[...] = (low_cot + slope).astype(BF)


def ffn_grads_kernel(parts, *refs):
    me_ref, normed, pre, hidden, down = refs[:5]
    mids = refs[5 : 5 + parts]
    outs = refs[5 + parts : -2]
    grad_mid, total = refs[-2:]
    own = mids[0].shape[0]
    rows = total.shape[0] // 8
    firsts = [me_ref[0] ^ mask for mask in (0, 2, 4, 6, 1, 3, 5, 7)]
    for index, piece in enumerate(mids):
        grad_mid[index * own : (index + 1) * own, :] = piece[...]
    total[...] = 0.5 * dot(grad_mid[...], hidden[...], 0, 0)
    hand_out(me_ref, total, firsts, rows, outs, down.shape[1])
    sigma = jax.nn.sigmoid(pre[...])
    slope = sigma * (1.0 + pre[...] * (1.0 - sigma))
    grad_hidden = (0.5 * dot(grad_mid[...], down[...], 1, 0) * slope).astype(BF)
    total[...] = dot(normed[...], grad_hidden, 0, 0)
    hand_out(me_ref, total, firsts, rows, outs, 0)


def pair_sum_kernel(keep, came, *refs):
    passed = (len(refs) - 4) // 2
    rows = keep.shape[0] // 4
    for at, out in enumerate(refs[passed : passed + 4]):
        mine = slice(at * rows, (at + 1) * rows)
        out[...] = (keep[mine, :].astype(F32) + came[mine, :].astype(F32)).astype(BF)
    for one, out in zip(refs[:passed], refs[passed + 4 :]):
        out[...] = one[...]


def pack_kernel(*refs):
    out, at = refs[-1], 0
    for piece in refs[:-1]:
        out[:, at : at + piece.shape[1]] = piece[...]
        at += piece.shape[1]


def pack(pieces, after=()):
    total = sum(one.shape[1] for one in pieces)
    return call(pack_kernel, [shape((pieces[0].shape[0], total), BF)], pieces, after=after)[0]


def stack_kernel(*refs):
    out, at = refs[-1], 0
    for piece in refs[:-1]:
        out[at : at + piece.shape[0], :] = piece[...]
        at += piece.shape[0]


def stack(pieces, after=()):
    total = sum(one.shape[0] for one in pieces)
    return call(stack_kernel, [shape((total, pieces[0].shape[1]), BF)], pieces, after=after)[0]


def per_device(
    frames_in,
    segment_ids,
    span_ids,
    ffn_gain,
    w_up,
    w_down,
    attn_gain,
    w_query,
    w_key,
    w_value,
    w_out,
    offset_bias,
    cotangent,
):
    dp, ctx = lax.axis_size("dp"), lax.axis_size("ctx")
    own, model = frames_in.shape[1:]
    frames = own * ctx
    heads = offset_bias.shape[0]
    window = offset_bias.shape[1] - 1
    hidden, inner = w_up.shape[1], w_query.shape[1]
    rows = w_up.shape[0]
    direct_rows = dp == 8 and rows % 16 == 0
    direct_frames = ctx == 4 and own % 16 == 0
    ids = (0, 6, 4, 2, 1, 7, 5, 3) if direct_rows else (0,)
    parts = ctx if direct_frames else 1
    part_rows = frames // parts
    me = lax.axis_index("dp").astype(jnp.int32).reshape(1)
    place = lax.axis_index("ctx").astype(jnp.int32).reshape(1)
    cot_scale = 1.0 / math.sqrt(dp * frames)

    def gather_frames(values):
        if not direct_frames:
            return [lax.all_gather(values, "ctx", axis=0, tiled=True)]
        return [values] + [exchange(values, "ctx", mask) for mask in (1, 2, 3)]

    def scatter_frames(pieces):
        if not direct_frames:
            return [lax.psum_scatter(pieces[0], "ctx", scatter_dimension=0, tiled=True)]
        return [pieces[0]] + [exchange(pieces[mask], "ctx", mask) for mask in (1, 2, 3)]

    def scatter_rows(pieces, passed=()):
        if not direct_rows:
            made = lax.psum_scatter(pieces[0], "dp", scatter_dimension=0, tiled=True)
            return [made], passed
        keep, send = pieces
        came = exchange(send, "dp", 1)
        outs = [shape((rows, keep.shape[1]), BF)] * 4 + [shape(one.shape, BF) for one in passed]
        sums = call(pair_sum_kernel, outs, [keep, came, *passed])
        terms = [sums[0]] + [exchange(sums[at], "dp", 2 * at) for at in (1, 2, 3)]
        return terms, sums[4:] if passed else sums[:1]

    def add_terms(terms):
        total = terms[0].astype(F32)
        for one in terms[1:]:
            total = total + one.astype(F32)
        return total

    frames_own, cot_own = frames_in[0], cotangent[0]
    both_parts = gather_frames(pack([frames_own, cot_own]))

    def gather_near(weight):
        return [weight] + [exchange(weight, "dp", mask) for mask in (6, 4, 2)]

    if direct_rows:
        ffn_near = stack(gather_near(pack([w_up, w_down])), both_parts[1:])
        ffn_weights = [ffn_near, exchange(ffn_near, "dp", 1)]
        attn_pieces = gather_near(pack([w_query, w_key, w_value, w_out], [ffn_near]))
    else:
        ffn_weights = [lax.all_gather(pack([w_up, w_down]), "dp", axis=0, tiled=True)]
        attn_weights = pack([w_query, w_key, w_value, w_out])
        attn_weights = [lax.all_gather(attn_weights, "dp", axis=0, tiled=True)]
        attn_pieces = []

    made = call(
        functools.partial(ffn_kernel, parts, ids),
        [
            shape((frames, model), BF),
            shape((frames, hidden), F32),
            shape((frames, hidden), BF),
            shape((model, hidden), BF),
        ]
        + [shape((part_rows, model), BF)] * parts,
        [me, ffn_gain] + both_parts + ffn_weights,
        [pltpu.VMEM((model, hidden), BF)],
        flops=4 * frames * model * hidden,
        smem=1,
    )
    ffn_normed, ffn_pre, ffn_hidden, down_full = made[:4]
    summed = scatter_frames(list(made[4:]))
    near = [shape((model // 2, 4 * inner), BF)] if direct_rows else []
    mid_own, normed_own, *near = call(
        functools.partial(mid_kernel, len(summed)),
        [shape((own, model), F32), shape((own, model), BF)] + near,
        [attn_gain, frames_own] + summed + attn_pieces,
    )
    normed_parts = gather_frames(normed_own)
    if direct_rows:
        attn_weights = [near[0], exchange(near[0], "dp", 1)]
    made = call(
        functools.partial(attention_kernel, parts, ids, window, cot_scale),
        [
            shape((frames, model), BF),
            shape((frames, model), BF),
            shape((frames, inner), BF),
            shape((frames, 3 * inner), BF),
            shape((frames, model), BF),
        ]
        + [shape((part_rows, model), BF)] * parts,
        [place, me, offset_bias, segment_ids, span_ids] + normed_parts + both_parts + attn_weights,
        [
            pltpu.VMEM((model, 4 * inner), BF),
            pltpu.VMEM((frames, 3 * inner), BF),
            pltpu.VMEM((frames, inner), BF),
            pltpu.VMEM((frames, inner // heads), F32),
            pltpu.VMEM((frames, inner // heads), F32),
            pltpu.VMEM((frames, model), F32),
        ],
        flops=16 * frames * model * inner + 12 * frames * frames * inner,
        smem=3,
    )
    attn_normed, scaled_cot, context, slopes = made[:4]
    attn_partial = made[4]
    upstream = scatter_frames(list(made[5:]))
    half = [shape((model // 2, 4 * inner), BF)] * 2
    attn_grads = call(
        attention_grads_kernel,
        half if direct_rows else [shape((model, 4 * inner), BF)],
        [me, attn_normed, scaled_cot, context, slopes],
        [pltpu.VMEM((model, inner), F32)],
        flops=8 * frames * model * inner,
        smem=1,
    )
    (grad_mid_own,) = call(
        functools.partial(grad_mid_kernel, len(upstream), cot_scale),
        [shape((own, model), BF)],
        [attn_gain, mid_own, cot_own] + upstream,
    )
    grad_mid_parts = gather_frames(grad_mid_own)
    attn_terms, attn_sums = scatter_rows(attn_grads)
    half = [shape((model // 2, 2 * hidden), BF)] * 2
    ffn_grads = call(
        functools.partial(ffn_grads_kernel, parts),
        half if direct_rows else [shape((model, 2 * hidden), BF)],
        [me, ffn_normed, ffn_pre, ffn_hidden, down_full] + grad_mid_parts,
        [pltpu.VMEM((frames, model), BF), pltpu.VMEM((model, hidden), F32)],
        flops=6 * frames * model * hidden,
        smem=1,
        after=attn_sums,
    )
    ffn_terms, passed = scatter_rows(ffn_grads, [attn_partial])
    if direct_frames:
        attn_sum = lax.all_to_all(passed[0], "ctx", 0, 0, tiled=True)
        attn_sum = add_terms([attn_sum[at * own : (at + 1) * own] for at in range(ctx)])
    else:
        attn_sum = lax.psum_scatter(passed[0], "ctx", scatter_dimension=0, tiled=True)
    block_out = (mid_own + attn_sum).astype(BF)[None]
    attn_total, ffn_total = add_terms(attn_terms), add_terms(ffn_terms)
    return (
        block_out,
        ffn_total[:, :hidden],
        ffn_total[:, hidden:],
        attn_total[:, :inner],
        attn_total[:, inner : 2 * inner],
        attn_total[:, 2 * inner : 3 * inner],
        attn_total[:, 3 * inner :],
    )


def solution(mesh):
    placed = (
        P("dp", "ctx", None),
        P("dp", None),
        P("dp", None),
        P(),
        P("dp", "ctx"),
        P("dp", "ctx"),
        P(),
        P("dp", "ctx"),
        P("dp", "ctx"),
        P("dp", "ctx"),
        P("dp", "ctx"),
        P("ctx", None),
        P("dp", "ctx", None),
    )
    return jax.shard_map(
        per_device,
        mesh=mesh,
        in_specs=placed,
        out_specs=(P("dp", "ctx", None),) + (P("dp", "ctx"),) * 6,
        check_vma=False,
    )
```

time: 164 us -> 154 us (0.939)
  waiting for transfers between devices: 60.8 us -> 51.1 us
  Pallas kernels: 30.6 us -> 39.8 us
  starting transfers between devices: 54.8 us -> 50.7 us
  local copies, waits for them, and re-layouts: 13.7 us -> 9.98 us
    ppermute x56 -> x31, waiting for transfers between devices: 60.8 us -> 48.1 us  [exchange(): lax.ppermute(values, axis, [(one, one ^ mask) for one in range(size)])]
    pallas_call x8 -> x12, Pallas kernels: 30.6 us -> 39.8 us  [call(): pl.pallas_call(lambda *refs: body(*refs[:count], *refs[count + len(after)...]
    ppermute x56 -> x31, starting transfers between devices: 54.8 us -> 46.7 us  [exchange(): lax.ppermute(values, axis, [(one, one ^ mask) for one in range(size)])]
    all_to_all x0 -> x1, starting transfers between devices: none -> 4.02 us  [per_device(): attn_sum = lax.all_to_all(passed[0], 'ctx', 0, 0, tiled=True)]
    another operation x6 -> x0, local copies, waits for them, and re-layouts: 3.05 us -> none  [the longest x1 0.79 us: per_device(): spans.reshape(frames, 1)]
    all_to_all x0 -> x1, waiting for transfers between devices: none -> 2.99 us  [per_device(): attn_sum = lax.all_to_all(passed[0], 'ctx', 0, 0, tiled=True)]
    unnamed x138 -> x68, local copies, waits for them, and re-layouts: 6.69 us -> 8.25 us
  transfers between devices with their start and end apart: 56 -> 32, of which waited for: 23 -> 15; matrix products, arithmetic and copies ran while one was open for 7% -> 1% of each run, Pallas kernels for 14% -> 10%
where the time goes in v2:
time: 154 us; the launch traced here: 153 us
  waiting for transfers between devices  51.1 us (33%)
  starting transfers between devices  50.7 us (33%)
  Pallas kernels  39.8 us (26%)
  local copies, waits for them, and re-layouts  9.98 us (6%)
    ppermute x31, waiting for transfers between devices, exchange(): lax.ppermute(values, axis, [(one, one ^ mask) for one in range(size)])  48.1 us
    ppermute x31, starting transfers between devices, exchange(): lax.ppermute(values, axis, [(one, one ^ mask) for one in range(size)])  46.7 us
    pallas_call x12, Pallas kernels, call(): pl.pallas_call(lambda *refs: body(*refs[:count], *refs[count + len(after)...  39.8 us
    unnamed x68, local copies, waits for them, and re-layouts  8.25 us
    all_to_all x1, starting transfers between devices, per_device(): attn_sum = lax.all_to_all(passed[0], 'ctx', 0, 0, tiled=True)  4.02 us
  transfers between devices with their start and end apart: 32, of which 15 were waited for; matrix products, arithmetic and copies ran while one was open for 1% of the time, Pallas kernels for 10%

profile of v2, /device:TPU:0, one launch (start us, length us, event | category | flops | bytes accessed | tf_op | source)
XLA Modules:
  0.0 153.4 jit_solution(4140714238640564881)
XLA Ops:
  0.6 1.6 %shard_map.180.refs_2_.refs_9_ = bf16[64,1536]{1,0:T(8,128)(2,1)} custom-call(bf16[64,768]{1,0:T(8,128)(2,1)} %bitcast.13, bf16[64,768]{1,0:T(8,128)(2,1)} %bitcast.15), custom_call_target="tpu_custom_call" | custom-call | bytes 393216 | tf_op jit(solution)/shard_map/pallas_call | solution.py:28
  2.3 5.0 %collective-permute-start.2 = (bf16[64,1536]{1,0:T(8,128)(2,1)}, bf16[64,1536]{1,0:T(8,128)(2,1)S(1)}, u32[]{:S(2)}, u32[]{:S(2)}) collective-permute-start(bf16[64,1536]{1,0:T(8,128)(2,1)} %shard_map.180.refs_2_.refs_9_), channel_id=1, source_target_pairs={{0,3},{1,2},{2,1},{3,0},{4,7},{5,6},{6,5},{7,4},{8,11},{9,10},{10,... | collective-permute-start | bytes 589832 | tf_op jit(solution)/shard_map/ppermute | solution.py:19
  7.3 1.7 %shard_map.181.refs_0_ = bf16[96,1536]{1,0:T(8,128)(2,1)} custom-call(bf16[96,768]{1,0:T(8,128)(2,1)} %refs_0_.4, bf16[96,768]{1,0:T(8,128)(2,1)} %refs_1_.3), custom_call_target="tpu_custom_call" | custom-call | bytes 589824 | tf_op jit(solution)/shard_map/pallas_call | solution.py:28
  9.0 1.5 collective-permute-start.5
  10.5 1.5 collective-permute-start.4
  12.5 9.0 %collective-permute-start = (bf16[64,1536]{1,0:T(8,128)(2,1)}, bf16[64,1536]{1,0:T(8,128)(2,1)S(1)}, u32[]{:S(2)}, u32[]{:S(2)}) collective-permute-start(bf16[64,1536]{1,0:T(8,128)(2,1)} %shard_map.180.refs_2_.refs_9_), channel_id=1, source_target_pairs={{0,1},{1,0},{2,3},{3,2},{4,5},{5,4},{6,7},{7,6},{8,9},{9,8},{10,11... | collective-permute-start | bytes 589832 | tf_op jit(solution)/shard_map/ppermute | solution.py:19
  21.5 2.8 %collective-permute-done.1.refs_5_.refs_4_.refs_11_ = bf16[64,1536]{1,0:T(8,128)(2,1)S(1)} collective-permute-done((bf16[64,1536]{1,0:T(8,128)(2,1)}, bf16[64,1536]{1,0:T(8,128)(2,1)S(1)}, u32[]{:S(2)}, u32[]{:S(2)}) %collective-permute-start.1) | collective-permute-done | bytes 196640 | tf_op jit(solution)/shard_map/ppermute | solution.py:19
  24.3 4.0 %collective-permute-done.refs_4_.refs_3_.refs_10_ = bf16[64,1536]{1,0:T(8,128)(2,1)S(1)} collective-permute-done((bf16[64,1536]{1,0:T(8,128)(2,1)}, bf16[64,1536]{1,0:T(8,128)(2,1)S(1)}, u32[]{:S(2)}, u32[]{:S(2)}) %collective-permute-start) | collective-permute-done | bytes 196640 | tf_op jit(solution)/shard_map/ppermute | solution.py:19
  29.9 2.3 %shard_map.182.refs_6_.refs_4_ = bf16[384,1536]{1,0:T(8,128)(2,1)} custom-call(bf16[96,1536]{1,0:T(8,128)(2,1)} %shard_map.181.refs_0_, bf16[96,1536]{1,0:T(8,128)(2,1)} %copy-done.13, bf16[96,1536]{1,0:T(8,128)(2,1)} %copy-done.12, bf16[96,1536]{1,0:T(8,128)(2,1)} %copy-done.11, bf16[64,1536]{1,0:T(8,128)(2,1)} %copy-done.7, bf16[64,1536]{1,0:T(8,128)(2,1)} %copy-done.6, ...), custom_call_target="tpu_custom_call" | custom-call | bytes 2359296 | tf_op jit(solution)/shard_map/pallas_call | solution.py:28
  32.3 1.8 %shard_map.184.refs_6_ = bf16[96,2048]{1,0:T(8,128)(2,1)} custom-call(bf16[96,512]{1,0:T(8,128)(2,1)} %refs_0_.5, bf16[96,512]{1,0:T(8,128)(2,1)} %refs_1_.5, bf16[96,512]{1,0:T(8,128)(2,1)} %refs_2_.2, bf16[96,512]{1,0:T(8,128)(2,1)} %refs_3_.2, bf16[384,1536]{1,0:T(8,128)(2,1)} %shard_map.182.refs_6_.refs_4_), custom_call_target="tpu_custom_call" | custom-call | bytes 786432 | tf_op jit(solution)/shard_map/pallas_call | solution.py:28
  34.1 1.5 collective-permute-start.12
  35.6 1.5 collective-permute-start.11
  38.6 4.1 %shard_map.183 = (bf16[256,768]{1,0:T(8,128)(2,1)}, f32[256,768]{1,0:T(8,128)}, bf16[256,768]{1,0:T(8,128)(2,1)}, bf16[768,768]{1,0:T(8,128)(2,1)}, bf16[64,768]...) custom-call(s32[1]{0:T(128)} %bitcast.1.refs_0_.refs_1_, ...), custom_call_target="tpu_custom_call" | custom-call | flops 603979776 | bytes 6294532 | tf_op jit(solution)/shard_map/pallas_call | solution.py:28
  42.7 2.8 %collective-permute-start.8 = (bf16[64,768]{1,0:T(8,128)(2,1)}, bf16[64,768]{1,0:T(8,128)(2,1)S(1)}, u32[]{:S(2)}, u32[]{:S(2)}) collective-permute-start(bf16[64,768]{1,0:T(8,128)(2,1)} %get-tuple-element.42), channel_id=1, source_target_pairs={{0,2},{1,3},{2,0},{3,1},{4,6},{5,7},{6,4},{7,5},{8,10},{9,11},{10,... | collective-permute-start | bytes 294920 | tf_op jit(solution)/shard_map/ppermute | solution.py:19
  46.2 2.3 %collective-permute-start.9 = (bf16[64,768]{1,0:T(8,128)(2,1)}, bf16[64,768]{1,0:T(8,128)(2,1)S(1)}, u32[]{:S(2)}, u32[]{:S(2)}) collective-permute-start(bf16[64,768]{1,0:T(8,128)(2,1)} %get-tuple-element.43), channel_id=1, source_target_pairs={{0,3},{1,2},{2,1},{3,0},{4,7},{5,6},{6,5},{7,4},{8,11},{9,10},{10,... | collective-permute-start | bytes 294920 | tf_op jit(solution)/shard_map/ppermute | solution.py:19
  48.5 7.0 %collective-permute-done.11.refs_8_ = bf16[96,2048]{1,0:T(8,128)(2,1)S(1)} collective-permute-done((bf16[96,2048]{1,0:T(8,128)(2,1)}, bf16[96,2048]{1,0:T(8,128)(2,1)S(1)}, u32[]{:S(2)}, u32[]{:S(2)}) %collective-permute-start.11) | collective-permute-done | bytes 393248 | tf_op jit(solution)/shard_map/ppermute | solution.py:19
  56.4 3.1 %shard_map.185 = (f32[64,768]{1,0:T(8,128)}, bf16[64,768]{1,0:T(8,128)(2,1)}, bf16[384,2048]{1,0:T(8,128)(2,1)}) custom-call(f32[768]{0:T(1024)} %refs_0_.7, bf16[64,768]{1,0:T(8,128)(2,1)} %bitcast.14, bf16[64,768]{1,0:T(8,128)(2,1)} %get-tuple-element.40.refs_2_, bf16[64,768]{1,0:T(8,128)(2,1)} %copy-done.15, bf16[64,768]{1,0:T(8,128)(2,1)} %copy-done.16, ...), custom_call_target="tpu_custom_call" | custom-call | bytes 3935232 | tf_op jit(solution)/shard_map/pallas_call | solution.py:28
  59.5 2.3 %collective-permute-start.15 = (bf16[64,768]{1,0:T(8,128)(2,1)}, bf16[64,768]{1,0:T(8,128)(2,1)S(1)}, u32[]{:S(2)}, u32[]{:S(2)}) collective-permute-start(bf16[64,768]{1,0:T(8,128)(2,1)} %get-tuple-element.49.refs_5_), channel_id=1, source_target_pairs={{0,3},{1,2},{2,1},{3,0},{4,7},{5,6},{6,5},{7,4},{8,11},{9,10},{10,... | collective-permute-start | bytes 294920 | tf_op jit(solution)/shard_map/ppermute | solution.py:19
  61.8 2.1 %collective-permute-start.13 = (bf16[64,768]{1,0:T(8,128)(2,1)}, bf16[64,768]{1,0:T(8,128)(2,1)S(1)}, u32[]{:S(2)}, u32[]{:S(2)}) collective-permute-start(bf16[64,768]{1,0:T(8,128)(2,1)} %get-tuple-element.49.refs_5_), channel_id=1, source_target_pairs={{0,1},{1,0},{2,3},{3,2},{4,5},{5,4},{6,7},{7,6},{8,9},{9,8},{10,11... | collective-permute-start | bytes 294920 | tf_op jit(solution)/shard_map/ppermute | solution.py:19
  63.9 3.3 %collective-permute-done.15.refs_8_ = bf16[64,768]{1,0:T(8,128)(2,1)S(1)} collective-permute-done((bf16[64,768]{1,0:T(8,128)(2,1)}, bf16[64,768]{1,0:T(8,128)(2,1)S(1)}, u32[]{:S(2)}, u32[]{:S(2)}) %collective-permute-start.15) | collective-permute-done | bytes 98336 | tf_op jit(solution)/shard_map/ppermute | solution.py:19
  67.2 3.7 %collective-permute-done.14.refs_7_ = bf16[64,768]{1,0:T(8,128)(2,1)S(1)} collective-permute-done((bf16[64,768]{1,0:T(8,128)(2,1)}, bf16[64,768]{1,0:T(8,128)(2,1)S(1)}, u32[]{:S(2)}, u32[]{:S(2)}) %collective-permute-start.14) | collective-permute-done | bytes 98336 | tf_op jit(solution)/shard_map/ppermute | solution.py:19
  72.1 7.7 %shard_map.186 = (bf16[256,768]{1,0:T(8,128)(2,1)}, bf16[256,768]{1,0:T(8,128)(2,1)}, bf16[256,512]{1,0:T(8,128)(2,1)}, bf16[256,1536]{1,0:T(8,128)(2,1)}, bf16[...) custom-call(s32[1]{0:T(128)} %bitcast.3.refs_0_, ...), custom_call_target="tpu_custom_call" | custom-call | flops 2013265920 | bytes 6949016 | tf_op jit(solution)/shard_map/pallas_call | solution.py:28
  79.8 4.5 %shard_map.188 = (bf16[384,2048]{1,0:T(8,128)(2,1)}, bf16[384,2048]{1,0:T(8,128)(2,1)}) custom-call(s32[1]{0:T(128)} %bitcast.1.refs_0_.refs_1_, bf16[256,768]{1,0:T(8,128)(2,1)} %get-tuple-element.55.refs_1_, bf16[256,768]{1,0:T(8,128)(2,1)} %get-tuple-element.56.refs_2_, bf16[256,512]{1,0:T(8,128)(2,1)} %get-tuple-element.57.refs_3_, ...), custom_call_target="tpu_custom_call" | custom-call | flops 805306368 | bytes 4980740 | tf_op jit(solution)/shard_map/pallas_call | solution.py:28
  84.9 2.4 %collective-permute-start.18 = (bf16[64,768]{1,0:T(8,128)(2,1)S(1)}, bf16[64,768]{1,0:T(8,128)(2,1)S(1)}, u32[]{:S(2)}, u32[]{:S(2)}) collective-permute-start(bf16[64,768]{1,0:T(8,128)(2,1)S(1)} %copy-done.30), channel_id=1, source_target_pairs={{0,2},{1,3},{2,0},{3,1},{4,6},{5,7},{6,4},{7,5},{8,10},{9,11},{10,... | collective-permute-start | bytes 294920 | tf_op jit(solution)/shard_map/ppermute | solution.py:19
  87.2 1.5 collective-permute-start.19
  88.8 2.2 %collective-permute-done.17.refs_4_ = bf16[64,768]{1,0:T(8,128)(2,1)S(1)} collective-permute-done((bf16[64,768]{1,0:T(8,128)(2,1)S(1)}, bf16[64,768]{1,0:T(8,128)(2,1)S(1)}, u32[]{:S(2)}, u32[]{:S(2)}) %collective-permute-start.17) | collective-permute-done | bytes 98336 | tf_op jit(solution)/shard_map/ppermute | solution.py:19
  91.0 4.7 %collective-permute-done.18.refs_5_ = bf16[64,768]{1,0:T(8,128)(2,1)S(1)} collective-permute-done((bf16[64,768]{1,0:T(8,128)(2,1)S(1)}, bf16[64,768]{1,0:T(8,128)(2,1)S(1)}, u32[]{:S(2)}, u32[]{:S(2)}) %collective-permute-start.18) | collective-permute-done | bytes 98336 | tf_op jit(solution)/shard_map/ppermute | solution.py:19
  96.4 2.1 %shard_map.187.refs_5_ = bf16[64,768]{1,0:T(8,128)(2,1)} custom-call(f32[768]{0:T(1024)} %refs_0_.7, f32[64,768]{1,0:T(8,128)} %get-tuple-element.44.refs_1_, bf16[64,768]{1,0:T(8,128)(2,1)} %bitcast.16, bf16[64,768]{1,0:T(8,128)(2,1)} %get-tuple-element.51.refs_3_, bf16[64,768]{1,0:T(8,128)(2,1)} %copy-done.18, bf16[64,768]{1,0:T(8,128)(2,1)} %copy-done.19, ...), custom_call_target="tpu_custom_call" | custom-call | bytes 789504 | tf_op jit(solution)/shard_map/pallas_call | solution.py:28
  98.5 1.8 %collective-permute-start.22 = (bf16[64,768]{1,0:T(8,128)(2,1)}, bf16[64,768]{1,0:T(8,128)(2,1)S(1)}, u32[]{:S(2)}, u32[]{:S(2)}) collective-permute-start(bf16[64,768]{1,0:T(8,128)(2,1)} %shard_map.187.refs_5_), channel_id=1, source_target_pairs={{0,3},{1,2},{2,1},{3,0},{4,7},{5,6},{6,5},{7,4},{8,11},{9,10},{10,... | collective-permute-start | bytes 294920 | tf_op jit(solution)/shard_map/ppermute | solution.py:19
  100.3 1.5 collective-permute-start.21
  101.8 1.1 collective-permute-start.20
  102.9 1.2 copy-done
  104.1 3.2 %shard_map.189 = (bf16[96,2048]{1,0:T(8,128)(2,1)}, bf16[96,2048]{1,0:T(8,128)(2,1)}, bf16[96,2048]{1,0:T(8,128)(2,1)}, bf16[96,2048]{1,0:T(8,128)(2,1)}) custom-call(bf16[384,2048]{1,0:T(8,128)(2,1)} %get-tuple-element.59.refs_0_, bf16[384,2048]{1,0:T(8,128)(2,1)} %copy-done), custom_call_target="tpu_custom_call" | custom-call | bytes 4718592 | tf_op jit(solution)/shard_map/pallas_call | solution.py:28
  107.3 2.6 %collective-permute-done.21.refs_7_ = bf16[64,768]{1,0:T(8,128)(2,1)S(1)} collective-permute-done((bf16[64,768]{1,0:T(8,128)(2,1)}, bf16[64,768]{1,0:T(8,128)(2,1)S(1)}, u32[]{:S(2)}, u32[]{:S(2)}) %collective-permute-start.21) | collective-permute-done | bytes 98336 | tf_op jit(solution)/shard_map/ppermute | solution.py:19
  110.5 4.6 %shard_map.190 = (bf16[384,1536]{1,0:T(8,128)(2,1)}, bf16[384,1536]{1,0:T(8,128)(2,1)}) custom-call(s32[1]{0:T(128)} %bitcast.1.refs_0_.refs_1_, bf16[256,768]{1,0:T(8,128)(2,1)} %get-tuple-element.45.refs_1_, f32[256,768]{1,0:T(8,128)} %get-tuple-element.46.refs_2_, bf16[256,768]{1,0:T(8,128)(2,1)} %get-tuple-element.47.refs_3_, ...), custom_call_target="tpu_custom_call" | custom-call | flops 905969664 | bytes 5505028 | tf_op jit(solution)/shard_map/pallas_call | solution.py:28
  115.1 1.2 collective-permute-start.28
  116.3 1.0 collective-permute-start.29
  117.4 1.3 collective-permute-start.30
  119.7 3.0 %shard_map.191 = (bf16[96,1536]{1,0:T(8,128)(2,1)}, bf16[96,1536]{1,0:T(8,128)(2,1)}, bf16[96,1536]{1,0:T(8,128)(2,1)}, bf16[96,1536]{1,0:T(8,128)(2,1)}, bf16[256,768]{1,0:T(8,128)(2,1)}) custom-call(bf16[384,1536]{1,0:T(8,128)(2,1)} %get-tuple-element.62.refs_0_, bf16[384,1536]{1,0:T(8,128)(2,1)} %copy-done.3, bf16[256,768]{1,0:T(8,128)(2,1)} %get-tuple-element.64.refs_2_), custom_call_target="tpu_custom_call" | custom-call | bytes 4325376 | tf_op jit(solution)/shard_map/pallas_call | solution.py:28
  122.7 1.1 collective-permute-start.25
  123.8 1.0 collective-permute-start.26
  124.9 2.3 %collective-permute-done.28 = bf16[96,2048]{1,0:T(8,128)(2,1)S(1)} collective-permute-done((bf16[96,2048]{1,0:T(8,128)(2,1)S(1)}, bf16[96,2048]{1,0:T(8,128)(2,1)S(1)}, u32[]{:S(2)}, u32[]{:S(2)}) %collective-permute-start.28) | collective-permute-done | bytes 393248 | tf_op jit(solution)/shard_map/ppermute | solution.py:19
  127.1 1.6 %collective-permute-start.27 = (bf16[96,1536]{1,0:T(8,128)(2,1)}, bf16[96,1536]{1,0:T(8,128)(2,1)S(1)}, u32[]{:S(2)}, u32[]{:S(2)}) collective-permute-start(bf16[96,1536]{1,0:T(8,128)(2,1)} %get-tuple-element.69), channel_id=1, source_target_pairs={{0,24},{4,28},{8,16},{12,20},{16,8},{20,12},{24,0},{28,4},{1,25},{... | collective-permute-start | bytes 884744 | tf_op jit(solution)/shard_map/ppermute | solution.py:19
  128.7 8.0 %collective-permute-done.29 = bf16[96,2048]{1,0:T(8,128)(2,1)S(1)} collective-permute-done((bf16[96,2048]{1,0:T(8,128)(2,1)S(1)}, bf16[96,2048]{1,0:T(8,128)(2,1)S(1)}, u32[]{:S(2)}, u32[]{:S(2)}) %collective-permute-start.29) | collective-permute-done | bytes 393248 | tf_op jit(solution)/shard_map/ppermute | solution.py:19
  137.8 4.0 %all-to-all-start = ((bf16[4,64,768]{2,1,0:T(8,128)(2,1)}), bf16[4,64,768]{2,1,0:T(8,128)(2,1)S(1)}, u32[]{:S(2)}, u32[]{:S(2)}) async-start(bf16[4,64,768]{2,1,0:T(8,128)(2,1)} %bitcast.4), calls=%async_computation | async-start | bytes 786432 | tf_op jit(solution)/shard_map/all_to_all | solution.py:427
  141.9 5.3 %collective-permute-done.26 = bf16[96,1536]{1,0:T(8,128)(2,1)S(1)} collective-permute-done((bf16[96,1536]{1,0:T(8,128)(2,1)}, bf16[96,1536]{1,0:T(8,128)(2,1)S(1)}, u32[]{:S(2)}, u32[]{:S(2)}) %collective-permute-start.26) | collective-permute-done | bytes 294944 | tf_op jit(solution)/shard_map/ppermute | solution.py:19
  147.3 1.5 collective-permute-done.27
  149.7 3.0 %all-to-all-done = bf16[4,64,768]{2,1,0:T(8,128)(2,1)S(1)} async-done(((bf16[4,64,768]{2,1,0:T(8,128)(2,1)}), bf16[4,64,768]{2,1,0:T(8,128)(2,1)S(1)}, u32[]{:S(2)}, u32[]{:S(2)}) %all-to-all-start) | async-done | bytes 393248 | tf_op jit(solution)/shard_map/all_to_all | solution.py:427
  (101 shorter events, 12.2 us)
Async XLA Ops:
  2.3 10.3 %collective-permute-start.2 = (bf16[64,1536]{1,0:T(8,128)(2,1)}, bf16[64,1536]{1,0:T(8,128)(2,1)S(1)}, u32[]{:S(2)}, u32[]{:S(2)}) collective-permute-start(bf16[64,1536]{1,0:T(8,128)(2,1)} %shard_map.180.refs_2_.refs_9_), channel_id=1, source_target_pairs={{0,3},{1,2},{2,1},{3,0},{4,7},{5,6},{6,5},{7,4},{8,11},{9,10},{10,... | collective-permute-start | bytes 589832 | tf_op jit(solution)/shard_map/ppermute | solution.py:19
  9.0 19.3 %collective-permute-start.5 = (bf16[96,1536]{1,0:T(8,128)(2,1)}, bf16[96,1536]{1,0:T(8,128)(2,1)S(1)}, u32[]{:S(2)}, u32[]{:S(2)}) collective-permute-start(bf16[96,1536]{1,0:T(8,128)(2,1)} %shard_map.181.refs_0_), channel_id=1, source_target_pairs={{0,8},{4,12},{8,0},{12,4},{16,24},{20,28},{24,16},{28,20},{1,9},{5... | collective-permute-start | bytes 884744 | tf_op jit(solution)/shard_map/ppermute | solution.py:19
  10.5 17.8 %collective-permute-start.4 = (bf16[96,1536]{1,0:T(8,128)(2,1)}, bf16[96,1536]{1,0:T(8,128)(2,1)S(1)}, u32[]{:S(2)}, u32[]{:S(2)}) collective-permute-start(bf16[96,1536]{1,0:T(8,128)(2,1)} %shard_map.181.refs_0_), channel_id=1, source_target_pairs={{0,16},{4,20},{8,24},{12,28},{16,0},{20,4},{24,8},{28,12},{1,17},{... | collective-permute-start | bytes 884744 | tf_op jit(solution)/shard_map/ppermute | solution.py:19
  12.0 16.3 %collective-permute-start.3 = (bf16[96,1536]{1,0:T(8,128)(2,1)}, bf16[96,1536]{1,0:T(8,128)(2,1)S(1)}, u32[]{:S(2)}, u32[]{:S(2)}) collective-permute-start(bf16[96,1536]{1,0:T(8,128)(2,1)} %shard_map.181.refs_0_), channel_id=1, source_target_pairs={{0,24},{4,28},{8,16},{12,20},{16,8},{20,12},{24,0},{28,4},{1,25},{... | collective-permute-start | bytes 884744 | tf_op jit(solution)/shard_map/ppermute | solution.py:19
  12.5 11.8 %collective-permute-start.1 = (bf16[64,1536]{1,0:T(8,128)(2,1)}, bf16[64,1536]{1,0:T(8,128)(2,1)S(1)}, u32[]{:S(2)}, u32[]{:S(2)}) collective-permute-start(bf16[64,1536]{1,0:T(8,128)(2,1)} %shard_map.180.refs_2_.refs_9_), channel_id=1, source_target_pairs={{0,2},{1,3},{2,0},{3,1},{4,6},{5,7},{6,4},{7,5},{8,10},{9,11},{10,... | collective-permute-start | bytes 589832 | tf_op jit(solution)/shard_map/ppermute | solution.py:19
  12.5 15.8 %copy-start.5 = (bf16[64,1536]{1,0:T(8,128)(2,1)}, bf16[64,1536]{1,0:T(8,128)(2,1)S(1)}, u32[]{:S(2)}) copy-start(bf16[64,1536]{1,0:T(8,128)(2,1)S(1)} %collective-permute-done.2.refs_6_.refs_5_.refs_12_) | copy-start | bytes 589828
  12.5 15.8 %collective-permute-start = (bf16[64,1536]{1,0:T(8,128)(2,1)}, bf16[64,1536]{1,0:T(8,128)(2,1)S(1)}, u32[]{:S(2)}, u32[]{:S(2)}) collective-permute-start(bf16[64,1536]{1,0:T(8,128)(2,1)} %shard_map.180.refs_2_.refs_9_), channel_id=1, source_target_pairs={{0,1},{1,0},{2,3},{3,2},{4,5},{5,4},{6,7},{7,6},{8,9},{9,8},{10,11... | collective-permute-start | bytes 589832 | tf_op jit(solution)/shard_map/ppermute | solution.py:19
  24.3 4.1 %copy-start.6 = (bf16[64,1536]{1,0:T(8,128)(2,1)}, bf16[64,1536]{1,0:T(8,128)(2,1)S(1)}, u32[]{:S(2)}) copy-start(bf16[64,1536]{1,0:T(8,128)(2,1)S(1)} %collective-permute-done.1.refs_5_.refs_4_.refs_11_) | copy-start | bytes 589828
  32.3 5.3 %collective-permute-start.6 = (bf16[384,1536]{1,0:T(8,128)(2,1)}, bf16[384,1536]{1,0:T(8,128)(2,1)S(1)}, u32[]{:S(2)}, u32[]{:S(2)}) collective-permute-start(bf16[384,1536]{1,0:T(8,128)(2,1)} %shard_map.182.refs_6_.refs_4_), channel_id=1, source_target_pairs={{0,4},{4,0},{8,12},{12,8},{16,20},{20,16},{24,28},{28,24},{1,5},{5... | collective-permute-start | bytes 3538952 | tf_op jit(solution)/shard_map/ppermute | solution.py:19
  34.1 12.1 %collective-permute-start.12 = (bf16[96,2048]{1,0:T(8,128)(2,1)}, bf16[96,2048]{1,0:T(8,128)(2,1)S(1)}, u32[]{:S(2)}, u32[]{:S(2)}) collective-permute-start(bf16[96,2048]{1,0:T(8,128)(2,1)} %shard_map.184.refs_6_), channel_id=1, source_target_pairs={{0,8},{4,12},{8,0},{12,4},{16,24},{20,28},{24,16},{28,20},{1,9},{5... | collective-permute-start | bytes 1179656 | tf_op jit(solution)/shard_map/ppermute | solution.py:19
  35.6 19.9 %collective-permute-start.11 = (bf16[96,2048]{1,0:T(8,128)(2,1)}, bf16[96,2048]{1,0:T(8,128)(2,1)S(1)}, u32[]{:S(2)}, u32[]{:S(2)}) collective-permute-start(bf16[96,2048]{1,0:T(8,128)(2,1)} %shard_map.184.refs_6_), channel_id=1, source_target_pairs={{0,16},{4,20},{8,24},{12,28},{16,0},{20,4},{24,8},{28,12},{1,17},{... | collective-permute-start | bytes 1179656 | tf_op jit(solution)/shard_map/ppermute | solution.py:19
  37.1 18.4 %collective-permute-start.10 = (bf16[96,2048]{1,0:T(8,128)(2,1)}, bf16[96,2048]{1,0:T(8,128)(2,1)S(1)}, u32[]{:S(2)}, u32[]{:S(2)}) collective-permute-start(bf16[96,2048]{1,0:T(8,128)(2,1)} %shard_map.184.refs_6_), channel_id=1, source_target_pairs={{0,24},{4,28},{8,16},{12,20},{16,8},{20,12},{24,0},{28,4},{1,25},{... | collective-permute-start | bytes 1179656 | tf_op jit(solution)/shard_map/ppermute | solution.py:19
  42.7 12.7 %collective-permute-start.7 = (bf16[64,768]{1,0:T(8,128)(2,1)}, bf16[64,768]{1,0:T(8,128)(2,1)S(1)}, u32[]{:S(2)}, u32[]{:S(2)}) collective-permute-start(bf16[64,768]{1,0:T(8,128)(2,1)} %get-tuple-element.41), channel_id=1, source_target_pairs={{0,1},{1,0},{2,3},{3,2},{4,5},{5,4},{6,7},{7,6},{8,9},{9,8},{10,11... | collective-permute-start | bytes 294920 | tf_op jit(solution)/shard_map/ppermute | solution.py:19
  42.7 12.7 %collective-permute-start.8 = (bf16[64,768]{1,0:T(8,128)(2,1)}, bf16[64,768]{1,0:T(8,128)(2,1)S(1)}, u32[]{:S(2)}, u32[]{:S(2)}) collective-permute-start(bf16[64,768]{1,0:T(8,128)(2,1)} %get-tuple-element.42), channel_id=1, source_target_pairs={{0,2},{1,3},{2,0},{3,1},{4,6},{5,7},{6,4},{7,5},{8,10},{9,11},{10,... | collective-permute-start | bytes 294920 | tf_op jit(solution)/shard_map/ppermute | solution.py:19
  46.2 9.3 %copy-start.8 = (bf16[96,2048]{1,0:T(8,128)(2,1)}, bf16[96,2048]{1,0:T(8,128)(2,1)S(1)}, u32[]{:S(2)}) copy-start(bf16[96,2048]{1,0:T(8,128)(2,1)S(1)} %collective-permute-done.12.refs_9_) | copy-start | bytes 1179652
  46.2 9.3 %collective-permute-start.9 = (bf16[64,768]{1,0:T(8,128)(2,1)}, bf16[64,768]{1,0:T(8,128)(2,1)S(1)}, u32[]{:S(2)}, u32[]{:S(2)}) collective-permute-start(bf16[64,768]{1,0:T(8,128)(2,1)} %get-tuple-element.43), channel_id=1, source_target_pairs={{0,3},{1,2},{2,1},{3,0},{4,7},{5,6},{6,5},{7,4},{8,11},{9,10},{10,... | collective-permute-start | bytes 294920 | tf_op jit(solution)/shard_map/ppermute | solution.py:19
  59.5 11.4 %collective-permute-start.16 = (bf16[384,2048]{1,0:T(8,128)(2,1)}, bf16[384,2048]{1,0:T(8,128)(2,1)S(1)}, u32[]{:S(2)}, u32[]{:S(2)}) collective-permute-start(bf16[384,2048]{1,0:T(8,128)(2,1)} %get-tuple-element.50.refs_13_), channel_id=1, source_target_pairs={{0,4},{4,0},{8,12},{12,8},{16,20},{20,16},{24,28},{28,24},{1,5},{5... | collective-permute-start | bytes 4718600 | tf_op jit(solution)/shard_map/ppermute | solution.py:19
  59.5 7.7 %collective-permute-start.15 = (bf16[64,768]{1,0:T(8,128)(2,1)}, bf16[64,768]{1,0:T(8,128)(2,1)S(1)}, u32[]{:S(2)}, u32[]{:S(2)}) collective-permute-start(bf16[64,768]{1,0:T(8,128)(2,1)} %get-tuple-element.49.refs_5_), channel_id=1, source_target_pairs={{0,3},{1,2},{2,1},{3,0},{4,7},{5,6},{6,5},{7,4},{8,11},{9,10},{10,... | collective-permute-start | bytes 294920 | tf_op jit(solution)/shard_map/ppermute | solution.py:19
  61.8 9.1 %collective-permute-start.14 = (bf16[64,768]{1,0:T(8,128)(2,1)}, bf16[64,768]{1,0:T(8,128)(2,1)S(1)}, u32[]{:S(2)}, u32[]{:S(2)}) collective-permute-start(bf16[64,768]{1,0:T(8,128)(2,1)} %get-tuple-element.49.refs_5_), channel_id=1, source_target_pairs={{0,2},{1,3},{2,0},{3,1},{4,6},{5,7},{6,4},{7,5},{8,10},{9,11},{10,... | collective-permute-start | bytes 294920 | tf_op jit(solution)/shard_map/ppermute | solution.py:19
  61.8 9.1 %collective-permute-start.13 = (bf16[64,768]{1,0:T(8,128)(2,1)}, bf16[64,768]{1,0:T(8,128)(2,1)S(1)}, u32[]{:S(2)}, u32[]{:S(2)}) collective-permute-start(bf16[64,768]{1,0:T(8,128)(2,1)} %get-tuple-element.49.refs_5_), channel_id=1, source_target_pairs={{0,1},{1,0},{2,3},{3,2},{4,5},{5,4},{6,7},{7,6},{8,9},{9,8},{10,11... | collective-permute-start | bytes 294920 | tf_op jit(solution)/shard_map/ppermute | solution.py:19
  67.2 3.8 %copy-start.29 = (bf16[64,768]{1,0:T(8,128)(2,1)}, bf16[64,768]{1,0:T(8,128)(2,1)S(1)}, u32[]{:S(2)}) copy-start(bf16[64,768]{1,0:T(8,128)(2,1)S(1)} %collective-permute-done.15.refs_8_) | copy-start | bytes 294916
  70.9 1.2 copy-start.24
  79.8 4.5 %copy-start.32 = (bf16[64,768]{1,0:T(8,128)(2,1)S(1)}, bf16[64,768]{1,0:T(8,128)(2,1)}, u32[]{:S(2)}) copy-start(bf16[64,768]{1,0:T(8,128)(2,1)} %get-tuple-element.52) | copy-start | bytes 294916
  79.8 5.1 %copy-start.30 = (bf16[64,768]{1,0:T(8,128)(2,1)S(1)}, bf16[64,768]{1,0:T(8,128)(2,1)}, u32[]{:S(2)}) copy-start(bf16[64,768]{1,0:T(8,128)(2,1)} %get-tuple-element.53) | copy-start | bytes 294916
  79.8 7.4 %copy-start.28 = (bf16[64,768]{1,0:T(8,128)(2,1)S(1)}, bf16[64,768]{1,0:T(8,128)(2,1)}, u32[]{:S(2)}) copy-start(bf16[64,768]{1,0:T(8,128)(2,1)} %get-tuple-element.54) | copy-start | bytes 294916
  84.3 18.6 %collective-permute-start.23 = (bf16[384,2048]{1,0:T(8,128)(2,1)}, bf16[384,2048]{1,0:T(8,128)(2,1)S(1)}, u32[]{:S(2)}, u32[]{:S(2)}) collective-permute-start(bf16[384,2048]{1,0:T(8,128)(2,1)} %get-tuple-element.60), channel_id=1, source_target_pairs={{0,4},{4,0},{8,12},{12,8},{16,20},{20,16},{24,28},{28,24},{1,5},{5... | collective-permute-start | bytes 4718600 | tf_op jit(solution)/shard_map/ppermute | solution.py:19
  84.4 6.6 %collective-permute-start.17 = (bf16[64,768]{1,0:T(8,128)(2,1)S(1)}, bf16[64,768]{1,0:T(8,128)(2,1)S(1)}, u32[]{:S(2)}, u32[]{:S(2)}) collective-permute-start(bf16[64,768]{1,0:T(8,128)(2,1)S(1)} %copy-done.32), channel_id=1, source_target_pairs={{0,1},{1,0},{2,3},{3,2},{4,5},{5,4},{6,7},{7,6},{8,9},{9,8},{10,11... | collective-permute-start | bytes 294920 | tf_op jit(solution)/shard_map/ppermute | solution.py:19
  84.9 10.8 %collective-permute-start.18 = (bf16[64,768]{1,0:T(8,128)(2,1)S(1)}, bf16[64,768]{1,0:T(8,128)(2,1)S(1)}, u32[]{:S(2)}, u32[]{:S(2)}) collective-permute-start(bf16[64,768]{1,0:T(8,128)(2,1)S(1)} %copy-done.30), channel_id=1, source_target_pairs={{0,2},{1,3},{2,0},{3,1},{4,6},{5,7},{6,4},{7,5},{8,10},{9,11},{10,... | collective-permute-start | bytes 294920 | tf_op jit(solution)/shard_map/ppermute | solution.py:19
  87.2 8.4 %collective-permute-start.19 = (bf16[64,768]{1,0:T(8,128)(2,1)S(1)}, bf16[64,768]{1,0:T(8,128)(2,1)S(1)}, u32[]{:S(2)}, u32[]{:S(2)}) collective-permute-start(bf16[64,768]{1,0:T(8,128)(2,1)S(1)} %copy-done.28), channel_id=1, source_target_pairs={{0,3},{1,2},{2,1},{3,0},{4,7},{5,6},{6,5},{7,4},{8,11},{9,10},{10,... | collective-permute-start | bytes 294920 | tf_op jit(solution)/shard_map/ppermute | solution.py:19
  91.0 4.7 %copy-start.18 = (bf16[64,768]{1,0:T(8,128)(2,1)}, bf16[64,768]{1,0:T(8,128)(2,1)S(1)}, u32[]{:S(2)}) copy-start(bf16[64,768]{1,0:T(8,128)(2,1)S(1)} %collective-permute-done.17.refs_4_) | copy-start | bytes 294916
  98.5 8.8 %collective-permute-start.22 = (bf16[64,768]{1,0:T(8,128)(2,1)}, bf16[64,768]{1,0:T(8,128)(2,1)S(1)}, u32[]{:S(2)}, u32[]{:S(2)}) collective-permute-start(bf16[64,768]{1,0:T(8,128)(2,1)} %shard_map.187.refs_5_), channel_id=1, source_target_pairs={{0,3},{1,2},{2,1},{3,0},{4,7},{5,6},{6,5},{7,4},{8,11},{9,10},{10,... | collective-permute-start | bytes 294920 | tf_op jit(solution)/shard_map/ppermute | solution.py:19
  100.3 9.5 %collective-permute-start.21 = (bf16[64,768]{1,0:T(8,128)(2,1)}, bf16[64,768]{1,0:T(8,128)(2,1)S(1)}, u32[]{:S(2)}, u32[]{:S(2)}) collective-permute-start(bf16[64,768]{1,0:T(8,128)(2,1)} %shard_map.187.refs_5_), channel_id=1, source_target_pairs={{0,2},{1,3},{2,0},{3,1},{4,6},{5,7},{6,4},{7,5},{8,10},{9,11},{10,... | collective-permute-start | bytes 294920 | tf_op jit(solution)/shard_map/ppermute | solution.py:19
  101.8 8.0 %collective-permute-start.20 = (bf16[64,768]{1,0:T(8,128)(2,1)}, bf16[64,768]{1,0:T(8,128)(2,1)S(1)}, u32[]{:S(2)}, u32[]{:S(2)}) collective-permute-start(bf16[64,768]{1,0:T(8,128)(2,1)} %shard_map.187.refs_5_), channel_id=1, source_target_pairs={{0,1},{1,0},{2,3},{3,2},{4,5},{5,4},{6,7},{7,6},{8,9},{9,8},{10,11... | collective-permute-start | bytes 294920 | tf_op jit(solution)/shard_map/ppermute | solution.py:19
  107.3 2.6 %copy-start.21 = (bf16[64,768]{1,0:T(8,128)(2,1)}, bf16[64,768]{1,0:T(8,128)(2,1)S(1)}, u32[]{:S(2)}) copy-start(bf16[64,768]{1,0:T(8,128)(2,1)S(1)} %collective-permute-done.22.refs_8_) | copy-start | bytes 294916
  110.5 4.6 %copy-start.27 = (bf16[96,2048]{1,0:T(8,128)(2,1)S(1)}, bf16[96,2048]{1,0:T(8,128)(2,1)}, u32[]{:S(2)}) copy-start(bf16[96,2048]{1,0:T(8,128)(2,1)} %get-tuple-element.70) | copy-start | bytes 1179652
  110.5 5.8 %copy-start.26 = (bf16[96,2048]{1,0:T(8,128)(2,1)S(1)}, bf16[96,2048]{1,0:T(8,128)(2,1)}, u32[]{:S(2)}) copy-start(bf16[96,2048]{1,0:T(8,128)(2,1)} %get-tuple-element.71) | copy-start | bytes 1179652
  110.5 6.9 %copy-start.25 = (bf16[96,2048]{1,0:T(8,128)(2,1)S(1)}, bf16[96,2048]{1,0:T(8,128)(2,1)}, u32[]{:S(2)}) copy-start(bf16[96,2048]{1,0:T(8,128)(2,1)} %get-tuple-element.72) | copy-start | bytes 1179652
  115.1 3.6 %collective-permute-start.24 = (bf16[384,1536]{1,0:T(8,128)(2,1)}, bf16[384,1536]{1,0:T(8,128)(2,1)S(1)}, u32[]{:S(2)}, u32[]{:S(2)}) collective-permute-start(bf16[384,1536]{1,0:T(8,128)(2,1)} %get-tuple-element.63), channel_id=1, source_target_pairs={{0,4},{4,0},{8,12},{12,8},{16,20},{20,16},{24,28},{28,24},{1,5},{5... | collective-permute-start | bytes 3538952 | tf_op jit(solution)/shard_map/ppermute | solution.py:19
  115.1 12.0 %collective-permute-start.28 = (bf16[96,2048]{1,0:T(8,128)(2,1)S(1)}, bf16[96,2048]{1,0:T(8,128)(2,1)S(1)}, u32[]{:S(2)}, u32[]{:S(2)}) collective-permute-start(bf16[96,2048]{1,0:T(8,128)(2,1)S(1)} %copy-done.27), channel_id=1, source_target_pairs={{0,8},{4,12},{8,0},{12,4},{16,24},{20,28},{24,16},{28,20},{1,9},{5... | collective-permute-start | bytes 1179656 | tf_op jit(solution)/shard_map/ppermute | solution.py:19
  116.3 20.4 %collective-permute-start.29 = (bf16[96,2048]{1,0:T(8,128)(2,1)S(1)}, bf16[96,2048]{1,0:T(8,128)(2,1)S(1)}, u32[]{:S(2)}, u32[]{:S(2)}) collective-permute-start(bf16[96,2048]{1,0:T(8,128)(2,1)S(1)} %copy-done.26), channel_id=1, source_target_pairs={{0,16},{4,20},{8,24},{12,28},{16,0},{20,4},{24,8},{28,12},{1,17},{... | collective-permute-start | bytes 1179656 | tf_op jit(solution)/shard_map/ppermute | solution.py:19
  117.4 19.3 %collective-permute-start.30 = (bf16[96,2048]{1,0:T(8,128)(2,1)S(1)}, bf16[96,2048]{1,0:T(8,128)(2,1)S(1)}, u32[]{:S(2)}, u32[]{:S(2)}) collective-permute-start(bf16[96,2048]{1,0:T(8,128)(2,1)S(1)} %copy-done.25), channel_id=1, source_target_pairs={{0,24},{4,28},{8,16},{12,20},{16,8},{20,12},{24,0},{28,4},{1,25},{... | collective-permute-start | bytes 1179656 | tf_op jit(solution)/shard_map/ppermute | solution.py:19
  119.7 17.0 %copy-start.1 = (bf16[96,2048]{1,0:T(8,128)(2,1)S(1)}, bf16[96,2048]{1,0:T(8,128)(2,1)}, u32[]{:S(2)}) copy-start(bf16[96,2048]{1,0:T(8,128)(2,1)} %get-tuple-element.61.refs_9_) | copy-start | bytes 1179652
  122.7 19.2 %collective-permute-start.25 = (bf16[96,1536]{1,0:T(8,128)(2,1)}, bf16[96,1536]{1,0:T(8,128)(2,1)S(1)}, u32[]{:S(2)}, u32[]{:S(2)}) collective-permute-start(bf16[96,1536]{1,0:T(8,128)(2,1)} %get-tuple-element.67), channel_id=1, source_target_pairs={{0,8},{4,12},{8,0},{12,4},{16,24},{20,28},{24,16},{28,20},{1,9},{5... | collective-permute-start | bytes 884744 | tf_op jit(solution)/shard_map/ppermute | solution.py:19
  123.8 23.4 %collective-permute-start.26 = (bf16[96,1536]{1,0:T(8,128)(2,1)}, bf16[96,1536]{1,0:T(8,128)(2,1)S(1)}, u32[]{:S(2)}, u32[]{:S(2)}) collective-permute-start(bf16[96,1536]{1,0:T(8,128)(2,1)} %get-tuple-element.68), channel_id=1, source_target_pairs={{0,16},{4,20},{8,24},{12,28},{16,0},{20,4},{24,8},{28,12},{1,17},{... | collective-permute-start | bytes 884744 | tf_op jit(solution)/shard_map/ppermute | solution.py:19
  127.1 21.6 %collective-permute-start.27 = (bf16[96,1536]{1,0:T(8,128)(2,1)}, bf16[96,1536]{1,0:T(8,128)(2,1)S(1)}, u32[]{:S(2)}, u32[]{:S(2)}) collective-permute-start(bf16[96,1536]{1,0:T(8,128)(2,1)} %get-tuple-element.69), channel_id=1, source_target_pairs={{0,24},{4,28},{8,16},{12,20},{16,8},{20,12},{24,0},{28,4},{1,25},{... | collective-permute-start | bytes 884744 | tf_op jit(solution)/shard_map/ppermute | solution.py:19
  136.9 11.8 %copy-start.14 = (bf16[96,1536]{1,0:T(8,128)(2,1)S(1)}, bf16[96,1536]{1,0:T(8,128)(2,1)}, u32[]{:S(2)}) copy-start(bf16[96,1536]{1,0:T(8,128)(2,1)} %get-tuple-element.66) | copy-start | bytes 884740
  137.8 14.9 %all-to-all-start = ((bf16[4,64,768]{2,1,0:T(8,128)(2,1)}), bf16[4,64,768]{2,1,0:T(8,128)(2,1)S(1)}, u32[]{:S(2)}, u32[]{:S(2)}) async-start(bf16[4,64,768]{2,1,0:T(8,128)(2,1)} %bitcast.4), calls=%async_computation | async-start | bytes 786432 | tf_op jit(solution)/shard_map/all_to_all | solution.py:427
  148.7 4.0 %copy-start.4 = (f32[64,768]{1,0:T(8,128)S(1)}, f32[64,768]{1,0:T(8,128)}, u32[]{:S(2)}) copy-start(f32[64,768]{1,0:T(8,128)} %get-tuple-element.44.refs_1_) | copy-start | bytes 589828
  (18 other events, 14.6 us)

commit v3 on v2

--- a/solution.py
+++ b/solution.py
@@ -11,7 +11,7 @@
 SPAN = 64
 BF = jnp.bfloat16
 F32 = jnp.float32
-VMEM_BYTES = 56 * 1024 * 1024
+MIB = 1024 * 1024
 
 
 def exchange(values, axis, mask):
@@ -19,19 +19,22 @@
     return lax.ppermute(values, axis, [(one, one ^ mask) for one in range(size)])
 
 
-def call(body, outs, args, scratch=(), flops=0, smem=0, after=()):
+def call(body, outs, args, scratch=(), flops=0, smem=0, far=0, after=()):
     count = len(args)
     specs = [pl.BlockSpec(memory_space=pltpu.SMEM)] * smem
-    specs += [pl.BlockSpec(memory_space=pltpu.VMEM)] * (count - smem)
-    specs += [pl.BlockSpec(memory_space=pl.ANY)] * len(after)
+    specs += [pl.BlockSpec(memory_space=pltpu.VMEM)] * (count - smem - far)
+    specs += [pl.BlockSpec(memory_space=pl.ANY)] * (far + len(after))
     moved = sum(math.prod(one.shape) * one.dtype.itemsize for one in list(args) + list(outs))
+    held = moved + sum(math.prod(one.shape) * jnp.dtype(one.dtype).itemsize for one in scratch)
+    if far:
+        scratch = [*scratch, pltpu.SemaphoreType.DMA((16,))]
     return pl.pallas_call(
         lambda *refs: body(*refs[:count], *refs[count + len(after) :]),
         out_shape=tuple(outs),
         in_specs=specs,
         out_specs=tuple(pl.BlockSpec(memory_space=pltpu.VMEM) for _ in outs),
         scratch_shapes=list(scratch),
-        compiler_params=pltpu.CompilerParams(vmem_limit_bytes=VMEM_BYTES),
+        compiler_params=pltpu.CompilerParams(vmem_limit_bytes=min(held + 6 * MIB, 56 * MIB)),
         cost_estimate=pl.CostEstimate(flops=flops, bytes_accessed=moved, transcendentals=0),
     )(*args, *after)
 
@@ -53,17 +56,33 @@
     return center * inverse, inverse
 
 
-def collect(me_ref, pieces, ids, first_column, target):
+def start_copies(pairs, sems, first_sem=0):
+    copies = []
+    for at, (source, target) in enumerate(pairs):
+        copies.append(pltpu.make_async_copy(source, target, sems.at[first_sem + at]))
+        copies[-1].start()
+    return copies
+
+
+def wait_copies(copies):
+    for one in copies:
+        one.wait()
+
+
+def collect(me_ref, pieces, ids, first_column, target, sems, first_sem=0):
     rows, width = target.shape
     rows = rows // len(ids)
     columns = slice(first_column, first_column + width)
     if len(ids) == 1:
         target[...] = pieces[0][:, columns]
-        return
+        return []
     blocks = [(piece, at) for piece in pieces for at in range(0, piece.shape[0], rows)]
+    pairs = []
     for (piece, at), mask in zip(blocks, ids):
         first = pl.multiple_of((me_ref[0] ^ mask) * rows, 16)
-        target[pl.ds(first, rows), :] = piece[at : at + rows, columns]
+        source = piece.at[pl.ds(at, rows), pl.ds(first_column, width)]
+        pairs.append((source, target.at[pl.ds(first, rows), :]))
+    return start_copies(pairs, sems, first_sem)
 
 
 def hand_out(me_ref, total, firsts, rows, outs, first_column):
@@ -78,69 +97,81 @@
         out[at : at + rows, columns] = block.astype(BF)
 
 
-def ffn_kernel(parts, ids, *refs):
-    me_ref, gain = refs[:2]
-    frames = refs[2 : 2 + parts]
-    at = 2 + parts + (1 if len(ids) == 1 else 2)
-    weights, rest = refs[2 + parts : at], refs[at:]
-    normed_out, pre_out, hidden_out, down = rest[:4]
-    partials = rest[4 : 4 + parts]
-    up = rest[4 + parts]
+def ffn_kernel(parts, ids, cot_scale, *refs):
+    place_ref, me_ref, gain = refs[:3]
+    both_parts = refs[3 : 3 + parts]
+    direct = len(ids) > 1
+    at = 3 + parts + (2 if direct else 1)
+    weights, rest = refs[3 + parts : at], refs[at:]
+    normed_out, pre_out, hidden_out, down, scaled = rest[:5]
+    partials = rest[5 : 5 + parts]
+    up = rest[5 + parts]
+    sems = rest[-1]
     model, width = up.shape
-    collect(me_ref, weights, ids, 0, up)
-    collect(me_ref, weights, ids, width, down)
-    own = frames[0].shape[0]
-    for index, piece in enumerate(frames):
-        normed = normalise(piece[:, :model].astype(F32))[0] * gain[...].reshape(1, -1)
+    up_copies = collect(me_ref, weights, ids, 0, up, sems)
+    down_copies = collect(me_ref, weights, ids, width, down, sems, 8)
+    own = both_parts[0].shape[0]
+    for index, (first, both) in enumerate(zip(places(place_ref, parts, own), both_parts)):
+        normed = normalise(both[:, :model].astype(F32))[0] * gain[...].reshape(1, -1)
         normed_out[index * own : (index + 1) * own, :] = normed.astype(BF)
+        cot = both[:, model:].astype(F32)
+        scaled[pl.ds(first, own), :] = (cot * cot_scale).astype(BF)
+    wait_copies(up_copies)
     pre = dot(normed_out[...], up[...], 1, 0)
     pre_out[...] = pre
     hidden_out[...] = (pre * jax.nn.sigmoid(pre)).astype(BF)
+    wait_copies(down_copies)
     made = dot(hidden_out[...], down[...], 1, 1)
     for index, out in enumerate(partials):
         out[...] = made[index * own : (index + 1) * own].astype(BF)
 
 
+def places(place_ref, parts, own):
+    if parts == 1:
+        return [0]
+    return [pl.multiple_of((place_ref[0] ^ mask) * own, 16) for mask in range(parts)]
+
+
 def mid_kernel(parts, *refs):
     gain, frames = refs[0], refs[1]
     pieces = refs[2 : 2 + parts]
-    stacked = (len(refs) - parts - 4) // 4 * 4
+    stacked = 4 if len(refs) > parts + 4 else 0
     weights = refs[2 + parts : 2 + parts + stacked]
     mid_out, normed_out = refs[2 + parts + stacked : 4 + parts + stacked]
+    copies = []
     if stacked:
-        stack_kernel(*weights, refs[-1])
+        near, sems = refs[-2:]
+        copies = start_copies(row_pairs(weights, near), sems)
     total = pieces[0][...].astype(F32)
     for piece in pieces[1:]:
         total = total + piece[...].astype(F32)
     mid = frames[...].astype(F32) + 0.5 * total
     mid_out[...] = mid
     normed_out[...] = (normalise(mid)[0] * gain[...].reshape(1, -1)).astype(BF)
-
-
-def attention_kernel(parts, ids, window, cot_scale, *refs):
+    wait_copies(copies)
+
+
+def attention_kernel(parts, ids, window, *refs):
     place_ref, me_ref, bias = refs[:3]
     segments, spans = refs[3:5]
     normed_parts = refs[5 : 5 + parts]
-    cot_parts = refs[5 + parts : 5 + 2 * parts]
-    at = 5 + 2 * parts + (1 if len(ids) == 1 else 2)
-    weights_in, rest = refs[5 + 2 * parts : at], refs[at:]
-    normed, scaled, context, slopes = rest[:4]
-    attn_out, outs = rest[4], rest[5 : 5 + parts]
-    weights, qkv, grad_context, key_total, value_total, total = rest[5 + parts :]
+    scaled = refs[5 + parts]
+    at = 6 + parts + (2 if len(ids) > 1 else 1)
+    weights_in, rest = refs[6 + parts : at], refs[at:]
+    normed, context, slopes = rest[:3]
+    attn_out, outs = rest[3], rest[4 : 4 + parts]
+    weights, qkv, grad_context, key_total, value_total, total = rest[4 + parts : 10 + parts]
+    copies = collect(me_ref, weights_in, ids, 0, weights, rest[-1])
     heads = bias.shape[0]
     frames = normed.shape[0]
     own = normed_parts[0].shape[0]
     inner = context.shape[1]
     width = inner // heads
     scale = width ** (-0.5)
-    firsts = [0]
-    if parts > 1:
-        firsts = [pl.multiple_of((place_ref[0] ^ mask) * own, 16) for mask in range(parts)]
-    for first, piece, both in zip(firsts, normed_parts, cot_parts):
+    firsts = places(place_ref, parts, own)
+    for first, piece in zip(firsts, normed_parts):
         normed[pl.ds(first, own), :] = piece[...]
-        cot = both[:, normed.shape[1] :].astype(F32)
-        scaled[pl.ds(first, own), :] = (cot * cot_scale).astype(BF)
-    collect(me_ref, weights_in, ids, 0, weights)
+    wait_copies(copies)
     qkv[...] = dot(normed[...], weights[:, : 3 * inner], 1, 0).astype(BF)
     grad_context[...] = dot(scaled[...], weights[:, 3 * inner :], 1, 0).astype(BF)
     seg_k, span_k = segments[...], spans[...]
@@ -248,28 +279,44 @@
         out[...] = one[...]
 
 
-def pack_kernel(*refs):
-    out, at = refs[-1], 0
-    for piece in refs[:-1]:
-        out[:, at : at + piece.shape[1]] = piece[...]
-        at += piece.shape[1]
-
-
-def pack(pieces, after=()):
-    total = sum(one.shape[1] for one in pieces)
-    return call(pack_kernel, [shape((pieces[0].shape[0], total), BF)], pieces, after=after)[0]
+def row_pairs(pieces, out):
+    starts = [sum(one.shape[0] for one in pieces[:at]) for at in range(len(pieces))]
+    return [(one, out.at[pl.ds(at, one.shape[0]), :]) for one, at in zip(pieces, starts)]
+
+
+def column_pairs(pieces, out):
+    starts = [sum(one.shape[1] for one in pieces[:at]) for at in range(len(pieces))]
+    return [(one, out.at[:, pl.ds(at, one.shape[1])]) for one, at in zip(pieces, starts)]
 
 
 def stack_kernel(*refs):
-    out, at = refs[-1], 0
-    for piece in refs[:-1]:
-        out[at : at + piece.shape[0], :] = piece[...]
-        at += piece.shape[0]
+    wait_copies(start_copies(row_pairs(refs[:-2], refs[-2]), refs[-1]))
+
+
+def pack_kernel(groups, *refs):
+    outs, pairs, at = refs[sum(groups) : -1], [], 0
+    for count, out in zip(groups, outs):
+        pairs += column_pairs(refs[at : at + count], out)
+        at += count
+    wait_copies(start_copies(pairs, refs[-1]))
 
 
 def stack(pieces, after=()):
     total = sum(one.shape[0] for one in pieces)
-    return call(stack_kernel, [shape((total, pieces[0].shape[1]), BF)], pieces, after=after)[0]
+    out = shape((total, pieces[0].shape[1]), BF)
+    return call(stack_kernel, [out], pieces, far=len(pieces), after=after)[0]
+
+
+def pack(groups, after=()):
+    outs = [
+        shape((group[0].shape[0], sum(one.shape[1] for one in group)), BF) for group in groups
+    ]
+    whole = all(one.shape[0] % 16 == 0 and one.shape[1] % 128 == 0 for group in groups for one in group)
+    if not whole:
+        return [jnp.concatenate(group, axis=1) for group in groups]
+    pieces = [one for group in groups for one in group]
+    body = functools.partial(pack_kernel, tuple(len(group) for group in groups))
+    return call(body, outs, pieces, far=len(pieces), after=after)
 
 
 def per_device(
@@ -331,57 +378,60 @@
         return total
 
     frames_own, cot_own = frames_in[0], cotangent[0]
-    both_parts = gather_frames(pack([frames_own, cot_own]))
+    both_own, ffn_rows = pack([[frames_own, cot_own], [w_up, w_down]])
+    both_parts = gather_frames(both_own)
 
     def gather_near(weight):
         return [weight] + [exchange(weight, "dp", mask) for mask in (6, 4, 2)]
 
     if direct_rows:
-        ffn_near = stack(gather_near(pack([w_up, w_down])), both_parts[1:])
+        ffn_near = stack(gather_near(ffn_rows), both_parts[1:])
         ffn_weights = [ffn_near, exchange(ffn_near, "dp", 1)]
-        attn_pieces = gather_near(pack([w_query, w_key, w_value, w_out], [ffn_near]))
+        attn_pieces = gather_near(pack([[w_query, w_key, w_value, w_out]], [ffn_near])[0])
     else:
-        ffn_weights = [lax.all_gather(pack([w_up, w_down]), "dp", axis=0, tiled=True)]
-        attn_weights = pack([w_query, w_key, w_value, w_out])
+        ffn_weights = [lax.all_gather(ffn_rows, "dp", axis=0, tiled=True)]
+        attn_weights = pack([[w_query, w_key, w_value, w_out]])[0]
         attn_weights = [lax.all_gather(attn_weights, "dp", axis=0, tiled=True)]
         attn_pieces = []
 
     made = call(
-        functools.partial(ffn_kernel, parts, ids),
+        functools.partial(ffn_kernel, parts, ids, cot_scale),
         [
             shape((frames, model), BF),
             shape((frames, hidden), F32),
             shape((frames, hidden), BF),
             shape((model, hidden), BF),
+            shape((frames, model), BF),
         ]
         + [shape((part_rows, model), BF)] * parts,
-        [me, ffn_gain] + both_parts + ffn_weights,
+        [place, me, ffn_gain] + both_parts + ffn_weights,
         [pltpu.VMEM((model, hidden), BF)],
         flops=4 * frames * model * hidden,
-        smem=1,
-    )
-    ffn_normed, ffn_pre, ffn_hidden, down_full = made[:4]
-    summed = scatter_frames(list(made[4:]))
+        smem=2,
+        far=2 if direct_rows else 0,
+    )
+    ffn_normed, ffn_pre, ffn_hidden, down_full, scaled_cot = made[:5]
+    summed = scatter_frames(list(made[5:]))
     near = [shape((model // 2, 4 * inner), BF)] if direct_rows else []
     mid_own, normed_own, *near = call(
         functools.partial(mid_kernel, len(summed)),
         [shape((own, model), F32), shape((own, model), BF)] + near,
         [attn_gain, frames_own] + summed + attn_pieces,
+        far=len(attn_pieces),
     )
     normed_parts = gather_frames(normed_own)
     if direct_rows:
         attn_weights = [near[0], exchange(near[0], "dp", 1)]
     made = call(
-        functools.partial(attention_kernel, parts, ids, window, cot_scale),
+        functools.partial(attention_kernel, parts, ids, window),
         [
-            shape((frames, model), BF),
             shape((frames, model), BF),
             shape((frames, inner), BF),
             shape((frames, 3 * inner), BF),
             shape((frames, model), BF),
         ]
         + [shape((part_rows, model), BF)] * parts,
-        [place, me, offset_bias, segment_ids, span_ids] + normed_parts + both_parts + attn_weights,
+        [place, me, offset_bias, segment_ids, span_ids] + normed_parts + [scaled_cot] + attn_weights,
         [
             pltpu.VMEM((model, 4 * inner), BF),
             pltpu.VMEM((frames, 3 * inner), BF),
@@ -392,10 +442,11 @@
         ],
         flops=16 * frames * model * inner + 12 * frames * frames * inner,
         smem=3,
-    )
-    attn_normed, scaled_cot, context, slopes = made[:4]
-    attn_partial = made[4]
-    upstream = scatter_frames(list(made[5:]))
+        far=2 if direct_rows else 0,
+    )
+    attn_normed, context, slopes = made[:3]
+    attn_partial = made[3]
+    upstream = scatter_frames(list(made[4:]))
     half = [shape((model // 2, 4 * inner), BF)] * 2
     attn_grads = call(
         attention_grads_kernel,
@@ -405,13 +456,13 @@
         flops=8 * frames * model * inner,
         smem=1,
     )
+    attn_terms, attn_sums = scatter_rows(attn_grads)
     (grad_mid_own,) = call(
         functools.partial(grad_mid_kernel, len(upstream), cot_scale),
         [shape((own, model), BF)],
         [attn_gain, mid_own, cot_own] + upstream,
     )
     grad_mid_parts = gather_frames(grad_mid_own)
-    attn_terms, attn_sums = scatter_rows(attn_grads)
     half = [shape((model // 2, 2 * hidden), BF)] * 2
     ffn_grads = call(
         functools.partial(ffn_grads_kernel, parts),
@@ -420,7 +471,7 @@
         [pltpu.VMEM((frames, model), BF), pltpu.VMEM((model, hidden), F32)],
         flops=6 * frames * model * hidden,
         smem=1,
-        after=attn_sums,
+        after=attn_terms[1:3],
     )
     ffn_terms, passed = scatter_rows(ffn_grads, [attn_partial])
     if direct_frames:

time: 154 us -> 132 us (0.86)
  Pallas kernels: 39.8 us -> 15.8 us
  waiting for transfers between devices: 51.1 us -> 58.2 us
  local copies, waits for them, and re-layouts: 9.98 us -> 5.39 us
    pallas_call x12 -> x11, Pallas kernels: 39.8 us -> 15.8 us  [call(): pl.pallas_call(lambda *refs: body(*refs[:count], *refs[count + len(after)...]
    ppermute x31, waiting for transfers between devices: 48.1 us -> 55.5 us  [exchange(): lax.ppermute(values, axis, [(one, one ^ mask) for one in range(size)])]
    unnamed x68 -> x30, local copies, waits for them, and re-layouts: 8.25 us -> 3.65 us
  transfers between devices with their start and end apart: 32 -> 32, of which waited for: 15 -> 18; matrix products, arithmetic and copies ran while one was open for 1% -> 2% of each run, Pallas kernels for 10% -> 3%
where the time goes in v3:
time: 132 us
  waiting for transfers between devices  58.2 us (44%)
  starting transfers between devices  50.3 us (38%)
  Pallas kernels  15.8 us (12%)
  local copies, waits for them, and re-layouts  5.39 us (4%)
    ppermute x31, waiting for transfers between devices, exchange(): lax.ppermute(values, axis, [(one, one ^ mask) for one in range(size)])  55.5 us
    ppermute x31, starting transfers between devices, exchange(): lax.ppermute(values, axis, [(one, one ^ mask) for one in range(size)])  46.8 us
    pallas_call x11, Pallas kernels, call(): pl.pallas_call(lambda *refs: body(*refs[:count], *refs[count + len(after)...  15.8 us
    unnamed x30, local copies, waits for them, and re-layouts  3.65 us
    all_to_all x1, starting transfers between devices, per_device(): attn_sum = lax.all_to_all(passed[0], 'ctx', 0, 0, tiled=True)  3.46 us
    all_to_all x1, waiting for transfers between devices, per_device(): attn_sum = lax.all_to_all(passed[0], 'ctx', 0, 0, tiled=True)  2.68 us
  transfers between devices with their start and end apart: 32, of which 18 were waited for; matrix products, arithmetic and copies ran while one was open for 2% of the time, Pallas kernels for 3%

profile of v3, /device:TPU:0, one launch (start us, length us, event | category | flops | bytes accessed | tf_op | source)
XLA Modules:
  0.0 131.7 jit_solution(10309750086799964995)
XLA Ops:
  0.6 0.9 copy-done
  1.5 0.9 copy-done.2
  2.4 0.9 copy-done.4
  3.3 0.9 copy-done.5
  4.5 5.1 %collective-permute-start.2 = (bf16[64,1536]{1,0:T(8,128)(2,1)S(1)}, bf16[64,1536]{1,0:T(8,128)(2,1)S(1)}, u32[]{:S(2)}, u32[]{:S(2)}) collective-permute-start(bf16[64,1536]{1,0:T(8,128)(2,1)S(1)} %get-tuple-element.42.refs_3_), channel_id=1, source_target_pairs={{0,3},{1,2},{2,1},{3,0},{4,7},{5,6},{6,5},{7,4},{8,11},{9,10},{10,... | collective-permute-start | bytes 589832 | tf_op jit(solution)/shard_map/ppermute | solution.py:19
  9.6 1.6 %collective-permute-start.5 = (bf16[96,1536]{1,0:T(8,128)(2,1)S(1)}, bf16[96,1536]{1,0:T(8,128)(2,1)S(1)}, u32[]{:S(2)}, u32[]{:S(2)}) collective-permute-start(bf16[96,1536]{1,0:T(8,128)(2,1)S(1)} %get-tuple-element.43.refs_0_), channel_id=1, source_target_pairs={{0,8},{4,12},{8,0},{12,4},{16,24},{20,28},{24,16},{28,20},{1,9},{5... | collective-permute-start | bytes 884744 | tf_op jit(solution)/shard_map/ppermute | solution.py:19
  11.1 1.5 %collective-permute-start.4 = (bf16[96,1536]{1,0:T(8,128)(2,1)S(1)}, bf16[96,1536]{1,0:T(8,128)(2,1)S(1)}, u32[]{:S(2)}, u32[]{:S(2)}) collective-permute-start(bf16[96,1536]{1,0:T(8,128)(2,1)S(1)} %get-tuple-element.43.refs_0_), channel_id=1, source_target_pairs={{0,16},{4,20},{8,24},{12,28},{16,0},{20,4},{24,8},{28,12},{1,17},{... | collective-permute-start | bytes 884744 | tf_op jit(solution)/shard_map/ppermute | solution.py:19
  13.1 1.7 %collective-permute-done.2.refs_6_ = bf16[64,1536]{1,0:T(8,128)(2,1)S(1)} collective-permute-done((bf16[64,1536]{1,0:T(8,128)(2,1)S(1)}, bf16[64,1536]{1,0:T(8,128)(2,1)S(1)}, u32[]{:S(2)}, u32[]{:S(2)}) %collective-permute-start.2) | collective-permute-done | bytes 196640 | tf_op jit(solution)/shard_map/ppermute | solution.py:19
  14.9 8.7 %collective-permute-start = (bf16[64,1536]{1,0:T(8,128)(2,1)S(1)}, bf16[64,1536]{1,0:T(8,128)(2,1)S(1)}, u32[]{:S(2)}, u32[]{:S(2)}) collective-permute-start(bf16[64,1536]{1,0:T(8,128)(2,1)S(1)} %get-tuple-element.42.refs_3_), channel_id=1, source_target_pairs={{0,1},{1,0},{2,3},{3,2},{4,5},{5,4},{6,7},{7,6},{8,9},{9,8},{10,11... | collective-permute-start | bytes 589832 | tf_op jit(solution)/shard_map/ppermute | solution.py:19
  23.6 2.8 %collective-permute-done.1.refs_5_ = bf16[64,1536]{1,0:T(8,128)(2,1)S(1)} collective-permute-done((bf16[64,1536]{1,0:T(8,128)(2,1)S(1)}, bf16[64,1536]{1,0:T(8,128)(2,1)S(1)}, u32[]{:S(2)}, u32[]{:S(2)}) %collective-permute-start.1) | collective-permute-done | bytes 196640 | tf_op jit(solution)/shard_map/ppermute | solution.py:19
  26.4 3.9 %collective-permute-done.refs_4_ = bf16[64,1536]{1,0:T(8,128)(2,1)S(1)} collective-permute-done((bf16[64,1536]{1,0:T(8,128)(2,1)S(1)}, bf16[64,1536]{1,0:T(8,128)(2,1)S(1)}, u32[]{:S(2)}, u32[]{:S(2)}) %collective-permute-start) | collective-permute-done | bytes 196640 | tf_op jit(solution)/shard_map/ppermute | solution.py:19
  31.0 1.6 %collective-permute-start.12 = (bf16[96,2048]{1,0:T(8,128)(2,1)S(1)}, bf16[96,2048]{1,0:T(8,128)(2,1)}, u32[]{:S(2)}, u32[]{:S(2)}) collective-permute-start(bf16[96,2048]{1,0:T(8,128)(2,1)S(1)} %shard_map.183.refs_6_), channel_id=1, source_target_pairs={{0,8},{4,12},{8,0},{12,4},{16,24},{20,28},{24,16},{28,20},{1,9},{5... | collective-permute-start | bytes 1179656 | tf_op jit(solution)/shard_map/ppermute | solution.py:19
  32.6 1.5 %collective-permute-start.11 = (bf16[96,2048]{1,0:T(8,128)(2,1)S(1)}, bf16[96,2048]{1,0:T(8,128)(2,1)}, u32[]{:S(2)}, u32[]{:S(2)}) collective-permute-start(bf16[96,2048]{1,0:T(8,128)(2,1)S(1)} %shard_map.183.refs_6_), channel_id=1, source_target_pairs={{0,16},{4,20},{8,24},{12,28},{16,0},{20,4},{24,8},{28,12},{1,17},{... | collective-permute-start | bytes 1179656 | tf_op jit(solution)/shard_map/ppermute | solution.py:19
  34.6 2.0 %shard_map.182 = (bf16[256,768]{1,0:T(8,128)(2,1)S(1)}, f32[256,768]{1,0:T(8,128)S(1)}, bf16[256,768]{1,0:T(8,128)(2,1)S(1)}, bf16[768,768]{1,0:T(8,128)(2,1)S(1...) custom-call(s32[1]{0:T(128)} %bitcast.1.refs_0_, ...), custom_call_target="tpu_custom_call" | custom-call | flops 603979776 | bytes 6687752 | tf_op jit(solution)/shard_map/pallas_call | solution.py:31
  36.7 2.8 %collective-permute-start.8 = (bf16[64,768]{1,0:T(8,128)(2,1)S(1)}, bf16[64,768]{1,0:T(8,128)(2,1)S(1)}, u32[]{:S(2)}, u32[]{:S(2)}) collective-permute-start(bf16[64,768]{1,0:T(8,128)(2,1)S(1)} %get-tuple-element.46), channel_id=1, source_target_pairs={{0,2},{1,3},{2,0},{3,1},{4,6},{5,7},{6,4},{7,5},{8,10},{9,11},{10,... | collective-permute-start | bytes 294920 | tf_op jit(solution)/shard_map/ppermute | solution.py:19
  39.6 3.5 %collective-permute-done.12.refs_9_ = bf16[96,2048]{1,0:T(8,128)(2,1)} collective-permute-done((bf16[96,2048]{1,0:T(8,128)(2,1)S(1)}, bf16[96,2048]{1,0:T(8,128)(2,1)}, u32[]{:S(2)}, u32[]{:S(2)}) %collective-permute-start.12) | collective-permute-done | bytes 393248 | tf_op jit(solution)/shard_map/ppermute | solution.py:19
  43.1 2.3 %collective-permute-start.9 = (bf16[64,768]{1,0:T(8,128)(2,1)S(1)}, bf16[64,768]{1,0:T(8,128)(2,1)S(1)}, u32[]{:S(2)}, u32[]{:S(2)}) collective-permute-start(bf16[64,768]{1,0:T(8,128)(2,1)S(1)} %get-tuple-element.47), channel_id=1, source_target_pairs={{0,3},{1,2},{2,1},{3,0},{4,7},{5,6},{6,5},{7,4},{8,11},{9,10},{10,... | collective-permute-start | bytes 294920 | tf_op jit(solution)/shard_map/ppermute | solution.py:19
  45.4 6.9 %collective-permute-done.11.refs_8_ = bf16[96,2048]{1,0:T(8,128)(2,1)} collective-permute-done((bf16[96,2048]{1,0:T(8,128)(2,1)S(1)}, bf16[96,2048]{1,0:T(8,128)(2,1)}, u32[]{:S(2)}, u32[]{:S(2)}) %collective-permute-start.11) | collective-permute-done | bytes 393248 | tf_op jit(solution)/shard_map/ppermute | solution.py:19
  52.4 1.6 %shard_map.184 = (f32[64,768]{1,0:T(8,128)S(1)}, bf16[64,768]{1,0:T(8,128)(2,1)S(1)}, bf16[384,2048]{1,0:T(8,128)(2,1)S(1)}) custom-call(f32[768]{0:T(1024)S(1)} %copy-done.10, bf16[64,768]{1,0:T(8,128)(2,1)S(1)} %bitcast.14, bf16[64,768]{1,0:T(8,128)(2,1)S(1)} %get-tuple-element.44.refs_2_, bf16[64,768]{1,0:T(8,128)(2,1)S(1)} %collective-permute-done.7.refs_3_, ...), custom_call_target="tpu_custom_call" | custom-call | bytes 3935232 | tf_op jit(solution)/shard_map/pallas_call | solution.py:31
  54.1 2.4 %collective-permute-start.15 = (bf16[64,768]{1,0:T(8,128)(2,1)S(1)}, bf16[64,768]{1,0:T(8,128)(2,1)S(1)}, u32[]{:S(2)}, u32[]{:S(2)}) collective-permute-start(bf16[64,768]{1,0:T(8,128)(2,1)S(1)} %get-tuple-element.53.refs_5_), channel_id=1, source_target_pairs={{0,3},{1,2},{2,1},{3,0},{4,7},{5,6},{6,5},{7,4},{8,11},{9,10},{10,... | collective-permute-start | bytes 294920 | tf_op jit(solution)/shard_map/ppermute | solution.py:19
  56.4 2.1 %collective-permute-start.13 = (bf16[64,768]{1,0:T(8,128)(2,1)S(1)}, bf16[64,768]{1,0:T(8,128)(2,1)S(1)}, u32[]{:S(2)}, u32[]{:S(2)}) collective-permute-start(bf16[64,768]{1,0:T(8,128)(2,1)S(1)} %get-tuple-element.53.refs_5_), channel_id=1, source_target_pairs={{0,1},{1,0},{2,3},{3,2},{4,5},{5,4},{6,7},{7,6},{8,9},{9,8},{10,11... | collective-permute-start | bytes 294920 | tf_op jit(solution)/shard_map/ppermute | solution.py:19
  58.5 3.1 %collective-permute-done.15.refs_8_ = bf16[64,768]{1,0:T(8,128)(2,1)S(1)} collective-permute-done((bf16[64,768]{1,0:T(8,128)(2,1)S(1)}, bf16[64,768]{1,0:T(8,128)(2,1)S(1)}, u32[]{:S(2)}, u32[]{:S(2)}) %collective-permute-start.15) | collective-permute-done | bytes 98336 | tf_op jit(solution)/shard_map/ppermute | solution.py:19
  61.6 3.7 %collective-permute-done.14.refs_7_ = bf16[64,768]{1,0:T(8,128)(2,1)S(1)} collective-permute-done((bf16[64,768]{1,0:T(8,128)(2,1)S(1)}, bf16[64,768]{1,0:T(8,128)(2,1)S(1)}, u32[]{:S(2)}, u32[]{:S(2)}) %collective-permute-start.14) | collective-permute-done | bytes 98336 | tf_op jit(solution)/shard_map/ppermute | solution.py:19
  65.3 6.8 %shard_map.185 = (bf16[256,768]{1,0:T(8,128)(2,1)S(1)}, bf16[256,512]{1,0:T(8,128)(2,1)S(1)}, bf16[256,1536]{1,0:T(8,128)(2,1)S(1)}, bf16[256,768]{1,0:T(8,128)(...) custom-call(s32[1]{0:T(128)} %bitcast.1.refs_0_, ...), custom_call_target="tpu_custom_call" | custom-call | flops 2013265920 | bytes 6162584 | tf_op jit(solution)/shard_map/pallas_call | solution.py:31
  72.1 1.5 %shard_map.187 = (bf16[384,2048]{1,0:T(8,128)(2,1)S(1)}, bf16[384,2048]{1,0:T(8,128)(2,1)S(1)}) custom-call(s32[1]{0:T(128)} %bitcast.2.refs_1_.refs_0_, bf16[256,768]{1,0:T(8,128)(2,1)S(1)} %get-tuple-element.60.refs_1_, bf16[256,768]{1,0:T(8,128)(2,1)S(1)} %get-tuple-element.54.refs_9_.refs_2_, bf16[256,512]{1,0:T(8,128)(2,1)S(1)} %get-tuple-element.61.refs_3_, ...), custom_call_target="tpu_custom_call" | custom-call | flops 805306368 | bytes 4980740 | tf_op jit(solution)/shard_map/pallas_call | solution.py:31
  73.7 3.4 %collective-permute-done.23.refs_1_ = bf16[384,2048]{1,0:T(8,128)(2,1)S(1)} collective-permute-done((bf16[384,2048]{1,0:T(8,128)(2,1)S(1)}, bf16[384,2048]{1,0:T(8,128)(2,1)S(1)}, u32[]{:S(2)}, u32[]{:S(2)}) %collective-permute-start.23) | collective-permute-done | bytes 1572896 | tf_op jit(solution)/shard_map/ppermute | solution.py:19
  77.4 1.3 collective-permute-start.24
  80.1 2.3 %collective-permute-start.18 = (bf16[64,768]{1,0:T(8,128)(2,1)S(1)}, bf16[64,768]{1,0:T(8,128)(2,1)S(1)}, u32[]{:S(2)}, u32[]{:S(2)}) collective-permute-start(bf16[64,768]{1,0:T(8,128)(2,1)S(1)} %get-tuple-element.58), channel_id=1, source_target_pairs={{0,2},{1,3},{2,0},{3,1},{4,6},{5,7},{6,4},{7,5},{8,10},{9,11},{10,... | collective-permute-start | bytes 294920 | tf_op jit(solution)/shard_map/ppermute | solution.py:19
  82.4 1.5 %collective-permute-start.19 = (bf16[64,768]{1,0:T(8,128)(2,1)S(1)}, bf16[64,768]{1,0:T(8,128)(2,1)S(1)}, u32[]{:S(2)}, u32[]{:S(2)}) collective-permute-start(bf16[64,768]{1,0:T(8,128)(2,1)S(1)} %get-tuple-element.59), channel_id=1, source_target_pairs={{0,3},{1,2},{2,1},{3,0},{4,7},{5,6},{6,5},{7,4},{8,11},{9,10},{10,... | collective-permute-start | bytes 294920 | tf_op jit(solution)/shard_map/ppermute | solution.py:19
  83.9 1.1 collective-permute-done.17.refs_4_
  85.1 5.2 %collective-permute-done.18.refs_5_ = bf16[64,768]{1,0:T(8,128)(2,1)S(1)} collective-permute-done((bf16[64,768]{1,0:T(8,128)(2,1)S(1)}, bf16[64,768]{1,0:T(8,128)(2,1)S(1)}, u32[]{:S(2)}, u32[]{:S(2)}) %collective-permute-start.18) | collective-permute-done | bytes 98336 | tf_op jit(solution)/shard_map/ppermute | solution.py:19
  90.5 2.2 %collective-permute-start.22 = (bf16[64,768]{1,0:T(8,128)(2,1)S(1)}, bf16[64,768]{1,0:T(8,128)(2,1)S(1)}, u32[]{:S(2)}, u32[]{:S(2)}) collective-permute-start(bf16[64,768]{1,0:T(8,128)(2,1)S(1)} %shard_map.186.refs_5_), channel_id=1, source_target_pairs={{0,3},{1,2},{2,1},{3,0},{4,7},{5,6},{6,5},{7,4},{8,11},{9,10},{10,... | collective-permute-start | bytes 294920 | tf_op jit(solution)/shard_map/ppermute | solution.py:19
  92.7 1.0 collective-permute-start.21
  93.7 1.3 collective-permute-start.20
  95.0 2.9 %collective-permute-done.22.refs_8_ = bf16[64,768]{1,0:T(8,128)(2,1)S(1)} collective-permute-done((bf16[64,768]{1,0:T(8,128)(2,1)S(1)}, bf16[64,768]{1,0:T(8,128)(2,1)S(1)}, u32[]{:S(2)}, u32[]{:S(2)}) %collective-permute-start.22) | collective-permute-done | bytes 98336 | tf_op jit(solution)/shard_map/ppermute | solution.py:19
  97.9 2.7 %collective-permute-done.21.refs_7_ = bf16[64,768]{1,0:T(8,128)(2,1)S(1)} collective-permute-done((bf16[64,768]{1,0:T(8,128)(2,1)S(1)}, bf16[64,768]{1,0:T(8,128)(2,1)S(1)}, u32[]{:S(2)}, u32[]{:S(2)}) %collective-permute-start.21) | collective-permute-done | bytes 98336 | tf_op jit(solution)/shard_map/ppermute | solution.py:19
  100.6 1.5 %shard_map.189 = (bf16[384,1536]{1,0:T(8,128)(2,1)S(1)}, bf16[384,1536]{1,0:T(8,128)(2,1)S(1)}) custom-call(s32[1]{0:T(128)} %bitcast.2.refs_1_.refs_0_, bf16[256,768]{1,0:T(8,128)(2,1)S(1)} %get-tuple-element.49.refs_1_, f32[256,768]{1,0:T(8,128)S(1)} %get-tuple-element.50.refs_2_, bf16[256,768]{1,0:T(8,128)(2,1)S(1)} %get-tuple-element.51.refs_3_, ...), custom_call_target="tpu_custom_call" | custom-call | flops 905969664 | bytes 5505028 | tf_op jit(solution)/shard_map/pallas_call | solution.py:31
  102.2 1.5 %collective-permute-start.30 = (bf16[96,2048]{1,0:T(8,128)(2,1)S(1)}, bf16[96,2048]{1,0:T(8,128)(2,1)S(1)}, u32[]{:S(2)}, u32[]{:S(2)}) collective-permute-start(bf16[96,2048]{1,0:T(8,128)(2,1)S(1)} %get-tuple-element.76), channel_id=1, source_target_pairs={{0,24},{4,28},{8,16},{12,20},{16,8},{20,12},{24,0},{28,4},{1,25},{... | collective-permute-start | bytes 1179656 | tf_op jit(solution)/shard_map/ppermute | solution.py:19
  103.7 1.3 %collective-permute-done.26.refs_1_ = bf16[384,1536]{1,0:T(8,128)(2,1)S(1)} collective-permute-done((bf16[384,1536]{1,0:T(8,128)(2,1)S(1)}, bf16[384,1536]{1,0:T(8,128)(2,1)S(1)}, u32[]{:S(2)}, u32[]{:S(2)}) %collective-permute-start.26) | collective-permute-done | bytes 1179680 | tf_op jit(solution)/shard_map/ppermute | solution.py:19
  105.0 1.0 shard_map.190
  106.0 1.5 %collective-permute-start.27 = (bf16[96,1536]{1,0:T(8,128)(2,1)S(1)}, bf16[96,1536]{1,0:T(8,128)(2,1)S(1)}, u32[]{:S(2)}, u32[]{:S(2)}) collective-permute-start(bf16[96,1536]{1,0:T(8,128)(2,1)S(1)} %get-tuple-element.72), channel_id=1, source_target_pairs={{0,8},{4,12},{8,0},{12,4},{16,24},{20,28},{24,16},{28,20},{1,9},{5... | collective-permute-start | bytes 884744 | tf_op jit(solution)/shard_map/ppermute | solution.py:19
  108.0 1.5 %collective-permute-start.29 = (bf16[96,1536]{1,0:T(8,128)(2,1)S(1)}, bf16[96,1536]{1,0:T(8,128)(2,1)S(1)}, u32[]{:S(2)}, u32[]{:S(2)}) collective-permute-start(bf16[96,1536]{1,0:T(8,128)(2,1)S(1)} %get-tuple-element.74), channel_id=1, source_target_pairs={{0,24},{4,28},{8,16},{12,20},{16,8},{20,12},{24,0},{28,4},{1,25},{... | collective-permute-start | bytes 884744 | tf_op jit(solution)/shard_map/ppermute | solution.py:19
  109.5 5.6 %collective-permute-done.30 = bf16[96,2048]{1,0:T(8,128)(2,1)S(1)} collective-permute-done((bf16[96,2048]{1,0:T(8,128)(2,1)S(1)}, bf16[96,2048]{1,0:T(8,128)(2,1)S(1)}, u32[]{:S(2)}, u32[]{:S(2)}) %collective-permute-start.30) | collective-permute-done | bytes 393248 | tf_op jit(solution)/shard_map/ppermute | solution.py:19
  115.3 0.9 fusion.2
  116.2 3.5 %all-to-all-start = ((bf16[4,64,768]{2,1,0:T(8,128)(2,1)}), bf16[4,64,768]{2,1,0:T(8,128)(2,1)S(1)}, u32[]{:S(2)}, u32[]{:S(2)}) async-start(bf16[4,64,768]{2,1,0:T(8,128)(2,1)} %bitcast.4), calls=%async_computation | async-start | bytes 786432 | tf_op jit(solution)/shard_map/all_to_all | solution.py:478
  119.7 1.5 %collective-permute-done.27 = bf16[96,1536]{1,0:T(8,128)(2,1)S(1)} collective-permute-done((bf16[96,1536]{1,0:T(8,128)(2,1)S(1)}, bf16[96,1536]{1,0:T(8,128)(2,1)S(1)}, u32[]{:S(2)}, u32[]{:S(2)}) %collective-permute-start.27) | collective-permute-done | bytes 294944 | tf_op jit(solution)/shard_map/ppermute | solution.py:19
  121.4 6.0 %collective-permute-done.29 = bf16[96,1536]{1,0:T(8,128)(2,1)S(1)} collective-permute-done((bf16[96,1536]{1,0:T(8,128)(2,1)S(1)}, bf16[96,1536]{1,0:T(8,128)(2,1)S(1)}, u32[]{:S(2)}, u32[]{:S(2)}) %collective-permute-start.29) | collective-permute-done | bytes 294944 | tf_op jit(solution)/shard_map/ppermute | solution.py:19
  128.3 2.7 %all-to-all-done = bf16[4,64,768]{2,1,0:T(8,128)(2,1)S(1)} async-done(((bf16[4,64,768]{2,1,0:T(8,128)(2,1)}), bf16[4,64,768]{2,1,0:T(8,128)(2,1)S(1)}, u32[]{:S(2)}, u32[]{:S(2)}) %all-to-all-start) | async-done | bytes 393248 | tf_op jit(solution)/shard_map/all_to_all | solution.py:478
  (62 shorter events, 6.8 us)
Async XLA Ops:
  0.6 0.9 copy-start
  1.5 0.9 copy-start.2
  2.4 0.9 copy-start.4
  3.3 0.9 copy-start.5
  4.5 10.4 %collective-permute-start.2 = (bf16[64,1536]{1,0:T(8,128)(2,1)S(1)}, bf16[64,1536]{1,0:T(8,128)(2,1)S(1)}, u32[]{:S(2)}, u32[]{:S(2)}) collective-permute-start(bf16[64,1536]{1,0:T(8,128)(2,1)S(1)} %get-tuple-element.42.refs_3_), channel_id=1, source_target_pairs={{0,3},{1,2},{2,1},{3,0},{4,7},{5,6},{6,5},{7,4},{8,11},{9,10},{10,... | collective-permute-start | bytes 589832 | tf_op jit(solution)/shard_map/ppermute | solution.py:19
  9.6 21.2 %copy-start.6 = (bf16[96,512]{1,0:T(8,128)(2,1)S(1)}, bf16[96,512]{1,0:T(8,128)(2,1)}, u32[]{:S(2)}) copy-start(bf16[96,512]{1,0:T(8,128)(2,1)} %refs_0_.3) | copy-start | bytes 294916
  9.6 21.2 %copy-start.7 = (bf16[96,512]{1,0:T(8,128)(2,1)S(1)}, bf16[96,512]{1,0:T(8,128)(2,1)}, u32[]{:S(2)}) copy-start(bf16[96,512]{1,0:T(8,128)(2,1)} %refs_1_.1) | copy-start | bytes 294916
  9.6 21.2 %copy-start.8 = (bf16[96,512]{1,0:T(8,128)(2,1)S(1)}, bf16[96,512]{1,0:T(8,128)(2,1)}, u32[]{:S(2)}) copy-start(bf16[96,512]{1,0:T(8,128)(2,1)} %refs_2_.6) | copy-start | bytes 294916
  9.6 21.2 %copy-start.9 = (bf16[96,512]{1,0:T(8,128)(2,1)S(1)}, bf16[96,512]{1,0:T(8,128)(2,1)}, u32[]{:S(2)}) copy-start(bf16[96,512]{1,0:T(8,128)(2,1)} %refs_3_.4) | copy-start | bytes 294916
  9.6 20.7 %collective-permute-start.5 = (bf16[96,1536]{1,0:T(8,128)(2,1)S(1)}, bf16[96,1536]{1,0:T(8,128)(2,1)S(1)}, u32[]{:S(2)}, u32[]{:S(2)}) collective-permute-start(bf16[96,1536]{1,0:T(8,128)(2,1)S(1)} %get-tuple-element.43.refs_0_), channel_id=1, source_target_pairs={{0,8},{4,12},{8,0},{12,4},{16,24},{20,28},{24,16},{28,20},{1,9},{5... | collective-permute-start | bytes 884744 | tf_op jit(solution)/shard_map/ppermute | solution.py:19
  11.1 19.1 %collective-permute-start.4 = (bf16[96,1536]{1,0:T(8,128)(2,1)S(1)}, bf16[96,1536]{1,0:T(8,128)(2,1)S(1)}, u32[]{:S(2)}, u32[]{:S(2)}) collective-permute-start(bf16[96,1536]{1,0:T(8,128)(2,1)S(1)} %get-tuple-element.43.refs_0_), channel_id=1, source_target_pairs={{0,16},{4,20},{8,24},{12,28},{16,0},{20,4},{24,8},{28,12},{1,17},{... | collective-permute-start | bytes 884744 | tf_op jit(solution)/shard_map/ppermute | solution.py:19
  12.7 17.6 %collective-permute-start.3 = (bf16[96,1536]{1,0:T(8,128)(2,1)S(1)}, bf16[96,1536]{1,0:T(8,128)(2,1)S(1)}, u32[]{:S(2)}, u32[]{:S(2)}) collective-permute-start(bf16[96,1536]{1,0:T(8,128)(2,1)S(1)} %get-tuple-element.43.refs_0_), channel_id=1, source_target_pairs={{0,24},{4,28},{8,16},{12,20},{16,8},{20,12},{24,0},{28,4},{1,25},{... | collective-permute-start | bytes 884744 | tf_op jit(solution)/shard_map/ppermute | solution.py:19
  13.1 13.2 %collective-permute-start.1 = (bf16[64,1536]{1,0:T(8,128)(2,1)S(1)}, bf16[64,1536]{1,0:T(8,128)(2,1)S(1)}, u32[]{:S(2)}, u32[]{:S(2)}) collective-permute-start(bf16[64,1536]{1,0:T(8,128)(2,1)S(1)} %get-tuple-element.42.refs_3_), channel_id=1, source_target_pairs={{0,2},{1,3},{2,0},{3,1},{4,6},{5,7},{6,4},{7,5},{8,10},{9,11},{10,... | collective-permute-start | bytes 589832 | tf_op jit(solution)/shard_map/ppermute | solution.py:19
  14.9 15.4 %collective-permute-start = (bf16[64,1536]{1,0:T(8,128)(2,1)S(1)}, bf16[64,1536]{1,0:T(8,128)(2,1)S(1)}, u32[]{:S(2)}, u32[]{:S(2)}) collective-permute-start(bf16[64,1536]{1,0:T(8,128)(2,1)S(1)} %get-tuple-element.42.refs_3_), channel_id=1, source_target_pairs={{0,1},{1,0},{2,3},{3,2},{4,5},{5,4},{6,7},{7,6},{8,9},{9,8},{10,11... | collective-permute-start | bytes 589832 | tf_op jit(solution)/shard_map/ppermute | solution.py:19
  30.7 3.9 %copy-start.11 = (f32[768]{0:T(1024)S(1)}, f32[768]{0:T(1024)}, u32[]{:S(2)}) copy-start(f32[768]{0:T(1024)} %refs_2_.5) | copy-start | bytes 9220
  30.7 3.9 %collective-permute-start.6 = (bf16[384,1536]{1,0:T(8,128)(2,1)S(1)}, bf16[384,1536]{1,0:T(8,128)(2,1)S(1)}, u32[]{:S(2)}, u32[]{:S(2)}) collective-permute-start(bf16[384,1536]{1,0:T(8,128)(2,1)S(1)} %shard_map.181.refs_7_.refs_4_), channel_id=1, source_target_pairs={{0,4},{4,0},{8,12},{12,8},{16,20},{20,16},{24,28},{28,24},{1,5},{5... | collective-permute-start | bytes 3538952 | tf_op jit(solution)/shard_map/ppermute | solution.py:19
  31.0 12.1 %collective-permute-start.12 = (bf16[96,2048]{1,0:T(8,128)(2,1)S(1)}, bf16[96,2048]{1,0:T(8,128)(2,1)}, u32[]{:S(2)}, u32[]{:S(2)}) collective-permute-start(bf16[96,2048]{1,0:T(8,128)(2,1)S(1)} %shard_map.183.refs_6_), channel_id=1, source_target_pairs={{0,8},{4,12},{8,0},{12,4},{16,24},{20,28},{24,16},{28,20},{1,9},{5... | collective-permute-start | bytes 1179656 | tf_op jit(solution)/shard_map/ppermute | solution.py:19
  32.6 19.7 %collective-permute-start.11 = (bf16[96,2048]{1,0:T(8,128)(2,1)S(1)}, bf16[96,2048]{1,0:T(8,128)(2,1)}, u32[]{:S(2)}, u32[]{:S(2)}) collective-permute-start(bf16[96,2048]{1,0:T(8,128)(2,1)S(1)} %shard_map.183.refs_6_), channel_id=1, source_target_pairs={{0,16},{4,20},{8,24},{12,28},{16,0},{20,4},{24,8},{28,12},{1,17},{... | collective-permute-start | bytes 1179656 | tf_op jit(solution)/shard_map/ppermute | solution.py:19
  34.1 18.2 %collective-permute-start.10 = (bf16[96,2048]{1,0:T(8,128)(2,1)S(1)}, bf16[96,2048]{1,0:T(8,128)(2,1)}, u32[]{:S(2)}, u32[]{:S(2)}) collective-permute-start(bf16[96,2048]{1,0:T(8,128)(2,1)S(1)} %shard_map.183.refs_6_), channel_id=1, source_target_pairs={{0,24},{4,28},{8,16},{12,20},{16,8},{20,12},{24,0},{28,4},{1,25},{... | collective-permute-start | bytes 1179656 | tf_op jit(solution)/shard_map/ppermute | solution.py:19
  34.6 17.8 %copy-start.1 = (bf16[1,64,768]{2,1,0:T(8,128)(2,1)S(1)}, bf16[1,64,768]{2,1,0:T(8,128)(2,1)}, u32[]{:S(2)}) copy-start(bf16[1,64,768]{2,1,0:T(8,128)(2,1)} %param.13) | copy-start | bytes 294916
  34.6 17.8 %copy-start.10 = (f32[768]{0:T(1024)S(1)}, f32[768]{0:T(1024)}, u32[]{:S(2)}) copy-start(f32[768]{0:T(1024)} %refs_0_.5) | copy-start | bytes 9220
  36.6 28.7 %copy-start.12 = (f32[4,9]{1,0:T(4,128)S(1)}, f32[4,9]{1,0:T(4,128)}, u32[]{:S(2)}) copy-start(f32[4,9]{1,0:T(4,128)} %refs_2_.7) | copy-start | bytes 436
  36.6 28.7 %copy-start.13 = (s32[1,256]{1,0:T(1,128)S(1)}, s32[1,256]{1,0:T(1,128)}, u32[]{:S(2)}) copy-start(s32[1,256]{1,0:T(1,128)} %refs_3_.5) | copy-start | bytes 3076
  36.6 28.7 %copy-start.14 = (s32[1,256]{1,0:T(1,128)S(1)}, s32[1,256]{1,0:T(1,128)}, u32[]{:S(2)}) copy-start(s32[1,256]{1,0:T(1,128)} %refs_4_.1) | copy-start | bytes 3076
  36.7 15.7 %collective-permute-start.7 = (bf16[64,768]{1,0:T(8,128)(2,1)S(1)}, bf16[64,768]{1,0:T(8,128)(2,1)S(1)}, u32[]{:S(2)}, u32[]{:S(2)}) collective-permute-start(bf16[64,768]{1,0:T(8,128)(2,1)S(1)} %get-tuple-element.45), channel_id=1, source_target_pairs={{0,1},{1,0},{2,3},{3,2},{4,5},{5,4},{6,7},{7,6},{8,9},{9,8},{10,11... | collective-permute-start | bytes 294920 | tf_op jit(solution)/shard_map/ppermute | solution.py:19
  36.7 15.6 %collective-permute-start.8 = (bf16[64,768]{1,0:T(8,128)(2,1)S(1)}, bf16[64,768]{1,0:T(8,128)(2,1)S(1)}, u32[]{:S(2)}, u32[]{:S(2)}) collective-permute-start(bf16[64,768]{1,0:T(8,128)(2,1)S(1)} %get-tuple-element.46), channel_id=1, source_target_pairs={{0,2},{1,3},{2,0},{3,1},{4,6},{5,7},{6,4},{7,5},{8,10},{9,11},{10,... | collective-permute-start | bytes 294920 | tf_op jit(solution)/shard_map/ppermute | solution.py:19
  43.1 9.2 %collective-permute-start.9 = (bf16[64,768]{1,0:T(8,128)(2,1)S(1)}, bf16[64,768]{1,0:T(8,128)(2,1)S(1)}, u32[]{:S(2)}, u32[]{:S(2)}) collective-permute-start(bf16[64,768]{1,0:T(8,128)(2,1)S(1)} %get-tuple-element.47), channel_id=1, source_target_pairs={{0,3},{1,2},{2,1},{3,0},{4,7},{5,6},{6,5},{7,4},{8,11},{9,10},{10,... | collective-permute-start | bytes 294920 | tf_op jit(solution)/shard_map/ppermute | solution.py:19
  54.0 11.3 %collective-permute-start.16 = (bf16[384,2048]{1,0:T(8,128)(2,1)S(1)}, bf16[384,2048]{1,0:T(8,128)(2,1)S(1)}, u32[]{:S(2)}, u32[]{:S(2)}) collective-permute-start(bf16[384,2048]{1,0:T(8,128)(2,1)S(1)} %get-tuple-element.55.refs_10_), channel_id=1, source_target_pairs={{0,4},{4,0},{8,12},{12,8},{16,20},{20,16},{24,28},{28,24},{1,5},{5... | collective-permute-start | bytes 4718600 | tf_op jit(solution)/shard_map/ppermute | solution.py:19
  54.1 7.6 %collective-permute-start.15 = (bf16[64,768]{1,0:T(8,128)(2,1)S(1)}, bf16[64,768]{1,0:T(8,128)(2,1)S(1)}, u32[]{:S(2)}, u32[]{:S(2)}) collective-permute-start(bf16[64,768]{1,0:T(8,128)(2,1)S(1)} %get-tuple-element.53.refs_5_), channel_id=1, source_target_pairs={{0,3},{1,2},{2,1},{3,0},{4,7},{5,6},{6,5},{7,4},{8,11},{9,10},{10,... | collective-permute-start | bytes 294920 | tf_op jit(solution)/shard_map/ppermute | solution.py:19
  56.4 8.9 %collective-permute-start.14 = (bf16[64,768]{1,0:T(8,128)(2,1)S(1)}, bf16[64,768]{1,0:T(8,128)(2,1)S(1)}, u32[]{:S(2)}, u32[]{:S(2)}) collective-permute-start(bf16[64,768]{1,0:T(8,128)(2,1)S(1)} %get-tuple-element.53.refs_5_), channel_id=1, source_target_pairs={{0,2},{1,3},{2,0},{3,1},{4,6},{5,7},{6,4},{7,5},{8,10},{9,11},{10,... | collective-permute-start | bytes 294920 | tf_op jit(solution)/shard_map/ppermute | solution.py:19
  56.4 8.9 %collective-permute-start.13 = (bf16[64,768]{1,0:T(8,128)(2,1)S(1)}, bf16[64,768]{1,0:T(8,128)(2,1)S(1)}, u32[]{:S(2)}, u32[]{:S(2)}) collective-permute-start(bf16[64,768]{1,0:T(8,128)(2,1)S(1)} %get-tuple-element.53.refs_5_), channel_id=1, source_target_pairs={{0,1},{1,0},{2,3},{3,2},{4,5},{5,4},{6,7},{7,6},{8,9},{9,8},{10,11... | collective-permute-start | bytes 294920 | tf_op jit(solution)/shard_map/ppermute | solution.py:19
  73.6 3.5 %collective-permute-start.23 = (bf16[384,2048]{1,0:T(8,128)(2,1)S(1)}, bf16[384,2048]{1,0:T(8,128)(2,1)S(1)}, u32[]{:S(2)}, u32[]{:S(2)}) collective-permute-start(bf16[384,2048]{1,0:T(8,128)(2,1)S(1)} %get-tuple-element.64), channel_id=1, source_target_pairs={{0,4},{4,0},{8,12},{12,8},{16,20},{20,16},{24,28},{28,24},{1,5},{5... | collective-permute-start | bytes 4718600 | tf_op jit(solution)/shard_map/ppermute | solution.py:19
  77.1 13.2 %copy-start.3 = (bf16[1,64,768]{2,1,0:T(8,128)(2,1)S(1)}, bf16[1,64,768]{2,1,0:T(8,128)(2,1)}, u32[]{:S(2)}) copy-start(bf16[1,64,768]{2,1,0:T(8,128)(2,1)} %param.25) | copy-start | bytes 294916
  77.4 23.2 %collective-permute-start.24 = (bf16[96,2048]{1,0:T(8,128)(2,1)S(1)}, bf16[96,2048]{1,0:T(8,128)(2,1)S(1)}, u32[]{:S(2)}, u32[]{:S(2)}) collective-permute-start(bf16[96,2048]{1,0:T(8,128)(2,1)S(1)} %get-tuple-element.65), channel_id=1, source_target_pairs={{0,8},{4,12},{8,0},{12,4},{16,24},{20,28},{24,16},{28,20},{1,9},{5... | collective-permute-start | bytes 1179656 | tf_op jit(solution)/shard_map/ppermute | solution.py:19
  78.7 21.9 %collective-permute-start.25 = (bf16[96,2048]{1,0:T(8,128)(2,1)S(1)}, bf16[96,2048]{1,0:T(8,128)(2,1)S(1)}, u32[]{:S(2)}, u32[]{:S(2)}) collective-permute-start(bf16[96,2048]{1,0:T(8,128)(2,1)S(1)} %get-tuple-element.66), channel_id=1, source_target_pairs={{0,16},{4,20},{8,24},{12,28},{16,0},{20,4},{24,8},{28,12},{1,17},{... | collective-permute-start | bytes 1179656 | tf_op jit(solution)/shard_map/ppermute | solution.py:19
  79.6 5.5 %collective-permute-start.17 = (bf16[64,768]{1,0:T(8,128)(2,1)S(1)}, bf16[64,768]{1,0:T(8,128)(2,1)S(1)}, u32[]{:S(2)}, u32[]{:S(2)}) collective-permute-start(bf16[64,768]{1,0:T(8,128)(2,1)S(1)} %get-tuple-element.57), channel_id=1, source_target_pairs={{0,1},{1,0},{2,3},{3,2},{4,5},{5,4},{6,7},{7,6},{8,9},{9,8},{10,11... | collective-permute-start | bytes 294920 | tf_op jit(solution)/shard_map/ppermute | solution.py:19
  80.1 10.2 %collective-permute-start.18 = (bf16[64,768]{1,0:T(8,128)(2,1)S(1)}, bf16[64,768]{1,0:T(8,128)(2,1)S(1)}, u32[]{:S(2)}, u32[]{:S(2)}) collective-permute-start(bf16[64,768]{1,0:T(8,128)(2,1)S(1)} %get-tuple-element.58), channel_id=1, source_target_pairs={{0,2},{1,3},{2,0},{3,1},{4,6},{5,7},{6,4},{7,5},{8,10},{9,11},{10,... | collective-permute-start | bytes 294920 | tf_op jit(solution)/shard_map/ppermute | solution.py:19
  82.4 7.8 %collective-permute-start.19 = (bf16[64,768]{1,0:T(8,128)(2,1)S(1)}, bf16[64,768]{1,0:T(8,128)(2,1)S(1)}, u32[]{:S(2)}, u32[]{:S(2)}) collective-permute-start(bf16[64,768]{1,0:T(8,128)(2,1)S(1)} %get-tuple-element.59), channel_id=1, source_target_pairs={{0,3},{1,2},{2,1},{3,0},{4,7},{5,6},{6,5},{7,4},{8,11},{9,10},{10,... | collective-permute-start | bytes 294920 | tf_op jit(solution)/shard_map/ppermute | solution.py:19
  90.5 7.3 %collective-permute-start.22 = (bf16[64,768]{1,0:T(8,128)(2,1)S(1)}, bf16[64,768]{1,0:T(8,128)(2,1)S(1)}, u32[]{:S(2)}, u32[]{:S(2)}) collective-permute-start(bf16[64,768]{1,0:T(8,128)(2,1)S(1)} %shard_map.186.refs_5_), channel_id=1, source_target_pairs={{0,3},{1,2},{2,1},{3,0},{4,7},{5,6},{6,5},{7,4},{8,11},{9,10},{10,... | collective-permute-start | bytes 294920 | tf_op jit(solution)/shard_map/ppermute | solution.py:19
  92.7 7.9 %collective-permute-start.21 = (bf16[64,768]{1,0:T(8,128)(2,1)S(1)}, bf16[64,768]{1,0:T(8,128)(2,1)S(1)}, u32[]{:S(2)}, u32[]{:S(2)}) collective-permute-start(bf16[64,768]{1,0:T(8,128)(2,1)S(1)} %shard_map.186.refs_5_), channel_id=1, source_target_pairs={{0,2},{1,3},{2,0},{3,1},{4,6},{5,7},{6,4},{7,5},{8,10},{9,11},{10,... | collective-permute-start | bytes 294920 | tf_op jit(solution)/shard_map/ppermute | solution.py:19
  93.7 6.9 %collective-permute-start.20 = (bf16[64,768]{1,0:T(8,128)(2,1)S(1)}, bf16[64,768]{1,0:T(8,128)(2,1)S(1)}, u32[]{:S(2)}, u32[]{:S(2)}) collective-permute-start(bf16[64,768]{1,0:T(8,128)(2,1)S(1)} %shard_map.186.refs_5_), channel_id=1, source_target_pairs={{0,1},{1,0},{2,3},{3,2},{4,5},{5,4},{6,7},{7,6},{8,9},{9,8},{10,11... | collective-permute-start | bytes 294920 | tf_op jit(solution)/shard_map/ppermute | solution.py:19
  102.1 2.9 %collective-permute-start.26 = (bf16[384,1536]{1,0:T(8,128)(2,1)S(1)}, bf16[384,1536]{1,0:T(8,128)(2,1)S(1)}, u32[]{:S(2)}, u32[]{:S(2)}) collective-permute-start(bf16[384,1536]{1,0:T(8,128)(2,1)S(1)} %get-tuple-element.68), channel_id=1, source_target_pairs={{0,4},{4,0},{8,12},{12,8},{16,20},{20,16},{24,28},{28,24},{1,5},{5... | collective-permute-start | bytes 3538952 | tf_op jit(solution)/shard_map/ppermute | solution.py:19
  102.2 12.9 %collective-permute-start.30 = (bf16[96,2048]{1,0:T(8,128)(2,1)S(1)}, bf16[96,2048]{1,0:T(8,128)(2,1)S(1)}, u32[]{:S(2)}, u32[]{:S(2)}) collective-permute-start(bf16[96,2048]{1,0:T(8,128)(2,1)S(1)} %get-tuple-element.76), channel_id=1, source_target_pairs={{0,24},{4,28},{8,16},{12,20},{16,8},{20,12},{24,0},{28,4},{1,25},{... | collective-permute-start | bytes 1179656 | tf_op jit(solution)/shard_map/ppermute | solution.py:19
  106.0 15.2 %collective-permute-start.27 = (bf16[96,1536]{1,0:T(8,128)(2,1)S(1)}, bf16[96,1536]{1,0:T(8,128)(2,1)S(1)}, u32[]{:S(2)}, u32[]{:S(2)}) collective-permute-start(bf16[96,1536]{1,0:T(8,128)(2,1)S(1)} %get-tuple-element.72), channel_id=1, source_target_pairs={{0,8},{4,12},{8,0},{12,4},{16,24},{20,28},{24,16},{28,20},{1,9},{5... | collective-permute-start | bytes 884744 | tf_op jit(solution)/shard_map/ppermute | solution.py:19
  107.5 13.8 %collective-permute-start.28 = (bf16[96,1536]{1,0:T(8,128)(2,1)S(1)}, bf16[96,1536]{1,0:T(8,128)(2,1)S(1)}, u32[]{:S(2)}, u32[]{:S(2)}) collective-permute-start(bf16[96,1536]{1,0:T(8,128)(2,1)S(1)} %get-tuple-element.73), channel_id=1, source_target_pairs={{0,16},{4,20},{8,24},{12,28},{16,0},{20,4},{24,8},{28,12},{1,17},{... | collective-permute-start | bytes 884744 | tf_op jit(solution)/shard_map/ppermute | solution.py:19
  108.0 19.3 %collective-permute-start.29 = (bf16[96,1536]{1,0:T(8,128)(2,1)S(1)}, bf16[96,1536]{1,0:T(8,128)(2,1)S(1)}, u32[]{:S(2)}, u32[]{:S(2)}) collective-permute-start(bf16[96,1536]{1,0:T(8,128)(2,1)S(1)} %get-tuple-element.74), channel_id=1, source_target_pairs={{0,24},{4,28},{8,16},{12,20},{16,8},{20,12},{24,0},{28,4},{1,25},{... | collective-permute-start | bytes 884744 | tf_op jit(solution)/shard_map/ppermute | solution.py:19
  116.2 14.8 %all-to-all-start = ((bf16[4,64,768]{2,1,0:T(8,128)(2,1)}), bf16[4,64,768]{2,1,0:T(8,128)(2,1)S(1)}, u32[]{:S(2)}, u32[]{:S(2)}) async-start(bf16[4,64,768]{2,1,0:T(8,128)(2,1)} %bitcast.4), calls=%async_computation | async-start | bytes 786432 | tf_op jit(solution)/shard_map/all_to_all | solution.py:478

commit v4 on v3

--- a/solution.py
+++ b/solution.py
@@ -19,7 +19,7 @@
     return lax.ppermute(values, axis, [(one, one ^ mask) for one in range(size)])
 
 
-def call(body, outs, args, scratch=(), flops=0, smem=0, far=0, after=()):
+def call(body, outs, args, scratch=(), flops=0, smem=0, far=0, after=(), alone=False):
     count = len(args)
     specs = [pl.BlockSpec(memory_space=pltpu.SMEM)] * smem
     specs += [pl.BlockSpec(memory_space=pltpu.VMEM)] * (count - smem - far)
@@ -34,7 +34,7 @@
         in_specs=specs,
         out_specs=tuple(pl.BlockSpec(memory_space=pltpu.VMEM) for _ in outs),
         scratch_shapes=list(scratch),
-        compiler_params=pltpu.CompilerParams(vmem_limit_bytes=min(held + 6 * MIB, 56 * MIB)),
+        compiler_params=pltpu.CompilerParams(vmem_limit_bytes=60 * MIB if alone else min(held + 6 * MIB, 56 * MIB)),
         cost_estimate=pl.CostEstimate(flops=flops, bytes_accessed=moved, transcendentals=0),
     )(*args, *after)
 
@@ -307,7 +307,7 @@
     return call(stack_kernel, [out], pieces, far=len(pieces), after=after)[0]
 
 
-def pack(groups, after=()):
+def pack(groups, after=(), alone=False):
     outs = [
         shape((group[0].shape[0], sum(one.shape[1] for one in group)), BF) for group in groups
     ]
@@ -316,7 +316,7 @@
         return [jnp.concatenate(group, axis=1) for group in groups]
     pieces = [one for group in groups for one in group]
     body = functools.partial(pack_kernel, tuple(len(group) for group in groups))
-    return call(body, outs, pieces, far=len(pieces), after=after)
+    return call(body, outs, pieces, far=len(pieces), after=after, alone=alone)
 
 
 def per_device(
@@ -350,24 +350,25 @@
     place = lax.axis_index("ctx").astype(jnp.int32).reshape(1)
     cot_scale = 1.0 / math.sqrt(dp * frames)
 
-    def gather_frames(values):
+    def gather_frames(values, relay=False):
         if not direct_frames:
             return [lax.all_gather(values, "ctx", axis=0, tiled=True)]
-        return [values] + [exchange(values, "ctx", mask) for mask in (1, 2, 3)]
+        parts = [values] + [exchange(values, "ctx", mask) for mask in (1, 2)]
+        return parts + [exchange(*((parts[2], "ctx", 1) if relay else (values, "ctx", 3)))]
 
     def scatter_frames(pieces):
         if not direct_frames:
             return [lax.psum_scatter(pieces[0], "ctx", scatter_dimension=0, tiled=True)]
         return [pieces[0]] + [exchange(pieces[mask], "ctx", mask) for mask in (1, 2, 3)]
 
-    def scatter_rows(pieces, passed=()):
+    def scatter_rows(pieces, passed=(), after=()):
         if not direct_rows:
             made = lax.psum_scatter(pieces[0], "dp", scatter_dimension=0, tiled=True)
             return [made], passed
         keep, send = pieces
         came = exchange(send, "dp", 1)
         outs = [shape((rows, keep.shape[1]), BF)] * 4 + [shape(one.shape, BF) for one in passed]
-        sums = call(pair_sum_kernel, outs, [keep, came, *passed])
+        sums = call(pair_sum_kernel, outs, [keep, came, *passed], after=after)
         terms = [sums[0]] + [exchange(sums[at], "dp", 2 * at) for at in (1, 2, 3)]
         return terms, sums[4:] if passed else sums[:1]
 
@@ -378,8 +379,8 @@
         return total
 
     frames_own, cot_own = frames_in[0], cotangent[0]
-    both_own, ffn_rows = pack([[frames_own, cot_own], [w_up, w_down]])
-    both_parts = gather_frames(both_own)
+    both_own, ffn_rows = pack([[frames_own, cot_own], [w_up, w_down]], alone=True)
+    both_parts = gather_frames(both_own, True)
 
     def gather_near(weight):
         return [weight] + [exchange(weight, "dp", mask) for mask in (6, 4, 2)]
@@ -456,7 +457,7 @@
         flops=8 * frames * model * inner,
         smem=1,
     )
-    attn_terms, attn_sums = scatter_rows(attn_grads)
+    attn_terms, attn_sums = scatter_rows(attn_grads, after=upstream[1:])
     (grad_mid_own,) = call(
         functools.partial(grad_mid_kernel, len(upstream), cot_scale),
         [shape((own, model), BF)],

time: 132 us -> 125 us (0.947)
  starting transfers between devices: 50.3 us -> 45.1 us
  local copies, waits for them, and re-layouts: 5.39 us -> 2.76 us
  Pallas kernels: 15.8 us -> 17.5 us
    ppermute x31, starting transfers between devices: 46.8 us -> 41.3 us  [exchange(): lax.ppermute(values, axis, [(one, one ^ mask) for one in range(size)])]
    unnamed x30 -> x26, local copies, waits for them, and re-layouts: 3.65 us -> 1.03 us
    pallas_call x11, Pallas kernels: 15.8 us -> 17.5 us  [call(): pl.pallas_call(lambda *refs: body(*refs[:count], *refs[count + len(after)...]
where the time goes in v4:
time: 125 us; the launch traced here: 124 us
  waiting for transfers between devices  57.1 us (46%)
  starting transfers between devices  45.1 us (36%)
  Pallas kernels  17.5 us (14%)
  local copies, waits for them, and re-layouts  2.76 us (2%)
    ppermute x31, waiting for transfers between devices, exchange(): lax.ppermute(values, axis, [(one, one ^ mask) for one in range(size)])  54.3 us
    ppermute x31, starting transfers between devices, exchange(): lax.ppermute(values, axis, [(one, one ^ mask) for one in range(size)])  41.3 us
    pallas_call x11, Pallas kernels, call(): pl.pallas_call(lambda *refs: body(*refs[:count], *refs[count + len(after)...  17.5 us
    all_to_all x1, starting transfers between devices, per_device(): attn_sum = lax.all_to_all(passed[0], 'ctx', 0, 0, tiled=True)  3.81 us
    all_to_all x1, waiting for transfers between devices, per_device(): attn_sum = lax.all_to_all(passed[0], 'ctx', 0, 0, tiled=True)  2.79 us
  transfers between devices with their start and end apart: 32, of which 18 were waited for; matrix products, arithmetic and copies ran while one was open for 2% of the time, Pallas kernels for 3%

profile of v4, /device:TPU:0, one launch (start us, length us, event | category | flops | bytes accessed | tf_op | source)
XLA Modules:
  0.0 124.5 jit_solution(5575424301617398684)
XLA Ops:
  0.7 2.1 %shard_map.180 = (bf16[64,1536]{1,0:T(8,128)(2,1)}, bf16[96,1536]{1,0:T(8,128)(2,1)}) custom-call(bf16[64,768]{1,0:T(8,128)(2,1)} %bitcast.13, bf16[64,768]{1,0:T(8,128)(2,1)} %bitcast.15, bf16[96,768]{1,0:T(8,128)(2,1)} %refs_2_.4, bf16[96,768]{1,0:T(8,128)(2,1)} %refs_3_.3), custom_call_target="tpu_custom_call" | custom-call | bytes 983040 | tf_op jit(solution)/shard_map/pallas_call | solution.py:31
  2.7 4.1 %collective-permute-start.1 = (bf16[64,1536]{1,0:T(8,128)(2,1)}, bf16[64,1536]{1,0:T(8,128)(2,1)S(1)}, u32[]{:S(2)}, u32[]{:S(2)}) collective-permute-start(bf16[64,1536]{1,0:T(8,128)(2,1)} %get-tuple-element.42.refs_3_), channel_id=1, source_target_pairs={{0,2},{1,3},{2,0},{3,1},{4,6},{5,7},{6,4},{7,5},{8,10},{9,11},{10,... | collective-permute-start | bytes 589832 | tf_op jit(solution)/shard_map/ppermute | solution.py:19
  6.8 1.5 %collective-permute-start.5 = (bf16[96,1536]{1,0:T(8,128)(2,1)}, bf16[96,1536]{1,0:T(8,128)(2,1)S(1)}, u32[]{:S(2)}, u32[]{:S(2)}) collective-permute-start(bf16[96,1536]{1,0:T(8,128)(2,1)} %get-tuple-element.43.refs_0_), channel_id=1, source_target_pairs={{0,8},{4,12},{8,0},{12,4},{16,24},{20,28},{24,16},{28,20},{1,9},{5... | collective-permute-start | bytes 884744 | tf_op jit(solution)/shard_map/ppermute | solution.py:19
  8.3 1.5 %collective-permute-start.4 = (bf16[96,1536]{1,0:T(8,128)(2,1)}, bf16[96,1536]{1,0:T(8,128)(2,1)S(1)}, u32[]{:S(2)}, u32[]{:S(2)}) collective-permute-start(bf16[96,1536]{1,0:T(8,128)(2,1)} %get-tuple-element.43.refs_0_), channel_id=1, source_target_pairs={{0,16},{4,20},{8,24},{12,28},{16,0},{20,4},{24,8},{28,12},{1,17},{... | collective-permute-start | bytes 884744 | tf_op jit(solution)/shard_map/ppermute | solution.py:19
  10.3 1.6 %collective-permute-start = (bf16[64,1536]{1,0:T(8,128)(2,1)}, bf16[64,1536]{1,0:T(8,128)(2,1)S(1)}, u32[]{:S(2)}, u32[]{:S(2)}) collective-permute-start(bf16[64,1536]{1,0:T(8,128)(2,1)} %get-tuple-element.42.refs_3_), channel_id=1, source_target_pairs={{0,1},{1,0},{2,3},{3,2},{4,5},{5,4},{6,7},{7,6},{8,9},{9,8},{10,11... | collective-permute-start | bytes 589832 | tf_op jit(solution)/shard_map/ppermute | solution.py:19
  11.9 4.4 %collective-permute-done.1.refs_5_ = bf16[64,1536]{1,0:T(8,128)(2,1)S(1)} collective-permute-done((bf16[64,1536]{1,0:T(8,128)(2,1)}, bf16[64,1536]{1,0:T(8,128)(2,1)S(1)}, u32[]{:S(2)}, u32[]{:S(2)}) %collective-permute-start.1) | collective-permute-done | bytes 196640 | tf_op jit(solution)/shard_map/ppermute | solution.py:19
  17.0 3.0 %collective-permute-done.refs_4_ = bf16[64,1536]{1,0:T(8,128)(2,1)S(1)} collective-permute-done((bf16[64,1536]{1,0:T(8,128)(2,1)}, bf16[64,1536]{1,0:T(8,128)(2,1)S(1)}, u32[]{:S(2)}, u32[]{:S(2)}) %collective-permute-start) | collective-permute-done | bytes 196640 | tf_op jit(solution)/shard_map/ppermute | solution.py:19
  20.1 3.0 %collective-permute-done.4.refs_2_ = bf16[96,1536]{1,0:T(8,128)(2,1)S(1)} collective-permute-done((bf16[96,1536]{1,0:T(8,128)(2,1)}, bf16[96,1536]{1,0:T(8,128)(2,1)S(1)}, u32[]{:S(2)}, u32[]{:S(2)}) %collective-permute-start.4) | collective-permute-done | bytes 294944 | tf_op jit(solution)/shard_map/ppermute | solution.py:19
  23.3 1.0 copy-done.2
  25.0 1.6 %collective-permute-start.12 = (bf16[96,2048]{1,0:T(8,128)(2,1)S(1)}, bf16[96,2048]{1,0:T(8,128)(2,1)}, u32[]{:S(2)}, u32[]{:S(2)}) collective-permute-start(bf16[96,2048]{1,0:T(8,128)(2,1)S(1)} %shard_map.183.refs_6_), channel_id=1, source_target_pairs={{0,8},{4,12},{8,0},{12,4},{16,24},{20,28},{24,16},{28,20},{1,9},{5... | collective-permute-start | bytes 1179656 | tf_op jit(solution)/shard_map/ppermute | solution.py:19
  26.6 1.5 %collective-permute-start.11 = (bf16[96,2048]{1,0:T(8,128)(2,1)S(1)}, bf16[96,2048]{1,0:T(8,128)(2,1)}, u32[]{:S(2)}, u32[]{:S(2)}) collective-permute-start(bf16[96,2048]{1,0:T(8,128)(2,1)S(1)} %shard_map.183.refs_6_), channel_id=1, source_target_pairs={{0,16},{4,20},{8,24},{12,28},{16,0},{20,4},{24,8},{28,12},{1,17},{... | collective-permute-start | bytes 1179656 | tf_op jit(solution)/shard_map/ppermute | solution.py:19
  28.6 2.0 %shard_map.182 = (bf16[256,768]{1,0:T(8,128)(2,1)S(1)}, f32[256,768]{1,0:T(8,128)S(1)}, bf16[256,768]{1,0:T(8,128)(2,1)S(1)}, bf16[768,768]{1,0:T(8,128)(2,1)S(1...) custom-call(s32[1]{0:T(128)} %bitcast.1.refs_0_, ...), custom_call_target="tpu_custom_call" | custom-call | flops 603979776 | bytes 6687752 | tf_op jit(solution)/shard_map/pallas_call | solution.py:31
  30.7 1.4 %collective-permute-start.7 = (bf16[64,768]{1,0:T(8,128)(2,1)S(1)}, bf16[64,768]{1,0:T(8,128)(2,1)S(1)}, u32[]{:S(2)}, u32[]{:S(2)}) collective-permute-start(bf16[64,768]{1,0:T(8,128)(2,1)S(1)} %get-tuple-element.45), channel_id=1, source_target_pairs={{0,1},{1,0},{2,3},{3,2},{4,5},{5,4},{6,7},{7,6},{8,9},{9,8},{10,11... | collective-permute-start | bytes 294920 | tf_op jit(solution)/shard_map/ppermute | solution.py:19
  32.1 2.5 %collective-permute-start.8 = (bf16[64,768]{1,0:T(8,128)(2,1)S(1)}, bf16[64,768]{1,0:T(8,128)(2,1)S(1)}, u32[]{:S(2)}, u32[]{:S(2)}) collective-permute-start(bf16[64,768]{1,0:T(8,128)(2,1)S(1)} %get-tuple-element.46), channel_id=1, source_target_pairs={{0,2},{1,3},{2,0},{3,1},{4,6},{5,7},{6,4},{7,5},{8,10},{9,11},{10,... | collective-permute-start | bytes 294920 | tf_op jit(solution)/shard_map/ppermute | solution.py:19
  34.6 2.6 %collective-permute-done.12.refs_9_ = bf16[96,2048]{1,0:T(8,128)(2,1)} collective-permute-done((bf16[96,2048]{1,0:T(8,128)(2,1)S(1)}, bf16[96,2048]{1,0:T(8,128)(2,1)}, u32[]{:S(2)}, u32[]{:S(2)}) %collective-permute-start.12) | collective-permute-done | bytes 393248 | tf_op jit(solution)/shard_map/ppermute | solution.py:19
  37.1 3.2 %collective-permute-start.9 = (bf16[64,768]{1,0:T(8,128)(2,1)S(1)}, bf16[64,768]{1,0:T(8,128)(2,1)S(1)}, u32[]{:S(2)}, u32[]{:S(2)}) collective-permute-start(bf16[64,768]{1,0:T(8,128)(2,1)S(1)} %get-tuple-element.47), channel_id=1, source_target_pairs={{0,3},{1,2},{2,1},{3,0},{4,7},{5,6},{6,5},{7,4},{8,11},{9,10},{10,... | collective-permute-start | bytes 294920 | tf_op jit(solution)/shard_map/ppermute | solution.py:19
  40.4 6.0 %collective-permute-done.11.refs_8_ = bf16[96,2048]{1,0:T(8,128)(2,1)} collective-permute-done((bf16[96,2048]{1,0:T(8,128)(2,1)S(1)}, bf16[96,2048]{1,0:T(8,128)(2,1)}, u32[]{:S(2)}, u32[]{:S(2)}) %collective-permute-start.11) | collective-permute-done | bytes 393248 | tf_op jit(solution)/shard_map/ppermute | solution.py:19
  46.4 1.6 %shard_map.184 = (f32[64,768]{1,0:T(8,128)S(1)}, bf16[64,768]{1,0:T(8,128)(2,1)S(1)}, bf16[384,2048]{1,0:T(8,128)(2,1)S(1)}) custom-call(f32[768]{0:T(1024)S(1)} %copy-done.8, bf16[64,768]{1,0:T(8,128)(2,1)S(1)} %bitcast.14, bf16[64,768]{1,0:T(8,128)(2,1)S(1)} %get-tuple-element.44.refs_2_, bf16[64,768]{1,0:T(8,128)(2,1)S(1)} %collective-permute-done.7.refs_3_, ...), custom_call_target="tpu_custom_call" | custom-call | bytes 3935232 | tf_op jit(solution)/shard_map/pallas_call | solution.py:31
  48.1 3.3 %collective-permute-start.15 = (bf16[64,768]{1,0:T(8,128)(2,1)S(1)}, bf16[64,768]{1,0:T(8,128)(2,1)S(1)}, u32[]{:S(2)}, u32[]{:S(2)}) collective-permute-start(bf16[64,768]{1,0:T(8,128)(2,1)S(1)} %get-tuple-element.53.refs_5_), channel_id=1, source_target_pairs={{0,3},{1,2},{2,1},{3,0},{4,7},{5,6},{6,5},{7,4},{8,11},{9,10},{10,... | collective-permute-start | bytes 294920 | tf_op jit(solution)/shard_map/ppermute | solution.py:19
  51.4 1.2 collective-permute-start.13
  52.6 3.1 %collective-permute-done.15.refs_8_ = bf16[64,768]{1,0:T(8,128)(2,1)S(1)} collective-permute-done((bf16[64,768]{1,0:T(8,128)(2,1)S(1)}, bf16[64,768]{1,0:T(8,128)(2,1)S(1)}, u32[]{:S(2)}, u32[]{:S(2)}) %collective-permute-start.15) | collective-permute-done | bytes 98336 | tf_op jit(solution)/shard_map/ppermute | solution.py:19
  55.7 4.4 %collective-permute-done.14.refs_7_ = bf16[64,768]{1,0:T(8,128)(2,1)S(1)} collective-permute-done((bf16[64,768]{1,0:T(8,128)(2,1)S(1)}, bf16[64,768]{1,0:T(8,128)(2,1)S(1)}, u32[]{:S(2)}, u32[]{:S(2)}) %collective-permute-start.14) | collective-permute-done | bytes 98336 | tf_op jit(solution)/shard_map/ppermute | solution.py:19
  60.1 6.6 %shard_map.185 = (bf16[256,768]{1,0:T(8,128)(2,1)S(1)}, bf16[256,512]{1,0:T(8,128)(2,1)S(1)}, bf16[256,1536]{1,0:T(8,128)(2,1)S(1)}, bf16[256,768]{1,0:T(8,128)(...) custom-call(s32[1]{0:T(128)} %bitcast.1.refs_0_, ...), custom_call_target="tpu_custom_call" | custom-call | flops 2013265920 | bytes 6162584 | tf_op jit(solution)/shard_map/pallas_call | solution.py:31
  66.7 1.5 %shard_map.187 = (bf16[384,2048]{1,0:T(8,128)(2,1)S(1)}, bf16[384,2048]{1,0:T(8,128)(2,1)S(1)}) custom-call(s32[1]{0:T(128)} %bitcast.2.refs_1_.refs_0_, bf16[256,768]{1,0:T(8,128)(2,1)S(1)} %get-tuple-element.60.refs_1_, bf16[256,768]{1,0:T(8,128)(2,1)S(1)} %get-tuple-element.54.refs_9_.refs_2_, bf16[256,512]{1,0:T(8,128)(2,1)S(1)} %get-tuple-element.61.refs_3_, ...), custom_call_target="tpu_custom_call" | custom-call | flops 805306368 | bytes 4980740 | tf_op jit(solution)/shard_map/pallas_call | solution.py:31
  69.0 2.4 %collective-permute-start.18 = (bf16[64,768]{1,0:T(8,128)(2,1)S(1)}, bf16[64,768]{1,0:T(8,128)(2,1)S(1)}, u32[]{:S(2)}, u32[]{:S(2)}) collective-permute-start(bf16[64,768]{1,0:T(8,128)(2,1)S(1)} %get-tuple-element.58), channel_id=1, source_target_pairs={{0,2},{1,3},{2,0},{3,1},{4,6},{5,7},{6,4},{7,5},{8,10},{9,11},{10,... | collective-permute-start | bytes 294920 | tf_op jit(solution)/shard_map/ppermute | solution.py:19
  71.4 1.3 %collective-permute-start.19 = (bf16[64,768]{1,0:T(8,128)(2,1)S(1)}, bf16[64,768]{1,0:T(8,128)(2,1)S(1)}, u32[]{:S(2)}, u32[]{:S(2)}) collective-permute-start(bf16[64,768]{1,0:T(8,128)(2,1)S(1)} %get-tuple-element.59), channel_id=1, source_target_pairs={{0,3},{1,2},{2,1},{3,0},{4,7},{5,6},{6,5},{7,4},{8,11},{9,10},{10,... | collective-permute-start | bytes 294920 | tf_op jit(solution)/shard_map/ppermute | solution.py:19
  72.7 2.2 %collective-permute-done.17.refs_4_.refs_2_ = bf16[64,768]{1,0:T(8,128)(2,1)S(1)} collective-permute-done((bf16[64,768]{1,0:T(8,128)(2,1)S(1)}, bf16[64,768]{1,0:T(8,128)(2,1)S(1)}, u32[]{:S(2)}, u32[]{:S(2)}) %collective-permute-start.17) | collective-permute-done | bytes 98336 | tf_op jit(solution)/shard_map/ppermute | solution.py:19
  75.0 4.9 %collective-permute-done.18.refs_5_.refs_3_ = bf16[64,768]{1,0:T(8,128)(2,1)S(1)} collective-permute-done((bf16[64,768]{1,0:T(8,128)(2,1)S(1)}, bf16[64,768]{1,0:T(8,128)(2,1)S(1)}, u32[]{:S(2)}, u32[]{:S(2)}) %collective-permute-start.18) | collective-permute-done | bytes 98336 | tf_op jit(solution)/shard_map/ppermute | solution.py:19
  80.2 1.3 %collective-permute-start.24 = (bf16[96,2048]{1,0:T(8,128)(2,1)S(1)}, bf16[96,2048]{1,0:T(8,128)(2,1)S(1)}, u32[]{:S(2)}, u32[]{:S(2)}) collective-permute-start(bf16[96,2048]{1,0:T(8,128)(2,1)S(1)} %get-tuple-element.65), channel_id=1, source_target_pairs={{0,8},{4,12},{8,0},{12,4},{16,24},{20,28},{24,16},{28,20},{1,9},{5... | collective-permute-start | bytes 1179656 | tf_op jit(solution)/shard_map/ppermute | solution.py:19
  81.5 0.8 collective-permute-start.25
  82.6 1.9 %collective-permute-start.22 = (bf16[64,768]{1,0:T(8,128)(2,1)S(1)}, bf16[64,768]{1,0:T(8,128)(2,1)S(1)}, u32[]{:S(2)}, u32[]{:S(2)}) collective-permute-start(bf16[64,768]{1,0:T(8,128)(2,1)S(1)} %shard_map.186.refs_5_), channel_id=1, source_target_pairs={{0,3},{1,2},{2,1},{3,0},{4,7},{5,6},{6,5},{7,4},{8,11},{9,10},{10,... | collective-permute-start | bytes 294920 | tf_op jit(solution)/shard_map/ppermute | solution.py:19
  84.5 1.5 %collective-permute-start.21 = (bf16[64,768]{1,0:T(8,128)(2,1)S(1)}, bf16[64,768]{1,0:T(8,128)(2,1)S(1)}, u32[]{:S(2)}, u32[]{:S(2)}) collective-permute-start(bf16[64,768]{1,0:T(8,128)(2,1)S(1)} %shard_map.186.refs_5_), channel_id=1, source_target_pairs={{0,2},{1,3},{2,0},{3,1},{4,6},{5,7},{6,4},{7,5},{8,10},{9,11},{10,... | collective-permute-start | bytes 294920 | tf_op jit(solution)/shard_map/ppermute | solution.py:19
  86.1 1.0 collective-permute-start.20
  87.1 3.1 %collective-permute-done.22.refs_8_ = bf16[64,768]{1,0:T(8,128)(2,1)S(1)} collective-permute-done((bf16[64,768]{1,0:T(8,128)(2,1)S(1)}, bf16[64,768]{1,0:T(8,128)(2,1)S(1)}, u32[]{:S(2)}, u32[]{:S(2)}) %collective-permute-start.22) | collective-permute-done | bytes 98336 | tf_op jit(solution)/shard_map/ppermute | solution.py:19
  90.2 3.1 %collective-permute-done.21.refs_7_ = bf16[64,768]{1,0:T(8,128)(2,1)S(1)} collective-permute-done((bf16[64,768]{1,0:T(8,128)(2,1)S(1)}, bf16[64,768]{1,0:T(8,128)(2,1)S(1)}, u32[]{:S(2)}, u32[]{:S(2)}) %collective-permute-start.21) | collective-permute-done | bytes 98336 | tf_op jit(solution)/shard_map/ppermute | solution.py:19
  93.3 1.5 %shard_map.189 = (bf16[384,1536]{1,0:T(8,128)(2,1)S(1)}, bf16[384,1536]{1,0:T(8,128)(2,1)S(1)}) custom-call(s32[1]{0:T(128)} %bitcast.2.refs_1_.refs_0_, bf16[256,768]{1,0:T(8,128)(2,1)S(1)} %get-tuple-element.49.refs_1_, f32[256,768]{1,0:T(8,128)S(1)} %get-tuple-element.50.refs_2_, bf16[256,768]{1,0:T(8,128)(2,1)S(1)} %get-tuple-element.51.refs_3_, ...), custom_call_target="tpu_custom_call" | custom-call | flops 905969664 | bytes 5505028 | tf_op jit(solution)/shard_map/pallas_call | solution.py:31
  94.9 1.5 %collective-permute-start.30 = (bf16[96,2048]{1,0:T(8,128)(2,1)S(1)}, bf16[96,2048]{1,0:T(8,128)(2,1)S(1)}, u32[]{:S(2)}, u32[]{:S(2)}) collective-permute-start(bf16[96,2048]{1,0:T(8,128)(2,1)S(1)} %get-tuple-element.76), channel_id=1, source_target_pairs={{0,24},{4,28},{8,16},{12,20},{16,8},{20,12},{24,0},{28,4},{1,25},{... | collective-permute-start | bytes 1179656 | tf_op jit(solution)/shard_map/ppermute | solution.py:19
  96.4 1.3 %collective-permute-done.26.refs_1_ = bf16[384,1536]{1,0:T(8,128)(2,1)S(1)} collective-permute-done((bf16[384,1536]{1,0:T(8,128)(2,1)S(1)}, bf16[384,1536]{1,0:T(8,128)(2,1)S(1)}, u32[]{:S(2)}, u32[]{:S(2)}) %collective-permute-start.26) | collective-permute-done | bytes 1179680 | tf_op jit(solution)/shard_map/ppermute | solution.py:19
  97.7 1.0 shard_map.190
  98.7 1.5 %collective-permute-start.27 = (bf16[96,1536]{1,0:T(8,128)(2,1)S(1)}, bf16[96,1536]{1,0:T(8,128)(2,1)S(1)}, u32[]{:S(2)}, u32[]{:S(2)}) collective-permute-start(bf16[96,1536]{1,0:T(8,128)(2,1)S(1)} %get-tuple-element.72), channel_id=1, source_target_pairs={{0,8},{4,12},{8,0},{12,4},{16,24},{20,28},{24,16},{28,20},{1,9},{5... | collective-permute-start | bytes 884744 | tf_op jit(solution)/shard_map/ppermute | solution.py:19
  100.7 1.5 %collective-permute-start.29 = (bf16[96,1536]{1,0:T(8,128)(2,1)S(1)}, bf16[96,1536]{1,0:T(8,128)(2,1)S(1)}, u32[]{:S(2)}, u32[]{:S(2)}) collective-permute-start(bf16[96,1536]{1,0:T(8,128)(2,1)S(1)} %get-tuple-element.74), channel_id=1, source_target_pairs={{0,24},{4,28},{8,16},{12,20},{16,8},{20,12},{24,0},{28,4},{1,25},{... | collective-permute-start | bytes 884744 | tf_op jit(solution)/shard_map/ppermute | solution.py:19
  102.2 5.6 %collective-permute-done.30 = bf16[96,2048]{1,0:T(8,128)(2,1)S(1)} collective-permute-done((bf16[96,2048]{1,0:T(8,128)(2,1)S(1)}, bf16[96,2048]{1,0:T(8,128)(2,1)S(1)}, u32[]{:S(2)}, u32[]{:S(2)}) %collective-permute-start.30) | collective-permute-done | bytes 393248 | tf_op jit(solution)/shard_map/ppermute | solution.py:19
  108.0 0.9 fusion.2
  108.9 3.8 %all-to-all-start = ((bf16[4,64,768]{2,1,0:T(8,128)(2,1)}), bf16[4,64,768]{2,1,0:T(8,128)(2,1)S(1)}, u32[]{:S(2)}, u32[]{:S(2)}) async-start(bf16[4,64,768]{2,1,0:T(8,128)(2,1)} %bitcast.4), calls=%async_computation | async-start | bytes 786432 | tf_op jit(solution)/shard_map/all_to_all | solution.py:479
  112.7 1.1 collective-permute-done.27
  114.0 6.0 %collective-permute-done.29 = bf16[96,1536]{1,0:T(8,128)(2,1)S(1)} collective-permute-done((bf16[96,1536]{1,0:T(8,128)(2,1)S(1)}, bf16[96,1536]{1,0:T(8,128)(2,1)S(1)}, u32[]{:S(2)}, u32[]{:S(2)}) %collective-permute-start.29) | collective-permute-done | bytes 294944 | tf_op jit(solution)/shard_map/ppermute | solution.py:19
  120.1 0.9 fusion.3
  121.0 2.8 %all-to-all-done = bf16[4,64,768]{2,1,0:T(8,128)(2,1)S(1)} async-done(((bf16[4,64,768]{2,1,0:T(8,128)(2,1)}), bf16[4,64,768]{2,1,0:T(8,128)(2,1)S(1)}, u32[]{:S(2)}, u32[]{:S(2)}) %all-to-all-start) | async-done | bytes 393248 | tf_op jit(solution)/shard_map/all_to_all | solution.py:479
  (58 shorter events, 6.1 us)
Async XLA Ops:
  0.6 24.2 %copy-start.4 = (bf16[96,512]{1,0:T(8,128)(2,1)S(1)}, bf16[96,512]{1,0:T(8,128)(2,1)}, u32[]{:S(2)}) copy-start(bf16[96,512]{1,0:T(8,128)(2,1)} %refs_0_.3) | copy-start | bytes 294916
  0.6 24.2 %copy-start.5 = (bf16[96,512]{1,0:T(8,128)(2,1)S(1)}, bf16[96,512]{1,0:T(8,128)(2,1)}, u32[]{:S(2)}) copy-start(bf16[96,512]{1,0:T(8,128)(2,1)} %refs_1_.1) | copy-start | bytes 294916
  0.7 24.2 %copy-start.6 = (bf16[96,512]{1,0:T(8,128)(2,1)S(1)}, bf16[96,512]{1,0:T(8,128)(2,1)}, u32[]{:S(2)}) copy-start(bf16[96,512]{1,0:T(8,128)(2,1)} %refs_2_.6) | copy-start | bytes 294916
  0.7 24.2 %copy-start.7 = (bf16[96,512]{1,0:T(8,128)(2,1)S(1)}, bf16[96,512]{1,0:T(8,128)(2,1)}, u32[]{:S(2)}) copy-start(bf16[96,512]{1,0:T(8,128)(2,1)} %refs_3_.4) | copy-start | bytes 294916
  2.7 13.5 %collective-permute-start.1 = (bf16[64,1536]{1,0:T(8,128)(2,1)}, bf16[64,1536]{1,0:T(8,128)(2,1)S(1)}, u32[]{:S(2)}, u32[]{:S(2)}) collective-permute-start(bf16[64,1536]{1,0:T(8,128)(2,1)} %get-tuple-element.42.refs_3_), channel_id=1, source_target_pairs={{0,2},{1,3},{2,0},{3,1},{4,6},{5,7},{6,4},{7,5},{8,10},{9,11},{10,... | collective-permute-start | bytes 589832 | tf_op jit(solution)/shard_map/ppermute | solution.py:19
  6.8 13.2 %collective-permute-start.5 = (bf16[96,1536]{1,0:T(8,128)(2,1)}, bf16[96,1536]{1,0:T(8,128)(2,1)S(1)}, u32[]{:S(2)}, u32[]{:S(2)}) collective-permute-start(bf16[96,1536]{1,0:T(8,128)(2,1)} %get-tuple-element.43.refs_0_), channel_id=1, source_target_pairs={{0,8},{4,12},{8,0},{12,4},{16,24},{20,28},{24,16},{28,20},{1,9},{5... | collective-permute-start | bytes 884744 | tf_op jit(solution)/shard_map/ppermute | solution.py:19
  8.3 14.7 %collective-permute-start.4 = (bf16[96,1536]{1,0:T(8,128)(2,1)}, bf16[96,1536]{1,0:T(8,128)(2,1)S(1)}, u32[]{:S(2)}, u32[]{:S(2)}) collective-permute-start(bf16[96,1536]{1,0:T(8,128)(2,1)} %get-tuple-element.43.refs_0_), channel_id=1, source_target_pairs={{0,16},{4,20},{8,24},{12,28},{16,0},{20,4},{24,8},{28,12},{1,17},{... | collective-permute-start | bytes 884744 | tf_op jit(solution)/shard_map/ppermute | solution.py:19
  9.9 13.2 %collective-permute-start.3 = (bf16[96,1536]{1,0:T(8,128)(2,1)}, bf16[96,1536]{1,0:T(8,128)(2,1)S(1)}, u32[]{:S(2)}, u32[]{:S(2)}) collective-permute-start(bf16[96,1536]{1,0:T(8,128)(2,1)} %get-tuple-element.43.refs_0_), channel_id=1, source_target_pairs={{0,24},{4,28},{8,16},{12,20},{16,8},{20,12},{24,0},{28,4},{1,25},{... | collective-permute-start | bytes 884744 | tf_op jit(solution)/shard_map/ppermute | solution.py:19
  10.3 9.7 %collective-permute-start = (bf16[64,1536]{1,0:T(8,128)(2,1)}, bf16[64,1536]{1,0:T(8,128)(2,1)S(1)}, u32[]{:S(2)}, u32[]{:S(2)}) collective-permute-start(bf16[64,1536]{1,0:T(8,128)(2,1)} %get-tuple-element.42.refs_3_), channel_id=1, source_target_pairs={{0,1},{1,0},{2,3},{3,2},{4,5},{5,4},{6,7},{7,6},{8,9},{9,8},{10,11... | collective-permute-start | bytes 589832 | tf_op jit(solution)/shard_map/ppermute | solution.py:19
  16.3 7.1 %collective-permute-start.2 = (bf16[64,1536]{1,0:T(8,128)(2,1)S(1)}, bf16[64,1536]{1,0:T(8,128)(2,1)S(1)}, u32[]{:S(2)}, u32[]{:S(2)}) collective-permute-start(bf16[64,1536]{1,0:T(8,128)(2,1)S(1)} %collective-permute-done.1.refs_5_), channel_id=1, source_target_pairs={{0,1},{1,0},{2,3},{3,2},{4,5},{5,4},{6,7},{7,6},{8,9},{9,8},{10,11... | collective-permute-start | bytes 589832 | tf_op jit(solution)/shard_map/ppermute | solution.py:19
  23.3 1.0 copy-start.2
  24.7 3.9 %copy-start.3 = (bf16[64,1536]{1,0:T(8,128)(2,1)S(1)}, bf16[64,1536]{1,0:T(8,128)(2,1)}, u32[]{:S(2)}) copy-start(bf16[64,1536]{1,0:T(8,128)(2,1)} %get-tuple-element.42.refs_3_) | copy-start | bytes 589828
  24.7 3.9 %copy-start.9 = (f32[768]{0:T(1024)S(1)}, f32[768]{0:T(1024)}, u32[]{:S(2)}) copy-start(f32[768]{0:T(1024)} %refs_2_.5) | copy-start | bytes 9220
  24.7 3.9 %collective-permute-start.6 = (bf16[384,1536]{1,0:T(8,128)(2,1)S(1)}, bf16[384,1536]{1,0:T(8,128)(2,1)S(1)}, u32[]{:S(2)}, u32[]{:S(2)}) collective-permute-start(bf16[384,1536]{1,0:T(8,128)(2,1)S(1)} %shard_map.181.refs_7_.refs_4_), channel_id=1, source_target_pairs={{0,4},{4,0},{8,12},{12,8},{16,20},{20,16},{24,28},{28,24},{1,5},{5... | collective-permute-start | bytes 3538952 | tf_op jit(solution)/shard_map/ppermute | solution.py:19
  25.0 12.1 %collective-permute-start.12 = (bf16[96,2048]{1,0:T(8,128)(2,1)S(1)}, bf16[96,2048]{1,0:T(8,128)(2,1)}, u32[]{:S(2)}, u32[]{:S(2)}) collective-permute-start(bf16[96,2048]{1,0:T(8,128)(2,1)S(1)} %shard_map.183.refs_6_), channel_id=1, source_target_pairs={{0,8},{4,12},{8,0},{12,4},{16,24},{20,28},{24,16},{28,20},{1,9},{5... | collective-permute-start | bytes 1179656 | tf_op jit(solution)/shard_map/ppermute | solution.py:19
  26.6 19.7 %collective-permute-start.11 = (bf16[96,2048]{1,0:T(8,128)(2,1)S(1)}, bf16[96,2048]{1,0:T(8,128)(2,1)}, u32[]{:S(2)}, u32[]{:S(2)}) collective-permute-start(bf16[96,2048]{1,0:T(8,128)(2,1)S(1)} %shard_map.183.refs_6_), channel_id=1, source_target_pairs={{0,16},{4,20},{8,24},{12,28},{16,0},{20,4},{24,8},{28,12},{1,17},{... | collective-permute-start | bytes 1179656 | tf_op jit(solution)/shard_map/ppermute | solution.py:19
  28.2 18.2 %collective-permute-start.10 = (bf16[96,2048]{1,0:T(8,128)(2,1)S(1)}, bf16[96,2048]{1,0:T(8,128)(2,1)}, u32[]{:S(2)}, u32[]{:S(2)}) collective-permute-start(bf16[96,2048]{1,0:T(8,128)(2,1)S(1)} %shard_map.183.refs_6_), channel_id=1, source_target_pairs={{0,24},{4,28},{8,16},{12,20},{16,8},{20,12},{24,0},{28,4},{1,25},{... | collective-permute-start | bytes 1179656 | tf_op jit(solution)/shard_map/ppermute | solution.py:19
  28.6 17.8 %copy-start = (bf16[1,64,768]{2,1,0:T(8,128)(2,1)S(1)}, bf16[1,64,768]{2,1,0:T(8,128)(2,1)}, u32[]{:S(2)}) copy-start(bf16[1,64,768]{2,1,0:T(8,128)(2,1)} %param.13) | copy-start | bytes 294916
  28.6 17.8 %copy-start.8 = (f32[768]{0:T(1024)S(1)}, f32[768]{0:T(1024)}, u32[]{:S(2)}) copy-start(f32[768]{0:T(1024)} %refs_0_.5) | copy-start | bytes 9220
  30.6 29.5 %copy-start.10 = (f32[4,9]{1,0:T(4,128)S(1)}, f32[4,9]{1,0:T(4,128)}, u32[]{:S(2)}) copy-start(f32[4,9]{1,0:T(4,128)} %refs_2_.7) | copy-start | bytes 436
  30.7 29.4 %copy-start.11 = (s32[1,256]{1,0:T(1,128)S(1)}, s32[1,256]{1,0:T(1,128)}, u32[]{:S(2)}) copy-start(s32[1,256]{1,0:T(1,128)} %refs_3_.5) | copy-start | bytes 3076
  30.7 29.4 %copy-start.12 = (s32[1,256]{1,0:T(1,128)S(1)}, s32[1,256]{1,0:T(1,128)}, u32[]{:S(2)}) copy-start(s32[1,256]{1,0:T(1,128)} %refs_4_.1) | copy-start | bytes 3076
  30.7 15.7 %collective-permute-start.7 = (bf16[64,768]{1,0:T(8,128)(2,1)S(1)}, bf16[64,768]{1,0:T(8,128)(2,1)S(1)}, u32[]{:S(2)}, u32[]{:S(2)}) collective-permute-start(bf16[64,768]{1,0:T(8,128)(2,1)S(1)} %get-tuple-element.45), channel_id=1, source_target_pairs={{0,1},{1,0},{2,3},{3,2},{4,5},{5,4},{6,7},{7,6},{8,9},{9,8},{10,11... | collective-permute-start | bytes 294920 | tf_op jit(solution)/shard_map/ppermute | solution.py:19
  32.1 14.3 %collective-permute-start.8 = (bf16[64,768]{1,0:T(8,128)(2,1)S(1)}, bf16[64,768]{1,0:T(8,128)(2,1)S(1)}, u32[]{:S(2)}, u32[]{:S(2)}) collective-permute-start(bf16[64,768]{1,0:T(8,128)(2,1)S(1)} %get-tuple-element.46), channel_id=1, source_target_pairs={{0,2},{1,3},{2,0},{3,1},{4,6},{5,7},{6,4},{7,5},{8,10},{9,11},{10,... | collective-permute-start | bytes 294920 | tf_op jit(solution)/shard_map/ppermute | solution.py:19
  37.1 9.3 %collective-permute-start.9 = (bf16[64,768]{1,0:T(8,128)(2,1)S(1)}, bf16[64,768]{1,0:T(8,128)(2,1)S(1)}, u32[]{:S(2)}, u32[]{:S(2)}) collective-permute-start(bf16[64,768]{1,0:T(8,128)(2,1)S(1)} %get-tuple-element.47), channel_id=1, source_target_pairs={{0,3},{1,2},{2,1},{3,0},{4,7},{5,6},{6,5},{7,4},{8,11},{9,10},{10,... | collective-permute-start | bytes 294920 | tf_op jit(solution)/shard_map/ppermute | solution.py:19
  48.0 12.0 %collective-permute-start.16 = (bf16[384,2048]{1,0:T(8,128)(2,1)S(1)}, bf16[384,2048]{1,0:T(8,128)(2,1)S(1)}, u32[]{:S(2)}, u32[]{:S(2)}) collective-permute-start(bf16[384,2048]{1,0:T(8,128)(2,1)S(1)} %get-tuple-element.55.refs_10_), channel_id=1, source_target_pairs={{0,4},{4,0},{8,12},{12,8},{16,20},{20,16},{24,28},{28,24},{1,5},{5... | collective-permute-start | bytes 4718600 | tf_op jit(solution)/shard_map/ppermute | solution.py:19
  48.1 7.6 %collective-permute-start.15 = (bf16[64,768]{1,0:T(8,128)(2,1)S(1)}, bf16[64,768]{1,0:T(8,128)(2,1)S(1)}, u32[]{:S(2)}, u32[]{:S(2)}) collective-permute-start(bf16[64,768]{1,0:T(8,128)(2,1)S(1)} %get-tuple-element.53.refs_5_), channel_id=1, source_target_pairs={{0,3},{1,2},{2,1},{3,0},{4,7},{5,6},{6,5},{7,4},{8,11},{9,10},{10,... | collective-permute-start | bytes 294920 | tf_op jit(solution)/shard_map/ppermute | solution.py:19
  51.4 8.7 %collective-permute-start.14 = (bf16[64,768]{1,0:T(8,128)(2,1)S(1)}, bf16[64,768]{1,0:T(8,128)(2,1)S(1)}, u32[]{:S(2)}, u32[]{:S(2)}) collective-permute-start(bf16[64,768]{1,0:T(8,128)(2,1)S(1)} %get-tuple-element.53.refs_5_), channel_id=1, source_target_pairs={{0,2},{1,3},{2,0},{3,1},{4,6},{5,7},{6,4},{7,5},{8,10},{9,11},{10,... | collective-permute-start | bytes 294920 | tf_op jit(solution)/shard_map/ppermute | solution.py:19
  51.4 8.7 %collective-permute-start.13 = (bf16[64,768]{1,0:T(8,128)(2,1)S(1)}, bf16[64,768]{1,0:T(8,128)(2,1)S(1)}, u32[]{:S(2)}, u32[]{:S(2)}) collective-permute-start(bf16[64,768]{1,0:T(8,128)(2,1)S(1)} %get-tuple-element.53.refs_5_), channel_id=1, source_target_pairs={{0,1},{1,0},{2,3},{3,2},{4,5},{5,4},{6,7},{7,6},{8,9},{9,8},{10,11... | collective-permute-start | bytes 294920 | tf_op jit(solution)/shard_map/ppermute | solution.py:19
  68.2 11.6 %collective-permute-start.23 = (bf16[384,2048]{1,0:T(8,128)(2,1)S(1)}, bf16[384,2048]{1,0:T(8,128)(2,1)S(1)}, u32[]{:S(2)}, u32[]{:S(2)}) collective-permute-start(bf16[384,2048]{1,0:T(8,128)(2,1)S(1)} %get-tuple-element.64), channel_id=1, source_target_pairs={{0,4},{4,0},{8,12},{12,8},{16,20},{20,16},{24,28},{28,24},{1,5},{5... | collective-permute-start | bytes 4718600 | tf_op jit(solution)/shard_map/ppermute | solution.py:19
  68.3 6.7 %collective-permute-start.17 = (bf16[64,768]{1,0:T(8,128)(2,1)S(1)}, bf16[64,768]{1,0:T(8,128)(2,1)S(1)}, u32[]{:S(2)}, u32[]{:S(2)}) collective-permute-start(bf16[64,768]{1,0:T(8,128)(2,1)S(1)} %get-tuple-element.57), channel_id=1, source_target_pairs={{0,1},{1,0},{2,3},{3,2},{4,5},{5,4},{6,7},{7,6},{8,9},{9,8},{10,11... | collective-permute-start | bytes 294920 | tf_op jit(solution)/shard_map/ppermute | solution.py:19
  69.0 10.8 %collective-permute-start.18 = (bf16[64,768]{1,0:T(8,128)(2,1)S(1)}, bf16[64,768]{1,0:T(8,128)(2,1)S(1)}, u32[]{:S(2)}, u32[]{:S(2)}) collective-permute-start(bf16[64,768]{1,0:T(8,128)(2,1)S(1)} %get-tuple-element.58), channel_id=1, source_target_pairs={{0,2},{1,3},{2,0},{3,1},{4,6},{5,7},{6,4},{7,5},{8,10},{9,11},{10,... | collective-permute-start | bytes 294920 | tf_op jit(solution)/shard_map/ppermute | solution.py:19
  71.4 8.4 %collective-permute-start.19 = (bf16[64,768]{1,0:T(8,128)(2,1)S(1)}, bf16[64,768]{1,0:T(8,128)(2,1)S(1)}, u32[]{:S(2)}, u32[]{:S(2)}) collective-permute-start(bf16[64,768]{1,0:T(8,128)(2,1)S(1)} %get-tuple-element.59), channel_id=1, source_target_pairs={{0,3},{1,2},{2,1},{3,0},{4,7},{5,6},{6,5},{7,4},{8,11},{9,10},{10,... | collective-permute-start | bytes 294920 | tf_op jit(solution)/shard_map/ppermute | solution.py:19
  79.8 2.5 %copy-start.1 = (bf16[1,64,768]{2,1,0:T(8,128)(2,1)S(1)}, bf16[1,64,768]{2,1,0:T(8,128)(2,1)}, u32[]{:S(2)}) copy-start(bf16[1,64,768]{2,1,0:T(8,128)(2,1)} %param.25) | copy-start | bytes 294916
  80.2 13.0 %collective-permute-start.24 = (bf16[96,2048]{1,0:T(8,128)(2,1)S(1)}, bf16[96,2048]{1,0:T(8,128)(2,1)S(1)}, u32[]{:S(2)}, u32[]{:S(2)}) collective-permute-start(bf16[96,2048]{1,0:T(8,128)(2,1)S(1)} %get-tuple-element.65), channel_id=1, source_target_pairs={{0,8},{4,12},{8,0},{12,4},{16,24},{20,28},{24,16},{28,20},{1,9},{5... | collective-permute-start | bytes 1179656 | tf_op jit(solution)/shard_map/ppermute | solution.py:19
  81.5 11.8 %collective-permute-start.25 = (bf16[96,2048]{1,0:T(8,128)(2,1)S(1)}, bf16[96,2048]{1,0:T(8,128)(2,1)S(1)}, u32[]{:S(2)}, u32[]{:S(2)}) collective-permute-start(bf16[96,2048]{1,0:T(8,128)(2,1)S(1)} %get-tuple-element.66), channel_id=1, source_target_pairs={{0,16},{4,20},{8,24},{12,28},{16,0},{20,4},{24,8},{28,12},{1,17},{... | collective-permute-start | bytes 1179656 | tf_op jit(solution)/shard_map/ppermute | solution.py:19
  82.6 7.5 %collective-permute-start.22 = (bf16[64,768]{1,0:T(8,128)(2,1)S(1)}, bf16[64,768]{1,0:T(8,128)(2,1)S(1)}, u32[]{:S(2)}, u32[]{:S(2)}) collective-permute-start(bf16[64,768]{1,0:T(8,128)(2,1)S(1)} %shard_map.186.refs_5_), channel_id=1, source_target_pairs={{0,3},{1,2},{2,1},{3,0},{4,7},{5,6},{6,5},{7,4},{8,11},{9,10},{10,... | collective-permute-start | bytes 294920 | tf_op jit(solution)/shard_map/ppermute | solution.py:19
  84.5 8.7 %collective-permute-start.21 = (bf16[64,768]{1,0:T(8,128)(2,1)S(1)}, bf16[64,768]{1,0:T(8,128)(2,1)S(1)}, u32[]{:S(2)}, u32[]{:S(2)}) collective-permute-start(bf16[64,768]{1,0:T(8,128)(2,1)S(1)} %shard_map.186.refs_5_), channel_id=1, source_target_pairs={{0,2},{1,3},{2,0},{3,1},{4,6},{5,7},{6,4},{7,5},{8,10},{9,11},{10,... | collective-permute-start | bytes 294920 | tf_op jit(solution)/shard_map/ppermute | solution.py:19
  86.1 7.2 %collective-permute-start.20 = (bf16[64,768]{1,0:T(8,128)(2,1)S(1)}, bf16[64,768]{1,0:T(8,128)(2,1)S(1)}, u32[]{:S(2)}, u32[]{:S(2)}) collective-permute-start(bf16[64,768]{1,0:T(8,128)(2,1)S(1)} %shard_map.186.refs_5_), channel_id=1, source_target_pairs={{0,1},{1,0},{2,3},{3,2},{4,5},{5,4},{6,7},{7,6},{8,9},{9,8},{10,11... | collective-permute-start | bytes 294920 | tf_op jit(solution)/shard_map/ppermute | solution.py:19
  94.8 2.9 %collective-permute-start.26 = (bf16[384,1536]{1,0:T(8,128)(2,1)S(1)}, bf16[384,1536]{1,0:T(8,128)(2,1)S(1)}, u32[]{:S(2)}, u32[]{:S(2)}) collective-permute-start(bf16[384,1536]{1,0:T(8,128)(2,1)S(1)} %get-tuple-element.68), channel_id=1, source_target_pairs={{0,4},{4,0},{8,12},{12,8},{16,20},{20,16},{24,28},{28,24},{1,5},{5... | collective-permute-start | bytes 3538952 | tf_op jit(solution)/shard_map/ppermute | solution.py:19
  94.9 12.9 %collective-permute-start.30 = (bf16[96,2048]{1,0:T(8,128)(2,1)S(1)}, bf16[96,2048]{1,0:T(8,128)(2,1)S(1)}, u32[]{:S(2)}, u32[]{:S(2)}) collective-permute-start(bf16[96,2048]{1,0:T(8,128)(2,1)S(1)} %get-tuple-element.76), channel_id=1, source_target_pairs={{0,24},{4,28},{8,16},{12,20},{16,8},{20,12},{24,0},{28,4},{1,25},{... | collective-permute-start | bytes 1179656 | tf_op jit(solution)/shard_map/ppermute | solution.py:19
  98.7 15.2 %collective-permute-start.27 = (bf16[96,1536]{1,0:T(8,128)(2,1)S(1)}, bf16[96,1536]{1,0:T(8,128)(2,1)S(1)}, u32[]{:S(2)}, u32[]{:S(2)}) collective-permute-start(bf16[96,1536]{1,0:T(8,128)(2,1)S(1)} %get-tuple-element.72), channel_id=1, source_target_pairs={{0,8},{4,12},{8,0},{12,4},{16,24},{20,28},{24,16},{28,20},{1,9},{5... | collective-permute-start | bytes 884744 | tf_op jit(solution)/shard_map/ppermute | solution.py:19
  100.2 13.9 %collective-permute-start.28 = (bf16[96,1536]{1,0:T(8,128)(2,1)S(1)}, bf16[96,1536]{1,0:T(8,128)(2,1)S(1)}, u32[]{:S(2)}, u32[]{:S(2)}) collective-permute-start(bf16[96,1536]{1,0:T(8,128)(2,1)S(1)} %get-tuple-element.73), channel_id=1, source_target_pairs={{0,16},{4,20},{8,24},{12,28},{16,0},{20,4},{24,8},{28,12},{1,17},{... | collective-permute-start | bytes 884744 | tf_op jit(solution)/shard_map/ppermute | solution.py:19
  100.7 19.3 %collective-permute-start.29 = (bf16[96,1536]{1,0:T(8,128)(2,1)S(1)}, bf16[96,1536]{1,0:T(8,128)(2,1)S(1)}, u32[]{:S(2)}, u32[]{:S(2)}) collective-permute-start(bf16[96,1536]{1,0:T(8,128)(2,1)S(1)} %get-tuple-element.74), channel_id=1, source_target_pairs={{0,24},{4,28},{8,16},{12,20},{16,8},{20,12},{24,0},{28,4},{1,25},{... | collective-permute-start | bytes 884744 | tf_op jit(solution)/shard_map/ppermute | solution.py:19
  108.9 14.9 %all-to-all-start = ((bf16[4,64,768]{2,1,0:T(8,128)(2,1)}), bf16[4,64,768]{2,1,0:T(8,128)(2,1)S(1)}, u32[]{:S(2)}, u32[]{:S(2)}) async-start(bf16[4,64,768]{2,1,0:T(8,128)(2,1)} %bitcast.4), calls=%async_computation | async-start | bytes 786432 | tf_op jit(solution)/shard_map/all_to_all | solution.py:479

commit v5 on v4

--- a/solution.py
+++ b/solution.py
@@ -151,17 +151,21 @@
     wait_copies(copies)
 
 
-def attention_kernel(parts, ids, window, *refs):
-    place_ref, me_ref, bias = refs[:3]
-    segments, spans = refs[3:5]
-    normed_parts = refs[5 : 5 + parts]
-    scaled = refs[5 + parts]
-    at = 6 + parts + (2 if len(ids) > 1 else 1)
-    weights_in, rest = refs[6 + parts : at], refs[at:]
+def collect_kernel(ids, me_ref, near, far, out, sems):
+    wait_copies(collect(me_ref, [near, far], ids, 0, out, sems))
+
+
+def attention_kernel(parts, window, *refs):
+    place_ref, bias = refs[:2]
+    segments, spans = refs[2:4]
+    normed_parts = refs[4 : 4 + parts]
+    scaled, weights = refs[4 + parts : 6 + parts]
+    rest = refs[6 + parts :]
     normed, context, slopes = rest[:3]
-    attn_out, outs = rest[3], rest[4 : 4 + parts]
-    weights, qkv, grad_context, key_total, value_total, total = rest[4 + parts : 10 + parts]
-    copies = collect(me_ref, weights_in, ids, 0, weights, rest[-1])
+    outs = rest[3 : 3 + parts]
+    halves = 1 if parts == 1 else 2
+    attn_outs = rest[3 + parts : 3 + parts + halves]
+    qkv, grad_context, key_total, value_total, total = rest[3 + parts + halves :]
     heads = bias.shape[0]
     frames = normed.shape[0]
     own = normed_parts[0].shape[0]
@@ -171,7 +175,6 @@
     firsts = places(place_ref, parts, own)
     for first, piece in zip(firsts, normed_parts):
         normed[pl.ds(first, own), :] = piece[...]
-    wait_copies(copies)
     qkv[...] = dot(normed[...], weights[:, : 3 * inner], 1, 0).astype(BF)
     grad_context[...] = dot(scaled[...], weights[:, 3 * inner :], 1, 0).astype(BF)
     seg_k, span_k = segments[...], spans[...]
@@ -218,7 +221,12 @@
     for first, out in zip(firsts, outs):
         out[...] = total[pl.ds(first, own), :].astype(BF)
     total[...] = dot(context[...], weights[:, 3 * inner :], 1, 1)
-    attn_out[...] = total[...].astype(BF)
+    if parts == 1:
+        attn_outs[0][...] = total[...].astype(BF)
+        return
+    for index, out in enumerate(attn_outs):
+        for at, first in enumerate((firsts[index], firsts[index + 2])):
+            out[at * own : (at + 1) * own, :] = total[pl.ds(first, own), :].astype(BF)
 
 
 def attention_grads_kernel(*refs):
@@ -277,6 +285,12 @@
         out[...] = (keep[mine, :].astype(F32) + came[mine, :].astype(F32)).astype(BF)
     for one, out in zip(refs[:passed], refs[passed + 4 :]):
         out[...] = one[...]
+
+
+def half_sum_kernel(keep, came, mine, other):
+    own = mine.shape[0]
+    mine[...] = keep[:own, :].astype(F32) + came[:own, :].astype(F32)
+    other[...] = (keep[own:, :].astype(F32) + came[own:, :].astype(F32)).astype(BF)
 
 
 def row_pairs(pieces, out):
@@ -353,13 +367,15 @@
     def gather_frames(values, relay=False):
         if not direct_frames:
             return [lax.all_gather(values, "ctx", axis=0, tiled=True)]
-        parts = [values] + [exchange(values, "ctx", mask) for mask in (1, 2)]
-        return parts + [exchange(*((parts[2], "ctx", 1) if relay else (values, "ctx", 3)))]
+        if relay:
+            second, first = exchange(values, "ctx", 2), exchange(values, "ctx", 1)
+            return [values, first, second, exchange(second, "ctx", 1)]
+        return [values] + [exchange(values, "ctx", mask) for mask in (3, 2, 1)][::-1]
 
     def scatter_frames(pieces):
         if not direct_frames:
             return [lax.psum_scatter(pieces[0], "ctx", scatter_dimension=0, tiled=True)]
-        return [pieces[0]] + [exchange(pieces[mask], "ctx", mask) for mask in (1, 2, 3)]
+        return [pieces[0]] + [exchange(pieces[mask], "ctx", mask) for mask in (3, 2, 1)][::-1]
 
     def scatter_rows(pieces, passed=(), after=()):
         if not direct_rows:
@@ -422,19 +438,25 @@
     )
     normed_parts = gather_frames(normed_own)
     if direct_rows:
-        attn_weights = [near[0], exchange(near[0], "dp", 1)]
+        attn_weights = call(
+            functools.partial(collect_kernel, ids),
+            [shape((model, 4 * inner), BF)],
+            [me, near[0], exchange(near[0], "dp", 1)],
+            smem=1,
+            far=2,
+        )
     made = call(
-        functools.partial(attention_kernel, parts, ids, window),
+        functools.partial(attention_kernel, parts, window),
         [
             shape((frames, model), BF),
             shape((frames, inner), BF),
             shape((frames, 3 * inner), BF),
-            shape((frames, model), BF),
         ]
-        + [shape((part_rows, model), BF)] * parts,
-        [place, me, offset_bias, segment_ids, span_ids] + normed_parts + [scaled_cot] + attn_weights,
+        + [shape((part_rows, model), BF)] * parts
+        + [shape((frames // 2, model), BF)] * 2 * (parts > 1)
+        + [shape((frames, model), BF)] * (parts == 1),
+        [place, offset_bias, segment_ids, span_ids, *normed_parts, scaled_cot, *attn_weights],
         [
-            pltpu.VMEM((model, 4 * inner), BF),
             pltpu.VMEM((frames, 3 * inner), BF),
             pltpu.VMEM((frames, inner), BF),
             pltpu.VMEM((frames, inner // heads), F32),
@@ -442,12 +464,11 @@
             pltpu.VMEM((frames, model), F32),
         ],
         flops=16 * frames * model * inner + 12 * frames * frames * inner,
-        smem=3,
-        far=2 if direct_rows else 0,
+        smem=2,
     )
     attn_normed, context, slopes = made[:3]
-    attn_partial = made[3]
-    upstream = scatter_frames(list(made[4:]))
+    attn_partials = made[3 + parts :]
+    upstream = scatter_frames(list(made[3 : 3 + parts]))
     half = [shape((model // 2, 4 * inner), BF)] * 2
     attn_grads = call(
         attention_grads_kernel,
@@ -474,12 +495,17 @@
         smem=1,
         after=attn_terms[1:3],
     )
-    ffn_terms, passed = scatter_rows(ffn_grads, [attn_partial])
+    ffn_terms, passed = scatter_rows(ffn_grads, list(attn_partials[1:]))
     if direct_frames:
-        attn_sum = lax.all_to_all(passed[0], "ctx", 0, 0, tiled=True)
-        attn_sum = add_terms([attn_sum[at * own : (at + 1) * own] for at in range(ctx)])
+        keep, send = attn_partials[0], passed[0]
+        attn_own, attn_far = call(
+            half_sum_kernel,
+            [shape((own, model), F32), shape((own, model), BF)],
+            [keep, exchange(send, "ctx", 1)],
+        )
+        attn_sum = attn_own + exchange(attn_far, "ctx", 2).astype(F32)
     else:
-        attn_sum = lax.psum_scatter(passed[0], "ctx", scatter_dimension=0, tiled=True)
+        attn_sum = lax.psum_scatter(attn_partials[0], "ctx", scatter_dimension=0, tiled=True)
     block_out = (mid_own + attn_sum).astype(BF)[None]
     attn_total, ffn_total = add_terms(attn_terms), add_terms(ffn_terms)
     return (

time: 125 us -> 122 us (0.976)
  waiting for transfers between devices: 57.1 us -> 54.5 us
    ppermute x31 -> x33, starting transfers between devices: 41.3 us -> 45.8 us  [exchange(): lax.ppermute(values, axis, [(one, one ^ mask) for one in range(size)])]
    all_to_all x1 -> x0, starting transfers between devices: 3.81 us -> none  [per_device(): attn_sum = lax.all_to_all(passed[0], 'ctx', 0, 0, tiled=True)]
    all_to_all x1 -> x0, waiting for transfers between devices: 2.79 us -> none  [per_device(): attn_sum = lax.all_to_all(passed[0], 'ctx', 0, 0, tiled=True)]
    pallas_call x11 -> x13, Pallas kernels: 17.5 us -> 16.9 us  [call(): pl.pallas_call(lambda *refs: body(*refs[:count], *refs[count + len(after)...]
    ppermute x31 -> x33, waiting for transfers between devices: 54.3 us -> 54.5 us  [exchange(): lax.ppermute(values, axis, [(one, one ^ mask) for one in range(size)])]
  transfers between devices with their start and end apart: 32 -> 33, of which waited for: 18 -> 18; matrix products, arithmetic and copies ran while one was open for 2% -> 2% of each run, Pallas kernels for 3% -> 4%
where the time goes in v5:
time: 122 us
  waiting for transfers between devices  54.5 us (45%)
  starting transfers between devices  45.8 us (38%)
  Pallas kernels  16.9 us (14%)
  local copies, waits for them, and re-layouts  2.76 us (2%)
    ppermute x33, waiting for transfers between devices, exchange(): lax.ppermute(values, axis, [(one, one ^ mask) for one in range(size)])  54.5 us
    ppermute x33, starting transfers between devices, exchange(): lax.ppermute(values, axis, [(one, one ^ mask) for one in range(size)])  45.8 us
    pallas_call x13, Pallas kernels, call(): pl.pallas_call(lambda *refs: body(*refs[:count], *refs[count + len(after)...  16.9 us
  transfers between devices with their start and end apart: 33, of which 18 were waited for; matrix products, arithmetic and copies ran while one was open for 2% of the time, Pallas kernels for 4%

profile of v5, /device:TPU:0, one launch (start us, length us, event | category | flops | bytes accessed | tf_op | source)
XLA Modules:
  0.0 121.9 jit_solution(16185017812822229499)
XLA Ops:
  0.7 2.1 %shard_map.180 = (bf16[64,1536]{1,0:T(8,128)(2,1)}, bf16[96,1536]{1,0:T(8,128)(2,1)}) custom-call(bf16[64,768]{1,0:T(8,128)(2,1)} %bitcast.6, bf16[64,768]{1,0:T(8,128)(2,1)} %bitcast.8, bf16[96,768]{1,0:T(8,128)(2,1)} %refs_2_.4, bf16[96,768]{1,0:T(8,128)(2,1)} %refs_3_.3), custom_call_target="tpu_custom_call" | custom-call | bytes 983040 | tf_op jit(solution)/shard_map/pallas_call | solution.py:31
  2.7 4.1 %collective-permute-start.1 = (bf16[64,1536]{1,0:T(8,128)(2,1)}, bf16[64,1536]{1,0:T(8,128)(2,1)S(1)}, u32[]{:S(2)}, u32[]{:S(2)}) collective-permute-start(bf16[64,1536]{1,0:T(8,128)(2,1)} %get-tuple-element.45.refs_3_), channel_id=1, source_target_pairs={{0,2},{1,3},{2,0},{3,1},{4,6},{5,7},{6,4},{7,5},{8,10},{9,11},{10,... | collective-permute-start | bytes 589832 | tf_op jit(solution)/shard_map/ppermute | solution.py:19
  6.8 2.4 %collective-permute-start.3 = (bf16[96,1536]{1,0:T(8,128)(2,1)}, bf16[96,1536]{1,0:T(8,128)(2,1)S(1)}, u32[]{:S(2)}, u32[]{:S(2)}) collective-permute-start(bf16[96,1536]{1,0:T(8,128)(2,1)} %get-tuple-element.46.refs_0_), channel_id=1, source_target_pairs={{0,24},{4,28},{8,16},{12,20},{16,8},{20,12},{24,0},{28,4},{1,25},{... | collective-permute-start | bytes 884744 | tf_op jit(solution)/shard_map/ppermute | solution.py:19
  10.3 1.6 %collective-permute-start = (bf16[64,1536]{1,0:T(8,128)(2,1)}, bf16[64,1536]{1,0:T(8,128)(2,1)S(1)}, u32[]{:S(2)}, u32[]{:S(2)}) collective-permute-start(bf16[64,1536]{1,0:T(8,128)(2,1)} %get-tuple-element.45.refs_3_), channel_id=1, source_target_pairs={{0,1},{1,0},{2,3},{3,2},{4,5},{5,4},{6,7},{7,6},{8,9},{9,8},{10,11... | collective-permute-start | bytes 589832 | tf_op jit(solution)/shard_map/ppermute | solution.py:19
  11.9 4.4 %collective-permute-done.1.refs_5_ = bf16[64,1536]{1,0:T(8,128)(2,1)S(1)} collective-permute-done((bf16[64,1536]{1,0:T(8,128)(2,1)}, bf16[64,1536]{1,0:T(8,128)(2,1)S(1)}, u32[]{:S(2)}, u32[]{:S(2)}) %collective-permute-start.1) | collective-permute-done | bytes 196640 | tf_op jit(solution)/shard_map/ppermute | solution.py:19
  16.3 0.8 collective-permute-start.2
  17.0 3.0 %collective-permute-done.refs_4_ = bf16[64,1536]{1,0:T(8,128)(2,1)S(1)} collective-permute-done((bf16[64,1536]{1,0:T(8,128)(2,1)}, bf16[64,1536]{1,0:T(8,128)(2,1)S(1)}, u32[]{:S(2)}, u32[]{:S(2)}) %collective-permute-start) | collective-permute-done | bytes 196640 | tf_op jit(solution)/shard_map/ppermute | solution.py:19
  20.1 2.7 %collective-permute-done.4.refs_2_ = bf16[96,1536]{1,0:T(8,128)(2,1)S(1)} collective-permute-done((bf16[96,1536]{1,0:T(8,128)(2,1)}, bf16[96,1536]{1,0:T(8,128)(2,1)S(1)}, u32[]{:S(2)}, u32[]{:S(2)}) %collective-permute-start.4) | collective-permute-done | bytes 294944 | tf_op jit(solution)/shard_map/ppermute | solution.py:19
  23.3 1.0 copy-done.2
  25.0 2.6 %collective-permute-start.10 = (bf16[96,2048]{1,0:T(8,128)(2,1)S(1)}, bf16[96,2048]{1,0:T(8,128)(2,1)}, u32[]{:S(2)}, u32[]{:S(2)}) collective-permute-start(bf16[96,2048]{1,0:T(8,128)(2,1)S(1)} %shard_map.183.refs_6_), channel_id=1, source_target_pairs={{0,24},{4,28},{8,16},{12,20},{16,8},{20,12},{24,0},{28,4},{1,25},{... | collective-permute-start | bytes 1179656 | tf_op jit(solution)/shard_map/ppermute | solution.py:19
  28.6 2.0 %shard_map.182 = (bf16[256,768]{1,0:T(8,128)(2,1)S(1)}, f32[256,768]{1,0:T(8,128)S(1)}, bf16[256,768]{1,0:T(8,128)(2,1)S(1)}, bf16[768,768]{1,0:T(8,128)(2,1)S(1...) custom-call(s32[1]{0:T(128)} %bitcast.1.refs_0_, ...), custom_call_target="tpu_custom_call" | custom-call | flops 603979776 | bytes 6687752 | tf_op jit(solution)/shard_map/pallas_call | solution.py:31
  30.6 1.2 collective-permute-start.7
  31.8 2.7 %collective-permute-start.8 = (bf16[64,768]{1,0:T(8,128)(2,1)S(1)}, bf16[64,768]{1,0:T(8,128)(2,1)S(1)}, u32[]{:S(2)}, u32[]{:S(2)}) collective-permute-start(bf16[64,768]{1,0:T(8,128)(2,1)S(1)} %get-tuple-element.49), channel_id=1, source_target_pairs={{0,2},{1,3},{2,0},{3,1},{4,6},{5,7},{6,4},{7,5},{8,10},{9,11},{10,... | collective-permute-start | bytes 294920 | tf_op jit(solution)/shard_map/ppermute | solution.py:19
  34.5 3.5 %collective-permute-done.10.refs_7_ = bf16[96,2048]{1,0:T(8,128)(2,1)} collective-permute-done((bf16[96,2048]{1,0:T(8,128)(2,1)S(1)}, bf16[96,2048]{1,0:T(8,128)(2,1)}, u32[]{:S(2)}, u32[]{:S(2)}) %collective-permute-start.10) | collective-permute-done | bytes 393248 | tf_op jit(solution)/shard_map/ppermute | solution.py:19
  38.1 3.2 %collective-permute-start.9 = (bf16[64,768]{1,0:T(8,128)(2,1)S(1)}, bf16[64,768]{1,0:T(8,128)(2,1)S(1)}, u32[]{:S(2)}, u32[]{:S(2)}) collective-permute-start(bf16[64,768]{1,0:T(8,128)(2,1)S(1)} %get-tuple-element.50), channel_id=1, source_target_pairs={{0,3},{1,2},{2,1},{3,0},{4,7},{5,6},{6,5},{7,4},{8,11},{9,10},{10,... | collective-permute-start | bytes 294920 | tf_op jit(solution)/shard_map/ppermute | solution.py:19
  41.3 4.7 %collective-permute-done.11.refs_8_ = bf16[96,2048]{1,0:T(8,128)(2,1)} collective-permute-done((bf16[96,2048]{1,0:T(8,128)(2,1)S(1)}, bf16[96,2048]{1,0:T(8,128)(2,1)}, u32[]{:S(2)}, u32[]{:S(2)}) %collective-permute-start.11) | collective-permute-done | bytes 393248 | tf_op jit(solution)/shard_map/ppermute | solution.py:19
  46.2 1.6 %shard_map.184 = (f32[64,768]{1,0:T(8,128)S(1)}, bf16[64,768]{1,0:T(8,128)(2,1)S(1)}, bf16[384,2048]{1,0:T(8,128)(2,1)S(1)}) custom-call(f32[768]{0:T(1024)S(1)} %copy-done.8, bf16[64,768]{1,0:T(8,128)(2,1)S(1)} %bitcast.7, bf16[64,768]{1,0:T(8,128)(2,1)S(1)} %get-tuple-element.47.refs_2_, bf16[64,768]{1,0:T(8,128)(2,1)S(1)} %collective-permute-done.7.refs_3_, ...), custom_call_target="tpu_custom_call" | custom-call | bytes 3935232 | tf_op jit(solution)/shard_map/pallas_call | solution.py:31
  47.9 1.0 collective-permute-start.13
  49.0 2.8 %collective-permute-start.14 = (bf16[64,768]{1,0:T(8,128)(2,1)S(1)}, bf16[64,768]{1,0:T(8,128)(2,1)S(1)}, u32[]{:S(2)}, u32[]{:S(2)}) collective-permute-start(bf16[64,768]{1,0:T(8,128)(2,1)S(1)} %get-tuple-element.52.refs_4_), channel_id=1, source_target_pairs={{0,2},{1,3},{2,0},{3,1},{4,6},{5,7},{6,4},{7,5},{8,10},{9,11},{10,... | collective-permute-start | bytes 294920 | tf_op jit(solution)/shard_map/ppermute | solution.py:19
  52.4 1.6 %shard_map.185.refs_9_ = bf16[768,2048]{1,0:T(8,128)(2,1)S(1)} custom-call(s32[1]{0:T(128)} %bitcast.2.refs_1_.refs_0_, bf16[384,2048]{1,0:T(8,128)(2,1)S(1)} %get-tuple-element.54.refs_1_, bf16[384,2048]{1,0:T(8,128)(2,1)S(1)} %collective-permute-done.16.refs_2_), custom_call_target="tpu_custom_call" | custom-call | bytes 6291460 | tf_op jit(solution)/shard_map/pallas_call | solution.py:31
  54.7 5.1 %collective-permute-done.14.refs_6_ = bf16[64,768]{1,0:T(8,128)(2,1)S(1)} collective-permute-done((bf16[64,768]{1,0:T(8,128)(2,1)S(1)}, bf16[64,768]{1,0:T(8,128)(2,1)S(1)}, u32[]{:S(2)}, u32[]{:S(2)}) %collective-permute-start.14) | collective-permute-done | bytes 98336 | tf_op jit(solution)/shard_map/ppermute | solution.py:19
  59.8 5.0 %shard_map.186 = (bf16[256,768]{1,0:T(8,128)(2,1)S(1)}, bf16[256,512]{1,0:T(8,128)(2,1)S(1)}, bf16[256,1536]{1,0:T(8,128)(2,1)S(1)}, bf16[64,768]{1,0:T(8,128)(2...) custom-call(s32[1]{0:T(128)} %bitcast.1.refs_0_, ...), custom_call_target="tpu_custom_call" | custom-call | flops 2013265920 | bytes 6162580 | tf_op jit(solution)/shard_map/pallas_call | solution.py:31
  64.7 1.5 %shard_map.188 = (bf16[384,2048]{1,0:T(8,128)(2,1)S(1)}, bf16[384,2048]{1,0:T(8,128)(2,1)S(1)}) custom-call(s32[1]{0:T(128)} %bitcast.2.refs_1_.refs_0_, bf16[256,768]{1,0:T(8,128)(2,1)S(1)} %get-tuple-element.64.refs_1_, bf16[256,768]{1,0:T(8,128)(2,1)S(1)} %get-tuple-element.53.refs_8_.refs_2_, bf16[256,512]{1,0:T(8,128)(2,1)S(1)} %get-tuple-element.65.refs_3_, ...), custom_call_target="tpu_custom_call" | custom-call | flops 805306368 | bytes 4980740 | tf_op jit(solution)/shard_map/pallas_call | solution.py:31
  66.3 2.1 %collective-permute-start.17 = (bf16[64,768]{1,0:T(8,128)(2,1)S(1)}, bf16[64,768]{1,0:T(8,128)(2,1)S(1)}, u32[]{:S(2)}, u32[]{:S(2)}) collective-permute-start(bf16[64,768]{1,0:T(8,128)(2,1)S(1)} %get-tuple-element.61), channel_id=1, source_target_pairs={{0,1},{1,0},{2,3},{3,2},{4,5},{5,4},{6,7},{7,6},{8,9},{9,8},{10,11... | collective-permute-start | bytes 294920 | tf_op jit(solution)/shard_map/ppermute | solution.py:19
  68.4 1.1 collective-permute-start.18
  69.5 1.4 %collective-permute-start.19 = (bf16[64,768]{1,0:T(8,128)(2,1)S(1)}, bf16[64,768]{1,0:T(8,128)(2,1)S(1)}, u32[]{:S(2)}, u32[]{:S(2)}) collective-permute-start(bf16[64,768]{1,0:T(8,128)(2,1)S(1)} %get-tuple-element.63), channel_id=1, source_target_pairs={{0,3},{1,2},{2,1},{3,0},{4,7},{5,6},{6,5},{7,4},{8,11},{9,10},{10,... | collective-permute-start | bytes 294920 | tf_op jit(solution)/shard_map/ppermute | solution.py:19
  70.8 0.9 collective-permute-done.17.refs_4_.refs_2_
  71.8 7.4 %collective-permute-done.18.refs_5_.refs_3_ = bf16[64,768]{1,0:T(8,128)(2,1)S(1)} collective-permute-done((bf16[64,768]{1,0:T(8,128)(2,1)S(1)}, bf16[64,768]{1,0:T(8,128)(2,1)S(1)}, u32[]{:S(2)}, u32[]{:S(2)}) %collective-permute-start.18) | collective-permute-done | bytes 98336 | tf_op jit(solution)/shard_map/ppermute | solution.py:19
  79.5 1.6 %collective-permute-start.24 = (bf16[96,2048]{1,0:T(8,128)(2,1)S(1)}, bf16[96,2048]{1,0:T(8,128)(2,1)S(1)}, u32[]{:S(2)}, u32[]{:S(2)}) collective-permute-start(bf16[96,2048]{1,0:T(8,128)(2,1)S(1)} %get-tuple-element.69), channel_id=1, source_target_pairs={{0,8},{4,12},{8,0},{12,4},{16,24},{20,28},{24,16},{28,20},{1,9},{5... | collective-permute-start | bytes 1179656 | tf_op jit(solution)/shard_map/ppermute | solution.py:19
  81.1 0.7 collective-permute-start.25
  82.1 1.9 %collective-permute-start.20 = (bf16[64,768]{1,0:T(8,128)(2,1)S(1)}, bf16[64,768]{1,0:T(8,128)(2,1)S(1)}, u32[]{:S(2)}, u32[]{:S(2)}) collective-permute-start(bf16[64,768]{1,0:T(8,128)(2,1)S(1)} %shard_map.187.refs_5_), channel_id=1, source_target_pairs={{0,1},{1,0},{2,3},{3,2},{4,5},{5,4},{6,7},{7,6},{8,9},{9,8},{10,11... | collective-permute-start | bytes 294920 | tf_op jit(solution)/shard_map/ppermute | solution.py:19
  84.1 1.0 collective-permute-start.21
  85.1 1.5 %collective-permute-start.22 = (bf16[64,768]{1,0:T(8,128)(2,1)S(1)}, bf16[64,768]{1,0:T(8,128)(2,1)S(1)}, u32[]{:S(2)}, u32[]{:S(2)}) collective-permute-start(bf16[64,768]{1,0:T(8,128)(2,1)S(1)} %shard_map.187.refs_5_), channel_id=1, source_target_pairs={{0,3},{1,2},{2,1},{3,0},{4,7},{5,6},{6,5},{7,4},{8,11},{9,10},{10,... | collective-permute-start | bytes 294920 | tf_op jit(solution)/shard_map/ppermute | solution.py:19
  86.6 1.3 %collective-permute-done.20.refs_6_ = bf16[64,768]{1,0:T(8,128)(2,1)S(1)} collective-permute-done((bf16[64,768]{1,0:T(8,128)(2,1)S(1)}, bf16[64,768]{1,0:T(8,128)(2,1)S(1)}, u32[]{:S(2)}, u32[]{:S(2)}) %collective-permute-start.20) | collective-permute-done | bytes 98336 | tf_op jit(solution)/shard_map/ppermute | solution.py:19
  87.9 5.6 %collective-permute-done.21.refs_7_ = bf16[64,768]{1,0:T(8,128)(2,1)S(1)} collective-permute-done((bf16[64,768]{1,0:T(8,128)(2,1)S(1)}, bf16[64,768]{1,0:T(8,128)(2,1)S(1)}, u32[]{:S(2)}, u32[]{:S(2)}) %collective-permute-start.21) | collective-permute-done | bytes 98336 | tf_op jit(solution)/shard_map/ppermute | solution.py:19
  93.5 1.5 %shard_map.190 = (bf16[384,1536]{1,0:T(8,128)(2,1)S(1)}, bf16[384,1536]{1,0:T(8,128)(2,1)S(1)}) custom-call(s32[1]{0:T(128)} %bitcast.2.refs_1_.refs_0_, bf16[256,768]{1,0:T(8,128)(2,1)S(1)} %get-tuple-element.56.refs_1_, f32[256,768]{1,0:T(8,128)S(1)} %get-tuple-element.57.refs_2_, bf16[256,768]{1,0:T(8,128)(2,1)S(1)} %get-tuple-element.58.refs_3_, ...), custom_call_target="tpu_custom_call" | custom-call | flops 905969664 | bytes 5505028 | tf_op jit(solution)/shard_map/pallas_call | solution.py:31
  95.1 1.3 %collective-permute-start.32 = (bf16[96,2048]{1,0:T(8,128)(2,1)S(1)}, bf16[96,2048]{1,0:T(8,128)(2,1)S(1)}, u32[]{:S(2)}, u32[]{:S(2)}) collective-permute-start(bf16[96,2048]{1,0:T(8,128)(2,1)S(1)} %get-tuple-element.82), channel_id=1, source_target_pairs={{0,24},{4,28},{8,16},{12,20},{16,8},{20,12},{24,0},{28,4},{1,25},{... | collective-permute-start | bytes 1179656 | tf_op jit(solution)/shard_map/ppermute | solution.py:19
  96.4 1.5 %collective-permute-done.26.refs_1_ = bf16[384,1536]{1,0:T(8,128)(2,1)S(1)} collective-permute-done((bf16[384,1536]{1,0:T(8,128)(2,1)S(1)}, bf16[384,1536]{1,0:T(8,128)(2,1)S(1)}, u32[]{:S(2)}, u32[]{:S(2)}) %collective-permute-start.26) | collective-permute-done | bytes 1179680 | tf_op jit(solution)/shard_map/ppermute | solution.py:19
  98.2 1.3 %collective-permute-start.29 = (bf16[96,1536]{1,0:T(8,128)(2,1)S(1)}, bf16[96,1536]{1,0:T(8,128)(2,1)S(1)}, u32[]{:S(2)}, u32[]{:S(2)}) collective-permute-start(bf16[96,1536]{1,0:T(8,128)(2,1)S(1)} %get-tuple-element.78), channel_id=1, source_target_pairs={{0,8},{4,12},{8,0},{12,4},{16,24},{20,28},{24,16},{28,20},{1,9},{5... | collective-permute-start | bytes 884744 | tf_op jit(solution)/shard_map/ppermute | solution.py:19
  100.1 1.7 %collective-permute-start.31 = (bf16[96,1536]{1,0:T(8,128)(2,1)S(1)}, bf16[96,1536]{1,0:T(8,128)(2,1)S(1)}, u32[]{:S(2)}, u32[]{:S(2)}) collective-permute-start(bf16[96,1536]{1,0:T(8,128)(2,1)S(1)} %get-tuple-element.80), channel_id=1, source_target_pairs={{0,24},{4,28},{8,16},{12,20},{16,8},{20,12},{24,0},{28,4},{1,25},{... | collective-permute-start | bytes 884744 | tf_op jit(solution)/shard_map/ppermute | solution.py:19
  101.8 6.3 %collective-permute-done.32 = bf16[96,2048]{1,0:T(8,128)(2,1)S(1)} collective-permute-done((bf16[96,2048]{1,0:T(8,128)(2,1)S(1)}, bf16[96,2048]{1,0:T(8,128)(2,1)S(1)}, u32[]{:S(2)}, u32[]{:S(2)}) %collective-permute-start.32) | collective-permute-done | bytes 393248 | tf_op jit(solution)/shard_map/ppermute | solution.py:19
  108.2 1.7 %collective-permute-start.27 = (bf16[128,768]{1,0:T(8,128)(2,1)S(1)}, bf16[128,768]{1,0:T(8,128)(2,1)S(1)}, u32[]{:S(2)}, u32[]{:S(2)}) collective-permute-start(bf16[128,768]{1,0:T(8,128)(2,1)S(1)} %get-tuple-element.74), channel_id=1, source_target_pairs={{0,1},{1,0},{2,3},{3,2},{4,5},{5,4},{6,7},{7,6},{8,9},{9,8},{10,11... | collective-permute-start | bytes 589832 | tf_op jit(solution)/shard_map/ppermute | solution.py:19
  109.9 0.9 fusion.1
  110.8 3.5 %collective-permute-done.27.refs_1_ = bf16[128,768]{1,0:T(8,128)(2,1)S(1)} collective-permute-done((bf16[128,768]{1,0:T(8,128)(2,1)S(1)}, bf16[128,768]{1,0:T(8,128)(2,1)S(1)}, u32[]{:S(2)}, u32[]{:S(2)}) %collective-permute-start.27) | collective-permute-done | bytes 196640 | tf_op jit(solution)/shard_map/ppermute | solution.py:19
  114.4 2.6 %collective-permute-start.28 = (bf16[64,768]{1,0:T(8,128)(2,1)S(1)}, bf16[64,768]{1,0:T(8,128)(2,1)S(1)}, u32[]{:S(2)}, u32[]{:S(2)}) collective-permute-start(bf16[64,768]{1,0:T(8,128)(2,1)S(1)} %get-tuple-element.76), channel_id=1, source_target_pairs={{0,2},{1,3},{2,0},{3,1},{4,6},{5,7},{6,4},{7,5},{8,10},{9,11},{10,... | collective-permute-start | bytes 294920 | tf_op jit(solution)/shard_map/ppermute | solution.py:19
  116.9 3.3 %collective-permute-done.31 = bf16[96,1536]{1,0:T(8,128)(2,1)S(1)} collective-permute-done((bf16[96,1536]{1,0:T(8,128)(2,1)S(1)}, bf16[96,1536]{1,0:T(8,128)(2,1)S(1)}, u32[]{:S(2)}, u32[]{:S(2)}) %collective-permute-start.31) | collective-permute-done | bytes 294944 | tf_op jit(solution)/shard_map/ppermute | solution.py:19
  120.4 0.9 fusion.2
  121.2 0.7 fusion
  (62 shorter events, 6.9 us)
Async XLA Ops:
  0.6 24.2 %copy-start.4 = (bf16[96,512]{1,0:T(8,128)(2,1)S(1)}, bf16[96,512]{1,0:T(8,128)(2,1)}, u32[]{:S(2)}) copy-start(bf16[96,512]{1,0:T(8,128)(2,1)} %refs_0_.3) | copy-start | bytes 294916
  0.6 24.2 %copy-start.5 = (bf16[96,512]{1,0:T(8,128)(2,1)S(1)}, bf16[96,512]{1,0:T(8,128)(2,1)}, u32[]{:S(2)}) copy-start(bf16[96,512]{1,0:T(8,128)(2,1)} %refs_1_.2) | copy-start | bytes 294916
  0.7 24.2 %copy-start.6 = (bf16[96,512]{1,0:T(8,128)(2,1)S(1)}, bf16[96,512]{1,0:T(8,128)(2,1)}, u32[]{:S(2)}) copy-start(bf16[96,512]{1,0:T(8,128)(2,1)} %refs_2_.6) | copy-start | bytes 294916
  0.7 24.2 %copy-start.7 = (bf16[96,512]{1,0:T(8,128)(2,1)S(1)}, bf16[96,512]{1,0:T(8,128)(2,1)}, u32[]{:S(2)}) copy-start(bf16[96,512]{1,0:T(8,128)(2,1)} %refs_3_.4) | copy-start | bytes 294916
  2.7 13.5 %collective-permute-start.1 = (bf16[64,1536]{1,0:T(8,128)(2,1)}, bf16[64,1536]{1,0:T(8,128)(2,1)S(1)}, u32[]{:S(2)}, u32[]{:S(2)}) collective-permute-start(bf16[64,1536]{1,0:T(8,128)(2,1)} %get-tuple-element.45.refs_3_), channel_id=1, source_target_pairs={{0,2},{1,3},{2,0},{3,1},{4,6},{5,7},{6,4},{7,5},{8,10},{9,11},{10,... | collective-permute-start | bytes 589832 | tf_op jit(solution)/shard_map/ppermute | solution.py:19
  6.8 13.2 %collective-permute-start.3 = (bf16[96,1536]{1,0:T(8,128)(2,1)}, bf16[96,1536]{1,0:T(8,128)(2,1)S(1)}, u32[]{:S(2)}, u32[]{:S(2)}) collective-permute-start(bf16[96,1536]{1,0:T(8,128)(2,1)} %get-tuple-element.46.refs_0_), channel_id=1, source_target_pairs={{0,24},{4,28},{8,16},{12,20},{16,8},{20,12},{24,0},{28,4},{1,25},{... | collective-permute-start | bytes 884744 | tf_op jit(solution)/shard_map/ppermute | solution.py:19
  9.3 13.4 %collective-permute-start.4 = (bf16[96,1536]{1,0:T(8,128)(2,1)}, bf16[96,1536]{1,0:T(8,128)(2,1)S(1)}, u32[]{:S(2)}, u32[]{:S(2)}) collective-permute-start(bf16[96,1536]{1,0:T(8,128)(2,1)} %get-tuple-element.46.refs_0_), channel_id=1, source_target_pairs={{0,16},{4,20},{8,24},{12,28},{16,0},{20,4},{24,8},{28,12},{1,17},{... | collective-permute-start | bytes 884744 | tf_op jit(solution)/shard_map/ppermute | solution.py:19
  9.8 13.0 %collective-permute-start.5 = (bf16[96,1536]{1,0:T(8,128)(2,1)}, bf16[96,1536]{1,0:T(8,128)(2,1)S(1)}, u32[]{:S(2)}, u32[]{:S(2)}) collective-permute-start(bf16[96,1536]{1,0:T(8,128)(2,1)} %get-tuple-element.46.refs_0_), channel_id=1, source_target_pairs={{0,8},{4,12},{8,0},{12,4},{16,24},{20,28},{24,16},{28,20},{1,9},{5... | collective-permute-start | bytes 884744 | tf_op jit(solution)/shard_map/ppermute | solution.py:19
  10.3 9.7 %collective-permute-start = (bf16[64,1536]{1,0:T(8,128)(2,1)}, bf16[64,1536]{1,0:T(8,128)(2,1)S(1)}, u32[]{:S(2)}, u32[]{:S(2)}) collective-permute-start(bf16[64,1536]{1,0:T(8,128)(2,1)} %get-tuple-element.45.refs_3_), channel_id=1, source_target_pairs={{0,1},{1,0},{2,3},{3,2},{4,5},{5,4},{6,7},{7,6},{8,9},{9,8},{10,11... | collective-permute-start | bytes 589832 | tf_op jit(solution)/shard_map/ppermute | solution.py:19
  16.3 7.1 %collective-permute-start.2 = (bf16[64,1536]{1,0:T(8,128)(2,1)S(1)}, bf16[64,1536]{1,0:T(8,128)(2,1)S(1)}, u32[]{:S(2)}, u32[]{:S(2)}) collective-permute-start(bf16[64,1536]{1,0:T(8,128)(2,1)S(1)} %collective-permute-done.1.refs_5_), channel_id=1, source_target_pairs={{0,1},{1,0},{2,3},{3,2},{4,5},{5,4},{6,7},{7,6},{8,9},{9,8},{10,11... | collective-permute-start | bytes 589832 | tf_op jit(solution)/shard_map/ppermute | solution.py:19
  23.3 1.0 copy-start.2
  24.7 3.9 %copy-start.3 = (bf16[64,1536]{1,0:T(8,128)(2,1)S(1)}, bf16[64,1536]{1,0:T(8,128)(2,1)}, u32[]{:S(2)}) copy-start(bf16[64,1536]{1,0:T(8,128)(2,1)} %get-tuple-element.45.refs_3_) | copy-start | bytes 589828
  24.7 3.9 %copy-start.9 = (f32[768]{0:T(1024)S(1)}, f32[768]{0:T(1024)}, u32[]{:S(2)}) copy-start(f32[768]{0:T(1024)} %refs_2_.5) | copy-start | bytes 9220
  24.7 3.9 %collective-permute-start.6 = (bf16[384,1536]{1,0:T(8,128)(2,1)S(1)}, bf16[384,1536]{1,0:T(8,128)(2,1)S(1)}, u32[]{:S(2)}, u32[]{:S(2)}) collective-permute-start(bf16[384,1536]{1,0:T(8,128)(2,1)S(1)} %shard_map.181.refs_7_.refs_4_), channel_id=1, source_target_pairs={{0,4},{4,0},{8,12},{12,8},{16,20},{20,16},{24,28},{28,24},{1,5},{5... | collective-permute-start | bytes 3538952 | tf_op jit(solution)/shard_map/ppermute | solution.py:19
  25.0 13.0 %collective-permute-start.10 = (bf16[96,2048]{1,0:T(8,128)(2,1)S(1)}, bf16[96,2048]{1,0:T(8,128)(2,1)}, u32[]{:S(2)}, u32[]{:S(2)}) collective-permute-start(bf16[96,2048]{1,0:T(8,128)(2,1)S(1)} %shard_map.183.refs_6_), channel_id=1, source_target_pairs={{0,24},{4,28},{8,16},{12,20},{16,8},{20,12},{24,0},{28,4},{1,25},{... | collective-permute-start | bytes 1179656 | tf_op jit(solution)/shard_map/ppermute | solution.py:19
  27.6 18.4 %collective-permute-start.11 = (bf16[96,2048]{1,0:T(8,128)(2,1)S(1)}, bf16[96,2048]{1,0:T(8,128)(2,1)}, u32[]{:S(2)}, u32[]{:S(2)}) collective-permute-start(bf16[96,2048]{1,0:T(8,128)(2,1)S(1)} %shard_map.183.refs_6_), channel_id=1, source_target_pairs={{0,16},{4,20},{8,24},{12,28},{16,0},{20,4},{24,8},{28,12},{1,17},{... | collective-permute-start | bytes 1179656 | tf_op jit(solution)/shard_map/ppermute | solution.py:19
  28.1 18.1 %collective-permute-start.12 = (bf16[96,2048]{1,0:T(8,128)(2,1)S(1)}, bf16[96,2048]{1,0:T(8,128)(2,1)}, u32[]{:S(2)}, u32[]{:S(2)}) collective-permute-start(bf16[96,2048]{1,0:T(8,128)(2,1)S(1)} %shard_map.183.refs_6_), channel_id=1, source_target_pairs={{0,8},{4,12},{8,0},{12,4},{16,24},{20,28},{24,16},{28,20},{1,9},{5... | collective-permute-start | bytes 1179656 | tf_op jit(solution)/shard_map/ppermute | solution.py:19
  28.6 17.6 %copy-start = (bf16[1,64,768]{2,1,0:T(8,128)(2,1)S(1)}, bf16[1,64,768]{2,1,0:T(8,128)(2,1)}, u32[]{:S(2)}) copy-start(bf16[1,64,768]{2,1,0:T(8,128)(2,1)} %param.13) | copy-start | bytes 294916
  28.6 17.6 %copy-start.8 = (f32[768]{0:T(1024)S(1)}, f32[768]{0:T(1024)}, u32[]{:S(2)}) copy-start(f32[768]{0:T(1024)} %refs_0_.5) | copy-start | bytes 9220
  30.6 15.5 %collective-permute-start.7 = (bf16[64,768]{1,0:T(8,128)(2,1)S(1)}, bf16[64,768]{1,0:T(8,128)(2,1)S(1)}, u32[]{:S(2)}, u32[]{:S(2)}) collective-permute-start(bf16[64,768]{1,0:T(8,128)(2,1)S(1)} %get-tuple-element.48), channel_id=1, source_target_pairs={{0,1},{1,0},{2,3},{3,2},{4,5},{5,4},{6,7},{7,6},{8,9},{9,8},{10,11... | collective-permute-start | bytes 294920 | tf_op jit(solution)/shard_map/ppermute | solution.py:19
  31.8 14.4 %collective-permute-start.8 = (bf16[64,768]{1,0:T(8,128)(2,1)S(1)}, bf16[64,768]{1,0:T(8,128)(2,1)S(1)}, u32[]{:S(2)}, u32[]{:S(2)}) collective-permute-start(bf16[64,768]{1,0:T(8,128)(2,1)S(1)} %get-tuple-element.49), channel_id=1, source_target_pairs={{0,2},{1,3},{2,0},{3,1},{4,6},{5,7},{6,4},{7,5},{8,10},{9,11},{10,... | collective-permute-start | bytes 294920 | tf_op jit(solution)/shard_map/ppermute | solution.py:19
  38.1 8.1 %collective-permute-start.9 = (bf16[64,768]{1,0:T(8,128)(2,1)S(1)}, bf16[64,768]{1,0:T(8,128)(2,1)S(1)}, u32[]{:S(2)}, u32[]{:S(2)}) collective-permute-start(bf16[64,768]{1,0:T(8,128)(2,1)S(1)} %get-tuple-element.50), channel_id=1, source_target_pairs={{0,3},{1,2},{2,1},{3,0},{4,7},{5,6},{6,5},{7,4},{8,11},{9,10},{10,... | collective-permute-start | bytes 294920 | tf_op jit(solution)/shard_map/ppermute | solution.py:19
  47.8 4.6 %collective-permute-start.16 = (bf16[384,2048]{1,0:T(8,128)(2,1)S(1)}, bf16[384,2048]{1,0:T(8,128)(2,1)S(1)}, u32[]{:S(2)}, u32[]{:S(2)}) collective-permute-start(bf16[384,2048]{1,0:T(8,128)(2,1)S(1)} %get-tuple-element.54.refs_1_), channel_id=1, source_target_pairs={{0,4},{4,0},{8,12},{12,8},{16,20},{20,16},{24,28},{28,24},{1,5},{5... | collective-permute-start | bytes 4718600 | tf_op jit(solution)/shard_map/ppermute | solution.py:19
  47.9 11.8 %copy-start.10 = (f32[4,9]{1,0:T(4,128)S(1)}, f32[4,9]{1,0:T(4,128)}, u32[]{:S(2)}) copy-start(f32[4,9]{1,0:T(4,128)} %refs_1_.3) | copy-start | bytes 436
  47.9 11.8 %copy-start.11 = (s32[1,256]{1,0:T(1,128)S(1)}, s32[1,256]{1,0:T(1,128)}, u32[]{:S(2)}) copy-start(s32[1,256]{1,0:T(1,128)} %refs_2_.7) | copy-start | bytes 3076
  47.9 11.8 %copy-start.12 = (s32[1,256]{1,0:T(1,128)S(1)}, s32[1,256]{1,0:T(1,128)}, u32[]{:S(2)}) copy-start(s32[1,256]{1,0:T(1,128)} %refs_3_.5) | copy-start | bytes 3076
  47.9 6.7 %collective-permute-start.13 = (bf16[64,768]{1,0:T(8,128)(2,1)S(1)}, bf16[64,768]{1,0:T(8,128)(2,1)S(1)}, u32[]{:S(2)}, u32[]{:S(2)}) collective-permute-start(bf16[64,768]{1,0:T(8,128)(2,1)S(1)} %get-tuple-element.52.refs_4_), channel_id=1, source_target_pairs={{0,1},{1,0},{2,3},{3,2},{4,5},{5,4},{6,7},{7,6},{8,9},{9,8},{10,11... | collective-permute-start | bytes 294920 | tf_op jit(solution)/shard_map/ppermute | solution.py:19
  49.0 10.8 %collective-permute-start.14 = (bf16[64,768]{1,0:T(8,128)(2,1)S(1)}, bf16[64,768]{1,0:T(8,128)(2,1)S(1)}, u32[]{:S(2)}, u32[]{:S(2)}) collective-permute-start(bf16[64,768]{1,0:T(8,128)(2,1)S(1)} %get-tuple-element.52.refs_4_), channel_id=1, source_target_pairs={{0,2},{1,3},{2,0},{3,1},{4,6},{5,7},{6,4},{7,5},{8,10},{9,11},{10,... | collective-permute-start | bytes 294920 | tf_op jit(solution)/shard_map/ppermute | solution.py:19
  51.8 8.0 %collective-permute-start.15 = (bf16[64,768]{1,0:T(8,128)(2,1)S(1)}, bf16[64,768]{1,0:T(8,128)(2,1)S(1)}, u32[]{:S(2)}, u32[]{:S(2)}) collective-permute-start(bf16[64,768]{1,0:T(8,128)(2,1)S(1)} %get-tuple-element.52.refs_4_), channel_id=1, source_target_pairs={{0,3},{1,2},{2,1},{3,0},{4,7},{5,6},{6,5},{7,4},{8,11},{9,10},{10,... | collective-permute-start | bytes 294920 | tf_op jit(solution)/shard_map/ppermute | solution.py:19
  66.2 12.9 %collective-permute-start.23 = (bf16[384,2048]{1,0:T(8,128)(2,1)S(1)}, bf16[384,2048]{1,0:T(8,128)(2,1)S(1)}, u32[]{:S(2)}, u32[]{:S(2)}) collective-permute-start(bf16[384,2048]{1,0:T(8,128)(2,1)S(1)} %get-tuple-element.68), channel_id=1, source_target_pairs={{0,4},{4,0},{8,12},{12,8},{16,20},{20,16},{24,28},{28,24},{1,5},{5... | collective-permute-start | bytes 4718600 | tf_op jit(solution)/shard_map/ppermute | solution.py:19
  66.3 5.5 %collective-permute-start.17 = (bf16[64,768]{1,0:T(8,128)(2,1)S(1)}, bf16[64,768]{1,0:T(8,128)(2,1)S(1)}, u32[]{:S(2)}, u32[]{:S(2)}) collective-permute-start(bf16[64,768]{1,0:T(8,128)(2,1)S(1)} %get-tuple-element.61), channel_id=1, source_target_pairs={{0,1},{1,0},{2,3},{3,2},{4,5},{5,4},{6,7},{7,6},{8,9},{9,8},{10,11... | collective-permute-start | bytes 294920 | tf_op jit(solution)/shard_map/ppermute | solution.py:19
  68.4 10.8 %collective-permute-start.18 = (bf16[64,768]{1,0:T(8,128)(2,1)S(1)}, bf16[64,768]{1,0:T(8,128)(2,1)S(1)}, u32[]{:S(2)}, u32[]{:S(2)}) collective-permute-start(bf16[64,768]{1,0:T(8,128)(2,1)S(1)} %get-tuple-element.62), channel_id=1, source_target_pairs={{0,2},{1,3},{2,0},{3,1},{4,6},{5,7},{6,4},{7,5},{8,10},{9,11},{10,... | collective-permute-start | bytes 294920 | tf_op jit(solution)/shard_map/ppermute | solution.py:19
  69.5 9.7 %collective-permute-start.19 = (bf16[64,768]{1,0:T(8,128)(2,1)S(1)}, bf16[64,768]{1,0:T(8,128)(2,1)S(1)}, u32[]{:S(2)}, u32[]{:S(2)}) collective-permute-start(bf16[64,768]{1,0:T(8,128)(2,1)S(1)} %get-tuple-element.63), channel_id=1, source_target_pairs={{0,3},{1,2},{2,1},{3,0},{4,7},{5,6},{6,5},{7,4},{8,11},{9,10},{10,... | collective-permute-start | bytes 294920 | tf_op jit(solution)/shard_map/ppermute | solution.py:19
  79.2 2.7 %copy-start.1 = (bf16[1,64,768]{2,1,0:T(8,128)(2,1)S(1)}, bf16[1,64,768]{2,1,0:T(8,128)(2,1)}, u32[]{:S(2)}) copy-start(bf16[1,64,768]{2,1,0:T(8,128)(2,1)} %param.25) | copy-start | bytes 294916
  79.5 14.0 %collective-permute-start.24 = (bf16[96,2048]{1,0:T(8,128)(2,1)S(1)}, bf16[96,2048]{1,0:T(8,128)(2,1)S(1)}, u32[]{:S(2)}, u32[]{:S(2)}) collective-permute-start(bf16[96,2048]{1,0:T(8,128)(2,1)S(1)} %get-tuple-element.69), channel_id=1, source_target_pairs={{0,8},{4,12},{8,0},{12,4},{16,24},{20,28},{24,16},{28,20},{1,9},{5... | collective-permute-start | bytes 1179656 | tf_op jit(solution)/shard_map/ppermute | solution.py:19
  81.1 12.4 %collective-permute-start.25 = (bf16[96,2048]{1,0:T(8,128)(2,1)S(1)}, bf16[96,2048]{1,0:T(8,128)(2,1)S(1)}, u32[]{:S(2)}, u32[]{:S(2)}) collective-permute-start(bf16[96,2048]{1,0:T(8,128)(2,1)S(1)} %get-tuple-element.70), channel_id=1, source_target_pairs={{0,16},{4,20},{8,24},{12,28},{16,0},{20,4},{24,8},{28,12},{1,17},{... | collective-permute-start | bytes 1179656 | tf_op jit(solution)/shard_map/ppermute | solution.py:19
  82.1 5.7 %collective-permute-start.20 = (bf16[64,768]{1,0:T(8,128)(2,1)S(1)}, bf16[64,768]{1,0:T(8,128)(2,1)S(1)}, u32[]{:S(2)}, u32[]{:S(2)}) collective-permute-start(bf16[64,768]{1,0:T(8,128)(2,1)S(1)} %shard_map.187.refs_5_), channel_id=1, source_target_pairs={{0,1},{1,0},{2,3},{3,2},{4,5},{5,4},{6,7},{7,6},{8,9},{9,8},{10,11... | collective-permute-start | bytes 294920 | tf_op jit(solution)/shard_map/ppermute | solution.py:19
  84.1 9.4 %collective-permute-start.21 = (bf16[64,768]{1,0:T(8,128)(2,1)S(1)}, bf16[64,768]{1,0:T(8,128)(2,1)S(1)}, u32[]{:S(2)}, u32[]{:S(2)}) collective-permute-start(bf16[64,768]{1,0:T(8,128)(2,1)S(1)} %shard_map.187.refs_5_), channel_id=1, source_target_pairs={{0,2},{1,3},{2,0},{3,1},{4,6},{5,7},{6,4},{7,5},{8,10},{9,11},{10,... | collective-permute-start | bytes 294920 | tf_op jit(solution)/shard_map/ppermute | solution.py:19
  85.1 8.4 %collective-permute-start.22 = (bf16[64,768]{1,0:T(8,128)(2,1)S(1)}, bf16[64,768]{1,0:T(8,128)(2,1)S(1)}, u32[]{:S(2)}, u32[]{:S(2)}) collective-permute-start(bf16[64,768]{1,0:T(8,128)(2,1)S(1)} %shard_map.187.refs_5_), channel_id=1, source_target_pairs={{0,3},{1,2},{2,1},{3,0},{4,7},{5,6},{6,5},{7,4},{8,11},{9,10},{10,... | collective-permute-start | bytes 294920 | tf_op jit(solution)/shard_map/ppermute | solution.py:19
  95.0 2.9 %collective-permute-start.26 = (bf16[384,1536]{1,0:T(8,128)(2,1)S(1)}, bf16[384,1536]{1,0:T(8,128)(2,1)S(1)}, u32[]{:S(2)}, u32[]{:S(2)}) collective-permute-start(bf16[384,1536]{1,0:T(8,128)(2,1)S(1)} %get-tuple-element.72), channel_id=1, source_target_pairs={{0,4},{4,0},{8,12},{12,8},{16,20},{20,16},{24,28},{28,24},{1,5},{5... | collective-permute-start | bytes 3538952 | tf_op jit(solution)/shard_map/ppermute | solution.py:19
  95.1 12.9 %collective-permute-start.32 = (bf16[96,2048]{1,0:T(8,128)(2,1)S(1)}, bf16[96,2048]{1,0:T(8,128)(2,1)S(1)}, u32[]{:S(2)}, u32[]{:S(2)}) collective-permute-start(bf16[96,2048]{1,0:T(8,128)(2,1)S(1)} %get-tuple-element.82), channel_id=1, source_target_pairs={{0,24},{4,28},{8,16},{12,20},{16,8},{20,12},{24,0},{28,4},{1,25},{... | collective-permute-start | bytes 1179656 | tf_op jit(solution)/shard_map/ppermute | solution.py:19
  98.2 18.7 %collective-permute-start.29 = (bf16[96,1536]{1,0:T(8,128)(2,1)S(1)}, bf16[96,1536]{1,0:T(8,128)(2,1)S(1)}, u32[]{:S(2)}, u32[]{:S(2)}) collective-permute-start(bf16[96,1536]{1,0:T(8,128)(2,1)S(1)} %get-tuple-element.78), channel_id=1, source_target_pairs={{0,8},{4,12},{8,0},{12,4},{16,24},{20,28},{24,16},{28,20},{1,9},{5... | collective-permute-start | bytes 884744 | tf_op jit(solution)/shard_map/ppermute | solution.py:19
  99.5 17.4 %collective-permute-start.30 = (bf16[96,1536]{1,0:T(8,128)(2,1)S(1)}, bf16[96,1536]{1,0:T(8,128)(2,1)S(1)}, u32[]{:S(2)}, u32[]{:S(2)}) collective-permute-start(bf16[96,1536]{1,0:T(8,128)(2,1)S(1)} %get-tuple-element.79), channel_id=1, source_target_pairs={{0,16},{4,20},{8,24},{12,28},{16,0},{20,4},{24,8},{28,12},{1,17},{... | collective-permute-start | bytes 884744 | tf_op jit(solution)/shard_map/ppermute | solution.py:19
  100.1 20.1 %collective-permute-start.31 = (bf16[96,1536]{1,0:T(8,128)(2,1)S(1)}, bf16[96,1536]{1,0:T(8,128)(2,1)S(1)}, u32[]{:S(2)}, u32[]{:S(2)}) collective-permute-start(bf16[96,1536]{1,0:T(8,128)(2,1)S(1)} %get-tuple-element.80), channel_id=1, source_target_pairs={{0,24},{4,28},{8,16},{12,20},{16,8},{20,12},{24,0},{28,4},{1,25},{... | collective-permute-start | bytes 884744 | tf_op jit(solution)/shard_map/ppermute | solution.py:19
  108.2 6.1 %collective-permute-start.27 = (bf16[128,768]{1,0:T(8,128)(2,1)S(1)}, bf16[128,768]{1,0:T(8,128)(2,1)S(1)}, u32[]{:S(2)}, u32[]{:S(2)}) collective-permute-start(bf16[128,768]{1,0:T(8,128)(2,1)S(1)} %get-tuple-element.74), channel_id=1, source_target_pairs={{0,1},{1,0},{2,3},{3,2},{4,5},{5,4},{6,7},{7,6},{8,9},{9,8},{10,11... | collective-permute-start | bytes 589832 | tf_op jit(solution)/shard_map/ppermute | solution.py:19
  114.4 6.9 %collective-permute-start.28 = (bf16[64,768]{1,0:T(8,128)(2,1)S(1)}, bf16[64,768]{1,0:T(8,128)(2,1)S(1)}, u32[]{:S(2)}, u32[]{:S(2)}) collective-permute-start(bf16[64,768]{1,0:T(8,128)(2,1)S(1)} %get-tuple-element.76), channel_id=1, source_target_pairs={{0,2},{1,3},{2,0},{3,1},{4,6},{5,7},{6,4},{7,5},{8,10},{9,11},{10,... | collective-permute-start | bytes 294920 | tf_op jit(solution)/shard_map/ppermute | solution.py:19

commit v6 on v5

--- a/solution.py
+++ b/solution.py
@@ -97,27 +97,31 @@
         out[at : at + rows, columns] = block.astype(BF)
 
 
-def ffn_kernel(parts, ids, cot_scale, *refs):
-    place_ref, me_ref, gain = refs[:3]
-    both_parts = refs[3 : 3 + parts]
-    direct = len(ids) > 1
-    at = 3 + parts + (2 if direct else 1)
-    weights, rest = refs[3 + parts : at], refs[at:]
-    normed_out, pre_out, hidden_out, down, scaled = rest[:5]
-    partials = rest[5 : 5 + parts]
-    up = rest[5 + parts]
-    sems = rest[-1]
-    model, width = up.shape
-    up_copies = collect(me_ref, weights, ids, 0, up, sems)
-    down_copies = collect(me_ref, weights, ids, width, down, sems, 8)
-    own = both_parts[0].shape[0]
+def prepare_kernel(parts, cot_scale, *refs):
+    place_ref, gain = refs[:2]
+    both_parts = refs[2 : 2 + parts]
+    normed_out, scaled = refs[2 + parts :]
+    own, model = both_parts[0].shape[0], normed_out.shape[1]
     for index, (first, both) in enumerate(zip(places(place_ref, parts, own), both_parts)):
         normed = normalise(both[:, :model].astype(F32))[0] * gain[...].reshape(1, -1)
         normed_out[index * own : (index + 1) * own, :] = normed.astype(BF)
         cot = both[:, model:].astype(F32)
         scaled[pl.ds(first, own), :] = (cot * cot_scale).astype(BF)
+
+
+def ffn_kernel(parts, ids, *refs):
+    me_ref, normed = refs[:2]
+    at = 3 if len(ids) == 1 else 4
+    weights, rest = refs[2:at], refs[at:]
+    pre_out, hidden_out, down = rest[:3]
+    partials = rest[3 : 3 + parts]
+    up, sems = rest[3 + parts], rest[-1]
+    width = up.shape[1]
+    up_copies = collect(me_ref, weights, ids, 0, up, sems)
+    down_copies = collect(me_ref, weights, ids, width, down, sems, 8)
+    own = partials[0].shape[0]
     wait_copies(up_copies)
-    pre = dot(normed_out[...], up[...], 1, 0)
+    pre = dot(normed[...], up[...], 1, 0)
     pre_out[...] = pre
     hidden_out[...] = (pre * jax.nn.sigmoid(pre)).astype(BF)
     wait_copies(down_copies)
@@ -151,21 +155,23 @@
     wait_copies(copies)
 
 
-def collect_kernel(ids, me_ref, near, far, out, sems):
+def collect_kernel(ids, me_ref, scaled, near, far, out, grad_context, sems):
     wait_copies(collect(me_ref, [near, far], ids, 0, out, sems))
+    inner = grad_context.shape[1]
+    grad_context[...] = dot(scaled[...], out[:, 3 * inner :], 1, 0).astype(BF)
 
 
 def attention_kernel(parts, window, *refs):
     place_ref, bias = refs[:2]
     segments, spans = refs[2:4]
     normed_parts = refs[4 : 4 + parts]
-    scaled, weights = refs[4 + parts : 6 + parts]
+    grad_context, weights = refs[4 + parts : 6 + parts]
     rest = refs[6 + parts :]
     normed, context, slopes = rest[:3]
     outs = rest[3 : 3 + parts]
     halves = 1 if parts == 1 else 2
     attn_outs = rest[3 + parts : 3 + parts + halves]
-    qkv, grad_context, key_total, value_total, total = rest[3 + parts + halves :]
+    qkv, key_total, value_total, total = rest[3 + parts + halves :]
     heads = bias.shape[0]
     frames = normed.shape[0]
     own = normed_parts[0].shape[0]
@@ -176,7 +182,6 @@
     for first, piece in zip(firsts, normed_parts):
         normed[pl.ds(first, own), :] = piece[...]
     qkv[...] = dot(normed[...], weights[:, : 3 * inner], 1, 0).astype(BF)
-    grad_context[...] = dot(scaled[...], weights[:, 3 * inner :], 1, 0).astype(BF)
     seg_k, span_k = segments[...], spans[...]
     seg_q = jnp.transpose(jnp.broadcast_to(seg_k, (8, frames)))[:, :1]
     span_q = jnp.transpose(jnp.broadcast_to(span_k, (8, frames)))[:, :1]
@@ -408,27 +413,26 @@
     else:
         ffn_weights = [lax.all_gather(ffn_rows, "dp", axis=0, tiled=True)]
         attn_weights = pack([[w_query, w_key, w_value, w_out]])[0]
-        attn_weights = [lax.all_gather(attn_weights, "dp", axis=0, tiled=True)]
+        attn_weights = lax.all_gather(attn_weights, "dp", axis=0, tiled=True)
         attn_pieces = []
 
-    made = call(
-        functools.partial(ffn_kernel, parts, ids, cot_scale),
-        [
-            shape((frames, model), BF),
-            shape((frames, hidden), F32),
-            shape((frames, hidden), BF),
-            shape((model, hidden), BF),
-            shape((frames, model), BF),
-        ]
+    ffn_normed, scaled_cot = call(
+        functools.partial(prepare_kernel, parts, cot_scale),
+        [shape((frames, model), BF)] * 2,
+        [place, ffn_gain] + both_parts,
+        smem=1,
+    )
+    ffn_pre, ffn_hidden, down_full, *ffn_partials = call(
+        functools.partial(ffn_kernel, parts, ids),
+        [shape((frames, hidden), F32), shape((frames, hidden), BF), shape((model, hidden), BF)]
         + [shape((part_rows, model), BF)] * parts,
-        [place, me, ffn_gain] + both_parts + ffn_weights,
+        [me, ffn_normed] + ffn_weights,
         [pltpu.VMEM((model, hidden), BF)],
         flops=4 * frames * model * hidden,
-        smem=2,
+        smem=1,
         far=2 if direct_rows else 0,
     )
-    ffn_normed, ffn_pre, ffn_hidden, down_full, scaled_cot = made[:5]
-    summed = scatter_frames(list(made[5:]))
+    summed = scatter_frames(ffn_partials)
     near = [shape((model // 2, 4 * inner), BF)] if direct_rows else []
     mid_own, normed_own, *near = call(
         functools.partial(mid_kernel, len(summed)),
@@ -438,13 +442,18 @@
     )
     normed_parts = gather_frames(normed_own)
     if direct_rows:
-        attn_weights = call(
+        attn_weights, grad_context = call(
             functools.partial(collect_kernel, ids),
-            [shape((model, 4 * inner), BF)],
-            [me, near[0], exchange(near[0], "dp", 1)],
+            [shape((model, 4 * inner), BF), shape((frames, inner), BF)],
+            [me, scaled_cot, near[0], exchange(near[0], "dp", 1)],
+            flops=2 * frames * model * inner,
             smem=1,
             far=2,
         )
+    else:
+        grad_context = jnp.dot(
+            scaled_cot, attn_weights[:, 3 * inner :], preferred_element_type=F32
+        ).astype(BF)
     made = call(
         functools.partial(attention_kernel, parts, window),
         [
@@ -455,10 +464,9 @@
         + [shape((part_rows, model), BF)] * parts
         + [shape((frames // 2, model), BF)] * 2 * (parts > 1)
         + [shape((frames, model), BF)] * (parts == 1),
-        [place, offset_bias, segment_ids, span_ids, *normed_parts, scaled_cot, *attn_weights],
+        [place, offset_bias, segment_ids, span_ids, *normed_parts, grad_context, attn_weights],
         [
             pltpu.VMEM((frames, 3 * inner), BF),
-            pltpu.VMEM((frames, inner), BF),
             pltpu.VMEM((frames, inner // heads), F32),
             pltpu.VMEM((frames, inner // heads), F32),
             pltpu.VMEM((frames, model), F32),

time: 122 us -> 122 us (level)
    pallas_call x13 -> x14, Pallas kernels: 16.9 us -> 17 us  [call(): pl.pallas_call(lambda *refs: body(*refs[:count], *refs[count + len(after)...]
where the time goes in v6:
time: 122 us
  waiting for transfers between devices  54.1 us (44%)
  starting transfers between devices  45.8 us (38%)
  Pallas kernels  17 us (14%)
  local copies, waits for them, and re-layouts  2.75 us (2%)
    ppermute x33, waiting for transfers between devices, exchange(): lax.ppermute(values, axis, [(one, one ^ mask) for one in range(size)])  54.1 us
    ppermute x33, starting transfers between devices, exchange(): lax.ppermute(values, axis, [(one, one ^ mask) for one in range(size)])  45.8 us
    pallas_call x14, Pallas kernels, call(): pl.pallas_call(lambda *refs: body(*refs[:count], *refs[count + len(after)...  17 us
  transfers between devices with their start and end apart: 33, of which 18 were waited for; matrix products, arithmetic and copies ran while one was open for 2% of the time, Pallas kernels for 4%

profile of v6, /device:TPU:0, one launch (start us, length us, event | category | flops | bytes accessed | tf_op | source)
XLA Modules:
  0.0 121.6 jit_solution(9515447859657218013)
XLA Ops:
  0.7 2.1 %shard_map.180 = (bf16[64,1536]{1,0:T(8,128)(2,1)}, bf16[96,1536]{1,0:T(8,128)(2,1)}) custom-call(bf16[64,768]{1,0:T(8,128)(2,1)} %bitcast.6, bf16[64,768]{1,0:T(8,128)(2,1)} %bitcast.8, bf16[96,768]{1,0:T(8,128)(2,1)} %refs_2_.3, bf16[96,768]{1,0:T(8,128)(2,1)} %refs_3_.3), custom_call_target="tpu_custom_call" | custom-call | bytes 983040 | tf_op jit(solution)/shard_map/pallas_call | solution.py:31
  2.7 4.1 %collective-permute-start.1 = (bf16[64,1536]{1,0:T(8,128)(2,1)}, bf16[64,1536]{1,0:T(8,128)(2,1)S(1)}, u32[]{:S(2)}, u32[]{:S(2)}) collective-permute-start(bf16[64,1536]{1,0:T(8,128)(2,1)} %get-tuple-element.47.refs_2_), channel_id=1, source_target_pairs={{0,2},{1,3},{2,0},{3,1},{4,6},{5,7},{6,4},{7,5},{8,10},{9,11},{10,... | collective-permute-start | bytes 589832 | tf_op jit(solution)/shard_map/ppermute | solution.py:19
  6.8 2.4 %collective-permute-start.3 = (bf16[96,1536]{1,0:T(8,128)(2,1)}, bf16[96,1536]{1,0:T(8,128)(2,1)S(1)}, u32[]{:S(2)}, u32[]{:S(2)}) collective-permute-start(bf16[96,1536]{1,0:T(8,128)(2,1)} %get-tuple-element.49.refs_0_), channel_id=1, source_target_pairs={{0,24},{4,28},{8,16},{12,20},{16,8},{20,12},{24,0},{28,4},{1,25},{... | collective-permute-start | bytes 884744 | tf_op jit(solution)/shard_map/ppermute | solution.py:19
  10.3 1.6 %collective-permute-start = (bf16[64,1536]{1,0:T(8,128)(2,1)}, bf16[64,1536]{1,0:T(8,128)(2,1)S(1)}, u32[]{:S(2)}, u32[]{:S(2)}) collective-permute-start(bf16[64,1536]{1,0:T(8,128)(2,1)} %get-tuple-element.47.refs_2_), channel_id=1, source_target_pairs={{0,1},{1,0},{2,3},{3,2},{4,5},{5,4},{6,7},{7,6},{8,9},{9,8},{10,11... | collective-permute-start | bytes 589832 | tf_op jit(solution)/shard_map/ppermute | solution.py:19
  11.9 4.4 %collective-permute-done.1.refs_4_.refs_5_ = bf16[64,1536]{1,0:T(8,128)(2,1)S(1)} collective-permute-done((bf16[64,1536]{1,0:T(8,128)(2,1)}, bf16[64,1536]{1,0:T(8,128)(2,1)S(1)}, u32[]{:S(2)}, u32[]{:S(2)}) %collective-permute-start.1) | collective-permute-done | bytes 196640 | tf_op jit(solution)/shard_map/ppermute | solution.py:19
  16.3 0.8 collective-permute-start.2
  17.0 3.0 %collective-permute-done.refs_3_.refs_4_ = bf16[64,1536]{1,0:T(8,128)(2,1)S(1)} collective-permute-done((bf16[64,1536]{1,0:T(8,128)(2,1)}, bf16[64,1536]{1,0:T(8,128)(2,1)S(1)}, u32[]{:S(2)}, u32[]{:S(2)}) %collective-permute-start) | collective-permute-done | bytes 196640 | tf_op jit(solution)/shard_map/ppermute | solution.py:19
  20.1 2.7 %collective-permute-done.4.refs_2_ = bf16[96,1536]{1,0:T(8,128)(2,1)S(1)} collective-permute-done((bf16[96,1536]{1,0:T(8,128)(2,1)}, bf16[96,1536]{1,0:T(8,128)(2,1)S(1)}, u32[]{:S(2)}, u32[]{:S(2)}) %collective-permute-start.4) | collective-permute-done | bytes 294944 | tf_op jit(solution)/shard_map/ppermute | solution.py:19
  23.3 1.0 copy-done.2
  25.0 2.6 %collective-permute-start.10 = (bf16[96,2048]{1,0:T(8,128)(2,1)S(1)}, bf16[96,2048]{1,0:T(8,128)(2,1)}, u32[]{:S(2)}, u32[]{:S(2)}) collective-permute-start(bf16[96,2048]{1,0:T(8,128)(2,1)S(1)} %shard_map.184.refs_6_), channel_id=1, source_target_pairs={{0,24},{4,28},{8,16},{12,20},{16,8},{20,12},{24,0},{28,4},{1,25},{... | collective-permute-start | bytes 1179656 | tf_op jit(solution)/shard_map/ppermute | solution.py:19
  29.0 1.7 %shard_map.183 = (f32[256,768]{1,0:T(8,128)S(1)}, bf16[256,768]{1,0:T(8,128)(2,1)S(1)}, bf16[768,768]{1,0:T(8,128)(2,1)S(1)}, bf16[64,768]{1,0:T(8,128)(2,1)S(1)...) custom-call(s32[1]{0:T(128)} %bitcast.1.refs_0_, ...), custom_call_target="tpu_custom_call" | custom-call | flops 603979776 | bytes 5505028 | tf_op jit(solution)/shard_map/pallas_call | solution.py:31
  30.6 1.2 collective-permute-start.7
  31.8 2.7 %collective-permute-start.8 = (bf16[64,768]{1,0:T(8,128)(2,1)S(1)}, bf16[64,768]{1,0:T(8,128)(2,1)S(1)}, u32[]{:S(2)}, u32[]{:S(2)}) collective-permute-start(bf16[64,768]{1,0:T(8,128)(2,1)S(1)} %get-tuple-element.52), channel_id=1, source_target_pairs={{0,2},{1,3},{2,0},{3,1},{4,6},{5,7},{6,4},{7,5},{8,10},{9,11},{10,... | collective-permute-start | bytes 294920 | tf_op jit(solution)/shard_map/ppermute | solution.py:19
  34.5 3.6 %collective-permute-done.10.refs_7_ = bf16[96,2048]{1,0:T(8,128)(2,1)} collective-permute-done((bf16[96,2048]{1,0:T(8,128)(2,1)S(1)}, bf16[96,2048]{1,0:T(8,128)(2,1)}, u32[]{:S(2)}, u32[]{:S(2)}) %collective-permute-start.10) | collective-permute-done | bytes 393248 | tf_op jit(solution)/shard_map/ppermute | solution.py:19
  38.1 3.2 %collective-permute-start.9 = (bf16[64,768]{1,0:T(8,128)(2,1)S(1)}, bf16[64,768]{1,0:T(8,128)(2,1)S(1)}, u32[]{:S(2)}, u32[]{:S(2)}) collective-permute-start(bf16[64,768]{1,0:T(8,128)(2,1)S(1)} %get-tuple-element.53), channel_id=1, source_target_pairs={{0,3},{1,2},{2,1},{3,0},{4,7},{5,6},{6,5},{7,4},{8,11},{9,10},{10,... | collective-permute-start | bytes 294920 | tf_op jit(solution)/shard_map/ppermute | solution.py:19
  41.3 4.7 %collective-permute-done.11.refs_8_ = bf16[96,2048]{1,0:T(8,128)(2,1)} collective-permute-done((bf16[96,2048]{1,0:T(8,128)(2,1)S(1)}, bf16[96,2048]{1,0:T(8,128)(2,1)}, u32[]{:S(2)}, u32[]{:S(2)}) %collective-permute-start.11) | collective-permute-done | bytes 393248 | tf_op jit(solution)/shard_map/ppermute | solution.py:19
  46.2 1.6 %shard_map.185 = (f32[64,768]{1,0:T(8,128)S(1)}, bf16[64,768]{1,0:T(8,128)(2,1)S(1)}, bf16[384,2048]{1,0:T(8,128)(2,1)S(1)}) custom-call(f32[768]{0:T(1024)S(1)} %copy-done.8, bf16[64,768]{1,0:T(8,128)(2,1)S(1)} %bitcast.7, bf16[64,768]{1,0:T(8,128)(2,1)S(1)} %get-tuple-element.50.refs_2_, bf16[64,768]{1,0:T(8,128)(2,1)S(1)} %collective-permute-done.7.refs_3_, ...), custom_call_target="tpu_custom_call" | custom-call | bytes 3935232 | tf_op jit(solution)/shard_map/pallas_call | solution.py:31
  47.9 1.0 collective-permute-start.13
  48.9 2.8 %collective-permute-start.14 = (bf16[64,768]{1,0:T(8,128)(2,1)S(1)}, bf16[64,768]{1,0:T(8,128)(2,1)S(1)}, u32[]{:S(2)}, u32[]{:S(2)}) collective-permute-start(bf16[64,768]{1,0:T(8,128)(2,1)S(1)} %get-tuple-element.55.refs_4_), channel_id=1, source_target_pairs={{0,2},{1,3},{2,0},{3,1},{4,6},{5,7},{6,4},{7,5},{8,10},{9,11},{10,... | collective-permute-start | bytes 294920 | tf_op jit(solution)/shard_map/ppermute | solution.py:19
  52.4 2.0 %shard_map.186 = (bf16[768,2048]{1,0:T(8,128)(2,1)S(1)}, bf16[256,512]{1,0:T(8,128)(2,1)S(1)}) custom-call(s32[1]{0:T(128)} %bitcast.1.refs_0_, bf16[256,768]{1,0:T(8,128)(2,1)S(1)} %get-tuple-element.56.refs_1_.refs_2_, bf16[384,2048]{1,0:T(8,128)(2,1)S(1)} %get-tuple-element.57.refs_2_, bf16[384,2048]{1,0:T(8,128)(2,1)S(1)} %collective-permute-done.16.refs_3_), custom_call_target="tpu_custom_call" | custom-call | flops 201326592 | bytes 6946820 | tf_op jit(solution)/shard_map/pallas_call | solution.py:31
  54.7 5.0 %collective-permute-done.14.refs_6_ = bf16[64,768]{1,0:T(8,128)(2,1)S(1)} collective-permute-done((bf16[64,768]{1,0:T(8,128)(2,1)S(1)}, bf16[64,768]{1,0:T(8,128)(2,1)S(1)}, u32[]{:S(2)}, u32[]{:S(2)}) %collective-permute-start.14) | collective-permute-done | bytes 98336 | tf_op jit(solution)/shard_map/ppermute | solution.py:19
  59.7 4.8 %shard_map.187 = (bf16[256,768]{1,0:T(8,128)(2,1)S(1)}, bf16[256,512]{1,0:T(8,128)(2,1)S(1)}, bf16[256,1536]{1,0:T(8,128)(2,1)S(1)}, bf16[64,768]{1,0:T(8,128)(2...) custom-call(s32[1]{0:T(128)} %bitcast.2.refs_0_, ...), custom_call_target="tpu_custom_call" | custom-call | flops 2013265920 | bytes 6031508 | tf_op jit(solution)/shard_map/pallas_call | solution.py:31
  64.5 1.5 %shard_map.189 = (bf16[384,2048]{1,0:T(8,128)(2,1)S(1)}, bf16[384,2048]{1,0:T(8,128)(2,1)S(1)}) custom-call(s32[1]{0:T(128)} %bitcast.1.refs_0_, bf16[256,768]{1,0:T(8,128)(2,1)S(1)} %get-tuple-element.68.refs_1_, bf16[256,768]{1,0:T(8,128)(2,1)S(1)} %get-tuple-element.56.refs_1_.refs_2_, bf16[256,512]{1,0:T(8,128)(2,1)S(1)} %get-tuple-element.69.refs_3_, ...), custom_call_target="tpu_custom_call" | custom-call | flops 805306368 | bytes 4980740 | tf_op jit(solution)/shard_map/pallas_call | solution.py:31
  66.1 2.1 %collective-permute-start.17 = (bf16[64,768]{1,0:T(8,128)(2,1)S(1)}, bf16[64,768]{1,0:T(8,128)(2,1)S(1)}, u32[]{:S(2)}, u32[]{:S(2)}) collective-permute-start(bf16[64,768]{1,0:T(8,128)(2,1)S(1)} %get-tuple-element.65), channel_id=1, source_target_pairs={{0,1},{1,0},{2,3},{3,2},{4,5},{5,4},{6,7},{7,6},{8,9},{9,8},{10,11... | collective-permute-start | bytes 294920 | tf_op jit(solution)/shard_map/ppermute | solution.py:19
  68.2 1.0 collective-permute-start.18
  69.3 1.4 %collective-permute-start.19 = (bf16[64,768]{1,0:T(8,128)(2,1)S(1)}, bf16[64,768]{1,0:T(8,128)(2,1)S(1)}, u32[]{:S(2)}, u32[]{:S(2)}) collective-permute-start(bf16[64,768]{1,0:T(8,128)(2,1)S(1)} %get-tuple-element.67), channel_id=1, source_target_pairs={{0,3},{1,2},{2,1},{3,0},{4,7},{5,6},{6,5},{7,4},{8,11},{9,10},{10,... | collective-permute-start | bytes 294920 | tf_op jit(solution)/shard_map/ppermute | solution.py:19
  70.7 0.9 collective-permute-done.17.refs_4_.refs_2_
  71.6 7.4 %collective-permute-done.18.refs_5_.refs_3_ = bf16[64,768]{1,0:T(8,128)(2,1)S(1)} collective-permute-done((bf16[64,768]{1,0:T(8,128)(2,1)S(1)}, bf16[64,768]{1,0:T(8,128)(2,1)S(1)}, u32[]{:S(2)}, u32[]{:S(2)}) %collective-permute-start.18) | collective-permute-done | bytes 98336 | tf_op jit(solution)/shard_map/ppermute | solution.py:19
  79.3 1.6 %collective-permute-start.24 = (bf16[96,2048]{1,0:T(8,128)(2,1)S(1)}, bf16[96,2048]{1,0:T(8,128)(2,1)S(1)}, u32[]{:S(2)}, u32[]{:S(2)}) collective-permute-start(bf16[96,2048]{1,0:T(8,128)(2,1)S(1)} %get-tuple-element.73), channel_id=1, source_target_pairs={{0,8},{4,12},{8,0},{12,4},{16,24},{20,28},{24,16},{28,20},{1,9},{5... | collective-permute-start | bytes 1179656 | tf_op jit(solution)/shard_map/ppermute | solution.py:19
  80.9 0.7 collective-permute-start.25
  81.9 1.9 %collective-permute-start.20 = (bf16[64,768]{1,0:T(8,128)(2,1)S(1)}, bf16[64,768]{1,0:T(8,128)(2,1)S(1)}, u32[]{:S(2)}, u32[]{:S(2)}) collective-permute-start(bf16[64,768]{1,0:T(8,128)(2,1)S(1)} %shard_map.188.refs_5_), channel_id=1, source_target_pairs={{0,1},{1,0},{2,3},{3,2},{4,5},{5,4},{6,7},{7,6},{8,9},{9,8},{10,11... | collective-permute-start | bytes 294920 | tf_op jit(solution)/shard_map/ppermute | solution.py:19
  83.9 1.0 collective-permute-start.21
  84.9 1.5 %collective-permute-start.22 = (bf16[64,768]{1,0:T(8,128)(2,1)S(1)}, bf16[64,768]{1,0:T(8,128)(2,1)S(1)}, u32[]{:S(2)}, u32[]{:S(2)}) collective-permute-start(bf16[64,768]{1,0:T(8,128)(2,1)S(1)} %shard_map.188.refs_5_), channel_id=1, source_target_pairs={{0,3},{1,2},{2,1},{3,0},{4,7},{5,6},{6,5},{7,4},{8,11},{9,10},{10,... | collective-permute-start | bytes 294920 | tf_op jit(solution)/shard_map/ppermute | solution.py:19
  86.4 1.3 %collective-permute-done.20.refs_6_ = bf16[64,768]{1,0:T(8,128)(2,1)S(1)} collective-permute-done((bf16[64,768]{1,0:T(8,128)(2,1)S(1)}, bf16[64,768]{1,0:T(8,128)(2,1)S(1)}, u32[]{:S(2)}, u32[]{:S(2)}) %collective-permute-start.20) | collective-permute-done | bytes 98336 | tf_op jit(solution)/shard_map/ppermute | solution.py:19
  87.6 5.6 %collective-permute-done.21.refs_7_ = bf16[64,768]{1,0:T(8,128)(2,1)S(1)} collective-permute-done((bf16[64,768]{1,0:T(8,128)(2,1)S(1)}, bf16[64,768]{1,0:T(8,128)(2,1)S(1)}, u32[]{:S(2)}, u32[]{:S(2)}) %collective-permute-start.21) | collective-permute-done | bytes 98336 | tf_op jit(solution)/shard_map/ppermute | solution.py:19
  93.3 1.5 %shard_map.191 = (bf16[384,1536]{1,0:T(8,128)(2,1)S(1)}, bf16[384,1536]{1,0:T(8,128)(2,1)S(1)}) custom-call(s32[1]{0:T(128)} %bitcast.1.refs_0_, bf16[256,768]{1,0:T(8,128)(2,1)S(1)} %get-tuple-element.48.refs_1_, f32[256,768]{1,0:T(8,128)S(1)} %get-tuple-element.61.refs_2_, bf16[256,768]{1,0:T(8,128)(2,1)S(1)} %get-tuple-element.62.refs_3_, ...), custom_call_target="tpu_custom_call" | custom-call | flops 905969664 | bytes 5505028 | tf_op jit(solution)/shard_map/pallas_call | solution.py:31
  94.9 1.3 %collective-permute-start.32 = (bf16[96,2048]{1,0:T(8,128)(2,1)S(1)}, bf16[96,2048]{1,0:T(8,128)(2,1)S(1)}, u32[]{:S(2)}, u32[]{:S(2)}) collective-permute-start(bf16[96,2048]{1,0:T(8,128)(2,1)S(1)} %get-tuple-element.86), channel_id=1, source_target_pairs={{0,24},{4,28},{8,16},{12,20},{16,8},{20,12},{24,0},{28,4},{1,25},{... | collective-permute-start | bytes 1179656 | tf_op jit(solution)/shard_map/ppermute | solution.py:19
  96.2 1.5 %collective-permute-done.26.refs_1_ = bf16[384,1536]{1,0:T(8,128)(2,1)S(1)} collective-permute-done((bf16[384,1536]{1,0:T(8,128)(2,1)S(1)}, bf16[384,1536]{1,0:T(8,128)(2,1)S(1)}, u32[]{:S(2)}, u32[]{:S(2)}) %collective-permute-start.26) | collective-permute-done | bytes 1179680 | tf_op jit(solution)/shard_map/ppermute | solution.py:19
  98.0 1.3 %collective-permute-start.29 = (bf16[96,1536]{1,0:T(8,128)(2,1)S(1)}, bf16[96,1536]{1,0:T(8,128)(2,1)S(1)}, u32[]{:S(2)}, u32[]{:S(2)}) collective-permute-start(bf16[96,1536]{1,0:T(8,128)(2,1)S(1)} %get-tuple-element.82), channel_id=1, source_target_pairs={{0,8},{4,12},{8,0},{12,4},{16,24},{20,28},{24,16},{28,20},{1,9},{5... | collective-permute-start | bytes 884744 | tf_op jit(solution)/shard_map/ppermute | solution.py:19
  99.9 1.7 %collective-permute-start.31 = (bf16[96,1536]{1,0:T(8,128)(2,1)S(1)}, bf16[96,1536]{1,0:T(8,128)(2,1)S(1)}, u32[]{:S(2)}, u32[]{:S(2)}) collective-permute-start(bf16[96,1536]{1,0:T(8,128)(2,1)S(1)} %get-tuple-element.84), channel_id=1, source_target_pairs={{0,24},{4,28},{8,16},{12,20},{16,8},{20,12},{24,0},{28,4},{1,25},{... | collective-permute-start | bytes 884744 | tf_op jit(solution)/shard_map/ppermute | solution.py:19
  101.5 6.3 %collective-permute-done.32 = bf16[96,2048]{1,0:T(8,128)(2,1)S(1)} collective-permute-done((bf16[96,2048]{1,0:T(8,128)(2,1)S(1)}, bf16[96,2048]{1,0:T(8,128)(2,1)S(1)}, u32[]{:S(2)}, u32[]{:S(2)}) %collective-permute-start.32) | collective-permute-done | bytes 393248 | tf_op jit(solution)/shard_map/ppermute | solution.py:19
  108.0 1.7 %collective-permute-start.27 = (bf16[128,768]{1,0:T(8,128)(2,1)S(1)}, bf16[128,768]{1,0:T(8,128)(2,1)S(1)}, u32[]{:S(2)}, u32[]{:S(2)}) collective-permute-start(bf16[128,768]{1,0:T(8,128)(2,1)S(1)} %get-tuple-element.78), channel_id=1, source_target_pairs={{0,1},{1,0},{2,3},{3,2},{4,5},{5,4},{6,7},{7,6},{8,9},{9,8},{10,11... | collective-permute-start | bytes 589832 | tf_op jit(solution)/shard_map/ppermute | solution.py:19
  109.7 0.9 fusion.1
  110.5 3.5 %collective-permute-done.27.refs_1_ = bf16[128,768]{1,0:T(8,128)(2,1)S(1)} collective-permute-done((bf16[128,768]{1,0:T(8,128)(2,1)S(1)}, bf16[128,768]{1,0:T(8,128)(2,1)S(1)}, u32[]{:S(2)}, u32[]{:S(2)}) %collective-permute-start.27) | collective-permute-done | bytes 196640 | tf_op jit(solution)/shard_map/ppermute | solution.py:19
  114.1 2.5 %collective-permute-start.28 = (bf16[64,768]{1,0:T(8,128)(2,1)S(1)}, bf16[64,768]{1,0:T(8,128)(2,1)S(1)}, u32[]{:S(2)}, u32[]{:S(2)}) collective-permute-start(bf16[64,768]{1,0:T(8,128)(2,1)S(1)} %get-tuple-element.80), channel_id=1, source_target_pairs={{0,2},{1,3},{2,0},{3,1},{4,6},{5,7},{6,4},{7,5},{8,10},{9,11},{10,... | collective-permute-start | bytes 294920 | tf_op jit(solution)/shard_map/ppermute | solution.py:19
  116.7 3.3 %collective-permute-done.31 = bf16[96,1536]{1,0:T(8,128)(2,1)S(1)} collective-permute-done((bf16[96,1536]{1,0:T(8,128)(2,1)S(1)}, bf16[96,1536]{1,0:T(8,128)(2,1)S(1)}, u32[]{:S(2)}, u32[]{:S(2)}) %collective-permute-start.31) | collective-permute-done | bytes 294944 | tf_op jit(solution)/shard_map/ppermute | solution.py:19
  120.1 0.9 fusion.2
  121.0 0.7 fusion
  (63 shorter events, 6.9 us)
Async XLA Ops:
  0.6 24.2 %copy-start.4 = (bf16[96,512]{1,0:T(8,128)(2,1)S(1)}, bf16[96,512]{1,0:T(8,128)(2,1)}, u32[]{:S(2)}) copy-start(bf16[96,512]{1,0:T(8,128)(2,1)} %refs_0_.3) | copy-start | bytes 294916
  0.6 24.2 %copy-start.5 = (bf16[96,512]{1,0:T(8,128)(2,1)S(1)}, bf16[96,512]{1,0:T(8,128)(2,1)}, u32[]{:S(2)}) copy-start(bf16[96,512]{1,0:T(8,128)(2,1)} %refs_1_.4) | copy-start | bytes 294916
  0.7 24.2 %copy-start.6 = (bf16[96,512]{1,0:T(8,128)(2,1)S(1)}, bf16[96,512]{1,0:T(8,128)(2,1)}, u32[]{:S(2)}) copy-start(bf16[96,512]{1,0:T(8,128)(2,1)} %refs_2_.4) | copy-start | bytes 294916
  0.7 24.2 %copy-start.7 = (bf16[96,512]{1,0:T(8,128)(2,1)S(1)}, bf16[96,512]{1,0:T(8,128)(2,1)}, u32[]{:S(2)}) copy-start(bf16[96,512]{1,0:T(8,128)(2,1)} %refs_3_.4) | copy-start | bytes 294916
  2.7 13.5 %collective-permute-start.1 = (bf16[64,1536]{1,0:T(8,128)(2,1)}, bf16[64,1536]{1,0:T(8,128)(2,1)S(1)}, u32[]{:S(2)}, u32[]{:S(2)}) collective-permute-start(bf16[64,1536]{1,0:T(8,128)(2,1)} %get-tuple-element.47.refs_2_), channel_id=1, source_target_pairs={{0,2},{1,3},{2,0},{3,1},{4,6},{5,7},{6,4},{7,5},{8,10},{9,11},{10,... | collective-permute-start | bytes 589832 | tf_op jit(solution)/shard_map/ppermute | solution.py:19
  6.8 13.2 %collective-permute-start.3 = (bf16[96,1536]{1,0:T(8,128)(2,1)}, bf16[96,1536]{1,0:T(8,128)(2,1)S(1)}, u32[]{:S(2)}, u32[]{:S(2)}) collective-permute-start(bf16[96,1536]{1,0:T(8,128)(2,1)} %get-tuple-element.49.refs_0_), channel_id=1, source_target_pairs={{0,24},{4,28},{8,16},{12,20},{16,8},{20,12},{24,0},{28,4},{1,25},{... | collective-permute-start | bytes 884744 | tf_op jit(solution)/shard_map/ppermute | solution.py:19
  9.3 13.4 %collective-permute-start.4 = (bf16[96,1536]{1,0:T(8,128)(2,1)}, bf16[96,1536]{1,0:T(8,128)(2,1)S(1)}, u32[]{:S(2)}, u32[]{:S(2)}) collective-permute-start(bf16[96,1536]{1,0:T(8,128)(2,1)} %get-tuple-element.49.refs_0_), channel_id=1, source_target_pairs={{0,16},{4,20},{8,24},{12,28},{16,0},{20,4},{24,8},{28,12},{1,17},{... | collective-permute-start | bytes 884744 | tf_op jit(solution)/shard_map/ppermute | solution.py:19
  9.8 13.0 %collective-permute-start.5 = (bf16[96,1536]{1,0:T(8,128)(2,1)}, bf16[96,1536]{1,0:T(8,128)(2,1)S(1)}, u32[]{:S(2)}, u32[]{:S(2)}) collective-permute-start(bf16[96,1536]{1,0:T(8,128)(2,1)} %get-tuple-element.49.refs_0_), channel_id=1, source_target_pairs={{0,8},{4,12},{8,0},{12,4},{16,24},{20,28},{24,16},{28,20},{1,9},{5... | collective-permute-start | bytes 884744 | tf_op jit(solution)/shard_map/ppermute | solution.py:19
  10.3 9.7 %collective-permute-start = (bf16[64,1536]{1,0:T(8,128)(2,1)}, bf16[64,1536]{1,0:T(8,128)(2,1)S(1)}, u32[]{:S(2)}, u32[]{:S(2)}) collective-permute-start(bf16[64,1536]{1,0:T(8,128)(2,1)} %get-tuple-element.47.refs_2_), channel_id=1, source_target_pairs={{0,1},{1,0},{2,3},{3,2},{4,5},{5,4},{6,7},{7,6},{8,9},{9,8},{10,11... | collective-permute-start | bytes 589832 | tf_op jit(solution)/shard_map/ppermute | solution.py:19
  16.3 7.1 %collective-permute-start.2 = (bf16[64,1536]{1,0:T(8,128)(2,1)S(1)}, bf16[64,1536]{1,0:T(8,128)(2,1)S(1)}, u32[]{:S(2)}, u32[]{:S(2)}) collective-permute-start(bf16[64,1536]{1,0:T(8,128)(2,1)S(1)} %collective-permute-done.1.refs_4_.refs_5_), channel_id=1, source_target_pairs={{0,1},{1,0},{2,3},{3,2},{4,5},{5,4},{6,7},{7,6},{8,9},{9,8},{10,11... | collective-permute-start | bytes 589832 | tf_op jit(solution)/shard_map/ppermute | solution.py:19
  23.3 1.0 copy-start.2
  24.7 3.9 %copy-start.3 = (bf16[64,1536]{1,0:T(8,128)(2,1)S(1)}, bf16[64,1536]{1,0:T(8,128)(2,1)}, u32[]{:S(2)}) copy-start(bf16[64,1536]{1,0:T(8,128)(2,1)} %get-tuple-element.47.refs_2_) | copy-start | bytes 589828
  24.7 3.9 %copy-start.9 = (f32[768]{0:T(1024)S(1)}, f32[768]{0:T(1024)}, u32[]{:S(2)}) copy-start(f32[768]{0:T(1024)} %refs_1_.3) | copy-start | bytes 9220
  24.7 4.2 %collective-permute-start.6 = (bf16[384,1536]{1,0:T(8,128)(2,1)S(1)}, bf16[384,1536]{1,0:T(8,128)(2,1)S(1)}, u32[]{:S(2)}, u32[]{:S(2)}) collective-permute-start(bf16[384,1536]{1,0:T(8,128)(2,1)S(1)} %shard_map.182.refs_2_.refs_4_), channel_id=1, source_target_pairs={{0,4},{4,0},{8,12},{12,8},{16,20},{20,16},{24,28},{28,24},{1,5},{5... | collective-permute-start | bytes 3538952 | tf_op jit(solution)/shard_map/ppermute | solution.py:19
  25.0 13.0 %collective-permute-start.10 = (bf16[96,2048]{1,0:T(8,128)(2,1)S(1)}, bf16[96,2048]{1,0:T(8,128)(2,1)}, u32[]{:S(2)}, u32[]{:S(2)}) collective-permute-start(bf16[96,2048]{1,0:T(8,128)(2,1)S(1)} %shard_map.184.refs_6_), channel_id=1, source_target_pairs={{0,24},{4,28},{8,16},{12,20},{16,8},{20,12},{24,0},{28,4},{1,25},{... | collective-permute-start | bytes 1179656 | tf_op jit(solution)/shard_map/ppermute | solution.py:19
  27.6 18.4 %collective-permute-start.11 = (bf16[96,2048]{1,0:T(8,128)(2,1)S(1)}, bf16[96,2048]{1,0:T(8,128)(2,1)}, u32[]{:S(2)}, u32[]{:S(2)}) collective-permute-start(bf16[96,2048]{1,0:T(8,128)(2,1)S(1)} %shard_map.184.refs_6_), channel_id=1, source_target_pairs={{0,16},{4,20},{8,24},{12,28},{16,0},{20,4},{24,8},{28,12},{1,17},{... | collective-permute-start | bytes 1179656 | tf_op jit(solution)/shard_map/ppermute | solution.py:19
  28.1 18.1 %collective-permute-start.12 = (bf16[96,2048]{1,0:T(8,128)(2,1)S(1)}, bf16[96,2048]{1,0:T(8,128)(2,1)}, u32[]{:S(2)}, u32[]{:S(2)}) collective-permute-start(bf16[96,2048]{1,0:T(8,128)(2,1)S(1)} %shard_map.184.refs_6_), channel_id=1, source_target_pairs={{0,8},{4,12},{8,0},{12,4},{16,24},{20,28},{24,16},{28,20},{1,9},{5... | collective-permute-start | bytes 1179656 | tf_op jit(solution)/shard_map/ppermute | solution.py:19
  28.9 17.3 %copy-start = (bf16[1,64,768]{2,1,0:T(8,128)(2,1)S(1)}, bf16[1,64,768]{2,1,0:T(8,128)(2,1)}, u32[]{:S(2)}) copy-start(bf16[1,64,768]{2,1,0:T(8,128)(2,1)} %param.13) | copy-start | bytes 294916
  28.9 17.3 %copy-start.8 = (f32[768]{0:T(1024)S(1)}, f32[768]{0:T(1024)}, u32[]{:S(2)}) copy-start(f32[768]{0:T(1024)} %refs_0_.5) | copy-start | bytes 9220
  30.6 15.5 %collective-permute-start.7 = (bf16[64,768]{1,0:T(8,128)(2,1)S(1)}, bf16[64,768]{1,0:T(8,128)(2,1)S(1)}, u32[]{:S(2)}, u32[]{:S(2)}) collective-permute-start(bf16[64,768]{1,0:T(8,128)(2,1)S(1)} %get-tuple-element.51), channel_id=1, source_target_pairs={{0,1},{1,0},{2,3},{3,2},{4,5},{5,4},{6,7},{7,6},{8,9},{9,8},{10,11... | collective-permute-start | bytes 294920 | tf_op jit(solution)/shard_map/ppermute | solution.py:19
  31.8 14.4 %collective-permute-start.8 = (bf16[64,768]{1,0:T(8,128)(2,1)S(1)}, bf16[64,768]{1,0:T(8,128)(2,1)S(1)}, u32[]{:S(2)}, u32[]{:S(2)}) collective-permute-start(bf16[64,768]{1,0:T(8,128)(2,1)S(1)} %get-tuple-element.52), channel_id=1, source_target_pairs={{0,2},{1,3},{2,0},{3,1},{4,6},{5,7},{6,4},{7,5},{8,10},{9,11},{10,... | collective-permute-start | bytes 294920 | tf_op jit(solution)/shard_map/ppermute | solution.py:19
  38.1 8.1 %collective-permute-start.9 = (bf16[64,768]{1,0:T(8,128)(2,1)S(1)}, bf16[64,768]{1,0:T(8,128)(2,1)S(1)}, u32[]{:S(2)}, u32[]{:S(2)}) collective-permute-start(bf16[64,768]{1,0:T(8,128)(2,1)S(1)} %get-tuple-element.53), channel_id=1, source_target_pairs={{0,3},{1,2},{2,1},{3,0},{4,7},{5,6},{6,5},{7,4},{8,11},{9,10},{10,... | collective-permute-start | bytes 294920 | tf_op jit(solution)/shard_map/ppermute | solution.py:19
  47.8 4.5 %collective-permute-start.16 = (bf16[384,2048]{1,0:T(8,128)(2,1)S(1)}, bf16[384,2048]{1,0:T(8,128)(2,1)S(1)}, u32[]{:S(2)}, u32[]{:S(2)}) collective-permute-start(bf16[384,2048]{1,0:T(8,128)(2,1)S(1)} %get-tuple-element.57.refs_2_), channel_id=1, source_target_pairs={{0,4},{4,0},{8,12},{12,8},{16,20},{20,16},{24,28},{28,24},{1,5},{5... | collective-permute-start | bytes 4718600 | tf_op jit(solution)/shard_map/ppermute | solution.py:19
  47.9 6.8 %collective-permute-start.13 = (bf16[64,768]{1,0:T(8,128)(2,1)S(1)}, bf16[64,768]{1,0:T(8,128)(2,1)S(1)}, u32[]{:S(2)}, u32[]{:S(2)}) collective-permute-start(bf16[64,768]{1,0:T(8,128)(2,1)S(1)} %get-tuple-element.55.refs_4_), channel_id=1, source_target_pairs={{0,1},{1,0},{2,3},{3,2},{4,5},{5,4},{6,7},{7,6},{8,9},{9,8},{10,11... | collective-permute-start | bytes 294920 | tf_op jit(solution)/shard_map/ppermute | solution.py:19
  48.9 10.8 %collective-permute-start.14 = (bf16[64,768]{1,0:T(8,128)(2,1)S(1)}, bf16[64,768]{1,0:T(8,128)(2,1)S(1)}, u32[]{:S(2)}, u32[]{:S(2)}) collective-permute-start(bf16[64,768]{1,0:T(8,128)(2,1)S(1)} %get-tuple-element.55.refs_4_), channel_id=1, source_target_pairs={{0,2},{1,3},{2,0},{3,1},{4,6},{5,7},{6,4},{7,5},{8,10},{9,11},{10,... | collective-permute-start | bytes 294920 | tf_op jit(solution)/shard_map/ppermute | solution.py:19
  51.7 8.0 %collective-permute-start.15 = (bf16[64,768]{1,0:T(8,128)(2,1)S(1)}, bf16[64,768]{1,0:T(8,128)(2,1)S(1)}, u32[]{:S(2)}, u32[]{:S(2)}) collective-permute-start(bf16[64,768]{1,0:T(8,128)(2,1)S(1)} %get-tuple-element.55.refs_4_), channel_id=1, source_target_pairs={{0,3},{1,2},{2,1},{3,0},{4,7},{5,6},{6,5},{7,4},{8,11},{9,10},{10,... | collective-permute-start | bytes 294920 | tf_op jit(solution)/shard_map/ppermute | solution.py:19
  52.4 7.3 %copy-start.10 = (f32[4,9]{1,0:T(4,128)S(1)}, f32[4,9]{1,0:T(4,128)}, u32[]{:S(2)}) copy-start(f32[4,9]{1,0:T(4,128)} %refs_1_.5) | copy-start | bytes 436
  52.4 7.3 %copy-start.11 = (s32[1,256]{1,0:T(1,128)S(1)}, s32[1,256]{1,0:T(1,128)}, u32[]{:S(2)}) copy-start(s32[1,256]{1,0:T(1,128)} %refs_2_.5) | copy-start | bytes 3076
  52.4 7.3 %copy-start.12 = (s32[1,256]{1,0:T(1,128)S(1)}, s32[1,256]{1,0:T(1,128)}, u32[]{:S(2)}) copy-start(s32[1,256]{1,0:T(1,128)} %refs_3_.5) | copy-start | bytes 3076
  66.0 13.0 %collective-permute-start.23 = (bf16[384,2048]{1,0:T(8,128)(2,1)S(1)}, bf16[384,2048]{1,0:T(8,128)(2,1)S(1)}, u32[]{:S(2)}, u32[]{:S(2)}) collective-permute-start(bf16[384,2048]{1,0:T(8,128)(2,1)S(1)} %get-tuple-element.72), channel_id=1, source_target_pairs={{0,4},{4,0},{8,12},{12,8},{16,20},{20,16},{24,28},{28,24},{1,5},{5... | collective-permute-start | bytes 4718600 | tf_op jit(solution)/shard_map/ppermute | solution.py:19
  66.1 5.5 %collective-permute-start.17 = (bf16[64,768]{1,0:T(8,128)(2,1)S(1)}, bf16[64,768]{1,0:T(8,128)(2,1)S(1)}, u32[]{:S(2)}, u32[]{:S(2)}) collective-permute-start(bf16[64,768]{1,0:T(8,128)(2,1)S(1)} %get-tuple-element.65), channel_id=1, source_target_pairs={{0,1},{1,0},{2,3},{3,2},{4,5},{5,4},{6,7},{7,6},{8,9},{9,8},{10,11... | collective-permute-start | bytes 294920 | tf_op jit(solution)/shard_map/ppermute | solution.py:19
  68.2 10.8 %collective-permute-start.18 = (bf16[64,768]{1,0:T(8,128)(2,1)S(1)}, bf16[64,768]{1,0:T(8,128)(2,1)S(1)}, u32[]{:S(2)}, u32[]{:S(2)}) collective-permute-start(bf16[64,768]{1,0:T(8,128)(2,1)S(1)} %get-tuple-element.66), channel_id=1, source_target_pairs={{0,2},{1,3},{2,0},{3,1},{4,6},{5,7},{6,4},{7,5},{8,10},{9,11},{10,... | collective-permute-start | bytes 294920 | tf_op jit(solution)/shard_map/ppermute | solution.py:19
  69.3 9.7 %collective-permute-start.19 = (bf16[64,768]{1,0:T(8,128)(2,1)S(1)}, bf16[64,768]{1,0:T(8,128)(2,1)S(1)}, u32[]{:S(2)}, u32[]{:S(2)}) collective-permute-start(bf16[64,768]{1,0:T(8,128)(2,1)S(1)} %get-tuple-element.67), channel_id=1, source_target_pairs={{0,3},{1,2},{2,1},{3,0},{4,7},{5,6},{6,5},{7,4},{8,11},{9,10},{10,... | collective-permute-start | bytes 294920 | tf_op jit(solution)/shard_map/ppermute | solution.py:19
  79.0 2.7 %copy-start.1 = (bf16[1,64,768]{2,1,0:T(8,128)(2,1)S(1)}, bf16[1,64,768]{2,1,0:T(8,128)(2,1)}, u32[]{:S(2)}) copy-start(bf16[1,64,768]{2,1,0:T(8,128)(2,1)} %param.25) | copy-start | bytes 294916
  79.3 13.9 %collective-permute-start.24 = (bf16[96,2048]{1,0:T(8,128)(2,1)S(1)}, bf16[96,2048]{1,0:T(8,128)(2,1)S(1)}, u32[]{:S(2)}, u32[]{:S(2)}) collective-permute-start(bf16[96,2048]{1,0:T(8,128)(2,1)S(1)} %get-tuple-element.73), channel_id=1, source_target_pairs={{0,8},{4,12},{8,0},{12,4},{16,24},{20,28},{24,16},{28,20},{1,9},{5... | collective-permute-start | bytes 1179656 | tf_op jit(solution)/shard_map/ppermute | solution.py:19
  80.9 12.4 %collective-permute-start.25 = (bf16[96,2048]{1,0:T(8,128)(2,1)S(1)}, bf16[96,2048]{1,0:T(8,128)(2,1)S(1)}, u32[]{:S(2)}, u32[]{:S(2)}) collective-permute-start(bf16[96,2048]{1,0:T(8,128)(2,1)S(1)} %get-tuple-element.74), channel_id=1, source_target_pairs={{0,16},{4,20},{8,24},{12,28},{16,0},{20,4},{24,8},{28,12},{1,17},{... | collective-permute-start | bytes 1179656 | tf_op jit(solution)/shard_map/ppermute | solution.py:19
  81.9 5.7 %collective-permute-start.20 = (bf16[64,768]{1,0:T(8,128)(2,1)S(1)}, bf16[64,768]{1,0:T(8,128)(2,1)S(1)}, u32[]{:S(2)}, u32[]{:S(2)}) collective-permute-start(bf16[64,768]{1,0:T(8,128)(2,1)S(1)} %shard_map.188.refs_5_), channel_id=1, source_target_pairs={{0,1},{1,0},{2,3},{3,2},{4,5},{5,4},{6,7},{7,6},{8,9},{9,8},{10,11... | collective-permute-start | bytes 294920 | tf_op jit(solution)/shard_map/ppermute | solution.py:19
  83.9 9.4 %collective-permute-start.21 = (bf16[64,768]{1,0:T(8,128)(2,1)S(1)}, bf16[64,768]{1,0:T(8,128)(2,1)S(1)}, u32[]{:S(2)}, u32[]{:S(2)}) collective-permute-start(bf16[64,768]{1,0:T(8,128)(2,1)S(1)} %shard_map.188.refs_5_), channel_id=1, source_target_pairs={{0,2},{1,3},{2,0},{3,1},{4,6},{5,7},{6,4},{7,5},{8,10},{9,11},{10,... | collective-permute-start | bytes 294920 | tf_op jit(solution)/shard_map/ppermute | solution.py:19
  84.9 8.4 %collective-permute-start.22 = (bf16[64,768]{1,0:T(8,128)(2,1)S(1)}, bf16[64,768]{1,0:T(8,128)(2,1)S(1)}, u32[]{:S(2)}, u32[]{:S(2)}) collective-permute-start(bf16[64,768]{1,0:T(8,128)(2,1)S(1)} %shard_map.188.refs_5_), channel_id=1, source_target_pairs={{0,3},{1,2},{2,1},{3,0},{4,7},{5,6},{6,5},{7,4},{8,11},{9,10},{10,... | collective-permute-start | bytes 294920 | tf_op jit(solution)/shard_map/ppermute | solution.py:19
  94.8 2.9 %collective-permute-start.26 = (bf16[384,1536]{1,0:T(8,128)(2,1)S(1)}, bf16[384,1536]{1,0:T(8,128)(2,1)S(1)}, u32[]{:S(2)}, u32[]{:S(2)}) collective-permute-start(bf16[384,1536]{1,0:T(8,128)(2,1)S(1)} %get-tuple-element.76), channel_id=1, source_target_pairs={{0,4},{4,0},{8,12},{12,8},{16,20},{20,16},{24,28},{28,24},{1,5},{5... | collective-permute-start | bytes 3538952 | tf_op jit(solution)/shard_map/ppermute | solution.py:19
  94.9 12.9 %collective-permute-start.32 = (bf16[96,2048]{1,0:T(8,128)(2,1)S(1)}, bf16[96,2048]{1,0:T(8,128)(2,1)S(1)}, u32[]{:S(2)}, u32[]{:S(2)}) collective-permute-start(bf16[96,2048]{1,0:T(8,128)(2,1)S(1)} %get-tuple-element.86), channel_id=1, source_target_pairs={{0,24},{4,28},{8,16},{12,20},{16,8},{20,12},{24,0},{28,4},{1,25},{... | collective-permute-start | bytes 1179656 | tf_op jit(solution)/shard_map/ppermute | solution.py:19
  98.0 18.7 %collective-permute-start.29 = (bf16[96,1536]{1,0:T(8,128)(2,1)S(1)}, bf16[96,1536]{1,0:T(8,128)(2,1)S(1)}, u32[]{:S(2)}, u32[]{:S(2)}) collective-permute-start(bf16[96,1536]{1,0:T(8,128)(2,1)S(1)} %get-tuple-element.82), channel_id=1, source_target_pairs={{0,8},{4,12},{8,0},{12,4},{16,24},{20,28},{24,16},{28,20},{1,9},{5... | collective-permute-start | bytes 884744 | tf_op jit(solution)/shard_map/ppermute | solution.py:19
  99.3 17.4 %collective-permute-start.30 = (bf16[96,1536]{1,0:T(8,128)(2,1)S(1)}, bf16[96,1536]{1,0:T(8,128)(2,1)S(1)}, u32[]{:S(2)}, u32[]{:S(2)}) collective-permute-start(bf16[96,1536]{1,0:T(8,128)(2,1)S(1)} %get-tuple-element.83), channel_id=1, source_target_pairs={{0,16},{4,20},{8,24},{12,28},{16,0},{20,4},{24,8},{28,12},{1,17},{... | collective-permute-start | bytes 884744 | tf_op jit(solution)/shard_map/ppermute | solution.py:19
  99.9 20.1 %collective-permute-start.31 = (bf16[96,1536]{1,0:T(8,128)(2,1)S(1)}, bf16[96,1536]{1,0:T(8,128)(2,1)S(1)}, u32[]{:S(2)}, u32[]{:S(2)}) collective-permute-start(bf16[96,1536]{1,0:T(8,128)(2,1)S(1)} %get-tuple-element.84), channel_id=1, source_target_pairs={{0,24},{4,28},{8,16},{12,20},{16,8},{20,12},{24,0},{28,4},{1,25},{... | collective-permute-start | bytes 884744 | tf_op jit(solution)/shard_map/ppermute | solution.py:19
  108.0 6.1 %collective-permute-start.27 = (bf16[128,768]{1,0:T(8,128)(2,1)S(1)}, bf16[128,768]{1,0:T(8,128)(2,1)S(1)}, u32[]{:S(2)}, u32[]{:S(2)}) collective-permute-start(bf16[128,768]{1,0:T(8,128)(2,1)S(1)} %get-tuple-element.78), channel_id=1, source_target_pairs={{0,1},{1,0},{2,3},{3,2},{4,5},{5,4},{6,7},{7,6},{8,9},{9,8},{10,11... | collective-permute-start | bytes 589832 | tf_op jit(solution)/shard_map/ppermute | solution.py:19
  114.1 6.8 %collective-permute-start.28 = (bf16[64,768]{1,0:T(8,128)(2,1)S(1)}, bf16[64,768]{1,0:T(8,128)(2,1)S(1)}, u32[]{:S(2)}, u32[]{:S(2)}) collective-permute-start(bf16[64,768]{1,0:T(8,128)(2,1)S(1)} %get-tuple-element.80), channel_id=1, source_target_pairs={{0,2},{1,3},{2,0},{3,1},{4,6},{5,7},{6,4},{7,5},{8,10},{9,11},{10,... | collective-permute-start | bytes 294920 | tf_op jit(solution)/shard_map/ppermute | solution.py:19

commit v7 on v6

--- a/solution.py
+++ b/solution.py
@@ -137,22 +137,15 @@
 
 
 def mid_kernel(parts, *refs):
-    gain, frames = refs[0], refs[1]
+    gain, frames = refs[:2]
     pieces = refs[2 : 2 + parts]
-    stacked = 4 if len(refs) > parts + 4 else 0
-    weights = refs[2 + parts : 2 + parts + stacked]
-    mid_out, normed_out = refs[2 + parts + stacked : 4 + parts + stacked]
-    copies = []
-    if stacked:
-        near, sems = refs[-2:]
-        copies = start_copies(row_pairs(weights, near), sems)
+    mid_out, normed_out = refs[2 + parts :]
     total = pieces[0][...].astype(F32)
     for piece in pieces[1:]:
         total = total + piece[...].astype(F32)
     mid = frames[...].astype(F32) + 0.5 * total
     mid_out[...] = mid
     normed_out[...] = (normalise(mid)[0] * gain[...].reshape(1, -1)).astype(BF)
-    wait_copies(copies)
 
 
 def collect_kernel(ids, me_ref, scaled, near, far, out, grad_context, sems):
@@ -433,19 +426,19 @@
         far=2 if direct_rows else 0,
     )
     summed = scatter_frames(ffn_partials)
-    near = [shape((model // 2, 4 * inner), BF)] if direct_rows else []
-    mid_own, normed_own, *near = call(
+    mid_own, normed_own = call(
         functools.partial(mid_kernel, len(summed)),
-        [shape((own, model), F32), shape((own, model), BF)] + near,
-        [attn_gain, frames_own] + summed + attn_pieces,
-        far=len(attn_pieces),
+        [shape((own, model), F32), shape((own, model), BF)],
+        [attn_gain, frames_own] + summed,
+        after=attn_pieces[1:],
     )
     normed_parts = gather_frames(normed_own)
     if direct_rows:
+        near = stack(attn_pieces, [normed_own])
         attn_weights, grad_context = call(
             functools.partial(collect_kernel, ids),
             [shape((model, 4 * inner), BF), shape((frames, inner), BF)],
-            [me, scaled_cot, near[0], exchange(near[0], "dp", 1)],
+            [me, scaled_cot, near, exchange(near, "dp", 1)],
             flops=2 * frames * model * inner,
             smem=1,
             far=2,

time: 122 us -> 121 us (level)
    pallas_call x14 -> x15, Pallas kernels: 17 us -> 17.4 us  [call(): pl.pallas_call(lambda *refs: body(*refs[:count], *refs[count + len(after)...]
  transfers between devices with their start and end apart: 33 -> 33, of which waited for: 18 -> 18; matrix products, arithmetic and copies ran while one was open for 2% -> 2% of each run, Pallas kernels for 4% -> 5%
where the time goes in v7:
time: 121 us
  waiting for transfers between devices  53.1 us (44%)
  starting transfers between devices  45.8 us (38%)
  Pallas kernels  17.4 us (14%)
  local copies, waits for them, and re-layouts  2.75 us (2%)
    ppermute x33, waiting for transfers between devices, exchange(): lax.ppermute(values, axis, [(one, one ^ mask) for one in range(size)])  53.1 us
    ppermute x33, starting transfers between devices, exchange(): lax.ppermute(values, axis, [(one, one ^ mask) for one in range(size)])  45.8 us
    pallas_call x15, Pallas kernels, call(): pl.pallas_call(lambda *refs: body(*refs[:count], *refs[count + len(after)...  17.4 us
  transfers between devices with their start and end apart: 33, of which 18 were waited for; matrix products, arithmetic and copies ran while one was open for 2% of the time, Pallas kernels for 5%

profile of v7, /device:TPU:0, one launch (start us, length us, event | category | flops | bytes accessed | tf_op | source)
XLA Modules:
  0.0 121.0 jit_solution(18399876830245313296)
XLA Ops:
  0.7 2.1 %shard_map.180 = (bf16[64,1536]{1,0:T(8,128)(2,1)}, bf16[96,1536]{1,0:T(8,128)(2,1)}) custom-call(bf16[64,768]{1,0:T(8,128)(2,1)} %bitcast.6, bf16[64,768]{1,0:T(8,128)(2,1)} %bitcast.8, bf16[96,768]{1,0:T(8,128)(2,1)} %refs_2_.3, bf16[96,768]{1,0:T(8,128)(2,1)} %refs_3_.3), custom_call_target="tpu_custom_call" | custom-call | bytes 983040 | tf_op jit(solution)/shard_map/pallas_call | solution.py:31
  2.7 4.1 %collective-permute-start.1 = (bf16[64,1536]{1,0:T(8,128)(2,1)}, bf16[64,1536]{1,0:T(8,128)(2,1)S(1)}, u32[]{:S(2)}, u32[]{:S(2)}) collective-permute-start(bf16[64,1536]{1,0:T(8,128)(2,1)} %get-tuple-element.46.refs_2_), channel_id=1, source_target_pairs={{0,2},{1,3},{2,0},{3,1},{4,6},{5,7},{6,4},{7,5},{8,10},{9,11},{10,... | collective-permute-start | bytes 589832 | tf_op jit(solution)/shard_map/ppermute | solution.py:19
  6.8 2.4 %collective-permute-start.3 = (bf16[96,1536]{1,0:T(8,128)(2,1)}, bf16[96,1536]{1,0:T(8,128)(2,1)S(1)}, u32[]{:S(2)}, u32[]{:S(2)}) collective-permute-start(bf16[96,1536]{1,0:T(8,128)(2,1)} %get-tuple-element.48.refs_0_), channel_id=1, source_target_pairs={{0,24},{4,28},{8,16},{12,20},{16,8},{20,12},{24,0},{28,4},{1,25},{... | collective-permute-start | bytes 884744 | tf_op jit(solution)/shard_map/ppermute | solution.py:19
  10.3 1.6 %collective-permute-start = (bf16[64,1536]{1,0:T(8,128)(2,1)}, bf16[64,1536]{1,0:T(8,128)(2,1)S(1)}, u32[]{:S(2)}, u32[]{:S(2)}) collective-permute-start(bf16[64,1536]{1,0:T(8,128)(2,1)} %get-tuple-element.46.refs_2_), channel_id=1, source_target_pairs={{0,1},{1,0},{2,3},{3,2},{4,5},{5,4},{6,7},{7,6},{8,9},{9,8},{10,11... | collective-permute-start | bytes 589832 | tf_op jit(solution)/shard_map/ppermute | solution.py:19
  11.9 4.4 %collective-permute-done.1.refs_4_.refs_5_ = bf16[64,1536]{1,0:T(8,128)(2,1)S(1)} collective-permute-done((bf16[64,1536]{1,0:T(8,128)(2,1)}, bf16[64,1536]{1,0:T(8,128)(2,1)S(1)}, u32[]{:S(2)}, u32[]{:S(2)}) %collective-permute-start.1) | collective-permute-done | bytes 196640 | tf_op jit(solution)/shard_map/ppermute | solution.py:19
  16.3 0.8 collective-permute-start.2
  17.0 3.0 %collective-permute-done.refs_3_.refs_4_ = bf16[64,1536]{1,0:T(8,128)(2,1)S(1)} collective-permute-done((bf16[64,1536]{1,0:T(8,128)(2,1)}, bf16[64,1536]{1,0:T(8,128)(2,1)S(1)}, u32[]{:S(2)}, u32[]{:S(2)}) %collective-permute-start) | collective-permute-done | bytes 196640 | tf_op jit(solution)/shard_map/ppermute | solution.py:19
  20.1 2.7 %collective-permute-done.4.refs_2_ = bf16[96,1536]{1,0:T(8,128)(2,1)S(1)} collective-permute-done((bf16[96,1536]{1,0:T(8,128)(2,1)}, bf16[96,1536]{1,0:T(8,128)(2,1)S(1)}, u32[]{:S(2)}, u32[]{:S(2)}) %collective-permute-start.4) | collective-permute-done | bytes 294944 | tf_op jit(solution)/shard_map/ppermute | solution.py:19
  23.3 1.0 copy-done.2
  25.0 2.6 %collective-permute-start.10 = (bf16[96,2048]{1,0:T(8,128)(2,1)S(1)}, bf16[96,2048]{1,0:T(8,128)(2,1)S(1)}, u32[]{:S(2)}, u32[]{:S(2)}) collective-permute-start(bf16[96,2048]{1,0:T(8,128)(2,1)S(1)} %shard_map.184.refs_0_), channel_id=1, source_target_pairs={{0,24},{4,28},{8,16},{12,20},{16,8},{20,12},{24,0},{28,4},{1,25},{... | collective-permute-start | bytes 1179656 | tf_op jit(solution)/shard_map/ppermute | solution.py:19
  29.0 2.5 %shard_map.183 = (f32[256,768]{1,0:T(8,128)S(1)}, bf16[256,768]{1,0:T(8,128)(2,1)S(1)}, bf16[768,768]{1,0:T(8,128)(2,1)S(1)}, bf16[64,768]{1,0:T(8,128)(2,1)S(1)...) custom-call(s32[1]{0:T(128)} %bitcast.1.refs_0_, ...), custom_call_target="tpu_custom_call" | custom-call | flops 603979776 | bytes 5505028 | tf_op jit(solution)/shard_map/pallas_call | solution.py:31
  31.5 1.2 collective-permute-start.7
  32.7 2.7 %collective-permute-start.8 = (bf16[64,768]{1,0:T(8,128)(2,1)S(1)}, bf16[64,768]{1,0:T(8,128)(2,1)S(1)}, u32[]{:S(2)}, u32[]{:S(2)}) collective-permute-start(bf16[64,768]{1,0:T(8,128)(2,1)S(1)} %get-tuple-element.51), channel_id=1, source_target_pairs={{0,2},{1,3},{2,0},{3,1},{4,6},{5,7},{6,4},{7,5},{8,10},{9,11},{10,... | collective-permute-start | bytes 294920 | tf_op jit(solution)/shard_map/ppermute | solution.py:19
  35.4 2.6 %collective-permute-done.10.refs_6_.refs_1_ = bf16[96,2048]{1,0:T(8,128)(2,1)S(1)} collective-permute-done((bf16[96,2048]{1,0:T(8,128)(2,1)S(1)}, bf16[96,2048]{1,0:T(8,128)(2,1)S(1)}, u32[]{:S(2)}, u32[]{:S(2)}) %collective-permute-start.10) | collective-permute-done | bytes 393248 | tf_op jit(solution)/shard_map/ppermute | solution.py:19
  38.0 3.2 %collective-permute-start.9 = (bf16[64,768]{1,0:T(8,128)(2,1)S(1)}, bf16[64,768]{1,0:T(8,128)(2,1)S(1)}, u32[]{:S(2)}, u32[]{:S(2)}) collective-permute-start(bf16[64,768]{1,0:T(8,128)(2,1)S(1)} %get-tuple-element.52), channel_id=1, source_target_pairs={{0,3},{1,2},{2,1},{3,0},{4,7},{5,6},{6,5},{7,4},{8,11},{9,10},{10,... | collective-permute-start | bytes 294920 | tf_op jit(solution)/shard_map/ppermute | solution.py:19
  41.2 4.7 %collective-permute-done.11.refs_7_.refs_2_ = bf16[96,2048]{1,0:T(8,128)(2,1)S(1)} collective-permute-done((bf16[96,2048]{1,0:T(8,128)(2,1)S(1)}, bf16[96,2048]{1,0:T(8,128)(2,1)S(1)}, u32[]{:S(2)}, u32[]{:S(2)}) %collective-permute-start.11) | collective-permute-done | bytes 393248 | tf_op jit(solution)/shard_map/ppermute | solution.py:19
  46.3 0.9 shard_map.186.refs_2_
  47.3 1.0 collective-permute-start.13
  48.3 2.8 %collective-permute-start.14 = (bf16[64,768]{1,0:T(8,128)(2,1)S(1)}, bf16[64,768]{1,0:T(8,128)(2,1)S(1)}, u32[]{:S(2)}, u32[]{:S(2)}) collective-permute-start(bf16[64,768]{1,0:T(8,128)(2,1)S(1)} %get-tuple-element.54.refs_4_), channel_id=1, source_target_pairs={{0,2},{1,3},{2,0},{3,1},{4,6},{5,7},{6,4},{7,5},{8,10},{9,11},{10,... | collective-permute-start | bytes 294920 | tf_op jit(solution)/shard_map/ppermute | solution.py:19
  51.8 2.0 %shard_map.187 = (bf16[768,2048]{1,0:T(8,128)(2,1)S(1)}, bf16[256,512]{1,0:T(8,128)(2,1)S(1)}) custom-call(s32[1]{0:T(128)} %bitcast.1.refs_0_, bf16[256,768]{1,0:T(8,128)(2,1)S(1)} %get-tuple-element.55.refs_1_.refs_2_, bf16[384,2048]{1,0:T(8,128)(2,1)S(1)} %shard_map.186.refs_2_, bf16[384,2048]{1,0:T(8,128)(2,1)S(1)} %collective-permute-done.16.refs_3_), custom_call_target="tpu_custom_call" | custom-call | flops 201326592 | bytes 6946820 | tf_op jit(solution)/shard_map/pallas_call | solution.py:31
  54.1 5.0 %collective-permute-done.14.refs_6_ = bf16[64,768]{1,0:T(8,128)(2,1)S(1)} collective-permute-done((bf16[64,768]{1,0:T(8,128)(2,1)S(1)}, bf16[64,768]{1,0:T(8,128)(2,1)S(1)}, u32[]{:S(2)}, u32[]{:S(2)}) %collective-permute-start.14) | collective-permute-done | bytes 98336 | tf_op jit(solution)/shard_map/ppermute | solution.py:19
  59.1 4.8 %shard_map.188 = (bf16[256,768]{1,0:T(8,128)(2,1)S(1)}, bf16[256,512]{1,0:T(8,128)(2,1)S(1)}, bf16[256,1536]{1,0:T(8,128)(2,1)S(1)}, bf16[64,768]{1,0:T(8,128)(2...) custom-call(s32[1]{0:T(128)} %bitcast.2.refs_0_, ...), custom_call_target="tpu_custom_call" | custom-call | flops 2013265920 | bytes 6031508 | tf_op jit(solution)/shard_map/pallas_call | solution.py:31
  63.9 1.5 %shard_map.190 = (bf16[384,2048]{1,0:T(8,128)(2,1)S(1)}, bf16[384,2048]{1,0:T(8,128)(2,1)S(1)}) custom-call(s32[1]{0:T(128)} %bitcast.1.refs_0_, bf16[256,768]{1,0:T(8,128)(2,1)S(1)} %get-tuple-element.66.refs_1_, bf16[256,768]{1,0:T(8,128)(2,1)S(1)} %get-tuple-element.55.refs_1_.refs_2_, bf16[256,512]{1,0:T(8,128)(2,1)S(1)} %get-tuple-element.67.refs_3_, ...), custom_call_target="tpu_custom_call" | custom-call | flops 805306368 | bytes 4980740 | tf_op jit(solution)/shard_map/pallas_call | solution.py:31
  65.5 2.1 %collective-permute-start.17 = (bf16[64,768]{1,0:T(8,128)(2,1)S(1)}, bf16[64,768]{1,0:T(8,128)(2,1)S(1)}, u32[]{:S(2)}, u32[]{:S(2)}) collective-permute-start(bf16[64,768]{1,0:T(8,128)(2,1)S(1)} %get-tuple-element.63), channel_id=1, source_target_pairs={{0,1},{1,0},{2,3},{3,2},{4,5},{5,4},{6,7},{7,6},{8,9},{9,8},{10,11... | collective-permute-start | bytes 294920 | tf_op jit(solution)/shard_map/ppermute | solution.py:19
  67.6 1.0 collective-permute-start.18
  68.7 1.4 %collective-permute-start.19 = (bf16[64,768]{1,0:T(8,128)(2,1)S(1)}, bf16[64,768]{1,0:T(8,128)(2,1)S(1)}, u32[]{:S(2)}, u32[]{:S(2)}) collective-permute-start(bf16[64,768]{1,0:T(8,128)(2,1)S(1)} %get-tuple-element.65), channel_id=1, source_target_pairs={{0,3},{1,2},{2,1},{3,0},{4,7},{5,6},{6,5},{7,4},{8,11},{9,10},{10,... | collective-permute-start | bytes 294920 | tf_op jit(solution)/shard_map/ppermute | solution.py:19
  70.1 0.9 collective-permute-done.17.refs_4_.refs_2_
  71.0 7.4 %collective-permute-done.18.refs_5_.refs_3_ = bf16[64,768]{1,0:T(8,128)(2,1)S(1)} collective-permute-done((bf16[64,768]{1,0:T(8,128)(2,1)S(1)}, bf16[64,768]{1,0:T(8,128)(2,1)S(1)}, u32[]{:S(2)}, u32[]{:S(2)}) %collective-permute-start.18) | collective-permute-done | bytes 98336 | tf_op jit(solution)/shard_map/ppermute | solution.py:19
  78.8 1.6 %collective-permute-start.24 = (bf16[96,2048]{1,0:T(8,128)(2,1)S(1)}, bf16[96,2048]{1,0:T(8,128)(2,1)S(1)}, u32[]{:S(2)}, u32[]{:S(2)}) collective-permute-start(bf16[96,2048]{1,0:T(8,128)(2,1)S(1)} %get-tuple-element.71), channel_id=1, source_target_pairs={{0,8},{4,12},{8,0},{12,4},{16,24},{20,28},{24,16},{28,20},{1,9},{5... | collective-permute-start | bytes 1179656 | tf_op jit(solution)/shard_map/ppermute | solution.py:19
  80.3 0.7 collective-permute-start.25
  81.3 1.9 %collective-permute-start.20 = (bf16[64,768]{1,0:T(8,128)(2,1)S(1)}, bf16[64,768]{1,0:T(8,128)(2,1)S(1)}, u32[]{:S(2)}, u32[]{:S(2)}) collective-permute-start(bf16[64,768]{1,0:T(8,128)(2,1)S(1)} %shard_map.189.refs_5_), channel_id=1, source_target_pairs={{0,1},{1,0},{2,3},{3,2},{4,5},{5,4},{6,7},{7,6},{8,9},{9,8},{10,11... | collective-permute-start | bytes 294920 | tf_op jit(solution)/shard_map/ppermute | solution.py:19
  83.3 1.0 collective-permute-start.21
  84.3 1.5 %collective-permute-start.22 = (bf16[64,768]{1,0:T(8,128)(2,1)S(1)}, bf16[64,768]{1,0:T(8,128)(2,1)S(1)}, u32[]{:S(2)}, u32[]{:S(2)}) collective-permute-start(bf16[64,768]{1,0:T(8,128)(2,1)S(1)} %shard_map.189.refs_5_), channel_id=1, source_target_pairs={{0,3},{1,2},{2,1},{3,0},{4,7},{5,6},{6,5},{7,4},{8,11},{9,10},{10,... | collective-permute-start | bytes 294920 | tf_op jit(solution)/shard_map/ppermute | solution.py:19
  85.8 1.3 %collective-permute-done.20.refs_6_ = bf16[64,768]{1,0:T(8,128)(2,1)S(1)} collective-permute-done((bf16[64,768]{1,0:T(8,128)(2,1)S(1)}, bf16[64,768]{1,0:T(8,128)(2,1)S(1)}, u32[]{:S(2)}, u32[]{:S(2)}) %collective-permute-start.20) | collective-permute-done | bytes 98336 | tf_op jit(solution)/shard_map/ppermute | solution.py:19
  87.1 5.6 %collective-permute-done.21.refs_7_ = bf16[64,768]{1,0:T(8,128)(2,1)S(1)} collective-permute-done((bf16[64,768]{1,0:T(8,128)(2,1)S(1)}, bf16[64,768]{1,0:T(8,128)(2,1)S(1)}, u32[]{:S(2)}, u32[]{:S(2)}) %collective-permute-start.21) | collective-permute-done | bytes 98336 | tf_op jit(solution)/shard_map/ppermute | solution.py:19
  92.7 1.5 %shard_map.192 = (bf16[384,1536]{1,0:T(8,128)(2,1)S(1)}, bf16[384,1536]{1,0:T(8,128)(2,1)S(1)}) custom-call(s32[1]{0:T(128)} %bitcast.1.refs_0_, bf16[256,768]{1,0:T(8,128)(2,1)S(1)} %get-tuple-element.47.refs_1_, f32[256,768]{1,0:T(8,128)S(1)} %get-tuple-element.59.refs_2_, bf16[256,768]{1,0:T(8,128)(2,1)S(1)} %get-tuple-element.60.refs_3_, ...), custom_call_target="tpu_custom_call" | custom-call | flops 905969664 | bytes 5505028 | tf_op jit(solution)/shard_map/pallas_call | solution.py:31
  94.3 1.3 %collective-permute-start.32 = (bf16[96,2048]{1,0:T(8,128)(2,1)S(1)}, bf16[96,2048]{1,0:T(8,128)(2,1)S(1)}, u32[]{:S(2)}, u32[]{:S(2)}) collective-permute-start(bf16[96,2048]{1,0:T(8,128)(2,1)S(1)} %get-tuple-element.84), channel_id=1, source_target_pairs={{0,24},{4,28},{8,16},{12,20},{16,8},{20,12},{24,0},{28,4},{1,25},{... | collective-permute-start | bytes 1179656 | tf_op jit(solution)/shard_map/ppermute | solution.py:19
  95.6 1.5 %collective-permute-done.26.refs_1_ = bf16[384,1536]{1,0:T(8,128)(2,1)S(1)} collective-permute-done((bf16[384,1536]{1,0:T(8,128)(2,1)S(1)}, bf16[384,1536]{1,0:T(8,128)(2,1)S(1)}, u32[]{:S(2)}, u32[]{:S(2)}) %collective-permute-start.26) | collective-permute-done | bytes 1179680 | tf_op jit(solution)/shard_map/ppermute | solution.py:19
  97.4 1.3 %collective-permute-start.29 = (bf16[96,1536]{1,0:T(8,128)(2,1)S(1)}, bf16[96,1536]{1,0:T(8,128)(2,1)S(1)}, u32[]{:S(2)}, u32[]{:S(2)}) collective-permute-start(bf16[96,1536]{1,0:T(8,128)(2,1)S(1)} %get-tuple-element.80), channel_id=1, source_target_pairs={{0,8},{4,12},{8,0},{12,4},{16,24},{20,28},{24,16},{28,20},{1,9},{5... | collective-permute-start | bytes 884744 | tf_op jit(solution)/shard_map/ppermute | solution.py:19
  99.3 1.7 %collective-permute-start.31 = (bf16[96,1536]{1,0:T(8,128)(2,1)S(1)}, bf16[96,1536]{1,0:T(8,128)(2,1)S(1)}, u32[]{:S(2)}, u32[]{:S(2)}) collective-permute-start(bf16[96,1536]{1,0:T(8,128)(2,1)S(1)} %get-tuple-element.82), channel_id=1, source_target_pairs={{0,24},{4,28},{8,16},{12,20},{16,8},{20,12},{24,0},{28,4},{1,25},{... | collective-permute-start | bytes 884744 | tf_op jit(solution)/shard_map/ppermute | solution.py:19
  100.9 6.3 %collective-permute-done.32 = bf16[96,2048]{1,0:T(8,128)(2,1)S(1)} collective-permute-done((bf16[96,2048]{1,0:T(8,128)(2,1)S(1)}, bf16[96,2048]{1,0:T(8,128)(2,1)S(1)}, u32[]{:S(2)}, u32[]{:S(2)}) %collective-permute-start.32) | collective-permute-done | bytes 393248 | tf_op jit(solution)/shard_map/ppermute | solution.py:19
  107.4 1.7 %collective-permute-start.27 = (bf16[128,768]{1,0:T(8,128)(2,1)S(1)}, bf16[128,768]{1,0:T(8,128)(2,1)S(1)}, u32[]{:S(2)}, u32[]{:S(2)}) collective-permute-start(bf16[128,768]{1,0:T(8,128)(2,1)S(1)} %get-tuple-element.76), channel_id=1, source_target_pairs={{0,1},{1,0},{2,3},{3,2},{4,5},{5,4},{6,7},{7,6},{8,9},{9,8},{10,11... | collective-permute-start | bytes 589832 | tf_op jit(solution)/shard_map/ppermute | solution.py:19
  109.1 0.9 fusion.1
  110.0 3.5 %collective-permute-done.27.refs_1_ = bf16[128,768]{1,0:T(8,128)(2,1)S(1)} collective-permute-done((bf16[128,768]{1,0:T(8,128)(2,1)S(1)}, bf16[128,768]{1,0:T(8,128)(2,1)S(1)}, u32[]{:S(2)}, u32[]{:S(2)}) %collective-permute-start.27) | collective-permute-done | bytes 196640 | tf_op jit(solution)/shard_map/ppermute | solution.py:19
  113.5 2.5 %collective-permute-start.28 = (bf16[64,768]{1,0:T(8,128)(2,1)S(1)}, bf16[64,768]{1,0:T(8,128)(2,1)S(1)}, u32[]{:S(2)}, u32[]{:S(2)}) collective-permute-start(bf16[64,768]{1,0:T(8,128)(2,1)S(1)} %get-tuple-element.78), channel_id=1, source_target_pairs={{0,2},{1,3},{2,0},{3,1},{4,6},{5,7},{6,4},{7,5},{8,10},{9,11},{10,... | collective-permute-start | bytes 294920 | tf_op jit(solution)/shard_map/ppermute | solution.py:19
  116.1 3.3 %collective-permute-done.31 = bf16[96,1536]{1,0:T(8,128)(2,1)S(1)} collective-permute-done((bf16[96,1536]{1,0:T(8,128)(2,1)S(1)}, bf16[96,1536]{1,0:T(8,128)(2,1)S(1)}, u32[]{:S(2)}, u32[]{:S(2)}) %collective-permute-start.31) | collective-permute-done | bytes 294944 | tf_op jit(solution)/shard_map/ppermute | solution.py:19
  119.5 0.9 fusion.2
  120.4 0.7 fusion
  (64 shorter events, 7.1 us)
Async XLA Ops:
  0.6 24.2 %copy-start.4 = (bf16[96,512]{1,0:T(8,128)(2,1)S(1)}, bf16[96,512]{1,0:T(8,128)(2,1)}, u32[]{:S(2)}) copy-start(bf16[96,512]{1,0:T(8,128)(2,1)} %refs_0_.3) | copy-start | bytes 294916
  0.6 24.2 %copy-start.5 = (bf16[96,512]{1,0:T(8,128)(2,1)S(1)}, bf16[96,512]{1,0:T(8,128)(2,1)}, u32[]{:S(2)}) copy-start(bf16[96,512]{1,0:T(8,128)(2,1)} %refs_1_.4) | copy-start | bytes 294916
  0.7 24.2 %copy-start.6 = (bf16[96,512]{1,0:T(8,128)(2,1)S(1)}, bf16[96,512]{1,0:T(8,128)(2,1)}, u32[]{:S(2)}) copy-start(bf16[96,512]{1,0:T(8,128)(2,1)} %refs_2_.4) | copy-start | bytes 294916
  0.7 24.2 %copy-start.7 = (bf16[96,512]{1,0:T(8,128)(2,1)S(1)}, bf16[96,512]{1,0:T(8,128)(2,1)}, u32[]{:S(2)}) copy-start(bf16[96,512]{1,0:T(8,128)(2,1)} %refs_3_.4) | copy-start | bytes 294916
  2.7 13.5 %collective-permute-start.1 = (bf16[64,1536]{1,0:T(8,128)(2,1)}, bf16[64,1536]{1,0:T(8,128)(2,1)S(1)}, u32[]{:S(2)}, u32[]{:S(2)}) collective-permute-start(bf16[64,1536]{1,0:T(8,128)(2,1)} %get-tuple-element.46.refs_2_), channel_id=1, source_target_pairs={{0,2},{1,3},{2,0},{3,1},{4,6},{5,7},{6,4},{7,5},{8,10},{9,11},{10,... | collective-permute-start | bytes 589832 | tf_op jit(solution)/shard_map/ppermute | solution.py:19
  6.8 13.2 %collective-permute-start.3 = (bf16[96,1536]{1,0:T(8,128)(2,1)}, bf16[96,1536]{1,0:T(8,128)(2,1)S(1)}, u32[]{:S(2)}, u32[]{:S(2)}) collective-permute-start(bf16[96,1536]{1,0:T(8,128)(2,1)} %get-tuple-element.48.refs_0_), channel_id=1, source_target_pairs={{0,24},{4,28},{8,16},{12,20},{16,8},{20,12},{24,0},{28,4},{1,25},{... | collective-permute-start | bytes 884744 | tf_op jit(solution)/shard_map/ppermute | solution.py:19
  9.3 13.4 %collective-permute-start.4 = (bf16[96,1536]{1,0:T(8,128)(2,1)}, bf16[96,1536]{1,0:T(8,128)(2,1)S(1)}, u32[]{:S(2)}, u32[]{:S(2)}) collective-permute-start(bf16[96,1536]{1,0:T(8,128)(2,1)} %get-tuple-element.48.refs_0_), channel_id=1, source_target_pairs={{0,16},{4,20},{8,24},{12,28},{16,0},{20,4},{24,8},{28,12},{1,17},{... | collective-permute-start | bytes 884744 | tf_op jit(solution)/shard_map/ppermute | solution.py:19
  9.8 13.0 %collective-permute-start.5 = (bf16[96,1536]{1,0:T(8,128)(2,1)}, bf16[96,1536]{1,0:T(8,128)(2,1)S(1)}, u32[]{:S(2)}, u32[]{:S(2)}) collective-permute-start(bf16[96,1536]{1,0:T(8,128)(2,1)} %get-tuple-element.48.refs_0_), channel_id=1, source_target_pairs={{0,8},{4,12},{8,0},{12,4},{16,24},{20,28},{24,16},{28,20},{1,9},{5... | collective-permute-start | bytes 884744 | tf_op jit(solution)/shard_map/ppermute | solution.py:19
  10.3 9.7 %collective-permute-start = (bf16[64,1536]{1,0:T(8,128)(2,1)}, bf16[64,1536]{1,0:T(8,128)(2,1)S(1)}, u32[]{:S(2)}, u32[]{:S(2)}) collective-permute-start(bf16[64,1536]{1,0:T(8,128)(2,1)} %get-tuple-element.46.refs_2_), channel_id=1, source_target_pairs={{0,1},{1,0},{2,3},{3,2},{4,5},{5,4},{6,7},{7,6},{8,9},{9,8},{10,11... | collective-permute-start | bytes 589832 | tf_op jit(solution)/shard_map/ppermute | solution.py:19
  16.3 7.1 %collective-permute-start.2 = (bf16[64,1536]{1,0:T(8,128)(2,1)S(1)}, bf16[64,1536]{1,0:T(8,128)(2,1)S(1)}, u32[]{:S(2)}, u32[]{:S(2)}) collective-permute-start(bf16[64,1536]{1,0:T(8,128)(2,1)S(1)} %collective-permute-done.1.refs_4_.refs_5_), channel_id=1, source_target_pairs={{0,1},{1,0},{2,3},{3,2},{4,5},{5,4},{6,7},{7,6},{8,9},{9,8},{10,11... | collective-permute-start | bytes 589832 | tf_op jit(solution)/shard_map/ppermute | solution.py:19
  23.3 1.0 copy-start.2
  24.7 3.9 %copy-start.3 = (bf16[64,1536]{1,0:T(8,128)(2,1)S(1)}, bf16[64,1536]{1,0:T(8,128)(2,1)}, u32[]{:S(2)}) copy-start(bf16[64,1536]{1,0:T(8,128)(2,1)} %get-tuple-element.46.refs_2_) | copy-start | bytes 589828
  24.7 3.9 %copy-start.9 = (f32[768]{0:T(1024)S(1)}, f32[768]{0:T(1024)}, u32[]{:S(2)}) copy-start(f32[768]{0:T(1024)} %refs_1_.3) | copy-start | bytes 9220
  24.7 4.2 %collective-permute-start.6 = (bf16[384,1536]{1,0:T(8,128)(2,1)S(1)}, bf16[384,1536]{1,0:T(8,128)(2,1)}, u32[]{:S(2)}, u32[]{:S(2)}) collective-permute-start(bf16[384,1536]{1,0:T(8,128)(2,1)S(1)} %shard_map.182.refs_2_.refs_4_), channel_id=1, source_target_pairs={{0,4},{4,0},{8,12},{12,8},{16,20},{20,16},{24,28},{28,24},{1,5},{5... | collective-permute-start | bytes 3538952 | tf_op jit(solution)/shard_map/ppermute | solution.py:19
  25.0 12.9 %collective-permute-start.10 = (bf16[96,2048]{1,0:T(8,128)(2,1)S(1)}, bf16[96,2048]{1,0:T(8,128)(2,1)S(1)}, u32[]{:S(2)}, u32[]{:S(2)}) collective-permute-start(bf16[96,2048]{1,0:T(8,128)(2,1)S(1)} %shard_map.184.refs_0_), channel_id=1, source_target_pairs={{0,24},{4,28},{8,16},{12,20},{16,8},{20,12},{24,0},{28,4},{1,25},{... | collective-permute-start | bytes 1179656 | tf_op jit(solution)/shard_map/ppermute | solution.py:19
  27.6 18.3 %collective-permute-start.11 = (bf16[96,2048]{1,0:T(8,128)(2,1)S(1)}, bf16[96,2048]{1,0:T(8,128)(2,1)S(1)}, u32[]{:S(2)}, u32[]{:S(2)}) collective-permute-start(bf16[96,2048]{1,0:T(8,128)(2,1)S(1)} %shard_map.184.refs_0_), channel_id=1, source_target_pairs={{0,16},{4,20},{8,24},{12,28},{16,0},{20,4},{24,8},{28,12},{1,17},{... | collective-permute-start | bytes 1179656 | tf_op jit(solution)/shard_map/ppermute | solution.py:19
  28.1 18.0 %collective-permute-start.12 = (bf16[96,2048]{1,0:T(8,128)(2,1)S(1)}, bf16[96,2048]{1,0:T(8,128)(2,1)S(1)}, u32[]{:S(2)}, u32[]{:S(2)}) collective-permute-start(bf16[96,2048]{1,0:T(8,128)(2,1)S(1)} %shard_map.184.refs_0_), channel_id=1, source_target_pairs={{0,8},{4,12},{8,0},{12,4},{16,24},{20,28},{24,16},{28,20},{1,9},{5... | collective-permute-start | bytes 1179656 | tf_op jit(solution)/shard_map/ppermute | solution.py:19
  28.9 17.2 %copy-start = (bf16[1,64,768]{2,1,0:T(8,128)(2,1)S(1)}, bf16[1,64,768]{2,1,0:T(8,128)(2,1)}, u32[]{:S(2)}) copy-start(bf16[1,64,768]{2,1,0:T(8,128)(2,1)} %param.13) | copy-start | bytes 294916
  28.9 17.2 %copy-start.8 = (f32[768]{0:T(1024)S(1)}, f32[768]{0:T(1024)}, u32[]{:S(2)}) copy-start(f32[768]{0:T(1024)} %refs_0_.5) | copy-start | bytes 9220
  31.5 14.5 %collective-permute-start.7 = (bf16[64,768]{1,0:T(8,128)(2,1)S(1)}, bf16[64,768]{1,0:T(8,128)(2,1)S(1)}, u32[]{:S(2)}, u32[]{:S(2)}) collective-permute-start(bf16[64,768]{1,0:T(8,128)(2,1)S(1)} %get-tuple-element.50), channel_id=1, source_target_pairs={{0,1},{1,0},{2,3},{3,2},{4,5},{5,4},{6,7},{7,6},{8,9},{9,8},{10,11... | collective-permute-start | bytes 294920 | tf_op jit(solution)/shard_map/ppermute | solution.py:19
  32.7 13.4 %collective-permute-start.8 = (bf16[64,768]{1,0:T(8,128)(2,1)S(1)}, bf16[64,768]{1,0:T(8,128)(2,1)S(1)}, u32[]{:S(2)}, u32[]{:S(2)}) collective-permute-start(bf16[64,768]{1,0:T(8,128)(2,1)S(1)} %get-tuple-element.51), channel_id=1, source_target_pairs={{0,2},{1,3},{2,0},{3,1},{4,6},{5,7},{6,4},{7,5},{8,10},{9,11},{10,... | collective-permute-start | bytes 294920 | tf_op jit(solution)/shard_map/ppermute | solution.py:19
  38.0 8.1 %collective-permute-start.9 = (bf16[64,768]{1,0:T(8,128)(2,1)S(1)}, bf16[64,768]{1,0:T(8,128)(2,1)S(1)}, u32[]{:S(2)}, u32[]{:S(2)}) collective-permute-start(bf16[64,768]{1,0:T(8,128)(2,1)S(1)} %get-tuple-element.52), channel_id=1, source_target_pairs={{0,3},{1,2},{2,1},{3,0},{4,7},{5,6},{6,5},{7,4},{8,11},{9,10},{10,... | collective-permute-start | bytes 294920 | tf_op jit(solution)/shard_map/ppermute | solution.py:19
  47.2 4.5 %collective-permute-start.16 = (bf16[384,2048]{1,0:T(8,128)(2,1)S(1)}, bf16[384,2048]{1,0:T(8,128)(2,1)S(1)}, u32[]{:S(2)}, u32[]{:S(2)}) collective-permute-start(bf16[384,2048]{1,0:T(8,128)(2,1)S(1)} %shard_map.186.refs_2_), channel_id=1, source_target_pairs={{0,4},{4,0},{8,12},{12,8},{16,20},{20,16},{24,28},{28,24},{1,5},{5... | collective-permute-start | bytes 4718600 | tf_op jit(solution)/shard_map/ppermute | solution.py:19
  47.3 6.8 %collective-permute-start.13 = (bf16[64,768]{1,0:T(8,128)(2,1)S(1)}, bf16[64,768]{1,0:T(8,128)(2,1)S(1)}, u32[]{:S(2)}, u32[]{:S(2)}) collective-permute-start(bf16[64,768]{1,0:T(8,128)(2,1)S(1)} %get-tuple-element.54.refs_4_), channel_id=1, source_target_pairs={{0,1},{1,0},{2,3},{3,2},{4,5},{5,4},{6,7},{7,6},{8,9},{9,8},{10,11... | collective-permute-start | bytes 294920 | tf_op jit(solution)/shard_map/ppermute | solution.py:19
  48.3 10.8 %collective-permute-start.14 = (bf16[64,768]{1,0:T(8,128)(2,1)S(1)}, bf16[64,768]{1,0:T(8,128)(2,1)S(1)}, u32[]{:S(2)}, u32[]{:S(2)}) collective-permute-start(bf16[64,768]{1,0:T(8,128)(2,1)S(1)} %get-tuple-element.54.refs_4_), channel_id=1, source_target_pairs={{0,2},{1,3},{2,0},{3,1},{4,6},{5,7},{6,4},{7,5},{8,10},{9,11},{10,... | collective-permute-start | bytes 294920 | tf_op jit(solution)/shard_map/ppermute | solution.py:19
  51.1 8.0 %collective-permute-start.15 = (bf16[64,768]{1,0:T(8,128)(2,1)S(1)}, bf16[64,768]{1,0:T(8,128)(2,1)S(1)}, u32[]{:S(2)}, u32[]{:S(2)}) collective-permute-start(bf16[64,768]{1,0:T(8,128)(2,1)S(1)} %get-tuple-element.54.refs_4_), channel_id=1, source_target_pairs={{0,3},{1,2},{2,1},{3,0},{4,7},{5,6},{6,5},{7,4},{8,11},{9,10},{10,... | collective-permute-start | bytes 294920 | tf_op jit(solution)/shard_map/ppermute | solution.py:19
  51.8 7.3 %copy-start.10 = (f32[4,9]{1,0:T(4,128)S(1)}, f32[4,9]{1,0:T(4,128)}, u32[]{:S(2)}) copy-start(f32[4,9]{1,0:T(4,128)} %refs_1_.5) | copy-start | bytes 436
  51.8 7.3 %copy-start.11 = (s32[1,256]{1,0:T(1,128)S(1)}, s32[1,256]{1,0:T(1,128)}, u32[]{:S(2)}) copy-start(s32[1,256]{1,0:T(1,128)} %refs_2_.5) | copy-start | bytes 3076
  51.8 7.3 %copy-start.12 = (s32[1,256]{1,0:T(1,128)S(1)}, s32[1,256]{1,0:T(1,128)}, u32[]{:S(2)}) copy-start(s32[1,256]{1,0:T(1,128)} %refs_3_.5) | copy-start | bytes 3076
  65.4 13.0 %collective-permute-start.23 = (bf16[384,2048]{1,0:T(8,128)(2,1)S(1)}, bf16[384,2048]{1,0:T(8,128)(2,1)S(1)}, u32[]{:S(2)}, u32[]{:S(2)}) collective-permute-start(bf16[384,2048]{1,0:T(8,128)(2,1)S(1)} %get-tuple-element.70), channel_id=1, source_target_pairs={{0,4},{4,0},{8,12},{12,8},{16,20},{20,16},{24,28},{28,24},{1,5},{5... | collective-permute-start | bytes 4718600 | tf_op jit(solution)/shard_map/ppermute | solution.py:19
  65.5 5.5 %collective-permute-start.17 = (bf16[64,768]{1,0:T(8,128)(2,1)S(1)}, bf16[64,768]{1,0:T(8,128)(2,1)S(1)}, u32[]{:S(2)}, u32[]{:S(2)}) collective-permute-start(bf16[64,768]{1,0:T(8,128)(2,1)S(1)} %get-tuple-element.63), channel_id=1, source_target_pairs={{0,1},{1,0},{2,3},{3,2},{4,5},{5,4},{6,7},{7,6},{8,9},{9,8},{10,11... | collective-permute-start | bytes 294920 | tf_op jit(solution)/shard_map/ppermute | solution.py:19
  67.6 10.8 %collective-permute-start.18 = (bf16[64,768]{1,0:T(8,128)(2,1)S(1)}, bf16[64,768]{1,0:T(8,128)(2,1)S(1)}, u32[]{:S(2)}, u32[]{:S(2)}) collective-permute-start(bf16[64,768]{1,0:T(8,128)(2,1)S(1)} %get-tuple-element.64), channel_id=1, source_target_pairs={{0,2},{1,3},{2,0},{3,1},{4,6},{5,7},{6,4},{7,5},{8,10},{9,11},{10,... | collective-permute-start | bytes 294920 | tf_op jit(solution)/shard_map/ppermute | solution.py:19
  68.7 9.7 %collective-permute-start.19 = (bf16[64,768]{1,0:T(8,128)(2,1)S(1)}, bf16[64,768]{1,0:T(8,128)(2,1)S(1)}, u32[]{:S(2)}, u32[]{:S(2)}) collective-permute-start(bf16[64,768]{1,0:T(8,128)(2,1)S(1)} %get-tuple-element.65), channel_id=1, source_target_pairs={{0,3},{1,2},{2,1},{3,0},{4,7},{5,6},{6,5},{7,4},{8,11},{9,10},{10,... | collective-permute-start | bytes 294920 | tf_op jit(solution)/shard_map/ppermute | solution.py:19
  78.4 2.7 %copy-start.1 = (bf16[1,64,768]{2,1,0:T(8,128)(2,1)S(1)}, bf16[1,64,768]{2,1,0:T(8,128)(2,1)}, u32[]{:S(2)}) copy-start(bf16[1,64,768]{2,1,0:T(8,128)(2,1)} %param.25) | copy-start | bytes 294916
  78.8 13.9 %collective-permute-start.24 = (bf16[96,2048]{1,0:T(8,128)(2,1)S(1)}, bf16[96,2048]{1,0:T(8,128)(2,1)S(1)}, u32[]{:S(2)}, u32[]{:S(2)}) collective-permute-start(bf16[96,2048]{1,0:T(8,128)(2,1)S(1)} %get-tuple-element.71), channel_id=1, source_target_pairs={{0,8},{4,12},{8,0},{12,4},{16,24},{20,28},{24,16},{28,20},{1,9},{5... | collective-permute-start | bytes 1179656 | tf_op jit(solution)/shard_map/ppermute | solution.py:19
  80.3 12.4 %collective-permute-start.25 = (bf16[96,2048]{1,0:T(8,128)(2,1)S(1)}, bf16[96,2048]{1,0:T(8,128)(2,1)S(1)}, u32[]{:S(2)}, u32[]{:S(2)}) collective-permute-start(bf16[96,2048]{1,0:T(8,128)(2,1)S(1)} %get-tuple-element.72), channel_id=1, source_target_pairs={{0,16},{4,20},{8,24},{12,28},{16,0},{20,4},{24,8},{28,12},{1,17},{... | collective-permute-start | bytes 1179656 | tf_op jit(solution)/shard_map/ppermute | solution.py:19
  81.3 5.7 %collective-permute-start.20 = (bf16[64,768]{1,0:T(8,128)(2,1)S(1)}, bf16[64,768]{1,0:T(8,128)(2,1)S(1)}, u32[]{:S(2)}, u32[]{:S(2)}) collective-permute-start(bf16[64,768]{1,0:T(8,128)(2,1)S(1)} %shard_map.189.refs_5_), channel_id=1, source_target_pairs={{0,1},{1,0},{2,3},{3,2},{4,5},{5,4},{6,7},{7,6},{8,9},{9,8},{10,11... | collective-permute-start | bytes 294920 | tf_op jit(solution)/shard_map/ppermute | solution.py:19
  83.3 9.4 %collective-permute-start.21 = (bf16[64,768]{1,0:T(8,128)(2,1)S(1)}, bf16[64,768]{1,0:T(8,128)(2,1)S(1)}, u32[]{:S(2)}, u32[]{:S(2)}) collective-permute-start(bf16[64,768]{1,0:T(8,128)(2,1)S(1)} %shard_map.189.refs_5_), channel_id=1, source_target_pairs={{0,2},{1,3},{2,0},{3,1},{4,6},{5,7},{6,4},{7,5},{8,10},{9,11},{10,... | collective-permute-start | bytes 294920 | tf_op jit(solution)/shard_map/ppermute | solution.py:19
  84.3 8.4 %collective-permute-start.22 = (bf16[64,768]{1,0:T(8,128)(2,1)S(1)}, bf16[64,768]{1,0:T(8,128)(2,1)S(1)}, u32[]{:S(2)}, u32[]{:S(2)}) collective-permute-start(bf16[64,768]{1,0:T(8,128)(2,1)S(1)} %shard_map.189.refs_5_), channel_id=1, source_target_pairs={{0,3},{1,2},{2,1},{3,0},{4,7},{5,6},{6,5},{7,4},{8,11},{9,10},{10,... | collective-permute-start | bytes 294920 | tf_op jit(solution)/shard_map/ppermute | solution.py:19
  94.2 2.9 %collective-permute-start.26 = (bf16[384,1536]{1,0:T(8,128)(2,1)S(1)}, bf16[384,1536]{1,0:T(8,128)(2,1)S(1)}, u32[]{:S(2)}, u32[]{:S(2)}) collective-permute-start(bf16[384,1536]{1,0:T(8,128)(2,1)S(1)} %get-tuple-element.74), channel_id=1, source_target_pairs={{0,4},{4,0},{8,12},{12,8},{16,20},{20,16},{24,28},{28,24},{1,5},{5... | collective-permute-start | bytes 3538952 | tf_op jit(solution)/shard_map/ppermute | solution.py:19
  94.3 12.9 %collective-permute-start.32 = (bf16[96,2048]{1,0:T(8,128)(2,1)S(1)}, bf16[96,2048]{1,0:T(8,128)(2,1)S(1)}, u32[]{:S(2)}, u32[]{:S(2)}) collective-permute-start(bf16[96,2048]{1,0:T(8,128)(2,1)S(1)} %get-tuple-element.84), channel_id=1, source_target_pairs={{0,24},{4,28},{8,16},{12,20},{16,8},{20,12},{24,0},{28,4},{1,25},{... | collective-permute-start | bytes 1179656 | tf_op jit(solution)/shard_map/ppermute | solution.py:19
  97.4 18.7 %collective-permute-start.29 = (bf16[96,1536]{1,0:T(8,128)(2,1)S(1)}, bf16[96,1536]{1,0:T(8,128)(2,1)S(1)}, u32[]{:S(2)}, u32[]{:S(2)}) collective-permute-start(bf16[96,1536]{1,0:T(8,128)(2,1)S(1)} %get-tuple-element.80), channel_id=1, source_target_pairs={{0,8},{4,12},{8,0},{12,4},{16,24},{20,28},{24,16},{28,20},{1,9},{5... | collective-permute-start | bytes 884744 | tf_op jit(solution)/shard_map/ppermute | solution.py:19
  98.7 17.4 %collective-permute-start.30 = (bf16[96,1536]{1,0:T(8,128)(2,1)S(1)}, bf16[96,1536]{1,0:T(8,128)(2,1)S(1)}, u32[]{:S(2)}, u32[]{:S(2)}) collective-permute-start(bf16[96,1536]{1,0:T(8,128)(2,1)S(1)} %get-tuple-element.81), channel_id=1, source_target_pairs={{0,16},{4,20},{8,24},{12,28},{16,0},{20,4},{24,8},{28,12},{1,17},{... | collective-permute-start | bytes 884744 | tf_op jit(solution)/shard_map/ppermute | solution.py:19
  99.3 20.1 %collective-permute-start.31 = (bf16[96,1536]{1,0:T(8,128)(2,1)S(1)}, bf16[96,1536]{1,0:T(8,128)(2,1)S(1)}, u32[]{:S(2)}, u32[]{:S(2)}) collective-permute-start(bf16[96,1536]{1,0:T(8,128)(2,1)S(1)} %get-tuple-element.82), channel_id=1, source_target_pairs={{0,24},{4,28},{8,16},{12,20},{16,8},{20,12},{24,0},{28,4},{1,25},{... | collective-permute-start | bytes 884744 | tf_op jit(solution)/shard_map/ppermute | solution.py:19
  107.4 6.1 %collective-permute-start.27 = (bf16[128,768]{1,0:T(8,128)(2,1)S(1)}, bf16[128,768]{1,0:T(8,128)(2,1)S(1)}, u32[]{:S(2)}, u32[]{:S(2)}) collective-permute-start(bf16[128,768]{1,0:T(8,128)(2,1)S(1)} %get-tuple-element.76), channel_id=1, source_target_pairs={{0,1},{1,0},{2,3},{3,2},{4,5},{5,4},{6,7},{7,6},{8,9},{9,8},{10,11... | collective-permute-start | bytes 589832 | tf_op jit(solution)/shard_map/ppermute | solution.py:19
  113.5 6.8 %collective-permute-start.28 = (bf16[64,768]{1,0:T(8,128)(2,1)S(1)}, bf16[64,768]{1,0:T(8,128)(2,1)S(1)}, u32[]{:S(2)}, u32[]{:S(2)}) collective-permute-start(bf16[64,768]{1,0:T(8,128)(2,1)S(1)} %get-tuple-element.78), channel_id=1, source_target_pairs={{0,2},{1,3},{2,0},{3,1},{4,6},{5,7},{6,4},{7,5},{8,10},{9,11},{10,... | collective-permute-start | bytes 294920 | tf_op jit(solution)/shard_map/ppermute | solution.py:19

commit v8 on v7

--- a/solution.py
+++ b/solution.py
@@ -180,24 +180,27 @@
     span_q = jnp.transpose(jnp.broadcast_to(span_k, (8, frames)))[:, :1]
     block = min(frames, 256)
     reach = min(window, (frames - 1) // SPAN)
+    starts = range(0, frames, block)
+    masks = []
+    for first in starts:
+        mine = slice(first, first + block)
+        distance = jnp.where(seg_q[mine, :] == seg_k, span_q[mine, :] - span_k, -1)
+        masks.append([distance == far for far in range(reach + 1)])
     for head in range(heads):
         cols = slice(head * width, (head + 1) * width)
         key_cols = slice(inner + head * width, inner + (head + 1) * width)
         value_cols = slice(2 * inner + head * width, 2 * inner + (head + 1) * width)
         key = qkv[:, key_cols]
         value = qkv[:, value_cols]
-        for first in range(0, frames, block):
+        for first, far_masks in zip(starts, masks):
             mine = slice(first, first + block)
             query = qkv[mine, cols]
-            distance = span_q[mine, :] - span_k
-            allowed = (seg_q[mine, :] == seg_k) & (distance >= 0) & (distance <= window)
-            added = jnp.full((block, frames), bias[head, 0], F32)
-            for far in range(1, reach + 1):
-                added = jnp.where(distance == far, bias[head, far], added)
+            added = jnp.full((block, frames), -1e30, F32)
+            for far, mask in enumerate(far_masks):
+                added = jnp.where(mask, bias[head, far], added)
             scores = dot(query, key, 1, 1) * scale + added
-            scores = jnp.where(allowed, scores, -1e30)
             expo = jnp.exp(scores - jnp.max(scores, axis=-1, keepdims=True))
-            soft = expo / jnp.sum(expo, axis=-1, keepdims=True)
+            soft = expo * (1.0 / jnp.sum(expo, axis=-1, keepdims=True))
             low = soft.astype(BF)
             context[mine, cols] = dot(low, value, 1, 0).astype(BF)
             slope = grad_context[mine, cols]

time: 121 us -> 121 us (level)
  no operation moved by 1% of the time
where the time goes in v8:
time: 121 us
  waiting for transfers between devices  53.1 us (44%)
  starting transfers between devices  45.8 us (38%)
  Pallas kernels  17.4 us (14%)
  local copies, waits for them, and re-layouts  2.75 us (2%)
    ppermute x33, waiting for transfers between devices, exchange(): lax.ppermute(values, axis, [(one, one ^ mask) for one in range(size)])  53.1 us
    ppermute x33, starting transfers between devices, exchange(): lax.ppermute(values, axis, [(one, one ^ mask) for one in range(size)])  45.8 us
    pallas_call x15, Pallas kernels, call(): pl.pallas_call(lambda *refs: body(*refs[:count], *refs[count + len(after)...  17.4 us
  transfers between devices with their start and end apart: 33, of which 18 were waited for; matrix products, arithmetic and copies ran while one was open for 2% of the time, Pallas kernels for 5%

profile of v8, /device:TPU:0, one launch (start us, length us, event | category | flops | bytes accessed | tf_op | source)
XLA Modules:
  0.0 121.0 jit_solution(2994876188374205918)
XLA Ops:
  0.7 2.1 %shard_map.180 = (bf16[64,1536]{1,0:T(8,128)(2,1)}, bf16[96,1536]{1,0:T(8,128)(2,1)}) custom-call(bf16[64,768]{1,0:T(8,128)(2,1)} %bitcast.6, bf16[64,768]{1,0:T(8,128)(2,1)} %bitcast.8, bf16[96,768]{1,0:T(8,128)(2,1)} %refs_2_.3, bf16[96,768]{1,0:T(8,128)(2,1)} %refs_3_.3), custom_call_target="tpu_custom_call" | custom-call | bytes 983040 | tf_op jit(solution)/shard_map/pallas_call | solution.py:31
  2.7 4.1 %collective-permute-start.1 = (bf16[64,1536]{1,0:T(8,128)(2,1)}, bf16[64,1536]{1,0:T(8,128)(2,1)S(1)}, u32[]{:S(2)}, u32[]{:S(2)}) collective-permute-start(bf16[64,1536]{1,0:T(8,128)(2,1)} %get-tuple-element.46.refs_2_), channel_id=1, source_target_pairs={{0,2},{1,3},{2,0},{3,1},{4,6},{5,7},{6,4},{7,5},{8,10},{9,11},{10,... | collective-permute-start | bytes 589832 | tf_op jit(solution)/shard_map/ppermute | solution.py:19
  6.8 2.4 %collective-permute-start.3 = (bf16[96,1536]{1,0:T(8,128)(2,1)}, bf16[96,1536]{1,0:T(8,128)(2,1)S(1)}, u32[]{:S(2)}, u32[]{:S(2)}) collective-permute-start(bf16[96,1536]{1,0:T(8,128)(2,1)} %get-tuple-element.48.refs_0_), channel_id=1, source_target_pairs={{0,24},{4,28},{8,16},{12,20},{16,8},{20,12},{24,0},{28,4},{1,25},{... | collective-permute-start | bytes 884744 | tf_op jit(solution)/shard_map/ppermute | solution.py:19
  10.3 1.6 %collective-permute-start = (bf16[64,1536]{1,0:T(8,128)(2,1)}, bf16[64,1536]{1,0:T(8,128)(2,1)S(1)}, u32[]{:S(2)}, u32[]{:S(2)}) collective-permute-start(bf16[64,1536]{1,0:T(8,128)(2,1)} %get-tuple-element.46.refs_2_), channel_id=1, source_target_pairs={{0,1},{1,0},{2,3},{3,2},{4,5},{5,4},{6,7},{7,6},{8,9},{9,8},{10,11... | collective-permute-start | bytes 589832 | tf_op jit(solution)/shard_map/ppermute | solution.py:19
  11.9 4.4 %collective-permute-done.1.refs_4_.refs_5_ = bf16[64,1536]{1,0:T(8,128)(2,1)S(1)} collective-permute-done((bf16[64,1536]{1,0:T(8,128)(2,1)}, bf16[64,1536]{1,0:T(8,128)(2,1)S(1)}, u32[]{:S(2)}, u32[]{:S(2)}) %collective-permute-start.1) | collective-permute-done | bytes 196640 | tf_op jit(solution)/shard_map/ppermute | solution.py:19
  16.3 0.8 collective-permute-start.2
  17.0 3.0 %collective-permute-done.refs_3_.refs_4_ = bf16[64,1536]{1,0:T(8,128)(2,1)S(1)} collective-permute-done((bf16[64,1536]{1,0:T(8,128)(2,1)}, bf16[64,1536]{1,0:T(8,128)(2,1)S(1)}, u32[]{:S(2)}, u32[]{:S(2)}) %collective-permute-start) | collective-permute-done | bytes 196640 | tf_op jit(solution)/shard_map/ppermute | solution.py:19
  20.1 2.7 %collective-permute-done.4.refs_2_ = bf16[96,1536]{1,0:T(8,128)(2,1)S(1)} collective-permute-done((bf16[96,1536]{1,0:T(8,128)(2,1)}, bf16[96,1536]{1,0:T(8,128)(2,1)S(1)}, u32[]{:S(2)}, u32[]{:S(2)}) %collective-permute-start.4) | collective-permute-done | bytes 294944 | tf_op jit(solution)/shard_map/ppermute | solution.py:19
  23.3 1.0 copy-done.2
  25.0 2.6 %collective-permute-start.10 = (bf16[96,2048]{1,0:T(8,128)(2,1)S(1)}, bf16[96,2048]{1,0:T(8,128)(2,1)S(1)}, u32[]{:S(2)}, u32[]{:S(2)}) collective-permute-start(bf16[96,2048]{1,0:T(8,128)(2,1)S(1)} %shard_map.184.refs_0_), channel_id=1, source_target_pairs={{0,24},{4,28},{8,16},{12,20},{16,8},{20,12},{24,0},{28,4},{1,25},{... | collective-permute-start | bytes 1179656 | tf_op jit(solution)/shard_map/ppermute | solution.py:19
  29.0 2.5 %shard_map.183 = (f32[256,768]{1,0:T(8,128)S(1)}, bf16[256,768]{1,0:T(8,128)(2,1)S(1)}, bf16[768,768]{1,0:T(8,128)(2,1)S(1)}, bf16[64,768]{1,0:T(8,128)(2,1)S(1)...) custom-call(s32[1]{0:T(128)} %bitcast.1.refs_0_, ...), custom_call_target="tpu_custom_call" | custom-call | flops 603979776 | bytes 5505028 | tf_op jit(solution)/shard_map/pallas_call | solution.py:31
  31.5 1.2 collective-permute-start.7
  32.7 2.7 %collective-permute-start.8 = (bf16[64,768]{1,0:T(8,128)(2,1)S(1)}, bf16[64,768]{1,0:T(8,128)(2,1)S(1)}, u32[]{:S(2)}, u32[]{:S(2)}) collective-permute-start(bf16[64,768]{1,0:T(8,128)(2,1)S(1)} %get-tuple-element.51), channel_id=1, source_target_pairs={{0,2},{1,3},{2,0},{3,1},{4,6},{5,7},{6,4},{7,5},{8,10},{9,11},{10,... | collective-permute-start | bytes 294920 | tf_op jit(solution)/shard_map/ppermute | solution.py:19
  35.4 2.6 %collective-permute-done.10.refs_6_.refs_1_ = bf16[96,2048]{1,0:T(8,128)(2,1)S(1)} collective-permute-done((bf16[96,2048]{1,0:T(8,128)(2,1)S(1)}, bf16[96,2048]{1,0:T(8,128)(2,1)S(1)}, u32[]{:S(2)}, u32[]{:S(2)}) %collective-permute-start.10) | collective-permute-done | bytes 393248 | tf_op jit(solution)/shard_map/ppermute | solution.py:19
  38.0 3.2 %collective-permute-start.9 = (bf16[64,768]{1,0:T(8,128)(2,1)S(1)}, bf16[64,768]{1,0:T(8,128)(2,1)S(1)}, u32[]{:S(2)}, u32[]{:S(2)}) collective-permute-start(bf16[64,768]{1,0:T(8,128)(2,1)S(1)} %get-tuple-element.52), channel_id=1, source_target_pairs={{0,3},{1,2},{2,1},{3,0},{4,7},{5,6},{6,5},{7,4},{8,11},{9,10},{10,... | collective-permute-start | bytes 294920 | tf_op jit(solution)/shard_map/ppermute | solution.py:19
  41.2 4.7 %collective-permute-done.11.refs_7_.refs_2_ = bf16[96,2048]{1,0:T(8,128)(2,1)S(1)} collective-permute-done((bf16[96,2048]{1,0:T(8,128)(2,1)S(1)}, bf16[96,2048]{1,0:T(8,128)(2,1)S(1)}, u32[]{:S(2)}, u32[]{:S(2)}) %collective-permute-start.11) | collective-permute-done | bytes 393248 | tf_op jit(solution)/shard_map/ppermute | solution.py:19
  46.3 0.9 shard_map.186.refs_2_
  47.3 1.0 collective-permute-start.13
  48.3 2.8 %collective-permute-start.14 = (bf16[64,768]{1,0:T(8,128)(2,1)S(1)}, bf16[64,768]{1,0:T(8,128)(2,1)S(1)}, u32[]{:S(2)}, u32[]{:S(2)}) collective-permute-start(bf16[64,768]{1,0:T(8,128)(2,1)S(1)} %get-tuple-element.54.refs_4_), channel_id=1, source_target_pairs={{0,2},{1,3},{2,0},{3,1},{4,6},{5,7},{6,4},{7,5},{8,10},{9,11},{10,... | collective-permute-start | bytes 294920 | tf_op jit(solution)/shard_map/ppermute | solution.py:19
  51.8 2.0 %shard_map.187 = (bf16[768,2048]{1,0:T(8,128)(2,1)S(1)}, bf16[256,512]{1,0:T(8,128)(2,1)S(1)}) custom-call(s32[1]{0:T(128)} %bitcast.1.refs_0_, bf16[256,768]{1,0:T(8,128)(2,1)S(1)} %get-tuple-element.55.refs_1_.refs_2_, bf16[384,2048]{1,0:T(8,128)(2,1)S(1)} %shard_map.186.refs_2_, bf16[384,2048]{1,0:T(8,128)(2,1)S(1)} %collective-permute-done.16.refs_3_), custom_call_target="tpu_custom_call" | custom-call | flops 201326592 | bytes 6946820 | tf_op jit(solution)/shard_map/pallas_call | solution.py:31
  54.1 5.0 %collective-permute-done.14.refs_6_ = bf16[64,768]{1,0:T(8,128)(2,1)S(1)} collective-permute-done((bf16[64,768]{1,0:T(8,128)(2,1)S(1)}, bf16[64,768]{1,0:T(8,128)(2,1)S(1)}, u32[]{:S(2)}, u32[]{:S(2)}) %collective-permute-start.14) | collective-permute-done | bytes 98336 | tf_op jit(solution)/shard_map/ppermute | solution.py:19
  59.1 4.7 %shard_map.188 = (bf16[256,768]{1,0:T(8,128)(2,1)S(1)}, bf16[256,512]{1,0:T(8,128)(2,1)S(1)}, bf16[256,1536]{1,0:T(8,128)(2,1)S(1)}, bf16[64,768]{1,0:T(8,128)(2...) custom-call(s32[1]{0:T(128)} %bitcast.2.refs_0_, ...), custom_call_target="tpu_custom_call" | custom-call | flops 2013265920 | bytes 6031508 | tf_op jit(solution)/shard_map/pallas_call | solution.py:31
  63.8 1.5 %shard_map.190 = (bf16[384,2048]{1,0:T(8,128)(2,1)S(1)}, bf16[384,2048]{1,0:T(8,128)(2,1)S(1)}) custom-call(s32[1]{0:T(128)} %bitcast.1.refs_0_, bf16[256,768]{1,0:T(8,128)(2,1)S(1)} %get-tuple-element.66.refs_1_, bf16[256,768]{1,0:T(8,128)(2,1)S(1)} %get-tuple-element.55.refs_1_.refs_2_, bf16[256,512]{1,0:T(8,128)(2,1)S(1)} %get-tuple-element.67.refs_3_, ...), custom_call_target="tpu_custom_call" | custom-call | flops 805306368 | bytes 4980740 | tf_op jit(solution)/shard_map/pallas_call | solution.py:31
  65.4 2.2 %collective-permute-start.17 = (bf16[64,768]{1,0:T(8,128)(2,1)S(1)}, bf16[64,768]{1,0:T(8,128)(2,1)S(1)}, u32[]{:S(2)}, u32[]{:S(2)}) collective-permute-start(bf16[64,768]{1,0:T(8,128)(2,1)S(1)} %get-tuple-element.63), channel_id=1, source_target_pairs={{0,1},{1,0},{2,3},{3,2},{4,5},{5,4},{6,7},{7,6},{8,9},{9,8},{10,11... | collective-permute-start | bytes 294920 | tf_op jit(solution)/shard_map/ppermute | solution.py:19
  67.6 1.0 collective-permute-start.18
  68.6 1.4 %collective-permute-start.19 = (bf16[64,768]{1,0:T(8,128)(2,1)S(1)}, bf16[64,768]{1,0:T(8,128)(2,1)S(1)}, u32[]{:S(2)}, u32[]{:S(2)}) collective-permute-start(bf16[64,768]{1,0:T(8,128)(2,1)S(1)} %get-tuple-element.65), channel_id=1, source_target_pairs={{0,3},{1,2},{2,1},{3,0},{4,7},{5,6},{6,5},{7,4},{8,11},{9,10},{10,... | collective-permute-start | bytes 294920 | tf_op jit(solution)/shard_map/ppermute | solution.py:19
  70.0 0.9 collective-permute-done.17.refs_4_.refs_2_
  71.0 7.4 %collective-permute-done.18.refs_5_.refs_3_ = bf16[64,768]{1,0:T(8,128)(2,1)S(1)} collective-permute-done((bf16[64,768]{1,0:T(8,128)(2,1)S(1)}, bf16[64,768]{1,0:T(8,128)(2,1)S(1)}, u32[]{:S(2)}, u32[]{:S(2)}) %collective-permute-start.18) | collective-permute-done | bytes 98336 | tf_op jit(solution)/shard_map/ppermute | solution.py:19
  78.7 1.5 %collective-permute-start.24 = (bf16[96,2048]{1,0:T(8,128)(2,1)S(1)}, bf16[96,2048]{1,0:T(8,128)(2,1)S(1)}, u32[]{:S(2)}, u32[]{:S(2)}) collective-permute-start(bf16[96,2048]{1,0:T(8,128)(2,1)S(1)} %get-tuple-element.71), channel_id=1, source_target_pairs={{0,8},{4,12},{8,0},{12,4},{16,24},{20,28},{24,16},{28,20},{1,9},{5... | collective-permute-start | bytes 1179656 | tf_op jit(solution)/shard_map/ppermute | solution.py:19
  80.3 0.7 collective-permute-start.25
  81.3 1.9 %collective-permute-start.20 = (bf16[64,768]{1,0:T(8,128)(2,1)S(1)}, bf16[64,768]{1,0:T(8,128)(2,1)S(1)}, u32[]{:S(2)}, u32[]{:S(2)}) collective-permute-start(bf16[64,768]{1,0:T(8,128)(2,1)S(1)} %shard_map.189.refs_5_), channel_id=1, source_target_pairs={{0,1},{1,0},{2,3},{3,2},{4,5},{5,4},{6,7},{7,6},{8,9},{9,8},{10,11... | collective-permute-start | bytes 294920 | tf_op jit(solution)/shard_map/ppermute | solution.py:19
  83.2 1.0 collective-permute-start.21
  84.2 1.5 %collective-permute-start.22 = (bf16[64,768]{1,0:T(8,128)(2,1)S(1)}, bf16[64,768]{1,0:T(8,128)(2,1)S(1)}, u32[]{:S(2)}, u32[]{:S(2)}) collective-permute-start(bf16[64,768]{1,0:T(8,128)(2,1)S(1)} %shard_map.189.refs_5_), channel_id=1, source_target_pairs={{0,3},{1,2},{2,1},{3,0},{4,7},{5,6},{6,5},{7,4},{8,11},{9,10},{10,... | collective-permute-start | bytes 294920 | tf_op jit(solution)/shard_map/ppermute | solution.py:19
  85.7 1.3 %collective-permute-done.20.refs_6_ = bf16[64,768]{1,0:T(8,128)(2,1)S(1)} collective-permute-done((bf16[64,768]{1,0:T(8,128)(2,1)S(1)}, bf16[64,768]{1,0:T(8,128)(2,1)S(1)}, u32[]{:S(2)}, u32[]{:S(2)}) %collective-permute-start.20) | collective-permute-done | bytes 98336 | tf_op jit(solution)/shard_map/ppermute | solution.py:19
  87.0 5.6 %collective-permute-done.21.refs_7_ = bf16[64,768]{1,0:T(8,128)(2,1)S(1)} collective-permute-done((bf16[64,768]{1,0:T(8,128)(2,1)S(1)}, bf16[64,768]{1,0:T(8,128)(2,1)S(1)}, u32[]{:S(2)}, u32[]{:S(2)}) %collective-permute-start.21) | collective-permute-done | bytes 98336 | tf_op jit(solution)/shard_map/ppermute | solution.py:19
  92.6 1.5 %shard_map.192 = (bf16[384,1536]{1,0:T(8,128)(2,1)S(1)}, bf16[384,1536]{1,0:T(8,128)(2,1)S(1)}) custom-call(s32[1]{0:T(128)} %bitcast.1.refs_0_, bf16[256,768]{1,0:T(8,128)(2,1)S(1)} %get-tuple-element.47.refs_1_, f32[256,768]{1,0:T(8,128)S(1)} %get-tuple-element.59.refs_2_, bf16[256,768]{1,0:T(8,128)(2,1)S(1)} %get-tuple-element.60.refs_3_, ...), custom_call_target="tpu_custom_call" | custom-call | flops 905969664 | bytes 5505028 | tf_op jit(solution)/shard_map/pallas_call | solution.py:31
  94.2 1.3 %collective-permute-start.32 = (bf16[96,2048]{1,0:T(8,128)(2,1)S(1)}, bf16[96,2048]{1,0:T(8,128)(2,1)S(1)}, u32[]{:S(2)}, u32[]{:S(2)}) collective-permute-start(bf16[96,2048]{1,0:T(8,128)(2,1)S(1)} %get-tuple-element.84), channel_id=1, source_target_pairs={{0,24},{4,28},{8,16},{12,20},{16,8},{20,12},{24,0},{28,4},{1,25},{... | collective-permute-start | bytes 1179656 | tf_op jit(solution)/shard_map/ppermute | solution.py:19
  95.5 1.5 %collective-permute-done.26.refs_1_ = bf16[384,1536]{1,0:T(8,128)(2,1)S(1)} collective-permute-done((bf16[384,1536]{1,0:T(8,128)(2,1)S(1)}, bf16[384,1536]{1,0:T(8,128)(2,1)S(1)}, u32[]{:S(2)}, u32[]{:S(2)}) %collective-permute-start.26) | collective-permute-done | bytes 1179680 | tf_op jit(solution)/shard_map/ppermute | solution.py:19
  97.3 1.3 %collective-permute-start.29 = (bf16[96,1536]{1,0:T(8,128)(2,1)S(1)}, bf16[96,1536]{1,0:T(8,128)(2,1)S(1)}, u32[]{:S(2)}, u32[]{:S(2)}) collective-permute-start(bf16[96,1536]{1,0:T(8,128)(2,1)S(1)} %get-tuple-element.80), channel_id=1, source_target_pairs={{0,8},{4,12},{8,0},{12,4},{16,24},{20,28},{24,16},{28,20},{1,9},{5... | collective-permute-start | bytes 884744 | tf_op jit(solution)/shard_map/ppermute | solution.py:19
  99.2 1.6 %collective-permute-start.31 = (bf16[96,1536]{1,0:T(8,128)(2,1)S(1)}, bf16[96,1536]{1,0:T(8,128)(2,1)S(1)}, u32[]{:S(2)}, u32[]{:S(2)}) collective-permute-start(bf16[96,1536]{1,0:T(8,128)(2,1)S(1)} %get-tuple-element.82), channel_id=1, source_target_pairs={{0,24},{4,28},{8,16},{12,20},{16,8},{20,12},{24,0},{28,4},{1,25},{... | collective-permute-start | bytes 884744 | tf_op jit(solution)/shard_map/ppermute | solution.py:19
  100.9 6.3 %collective-permute-done.32 = bf16[96,2048]{1,0:T(8,128)(2,1)S(1)} collective-permute-done((bf16[96,2048]{1,0:T(8,128)(2,1)S(1)}, bf16[96,2048]{1,0:T(8,128)(2,1)S(1)}, u32[]{:S(2)}, u32[]{:S(2)}) %collective-permute-start.32) | collective-permute-done | bytes 393248 | tf_op jit(solution)/shard_map/ppermute | solution.py:19
  107.3 1.7 %collective-permute-start.27 = (bf16[128,768]{1,0:T(8,128)(2,1)S(1)}, bf16[128,768]{1,0:T(8,128)(2,1)S(1)}, u32[]{:S(2)}, u32[]{:S(2)}) collective-permute-start(bf16[128,768]{1,0:T(8,128)(2,1)S(1)} %get-tuple-element.76), channel_id=1, source_target_pairs={{0,1},{1,0},{2,3},{3,2},{4,5},{5,4},{6,7},{7,6},{8,9},{9,8},{10,11... | collective-permute-start | bytes 589832 | tf_op jit(solution)/shard_map/ppermute | solution.py:19
  109.0 0.9 fusion.1
  109.9 3.5 %collective-permute-done.27.refs_1_ = bf16[128,768]{1,0:T(8,128)(2,1)S(1)} collective-permute-done((bf16[128,768]{1,0:T(8,128)(2,1)S(1)}, bf16[128,768]{1,0:T(8,128)(2,1)S(1)}, u32[]{:S(2)}, u32[]{:S(2)}) %collective-permute-start.27) | collective-permute-done | bytes 196640 | tf_op jit(solution)/shard_map/ppermute | solution.py:19
  113.5 2.5 %collective-permute-start.28 = (bf16[64,768]{1,0:T(8,128)(2,1)S(1)}, bf16[64,768]{1,0:T(8,128)(2,1)S(1)}, u32[]{:S(2)}, u32[]{:S(2)}) collective-permute-start(bf16[64,768]{1,0:T(8,128)(2,1)S(1)} %get-tuple-element.78), channel_id=1, source_target_pairs={{0,2},{1,3},{2,0},{3,1},{4,6},{5,7},{6,4},{7,5},{8,10},{9,11},{10,... | collective-permute-start | bytes 294920 | tf_op jit(solution)/shard_map/ppermute | solution.py:19
  116.0 3.3 %collective-permute-done.31 = bf16[96,1536]{1,0:T(8,128)(2,1)S(1)} collective-permute-done((bf16[96,1536]{1,0:T(8,128)(2,1)S(1)}, bf16[96,1536]{1,0:T(8,128)(2,1)S(1)}, u32[]{:S(2)}, u32[]{:S(2)}) %collective-permute-start.31) | collective-permute-done | bytes 294944 | tf_op jit(solution)/shard_map/ppermute | solution.py:19
  119.5 0.9 fusion.2
  120.3 0.7 fusion
  (64 shorter events, 7.1 us)
Async XLA Ops:
  0.6 24.2 %copy-start.4 = (bf16[96,512]{1,0:T(8,128)(2,1)S(1)}, bf16[96,512]{1,0:T(8,128)(2,1)}, u32[]{:S(2)}) copy-start(bf16[96,512]{1,0:T(8,128)(2,1)} %refs_0_.3) | copy-start | bytes 294916
  0.6 24.2 %copy-start.5 = (bf16[96,512]{1,0:T(8,128)(2,1)S(1)}, bf16[96,512]{1,0:T(8,128)(2,1)}, u32[]{:S(2)}) copy-start(bf16[96,512]{1,0:T(8,128)(2,1)} %refs_1_.4) | copy-start | bytes 294916
  0.7 24.2 %copy-start.6 = (bf16[96,512]{1,0:T(8,128)(2,1)S(1)}, bf16[96,512]{1,0:T(8,128)(2,1)}, u32[]{:S(2)}) copy-start(bf16[96,512]{1,0:T(8,128)(2,1)} %refs_2_.4) | copy-start | bytes 294916
  0.7 24.2 %copy-start.7 = (bf16[96,512]{1,0:T(8,128)(2,1)S(1)}, bf16[96,512]{1,0:T(8,128)(2,1)}, u32[]{:S(2)}) copy-start(bf16[96,512]{1,0:T(8,128)(2,1)} %refs_3_.4) | copy-start | bytes 294916
  2.7 13.5 %collective-permute-start.1 = (bf16[64,1536]{1,0:T(8,128)(2,1)}, bf16[64,1536]{1,0:T(8,128)(2,1)S(1)}, u32[]{:S(2)}, u32[]{:S(2)}) collective-permute-start(bf16[64,1536]{1,0:T(8,128)(2,1)} %get-tuple-element.46.refs_2_), channel_id=1, source_target_pairs={{0,2},{1,3},{2,0},{3,1},{4,6},{5,7},{6,4},{7,5},{8,10},{9,11},{10,... | collective-permute-start | bytes 589832 | tf_op jit(solution)/shard_map/ppermute | solution.py:19
  6.8 13.2 %collective-permute-start.3 = (bf16[96,1536]{1,0:T(8,128)(2,1)}, bf16[96,1536]{1,0:T(8,128)(2,1)S(1)}, u32[]{:S(2)}, u32[]{:S(2)}) collective-permute-start(bf16[96,1536]{1,0:T(8,128)(2,1)} %get-tuple-element.48.refs_0_), channel_id=1, source_target_pairs={{0,24},{4,28},{8,16},{12,20},{16,8},{20,12},{24,0},{28,4},{1,25},{... | collective-permute-start | bytes 884744 | tf_op jit(solution)/shard_map/ppermute | solution.py:19
  9.3 13.4 %collective-permute-start.4 = (bf16[96,1536]{1,0:T(8,128)(2,1)}, bf16[96,1536]{1,0:T(8,128)(2,1)S(1)}, u32[]{:S(2)}, u32[]{:S(2)}) collective-permute-start(bf16[96,1536]{1,0:T(8,128)(2,1)} %get-tuple-element.48.refs_0_), channel_id=1, source_target_pairs={{0,16},{4,20},{8,24},{12,28},{16,0},{20,4},{24,8},{28,12},{1,17},{... | collective-permute-start | bytes 884744 | tf_op jit(solution)/shard_map/ppermute | solution.py:19
  9.8 13.0 %collective-permute-start.5 = (bf16[96,1536]{1,0:T(8,128)(2,1)}, bf16[96,1536]{1,0:T(8,128)(2,1)S(1)}, u32[]{:S(2)}, u32[]{:S(2)}) collective-permute-start(bf16[96,1536]{1,0:T(8,128)(2,1)} %get-tuple-element.48.refs_0_), channel_id=1, source_target_pairs={{0,8},{4,12},{8,0},{12,4},{16,24},{20,28},{24,16},{28,20},{1,9},{5... | collective-permute-start | bytes 884744 | tf_op jit(solution)/shard_map/ppermute | solution.py:19
  10.3 9.7 %collective-permute-start = (bf16[64,1536]{1,0:T(8,128)(2,1)}, bf16[64,1536]{1,0:T(8,128)(2,1)S(1)}, u32[]{:S(2)}, u32[]{:S(2)}) collective-permute-start(bf16[64,1536]{1,0:T(8,128)(2,1)} %get-tuple-element.46.refs_2_), channel_id=1, source_target_pairs={{0,1},{1,0},{2,3},{3,2},{4,5},{5,4},{6,7},{7,6},{8,9},{9,8},{10,11... | collective-permute-start | bytes 589832 | tf_op jit(solution)/shard_map/ppermute | solution.py:19
  16.3 7.1 %collective-permute-start.2 = (bf16[64,1536]{1,0:T(8,128)(2,1)S(1)}, bf16[64,1536]{1,0:T(8,128)(2,1)S(1)}, u32[]{:S(2)}, u32[]{:S(2)}) collective-permute-start(bf16[64,1536]{1,0:T(8,128)(2,1)S(1)} %collective-permute-done.1.refs_4_.refs_5_), channel_id=1, source_target_pairs={{0,1},{1,0},{2,3},{3,2},{4,5},{5,4},{6,7},{7,6},{8,9},{9,8},{10,11... | collective-permute-start | bytes 589832 | tf_op jit(solution)/shard_map/ppermute | solution.py:19
  23.3 1.0 copy-start.2
  24.7 3.9 %copy-start.3 = (bf16[64,1536]{1,0:T(8,128)(2,1)S(1)}, bf16[64,1536]{1,0:T(8,128)(2,1)}, u32[]{:S(2)}) copy-start(bf16[64,1536]{1,0:T(8,128)(2,1)} %get-tuple-element.46.refs_2_) | copy-start | bytes 589828
  24.7 3.9 %copy-start.9 = (f32[768]{0:T(1024)S(1)}, f32[768]{0:T(1024)}, u32[]{:S(2)}) copy-start(f32[768]{0:T(1024)} %refs_1_.3) | copy-start | bytes 9220
  24.7 4.2 %collective-permute-start.6 = (bf16[384,1536]{1,0:T(8,128)(2,1)S(1)}, bf16[384,1536]{1,0:T(8,128)(2,1)}, u32[]{:S(2)}, u32[]{:S(2)}) collective-permute-start(bf16[384,1536]{1,0:T(8,128)(2,1)S(1)} %shard_map.182.refs_2_.refs_4_), channel_id=1, source_target_pairs={{0,4},{4,0},{8,12},{12,8},{16,20},{20,16},{24,28},{28,24},{1,5},{5... | collective-permute-start | bytes 3538952 | tf_op jit(solution)/shard_map/ppermute | solution.py:19
  25.0 12.9 %collective-permute-start.10 = (bf16[96,2048]{1,0:T(8,128)(2,1)S(1)}, bf16[96,2048]{1,0:T(8,128)(2,1)S(1)}, u32[]{:S(2)}, u32[]{:S(2)}) collective-permute-start(bf16[96,2048]{1,0:T(8,128)(2,1)S(1)} %shard_map.184.refs_0_), channel_id=1, source_target_pairs={{0,24},{4,28},{8,16},{12,20},{16,8},{20,12},{24,0},{28,4},{1,25},{... | collective-permute-start | bytes 1179656 | tf_op jit(solution)/shard_map/ppermute | solution.py:19
  27.6 18.3 %collective-permute-start.11 = (bf16[96,2048]{1,0:T(8,128)(2,1)S(1)}, bf16[96,2048]{1,0:T(8,128)(2,1)S(1)}, u32[]{:S(2)}, u32[]{:S(2)}) collective-permute-start(bf16[96,2048]{1,0:T(8,128)(2,1)S(1)} %shard_map.184.refs_0_), channel_id=1, source_target_pairs={{0,16},{4,20},{8,24},{12,28},{16,0},{20,4},{24,8},{28,12},{1,17},{... | collective-permute-start | bytes 1179656 | tf_op jit(solution)/shard_map/ppermute | solution.py:19
  28.1 18.0 %collective-permute-start.12 = (bf16[96,2048]{1,0:T(8,128)(2,1)S(1)}, bf16[96,2048]{1,0:T(8,128)(2,1)S(1)}, u32[]{:S(2)}, u32[]{:S(2)}) collective-permute-start(bf16[96,2048]{1,0:T(8,128)(2,1)S(1)} %shard_map.184.refs_0_), channel_id=1, source_target_pairs={{0,8},{4,12},{8,0},{12,4},{16,24},{20,28},{24,16},{28,20},{1,9},{5... | collective-permute-start | bytes 1179656 | tf_op jit(solution)/shard_map/ppermute | solution.py:19
  28.9 17.2 %copy-start = (bf16[1,64,768]{2,1,0:T(8,128)(2,1)S(1)}, bf16[1,64,768]{2,1,0:T(8,128)(2,1)}, u32[]{:S(2)}) copy-start(bf16[1,64,768]{2,1,0:T(8,128)(2,1)} %param.13) | copy-start | bytes 294916
  28.9 17.2 %copy-start.8 = (f32[768]{0:T(1024)S(1)}, f32[768]{0:T(1024)}, u32[]{:S(2)}) copy-start(f32[768]{0:T(1024)} %refs_0_.5) | copy-start | bytes 9220
  31.5 14.5 %collective-permute-start.7 = (bf16[64,768]{1,0:T(8,128)(2,1)S(1)}, bf16[64,768]{1,0:T(8,128)(2,1)S(1)}, u32[]{:S(2)}, u32[]{:S(2)}) collective-permute-start(bf16[64,768]{1,0:T(8,128)(2,1)S(1)} %get-tuple-element.50), channel_id=1, source_target_pairs={{0,1},{1,0},{2,3},{3,2},{4,5},{5,4},{6,7},{7,6},{8,9},{9,8},{10,11... | collective-permute-start | bytes 294920 | tf_op jit(solution)/shard_map/ppermute | solution.py:19
  32.7 13.4 %collective-permute-start.8 = (bf16[64,768]{1,0:T(8,128)(2,1)S(1)}, bf16[64,768]{1,0:T(8,128)(2,1)S(1)}, u32[]{:S(2)}, u32[]{:S(2)}) collective-permute-start(bf16[64,768]{1,0:T(8,128)(2,1)S(1)} %get-tuple-element.51), channel_id=1, source_target_pairs={{0,2},{1,3},{2,0},{3,1},{4,6},{5,7},{6,4},{7,5},{8,10},{9,11},{10,... | collective-permute-start | bytes 294920 | tf_op jit(solution)/shard_map/ppermute | solution.py:19
  38.0 8.1 %collective-permute-start.9 = (bf16[64,768]{1,0:T(8,128)(2,1)S(1)}, bf16[64,768]{1,0:T(8,128)(2,1)S(1)}, u32[]{:S(2)}, u32[]{:S(2)}) collective-permute-start(bf16[64,768]{1,0:T(8,128)(2,1)S(1)} %get-tuple-element.52), channel_id=1, source_target_pairs={{0,3},{1,2},{2,1},{3,0},{4,7},{5,6},{6,5},{7,4},{8,11},{9,10},{10,... | collective-permute-start | bytes 294920 | tf_op jit(solution)/shard_map/ppermute | solution.py:19
  47.2 4.5 %collective-permute-start.16 = (bf16[384,2048]{1,0:T(8,128)(2,1)S(1)}, bf16[384,2048]{1,0:T(8,128)(2,1)S(1)}, u32[]{:S(2)}, u32[]{:S(2)}) collective-permute-start(bf16[384,2048]{1,0:T(8,128)(2,1)S(1)} %shard_map.186.refs_2_), channel_id=1, source_target_pairs={{0,4},{4,0},{8,12},{12,8},{16,20},{20,16},{24,28},{28,24},{1,5},{5... | collective-permute-start | bytes 4718600 | tf_op jit(solution)/shard_map/ppermute | solution.py:19
  47.3 6.8 %collective-permute-start.13 = (bf16[64,768]{1,0:T(8,128)(2,1)S(1)}, bf16[64,768]{1,0:T(8,128)(2,1)S(1)}, u32[]{:S(2)}, u32[]{:S(2)}) collective-permute-start(bf16[64,768]{1,0:T(8,128)(2,1)S(1)} %get-tuple-element.54.refs_4_), channel_id=1, source_target_pairs={{0,1},{1,0},{2,3},{3,2},{4,5},{5,4},{6,7},{7,6},{8,9},{9,8},{10,11... | collective-permute-start | bytes 294920 | tf_op jit(solution)/shard_map/ppermute | solution.py:19
  48.3 10.8 %collective-permute-start.14 = (bf16[64,768]{1,0:T(8,128)(2,1)S(1)}, bf16[64,768]{1,0:T(8,128)(2,1)S(1)}, u32[]{:S(2)}, u32[]{:S(2)}) collective-permute-start(bf16[64,768]{1,0:T(8,128)(2,1)S(1)} %get-tuple-element.54.refs_4_), channel_id=1, source_target_pairs={{0,2},{1,3},{2,0},{3,1},{4,6},{5,7},{6,4},{7,5},{8,10},{9,11},{10,... | collective-permute-start | bytes 294920 | tf_op jit(solution)/shard_map/ppermute | solution.py:19
  51.1 8.0 %collective-permute-start.15 = (bf16[64,768]{1,0:T(8,128)(2,1)S(1)}, bf16[64,768]{1,0:T(8,128)(2,1)S(1)}, u32[]{:S(2)}, u32[]{:S(2)}) collective-permute-start(bf16[64,768]{1,0:T(8,128)(2,1)S(1)} %get-tuple-element.54.refs_4_), channel_id=1, source_target_pairs={{0,3},{1,2},{2,1},{3,0},{4,7},{5,6},{6,5},{7,4},{8,11},{9,10},{10,... | collective-permute-start | bytes 294920 | tf_op jit(solution)/shard_map/ppermute | solution.py:19
  51.8 7.3 %copy-start.10 = (f32[4,9]{1,0:T(4,128)S(1)}, f32[4,9]{1,0:T(4,128)}, u32[]{:S(2)}) copy-start(f32[4,9]{1,0:T(4,128)} %refs_1_.5) | copy-start | bytes 436
  51.8 7.3 %copy-start.11 = (s32[1,256]{1,0:T(1,128)S(1)}, s32[1,256]{1,0:T(1,128)}, u32[]{:S(2)}) copy-start(s32[1,256]{1,0:T(1,128)} %refs_2_.5) | copy-start | bytes 3076
  51.8 7.3 %copy-start.12 = (s32[1,256]{1,0:T(1,128)S(1)}, s32[1,256]{1,0:T(1,128)}, u32[]{:S(2)}) copy-start(s32[1,256]{1,0:T(1,128)} %refs_3_.5) | copy-start | bytes 3076
  65.3 13.0 %collective-permute-start.23 = (bf16[384,2048]{1,0:T(8,128)(2,1)S(1)}, bf16[384,2048]{1,0:T(8,128)(2,1)S(1)}, u32[]{:S(2)}, u32[]{:S(2)}) collective-permute-start(bf16[384,2048]{1,0:T(8,128)(2,1)S(1)} %get-tuple-element.70), channel_id=1, source_target_pairs={{0,4},{4,0},{8,12},{12,8},{16,20},{20,16},{24,28},{28,24},{1,5},{5... | collective-permute-start | bytes 4718600 | tf_op jit(solution)/shard_map/ppermute | solution.py:19
  65.4 5.5 %collective-permute-start.17 = (bf16[64,768]{1,0:T(8,128)(2,1)S(1)}, bf16[64,768]{1,0:T(8,128)(2,1)S(1)}, u32[]{:S(2)}, u32[]{:S(2)}) collective-permute-start(bf16[64,768]{1,0:T(8,128)(2,1)S(1)} %get-tuple-element.63), channel_id=1, source_target_pairs={{0,1},{1,0},{2,3},{3,2},{4,5},{5,4},{6,7},{7,6},{8,9},{9,8},{10,11... | collective-permute-start | bytes 294920 | tf_op jit(solution)/shard_map/ppermute | solution.py:19
  67.6 10.8 %collective-permute-start.18 = (bf16[64,768]{1,0:T(8,128)(2,1)S(1)}, bf16[64,768]{1,0:T(8,128)(2,1)S(1)}, u32[]{:S(2)}, u32[]{:S(2)}) collective-permute-start(bf16[64,768]{1,0:T(8,128)(2,1)S(1)} %get-tuple-element.64), channel_id=1, source_target_pairs={{0,2},{1,3},{2,0},{3,1},{4,6},{5,7},{6,4},{7,5},{8,10},{9,11},{10,... | collective-permute-start | bytes 294920 | tf_op jit(solution)/shard_map/ppermute | solution.py:19
  68.6 9.7 %collective-permute-start.19 = (bf16[64,768]{1,0:T(8,128)(2,1)S(1)}, bf16[64,768]{1,0:T(8,128)(2,1)S(1)}, u32[]{:S(2)}, u32[]{:S(2)}) collective-permute-start(bf16[64,768]{1,0:T(8,128)(2,1)S(1)} %get-tuple-element.65), channel_id=1, source_target_pairs={{0,3},{1,2},{2,1},{3,0},{4,7},{5,6},{6,5},{7,4},{8,11},{9,10},{10,... | collective-permute-start | bytes 294920 | tf_op jit(solution)/shard_map/ppermute | solution.py:19
  78.3 2.7 %copy-start.1 = (bf16[1,64,768]{2,1,0:T(8,128)(2,1)S(1)}, bf16[1,64,768]{2,1,0:T(8,128)(2,1)}, u32[]{:S(2)}) copy-start(bf16[1,64,768]{2,1,0:T(8,128)(2,1)} %param.25) | copy-start | bytes 294916
  78.7 13.9 %collective-permute-start.24 = (bf16[96,2048]{1,0:T(8,128)(2,1)S(1)}, bf16[96,2048]{1,0:T(8,128)(2,1)S(1)}, u32[]{:S(2)}, u32[]{:S(2)}) collective-permute-start(bf16[96,2048]{1,0:T(8,128)(2,1)S(1)} %get-tuple-element.71), channel_id=1, source_target_pairs={{0,8},{4,12},{8,0},{12,4},{16,24},{20,28},{24,16},{28,20},{1,9},{5... | collective-permute-start | bytes 1179656 | tf_op jit(solution)/shard_map/ppermute | solution.py:19
  80.3 12.4 %collective-permute-start.25 = (bf16[96,2048]{1,0:T(8,128)(2,1)S(1)}, bf16[96,2048]{1,0:T(8,128)(2,1)S(1)}, u32[]{:S(2)}, u32[]{:S(2)}) collective-permute-start(bf16[96,2048]{1,0:T(8,128)(2,1)S(1)} %get-tuple-element.72), channel_id=1, source_target_pairs={{0,16},{4,20},{8,24},{12,28},{16,0},{20,4},{24,8},{28,12},{1,17},{... | collective-permute-start | bytes 1179656 | tf_op jit(solution)/shard_map/ppermute | solution.py:19
  81.3 5.7 %collective-permute-start.20 = (bf16[64,768]{1,0:T(8,128)(2,1)S(1)}, bf16[64,768]{1,0:T(8,128)(2,1)S(1)}, u32[]{:S(2)}, u32[]{:S(2)}) collective-permute-start(bf16[64,768]{1,0:T(8,128)(2,1)S(1)} %shard_map.189.refs_5_), channel_id=1, source_target_pairs={{0,1},{1,0},{2,3},{3,2},{4,5},{5,4},{6,7},{7,6},{8,9},{9,8},{10,11... | collective-permute-start | bytes 294920 | tf_op jit(solution)/shard_map/ppermute | solution.py:19
  83.2 9.4 %collective-permute-start.21 = (bf16[64,768]{1,0:T(8,128)(2,1)S(1)}, bf16[64,768]{1,0:T(8,128)(2,1)S(1)}, u32[]{:S(2)}, u32[]{:S(2)}) collective-permute-start(bf16[64,768]{1,0:T(8,128)(2,1)S(1)} %shard_map.189.refs_5_), channel_id=1, source_target_pairs={{0,2},{1,3},{2,0},{3,1},{4,6},{5,7},{6,4},{7,5},{8,10},{9,11},{10,... | collective-permute-start | bytes 294920 | tf_op jit(solution)/shard_map/ppermute | solution.py:19
  84.2 8.4 %collective-permute-start.22 = (bf16[64,768]{1,0:T(8,128)(2,1)S(1)}, bf16[64,768]{1,0:T(8,128)(2,1)S(1)}, u32[]{:S(2)}, u32[]{:S(2)}) collective-permute-start(bf16[64,768]{1,0:T(8,128)(2,1)S(1)} %shard_map.189.refs_5_), channel_id=1, source_target_pairs={{0,3},{1,2},{2,1},{3,0},{4,7},{5,6},{6,5},{7,4},{8,11},{9,10},{10,... | collective-permute-start | bytes 294920 | tf_op jit(solution)/shard_map/ppermute | solution.py:19
  94.1 2.9 %collective-permute-start.26 = (bf16[384,1536]{1,0:T(8,128)(2,1)S(1)}, bf16[384,1536]{1,0:T(8,128)(2,1)S(1)}, u32[]{:S(2)}, u32[]{:S(2)}) collective-permute-start(bf16[384,1536]{1,0:T(8,128)(2,1)S(1)} %get-tuple-element.74), channel_id=1, source_target_pairs={{0,4},{4,0},{8,12},{12,8},{16,20},{20,16},{24,28},{28,24},{1,5},{5... | collective-permute-start | bytes 3538952 | tf_op jit(solution)/shard_map/ppermute | solution.py:19
  94.2 12.9 %collective-permute-start.32 = (bf16[96,2048]{1,0:T(8,128)(2,1)S(1)}, bf16[96,2048]{1,0:T(8,128)(2,1)S(1)}, u32[]{:S(2)}, u32[]{:S(2)}) collective-permute-start(bf16[96,2048]{1,0:T(8,128)(2,1)S(1)} %get-tuple-element.84), channel_id=1, source_target_pairs={{0,24},{4,28},{8,16},{12,20},{16,8},{20,12},{24,0},{28,4},{1,25},{... | collective-permute-start | bytes 1179656 | tf_op jit(solution)/shard_map/ppermute | solution.py:19
  97.3 18.7 %collective-permute-start.29 = (bf16[96,1536]{1,0:T(8,128)(2,1)S(1)}, bf16[96,1536]{1,0:T(8,128)(2,1)S(1)}, u32[]{:S(2)}, u32[]{:S(2)}) collective-permute-start(bf16[96,1536]{1,0:T(8,128)(2,1)S(1)} %get-tuple-element.80), channel_id=1, source_target_pairs={{0,8},{4,12},{8,0},{12,4},{16,24},{20,28},{24,16},{28,20},{1,9},{5... | collective-permute-start | bytes 884744 | tf_op jit(solution)/shard_map/ppermute | solution.py:19
  98.6 17.4 %collective-permute-start.30 = (bf16[96,1536]{1,0:T(8,128)(2,1)S(1)}, bf16[96,1536]{1,0:T(8,128)(2,1)S(1)}, u32[]{:S(2)}, u32[]{:S(2)}) collective-permute-start(bf16[96,1536]{1,0:T(8,128)(2,1)S(1)} %get-tuple-element.81), channel_id=1, source_target_pairs={{0,16},{4,20},{8,24},{12,28},{16,0},{20,4},{24,8},{28,12},{1,17},{... | collective-permute-start | bytes 884744 | tf_op jit(solution)/shard_map/ppermute | solution.py:19
  99.2 20.1 %collective-permute-start.31 = (bf16[96,1536]{1,0:T(8,128)(2,1)S(1)}, bf16[96,1536]{1,0:T(8,128)(2,1)S(1)}, u32[]{:S(2)}, u32[]{:S(2)}) collective-permute-start(bf16[96,1536]{1,0:T(8,128)(2,1)S(1)} %get-tuple-element.82), channel_id=1, source_target_pairs={{0,24},{4,28},{8,16},{12,20},{16,8},{20,12},{24,0},{28,4},{1,25},{... | collective-permute-start | bytes 884744 | tf_op jit(solution)/shard_map/ppermute | solution.py:19
  107.3 6.1 %collective-permute-start.27 = (bf16[128,768]{1,0:T(8,128)(2,1)S(1)}, bf16[128,768]{1,0:T(8,128)(2,1)S(1)}, u32[]{:S(2)}, u32[]{:S(2)}) collective-permute-start(bf16[128,768]{1,0:T(8,128)(2,1)S(1)} %get-tuple-element.76), channel_id=1, source_target_pairs={{0,1},{1,0},{2,3},{3,2},{4,5},{5,4},{6,7},{7,6},{8,9},{9,8},{10,11... | collective-permute-start | bytes 589832 | tf_op jit(solution)/shard_map/ppermute | solution.py:19
  113.5 6.8 %collective-permute-start.28 = (bf16[64,768]{1,0:T(8,128)(2,1)S(1)}, bf16[64,768]{1,0:T(8,128)(2,1)S(1)}, u32[]{:S(2)}, u32[]{:S(2)}) collective-permute-start(bf16[64,768]{1,0:T(8,128)(2,1)S(1)} %get-tuple-element.78), channel_id=1, source_target_pairs={{0,2},{1,3},{2,0},{3,1},{4,6},{5,7},{6,4},{7,5},{8,10},{9,11},{10,... | collective-permute-start | bytes 294920 | tf_op jit(solution)/shard_map/ppermute | solution.py:19
